TPU v7x, 256 devices: a whole 4x4x8 slice. The times are simulated.
256 devices in a mesh: ha: 16 (over x, z_lo), wa: 16 (over z_hi, y, core).
Axes of the slice: x: 4, y: 4, z: 8 (z_hi: 2, z_lo: 4; z = z_hi * 4 + z_lo), core: 2. Of those that a mesh axis runs over, the one named last changes fastest.
Arguments:
- features: float32 [2, 256, 512, 128], P(None, 'ha', 'wa'), may hold values from -6 to 6
- weight_one: float32 [3, 3, 3, 128, 128], replicated, may hold values from -0.109375 to 0.109375
- flow_feats: float32 [2, 128, 256, 256], P(None, 'ha', 'wa'), may hold values from -6 to 6
- weight_two: float32 [3, 3, 3, 256, 128], replicated, may hold values from -0.078125 to 0.078125
- cotangent: float32 [2, 128, 256, 128], P(None, 'ha', 'wa'), may hold values from -6 to 6
Outputs:
- grad_features: float32 [2, 256, 512, 128], P(None, 'ha', 'wa')
- grad_weight_one: float32 [3, 3, 3, 128, 128], P(None, None, None, 'wa')
- grad_flow: float32 [2, 128, 256, 256], P(None, 'ha', 'wa')
- grad_weight_two: float32 [3, 3, 3, 256, 128], P(None, None, None, 'wa')
All inputs are finite; a program needn't handle non-finite values.
Results may differ from a plain program's by a relative error of at most 0.0003.
Values sent between devices are 32-bit elements; how exact they have to be, the bound alone decides.
No kernel may reach another device: no remote copies, remote signals or barrier semaphores. Data moves between devices by JAX's collectives and lax.ppermute only.
A program may use at most 128 MiB of HBM per device.

v0:
```python
import jax
import jax.numpy as jnp
from jax import lax
from jax.sharding import PartitionSpec as P

exact_mode = lax.Precision.HIGHEST


def extended(block, sides, width):
    for axis, dim in sides:
        count = lax.axis_size(axis)
        forward = [(i, i + 1) for i in range(count - 1)]
        backward = [(target, source) for source, target in forward]
        low = lax.ppermute(
            lax.slice_in_dim(block, block.shape[dim] - width, None, axis=dim), axis, forward
        )
        high = lax.ppermute(lax.slice_in_dim(block, 0, width, axis=dim), axis, backward)
        block = jnp.concatenate([low, block, high], axis=dim)
    return block


def frame_pad(values):
    return jnp.pad(values, ((1, 1), (0, 0), (0, 0), (0, 0)))


def conv_forward(padded, kernel, rows, cols):
    frames = padded.shape[0] - 2
    total = None
    for time_tap in range(3):
        for row_tap in range(3):
            for col_tap in range(3):
                window = padded[
                    time_tap : time_tap + frames, row_tap : row_tap + rows, col_tap : col_tap + cols
                ]
                term = jnp.einsum(
                    "fhwc,cd->fhwd",
                    window,
                    kernel[time_tap, row_tap, col_tap],
                    precision=exact_mode,
                )
                total = term if total is None else total + term
    return total


def conv_adjoint(padded, kernel, rows, cols):
    frames = padded.shape[0] - 2
    total = None
    for time_tap in range(3):
        for row_tap in range(3):
            for col_tap in range(3):
                window = padded[
                    2 - time_tap : 2 - time_tap + frames,
                    2 - row_tap : 2 - row_tap + rows,
                    2 - col_tap : 2 - col_tap + cols,
                ]
                term = jnp.einsum(
                    "fhwd,cd->fhwc",
                    window,
                    kernel[time_tap, row_tap, col_tap],
                    precision=exact_mode,
                )
                total = term if total is None else total + term
    return total


def kernel_terms(padded, gradient, rows, cols):
    frames = gradient.shape[0]
    pieces = []
    for time_tap in range(3):
        for row_tap in range(3):
            for col_tap in range(3):
                window = padded[
                    time_tap : time_tap + frames, row_tap : row_tap + rows, col_tap : col_tap + cols
                ]
                pieces.append(jnp.einsum("fhwc,fhwd->cd", window, gradient, precision=exact_mode))
    stacked = jnp.stack(pieces)
    return stacked.reshape(3, 3, 3, stacked.shape[1], stacked.shape[2])


def silu_slope(values):
    sigma = jax.nn.sigmoid(values)
    return sigma * (1.0 + values * (1.0 - sigma))


def widen(gradient):
    return 0.5 * jnp.repeat(jnp.repeat(gradient, 2, axis=1), 2, axis=2)


def local(features, weight_one, flow_feats, weight_two, cotangent):
    frames, rows, cols, channels = features.shape
    half_rows, half_cols = (cotangent.shape[1], cotangent.shape[2])
    cot_padded = extended(cotangent, (("ha", 1), ("wa", 2)), 1)
    feat_padded = frame_pad(extended(features, (("ha", 1), ("wa", 2)), 1))
    block = conv_forward(feat_padded, weight_one, rows, cols)
    grad_block = widen(cotangent) * silu_slope(block)
    grad_padded = frame_pad(extended(grad_block, (("ha", 1), ("wa", 2)), 1))
    grad_features = conv_adjoint(grad_padded, weight_one, rows, cols)
    term_one = kernel_terms(feat_padded, grad_block, rows, cols)
    grad_flow = conv_adjoint(frame_pad(cot_padded), weight_two, half_rows, half_cols)
    flow_padded = frame_pad(extended(flow_feats, (("ha", 1), ("wa", 2)), 1))
    term_two = kernel_terms(flow_padded, cotangent, half_rows, half_cols)
    width_count = lax.axis_size("wa")
    total_rows = rows * lax.axis_size("ha")
    total_cols = cols * width_count
    summed_one, summed_two = lax.psum((term_one, term_two), ("ha", "wa"))
    place = lax.axis_index("wa")
    share_one = summed_one.shape[3] // width_count
    share_two = summed_two.shape[3] // width_count
    owned_one = lax.dynamic_slice_in_dim(summed_one, place * share_one, share_one, 3)
    owned_two = lax.dynamic_slice_in_dim(summed_two, place * share_two, share_two, 3)
    grad_one = owned_one * (1.0 / (frames * total_rows * total_cols) ** 0.5)
    grad_two = owned_two * (1.0 / (frames * (total_rows // 2) * (total_cols // 2)) ** 0.5)
    return (grad_features, grad_one, grad_flow, grad_two)


def solution(mesh):
    in_specs = (
        P(None, "ha", "wa", None),
        P(),
        P(None, "ha", "wa", None),
        P(),
        P(None, "ha", "wa", None),
    )
    out_specs = (
        P(None, "ha", "wa", None),
        P(None, None, None, "wa", None),
        P(None, "ha", "wa", None),
        P(None, None, None, "wa", None),
    )
    return jax.shard_map(local, mesh=mesh, in_specs=in_specs, out_specs=out_specs, check_vma=False)
```

profile of v0, /device:TPU:97, one launch (start us, length us, event | category | flops | bytes accessed | tf_op | source)
XLA Modules:
  0.0 466.7 jit_solution(11168904568810505299)
XLA Ops:
  8.6 1.9 collective-permute-start.12
  10.5 3.4 collective-permute-start.13
  15.3 4.6 collective-permute-start
  21.3 1.9 collective-permute-start.8
  23.2 3.6 collective-permute-start.9
  26.8 2.4 fusion.399
  29.2 2.0 fusion.315
  33.0 5.0 %collective-permute-start.10 = (f32[2,10,1,128]{3,2,1,0:T(1,128)S(1)}, f32[2,10,1,128]{3,2,1,0:T(1,128)S(1)}, u32[]{:S(2)}, u32[]{:S(2)}) collective-permute-start(f32[2,10,1,128]{3,2,1,0:T(1,128)S(1)} %get-tuple-element.23), channel_id=1, source_target_pairs={{0,1},{1,2},{2,3},{3,4},{4,5},{5,6},{6,7},{7,8},{8,9},{9,10},{10,1... | collective-permute-start | bytes 30728 | tf_op jit(solution)/shard_map/ppermute | solution.py:14
  38.0 1.9 collective-permute-start.11
  42.6 1.9 collective-permute-start.1
  53.6 2.1 convolution_add_fusion.4
  57.3 3.6 collective-permute-start.14
  61.0 1.9 collective-permute-start.15
  63.9 3.6 collective-permute-start.2
  67.6 2.1 collective-permute-start.3
  70.9 1.8 collective-permute-done.3
  116.5 1.9 collective-permute-start.5
  118.4 6.5 %collective-permute-start.4 = (f32[2,1,32,128]{3,2,1,0:T(8,128)S(1)}, f32[2,1,32,128]{3,2,1,0:T(8,128)S(1)}, u32[]{:S(2)}, u32[]{:S(2)}) collective-permute-start(f32[2,1,32,128]{3,2,1,0:T(8,128)S(1)} %get-tuple-element.12), channel_id=1, source_target_pairs={{0,16},{16,32},{32,48},{48,64},{64,80},{80,96},{96,112},{112,128},... | collective-permute-start | bytes 98312 | tf_op jit(solution)/shard_map/ppermute | solution.py:14
  137.5 2.0 fusion.58
  145.8 2.0 fusion.57
  160.7 2.2 collective-permute-start.6
  163.0 2.1 collective-permute-start.7
  166.3 1.8 collective-permute-done.7
  183.9 272.6 %all-reduce.7.cloned.1.call-done = (f32[3,3,3,128,128]{4,3,2,1,0:T(8,128)}, f32[3,3,3,256,128]{4,3,2,1,0:T(8,128)}) async-done(((f32[3,3,3,128,128]{4,3,2,1,0:T(8,128)}, f32[3,3,3,256,128]{4,3,2,1,0:T(8,128)}), (f32[3,3,3,128,128]{4,3,2,1,0:T(8,128)}, f32[3,3,3,256,128]{4,3,2,1,0:T(8,128)})) %all-reduce.7.cloned.1.call-update) | async-done | bytes 5308432 | tf_op jit(solution)/shard_map/psum | solution.py:105
  (188 shorter events, 116.3 us)
Async XLA Ops:
  7.2 449.3 %all-reduce.7.cloned.1.call-start = ((), (), s32[]{:S(2)}) async-start(), calls=%async_computation | async-start | bytes 10616832 | tf_op jit(solution)/shard_map/psum | solution.py:105
  8.6 47.1 %collective-permute-start.12 = (f32[2,1,16,256]{3,2,1,0:T(8,128)}, f32[2,1,16,256]{3,2,1,0:T(8,128)}, u32[]{:S(2)}, u32[]{:S(2)}) collective-permute-start(f32[2,1,16,256]{3,2,1,0:T(8,128)} %get-tuple-element.22), channel_id=1, source_target_pairs={{0,16},{16,32},{32,48},{48,64},{64,80},{80,96},{96,112},{112,128},... | collective-permute-start | bytes 98312 | tf_op jit(solution)/shard_map/ppermute | solution.py:14
  10.5 46.0 %collective-permute-start.13 = (f32[2,1,16,256]{3,2,1,0:T(8,128)}, f32[2,1,16,256]{3,2,1,0:T(8,128)}, u32[]{:S(2)}, u32[]{:S(2)}) collective-permute-start(f32[2,1,16,256]{3,2,1,0:T(8,128)} %get-tuple-element.21), channel_id=1, source_target_pairs={{16,0},{32,16},{48,32},{64,48},{80,64},{96,80},{112,96},{128,112},... | collective-permute-start | bytes 98312 | tf_op jit(solution)/shard_map/ppermute | solution.py:17
  15.3 47.6 %collective-permute-start = (f32[2,1,32,128]{3,2,1,0:T(8,128)}, f32[2,1,32,128]{3,2,1,0:T(8,128)}, u32[]{:S(2)}, u32[]{:S(2)}) collective-permute-start(f32[2,1,32,128]{3,2,1,0:T(8,128)} %get-tuple-element.18), channel_id=1, source_target_pairs={{0,16},{16,32},{32,48},{48,64},{64,80},{80,96},{96,112},{112,128},... | collective-permute-start | bytes 98312 | tf_op jit(solution)/shard_map/ppermute | solution.py:14
  21.3 10.0 %collective-permute-start.8 = (f32[2,1,16,128]{3,2,1,0:T(8,128)}, f32[2,1,16,128]{3,2,1,0:T(8,128)S(1)}, u32[]{:S(2)}, u32[]{:S(2)}) collective-permute-start(f32[2,1,16,128]{3,2,1,0:T(8,128)} %get-tuple-element.26), channel_id=1, source_target_pairs={{0,16},{16,32},{32,48},{48,64},{64,80},{80,96},{96,112},{112,128},... | collective-permute-start | bytes 49160 | tf_op jit(solution)/shard_map/ppermute | solution.py:14
  23.2 21.4 %copy-start.2 = (f32[3,3,3,256,128]{4,3,2,1,0:T(8,128)S(1)}, f32[3,3,3,256,128]{4,3,2,1,0:T(8,128)}, u32[]{:S(2)}) copy-start(f32[3,3,3,256,128]{4,3,2,1,0:T(8,128)} %param.8) | copy-start | bytes 10616836
  23.2 9.0 %collective-permute-start.9 = (f32[2,1,16,128]{3,2,1,0:T(8,128)}, f32[2,1,16,128]{3,2,1,0:T(8,128)}, u32[]{:S(2)}, u32[]{:S(2)}) collective-permute-start(f32[2,1,16,128]{3,2,1,0:T(8,128)} %get-tuple-element.25), channel_id=1, source_target_pairs={{16,0},{32,16},{48,32},{64,48},{80,64},{96,80},{112,96},{128,112},... | collective-permute-start | bytes 49160 | tf_op jit(solution)/shard_map/ppermute | solution.py:17
  33.0 9.7 %collective-permute-start.10 = (f32[2,10,1,128]{3,2,1,0:T(1,128)S(1)}, f32[2,10,1,128]{3,2,1,0:T(1,128)S(1)}, u32[]{:S(2)}, u32[]{:S(2)}) collective-permute-start(f32[2,10,1,128]{3,2,1,0:T(1,128)S(1)} %get-tuple-element.23), channel_id=1, source_target_pairs={{0,1},{1,2},{2,3},{3,4},{4,5},{5,6},{6,7},{7,8},{8,9},{9,10},{10,1... | collective-permute-start | bytes 30728 | tf_op jit(solution)/shard_map/ppermute | solution.py:14
  38.0 6.6 %collective-permute-start.11 = (f32[2,10,1,128]{3,2,1,0:T(1,128)S(1)}, f32[2,10,1,128]{3,2,1,0:T(1,128)S(1)}, u32[]{:S(2)}, u32[]{:S(2)}) collective-permute-start(f32[2,10,1,128]{3,2,1,0:T(1,128)S(1)} %get-tuple-element.24), channel_id=1, source_target_pairs={{1,0},{2,1},{3,2},{4,3},{5,4},{6,5},{7,6},{8,7},{9,8},{10,9},{11,1... | collective-permute-start | bytes 30728 | tf_op jit(solution)/shard_map/ppermute | solution.py:17
  42.6 21.2 %collective-permute-start.1 = (f32[2,1,32,128]{3,2,1,0:T(8,128)}, f32[2,1,32,128]{3,2,1,0:T(8,128)S(1)}, u32[]{:S(2)}, u32[]{:S(2)}) collective-permute-start(f32[2,1,32,128]{3,2,1,0:T(8,128)} %get-tuple-element.17), channel_id=1, source_target_pairs={{16,0},{32,16},{48,32},{64,48},{80,64},{96,80},{112,96},{128,112},... | collective-permute-start | bytes 98312 | tf_op jit(solution)/shard_map/ppermute | solution.py:17
  47.7 2.3 copy-start.6
  52.4 4.1 copy-start.7
  52.8 10.9 %copy-start.1 = (f32[2,16,32,128]{3,2,1,0:T(8,128)S(1)}, f32[2,16,32,128]{3,2,1,0:T(8,128)}, u32[]{:S(2)}) copy-start(f32[2,16,32,128]{3,2,1,0:T(8,128)} %param.5) | copy-start | bytes 1572868
  53.6 16.1 %copy-start = (f32[3,3,3,128,128]{4,3,2,1,0:T(8,128)S(1)}, f32[3,3,3,128,128]{4,3,2,1,0:T(8,128)}, u32[]{:S(2)}) copy-start(f32[3,3,3,128,128]{4,3,2,1,0:T(8,128)} %param.6) | copy-start | bytes 5308420
  57.3 67.6 %collective-permute-start.14 = (f32[2,10,1,256]{3,2,1,0:T(1,128)S(1)}, f32[2,10,1,256]{3,2,1,0:T(1,128)S(1)}, u32[]{:S(2)}, u32[]{:S(2)}) collective-permute-start(f32[2,10,1,256]{3,2,1,0:T(1,128)S(1)} %get-tuple-element.19), channel_id=1, source_target_pairs={{0,1},{1,2},{2,3},{3,4},{4,5},{5,6},{6,7},{7,8},{8,9},{9,10},{10,1... | collective-permute-start | bytes 61448 | tf_op jit(solution)/shard_map/ppermute | solution.py:14
  61.0 64.0 %collective-permute-start.15 = (f32[2,10,1,256]{3,2,1,0:T(1,128)S(1)}, f32[2,10,1,256]{3,2,1,0:T(1,128)S(1)}, u32[]{:S(2)}, u32[]{:S(2)}) collective-permute-start(f32[2,10,1,256]{3,2,1,0:T(1,128)S(1)} %get-tuple-element.20), channel_id=1, source_target_pairs={{1,0},{2,1},{3,2},{4,3},{5,4},{6,5},{7,6},{8,7},{9,8},{10,9},{11,1... | collective-permute-start | bytes 61448 | tf_op jit(solution)/shard_map/ppermute | solution.py:17
  63.9 6.9 %collective-permute-start.2 = (f32[2,18,1,128]{3,2,1,0:T(1,128)S(1)}, f32[2,18,1,128]{3,2,1,0:T(1,128)S(1)}, u32[]{:S(2)}, u32[]{:S(2)}) collective-permute-start(f32[2,18,1,128]{3,2,1,0:T(1,128)S(1)} %get-tuple-element.10), channel_id=1, source_target_pairs={{0,1},{1,2},{2,3},{3,4},{4,5},{5,6},{6,7},{7,8},{8,9},{9,10},{10,1... | collective-permute-start | bytes 55304 | tf_op jit(solution)/shard_map/ppermute | solution.py:14
  67.6 5.1 %collective-permute-start.3 = (f32[2,18,1,128]{3,2,1,0:T(1,128)S(1)}, f32[2,18,1,128]{3,2,1,0:T(1,128)S(1)}, u32[]{:S(2)}, u32[]{:S(2)}) collective-permute-start(f32[2,18,1,128]{3,2,1,0:T(1,128)S(1)} %get-tuple-element.11), channel_id=1, source_target_pairs={{1,0},{2,1},{3,2},{4,3},{5,4},{6,5},{7,6},{8,7},{9,8},{10,9},{11,1... | collective-permute-start | bytes 55304 | tf_op jit(solution)/shard_map/ppermute | solution.py:17
  114.4 10.7 %copy-start.3 = (f32[2,8,16,128]{3,2,1,0:T(8,128)S(1)}, f32[2,8,16,128]{3,2,1,0:T(8,128)}, u32[]{:S(2)}) copy-start(f32[2,8,16,128]{3,2,1,0:T(8,128)} %param.9) | copy-start | bytes 393220
  116.4 12.4 %copy-start.5 = (f32[27,128,128]{2,1,0:T(8,128)}, f32[27,128,128]{2,1,0:T(8,128)S(1)}, u32[]{:S(2)}) copy-start(f32[27,128,128]{2,1,0:T(8,128)S(1)} %fusion.86) | copy-start | bytes 5308420
  116.5 44.2 %collective-permute-start.5 = (f32[2,1,32,128]{3,2,1,0:T(8,128)S(1)}, f32[2,1,32,128]{3,2,1,0:T(8,128)S(1)}, u32[]{:S(2)}, u32[]{:S(2)}) collective-permute-start(f32[2,1,32,128]{3,2,1,0:T(8,128)S(1)} %get-tuple-element.13), channel_id=1, source_target_pairs={{16,0},{32,16},{48,32},{64,48},{80,64},{96,80},{112,96},{128,112},... | collective-permute-start | bytes 98312 | tf_op jit(solution)/shard_map/ppermute | solution.py:17
  118.4 42.3 %collective-permute-start.4 = (f32[2,1,32,128]{3,2,1,0:T(8,128)S(1)}, f32[2,1,32,128]{3,2,1,0:T(8,128)S(1)}, u32[]{:S(2)}, u32[]{:S(2)}) collective-permute-start(f32[2,1,32,128]{3,2,1,0:T(8,128)S(1)} %get-tuple-element.12), channel_id=1, source_target_pairs={{0,16},{16,32},{32,48},{48,64},{64,80},{80,96},{96,112},{112,128},... | collective-permute-start | bytes 98312 | tf_op jit(solution)/shard_map/ppermute | solution.py:14
  160.7 5.5 %collective-permute-start.6 = (f32[2,18,1,128]{3,2,1,0:T(1,128)S(1)}, f32[2,18,1,128]{3,2,1,0:T(1,128)S(1)}, u32[]{:S(2)}, u32[]{:S(2)}) collective-permute-start(f32[2,18,1,128]{3,2,1,0:T(1,128)S(1)} %get-tuple-element.8), channel_id=1, source_target_pairs={{0,1},{1,2},{2,3},{3,4},{4,5},{5,6},{6,7},{7,8},{8,9},{9,10},{10,1... | collective-permute-start | bytes 55304 | tf_op jit(solution)/shard_map/ppermute | solution.py:14
  163.0 5.1 %collective-permute-start.7 = (f32[2,18,1,128]{3,2,1,0:T(1,128)S(1)}, f32[2,18,1,128]{3,2,1,0:T(1,128)S(1)}, u32[]{:S(2)}, u32[]{:S(2)}) collective-permute-start(f32[2,18,1,128]{3,2,1,0:T(1,128)S(1)} %get-tuple-element.9), channel_id=1, source_target_pairs={{1,0},{2,1},{3,2},{4,3},{5,4},{6,5},{7,6},{8,7},{9,8},{10,9},{11,1... | collective-permute-start | bytes 55304 | tf_op jit(solution)/shard_map/ppermute | solution.py:17
  (1 other events, 2.0 us)
Sparse Core Ops, SparseCore 0:
  160.8 295.6 all-reduce.6
where the time goes:
time: 476 us; the launch traced here: 467 us
  waiting for transfers between devices  276 us (58%)
  matrix products  114 us (24%)
  starting transfers between devices  48.4 us (10%)
  between operations  15.3 us (3%)
  local copies, waits for them, and re-layouts  7.8 us (2%)
    psum x1, waiting for transfers between devices, local(): summed_one, summed_two = lax.psum((term_one, term_two), ('ha', 'wa'))  273 us
    dot_general x54, matrix products, kernel_terms(): jnp.einsum('fhwc,fhwd->cd', window, gradient, precision=exact_mode)  63.6 us
    dot_general x54, matrix products, conv_adjoint(): jnp.einsum('fhwd,cd->fhwc', window, kernel[time_tap, row_tap, col_tap], p...  32.8 us
    ppermute x8, starting transfers between devices, extended(): lax.ppermute(lax.slice_in_dim(block, block.shape[dim] - width, None, axis...  29.5 us
    ppermute x8, starting transfers between devices, extended(): lax.ppermute(lax.slice_in_dim(block, 0, width, axis=dim), axis, backward)  18.9 us
    dot_general x27, matrix products, conv_forward(): jnp.einsum('fhwc,cd->fhwd', window, kernel[time_tap, row_tap, col_tap], p...  17.9 us
  transfers between devices with their start and end apart: 17, of which 3 were waited for; matrix products, arithmetic and copies ran while one was open for 26% of the time, Pallas kernels for 0%

commit v1 on v0

v1 whole, which is shorter than its diff:
```python
import functools

import jax
import jax.numpy as jnp
from jax import lax
from jax.experimental import pallas as pl
from jax.experimental.pallas import tpu as pltpu
from jax.sharding import Mesh
from jax.sharding import PartitionSpec as P

FR, R, W, C = 2, 16, 32, 128
R2, W2, CF = 8, 16, 256
PITCH = 40
EXT = (R + 2) * PITCH
HA, WA = ("x", "zl"), ("zh", "y", "core")

f32, bf16 = jnp.float32, jnp.bfloat16
VMEM = pl.BlockSpec(memory_space=pltpu.VMEM)
SMEM = pl.BlockSpec(memory_space=pltpu.SMEM)


def split(values):
    high = values.astype(bf16)
    return high, (values - high.astype(f32)).astype(bf16)


def product(left, right, dims):
    dot = functools.partial(
        lax.dot_general, dimension_numbers=(dims, ((), ())), preferred_element_type=f32
    )
    return dot(left[0], right[0]) + (dot(left[0], right[1]) + dot(left[1], right[0]))


NN = ((1,), (0,))
NT = ((1,), (1,))


def both_frames(kernel, tap):
    first = jnp.concatenate([kernel[9 + tap], kernel[tap]], axis=1)
    second = jnp.concatenate([kernel[18 + tap], kernel[9 + tap]], axis=1)
    return jnp.concatenate([first, second], axis=0)


def store_terms(place_ref, out_ref, tap, value, depth):
    half = value.shape[0] // 2
    taps = (
        (0, value[:half, C:]),
        (1, value[:half, :C] + value[half:, C:]),
        (2, value[half:, :C]),
    )
    core, y, x, zh = place_ref[0], place_ref[1], place_ref[2], place_ref[3]
    for time_tap, part in taps:
        number = 9 * time_tap + tap
        chunk = lax.rem(number // 7 - x + 4, 4)
        for owner in range(16):
            slot_core = lax.rem(owner % 2 - core + 2, 2)
            slot_y = lax.rem((owner // 2) % 4 - y + 4, 4)
            slot_zh = lax.rem(owner // 8 - zh + 2, 2)
            out_ref[slot_core, slot_y, chunk, slot_zh, number % 7] = part[owner * depth : (owner + 1) * depth]


def shifted_cot(cot_ref, e):
    both = jnp.concatenate([cot_ref[0, :, e : e + W2, :], cot_ref[1, :, e : e + W2, :]], axis=-1)
    return split(both)


def flow_terms_kernel(place_ref, flow_ref, cot_ref, out_ref):
    flow = jnp.concatenate(
        [flow_ref[0].reshape(R2 * W2, CF).T, flow_ref[1].reshape(R2 * W2, CF).T], axis=0
    )
    flow = split(flow)
    for col_tap in range(3):
        cot = shifted_cot(cot_ref, 2 - col_tap)
        for row_tap in range(3):
            window = [v[2 - row_tap : 2 - row_tap + R2].reshape(R2 * W2, 2 * C) for v in cot]
            store_terms(place_ref, out_ref, 3 * row_tap + col_tap, product(flow, window, NN), 16)


def block_kernel(
    place_ref, feat_ref, top_ref, bottom_ref, left_ref, right_ref, weight_ref, cot_ref,
    out_ref, grad_high_ref, grad_low_ref,
    ext_ref, wide_ref, taps_high, taps_low, even_high, even_low, odd_high, odd_low, grad_ref,
):
    ext_ref[...] = jnp.zeros_like(ext_ref)
    for t in range(FR):
        lanes = slice(t * C, (t + 1) * C)
        ext_ref[2 : 2 + R, 3 : 3 + W, lanes] = feat_ref[t]
        ext_ref[0:2, 3 : 3 + W, lanes] = top_ref[t]
        ext_ref[2 + R : 4 + R, 3 : 3 + W, lanes] = bottom_ref[t]
        ext_ref[0 : R + 4, 1:3, lanes] = left_ref[t]
        ext_ref[0 : R + 4, 3 + W : 5 + W, lanes] = right_ref[t]
    for t in range(FR):
        lanes = slice(t * C, (t + 1) * C)
        for row in range(R2 + 2):
            line = cot_ref[t, row] * 0.5
            for target in (2 * row - 1, 2 * row):
                if 0 <= target < R + 2:
                    wide_ref[t, target, pl.ds(0, W2 + 2, stride=2), :] = line
                    wide_ref[t, target, pl.ds(1, W2 + 2, stride=2), :] = line
    for tap in range(9):
        high, low = split(both_frames(weight_ref, tap))
        taps_high[tap] = high
        taps_low[tap] = low
    rows = R + 4
    for e in range(3):
        shifted = ext_ref[:, e : e + PITCH, :].reshape(rows * PITCH, 2 * C)
        high, low = split(shifted)
        even_high[e] = high
        even_low[e] = low
        odd_high[e] = high[PITCH : PITCH + EXT]
        odd_low[e] = low[PITCH : PITCH + EXT]
    step = EXT // 3
    for part in range(3):
        start = part * step
        total = jnp.zeros((step, 2 * C), f32)
        for row_tap in range(3):
            for e in range(3):
                if row_tap == 1:
                    window = (odd_high[e, start : start + step], odd_low[e, start : start + step])
                else:
                    first = start + row_tap * PITCH
                    window = (even_high[e, first : first + step], even_low[e, first : first + step])
                tap = 3 * row_tap + e
                total = total + product(window, (taps_high[tap], taps_low[tap]), NN)
        sigma = jax.nn.sigmoid(total)
        slope = sigma * (1.0 + total * (1.0 - sigma))
        lines = step // PITCH
        grad_ref[part * lines : (part + 1) * lines] = slope.reshape(lines, PITCH, 2 * C)
    for t in range(FR):
        lanes = slice(t * C, (t + 1) * C)
        grad_ref[:, :, lanes] = grad_ref[:, :, lanes] * wide_ref[t]
    for e in range(3):
        high, low = split(grad_ref[:, 3 - e : 3 - e + W, :])
        grad_high_ref[e] = high
        grad_low_ref[e] = low
    feat = split(
        jnp.concatenate([feat_ref[t].reshape(R * W, C).T for t in range(FR)], axis=0)
    )
    for row_tap in range(3):
        for e in range(3):
            window = [
                ref[e, 2 - row_tap : 2 - row_tap + R].reshape(R * W, 2 * C)
                for ref in (grad_high_ref, grad_low_ref)
            ]
            store_terms(place_ref, out_ref, 3 * row_tap + e, product(feat, window, NN), 8)


def adjoint_kernel(grad_high_ref, grad_low_ref, weight_one_ref, cot_ref, weight_two_ref, feat_out, flow_out):
    total = jnp.zeros((R * W, 2 * C), f32)
    for row_tap in range(3):
        for e in range(3):
            window = [
                ref[e, 2 - row_tap : 2 - row_tap + R].reshape(R * W, 2 * C)
                for ref in (grad_high_ref, grad_low_ref)
            ]
            total = total + product(window, split(both_frames(weight_one_ref, 3 * row_tap + e)), NT)
    for t in range(FR):
        feat_out[t] = total[:, t * C : (t + 1) * C].reshape(R, W, C)
    total = jnp.zeros((R2 * W2, 2 * CF), f32)
    for e in range(3):
        cot = shifted_cot(cot_ref, 2 - e)
        for row_tap in range(3):
            window = [v[2 - row_tap : 2 - row_tap + R2].reshape(R2 * W2, 2 * C) for v in cot]
            total = total + product(window, split(both_frames(weight_two_ref, 3 * row_tap + e)), NT)
    for t in range(FR):
        flow_out[t] = total[:, t * CF : (t + 1) * CF].reshape(R2, W2, CF)


def params():
    return pltpu.CompilerParams(vmem_limit_bytes=48 * 2**20)


def flow_terms(place, flow, cot):
    return pl.pallas_call(
        flow_terms_kernel,
        out_shape=jax.ShapeDtypeStruct((2, 4, 4, 2, 7, 16, C), f32),
        in_specs=[SMEM, VMEM, VMEM],
        out_specs=VMEM,
        compiler_params=params(),
        cost_estimate=pl.CostEstimate(flops=2 * 10**9, bytes_accessed=5 * 10**6, transcendentals=0),
        name="flow_terms",
    )(place, flow, cot)


def block_terms(place, feat, top, bottom, left, right, weight, cot):
    wins = jax.ShapeDtypeStruct((3, R + 2, W, 2 * C), bf16)
    return pl.pallas_call(
        block_kernel,
        out_shape=(jax.ShapeDtypeStruct((2, 4, 4, 2, 7, 8, C), f32), wins, wins),
        in_specs=[SMEM] + [VMEM] * 7,
        out_specs=(VMEM,) * 3,
        scratch_shapes=[
            pltpu.VMEM((R + 4, PITCH + 8, 2 * C), f32),
            pltpu.VMEM((FR, R + 2, PITCH, C), f32),
            pltpu.VMEM((9, 2 * C, 2 * C), bf16),
            pltpu.VMEM((9, 2 * C, 2 * C), bf16),
            pltpu.VMEM((3, (R + 4) * PITCH, 2 * C), bf16),
            pltpu.VMEM((3, (R + 4) * PITCH, 2 * C), bf16),
            pltpu.VMEM((3, EXT, 2 * C), bf16),
            pltpu.VMEM((3, EXT, 2 * C), bf16),
            pltpu.VMEM((R + 2, PITCH, 2 * C), f32),
        ],
        compiler_params=params(),
        cost_estimate=pl.CostEstimate(flops=5 * 10**9, bytes_accessed=6 * 10**6, transcendentals=200000),
        name="block_terms",
    )(place, feat, top, bottom, left, right, weight, cot)


def adjoints(grad_high, grad_low, weight_one, cot, weight_two):
    return pl.pallas_call(
        adjoint_kernel,
        out_shape=(
            jax.ShapeDtypeStruct((FR, R, W, C), f32),
            jax.ShapeDtypeStruct((FR, R2, W2, CF), f32),
        ),
        in_specs=[VMEM] * 5,
        out_specs=(VMEM,) * 2,
        compiler_params=params(),
        cost_estimate=pl.CostEstimate(flops=4 * 10**9, bytes_accessed=10**7, transcendentals=0),
        name="adjoints",
    )(grad_high, grad_low, weight_one, cot, weight_two)


def ring(steps, count=4):
    return [(i, (i + steps) % count) for i in range(count)]


def line(count, step):
    return [(i, i + step) for i in range(count) if 0 <= i + step < count]


def scatter_sum(parts, axis):
    arrived = [lax.ppermute(parts[k], axis, ring(k)) for k in (2, 1, 3)]
    return (parts[0] + arrived[0]) + (arrived[1] + arrived[2])


def local(features, weight_one, flow_feats, weight_two, cotangent):
    place = jnp.stack([lax.axis_index(a) for a in ("core", "y", "x", "zh")]).astype(jnp.int32)
    kernel_one = weight_one.reshape(27, C, C)
    kernel_two = weight_two.reshape(27, CF, C)
    def rows_of(feat, cot):
        return jnp.concatenate([feat.reshape(FR, 2 * W, C), cot.reshape(FR, W2, C)], axis=1)

    top = lax.ppermute(rows_of(features[:, R - 2 :], cotangent[:, R2 - 1 :]), HA, line(16, 1))
    bottom = lax.ppermute(rows_of(features[:, :2], cotangent[:, :1]), HA, line(16, -1))
    top_feat, top_cot = top[:, : 2 * W].reshape(FR, 2, W, C), top[:, 2 * W :][:, None]
    bottom_feat, bottom_cot = bottom[:, : 2 * W].reshape(FR, 2, W, C), bottom[:, 2 * W :][:, None]
    tall = jnp.concatenate([top_cot, cotangent, bottom_cot], axis=1)

    def cols_of(place, cot_place):
        cols = [v[:, :, place : place + 2] for v in (top_feat, features, bottom_feat)]
        cols = jnp.concatenate(cols, axis=1).reshape(FR, (R + 4) * 2, C)
        return jnp.concatenate([cols, tall[:, :, cot_place]], axis=1)

    left = lax.ppermute(cols_of(W - 2, W2 - 1), WA, line(16, 1))
    right = lax.ppermute(cols_of(0, 0), WA, line(16, -1))
    edge = 2 * (R + 4)
    left_feat, right_feat = [v[:, :edge].reshape(FR, R + 4, 2, C) for v in (left, right)]
    cot = jnp.concatenate([left[:, edge:, None], tall, right[:, edge:, None]], axis=2)

    terms_two = flow_terms(place, flow_feats, cot)
    terms_one, grad_high, grad_low = block_terms(
        place, features, top_feat, bottom_feat, left_feat, right_feat, kernel_one, cot
    )
    swap = [(0, 1), (1, 0)]
    sums = []
    for terms in (terms_two, terms_one):
        terms = terms[0] + lax.ppermute(terms[1], "core", swap)
        sums.append(scatter_sum([terms[k] for k in range(4)], "y"))
    chunks = jnp.concatenate([sums[1], sums[0]], axis=-2)
    chunk = scatter_sum([chunks[k] for k in range(4)], "x")
    chunk = chunk[0] + lax.ppermute(chunk[1], "zh", swap)
    arrived = [lax.ppermute(chunk, "zl", ring(k)) for k in (2, 1, 3)]
    chunk = (chunk + arrived[0]) + (arrived[1] + arrived[2])
    pieces = jnp.stack([chunk] + [lax.ppermute(chunk, "x", ring(k)) for k in (1, 2, 3)])
    order = lax.rem(place[2] - jnp.arange(4) + 4, 4)
    taps = jnp.concatenate([lax.dynamic_index_in_dim(pieces, order[k], 0, False) for k in range(4)])[:27]
    scale_one = 1.0 / (FR * R * W * 256) ** 0.5
    scale_two = 1.0 / (FR * R2 * W2 * 256) ** 0.5
    grad_one = (taps[:, :8] * scale_one).reshape(3, 3, 3, 8, C)
    grad_two = (taps[:, 8:] * scale_two).reshape(3, 3, 3, 16, C)
    grad_features, grad_flow = adjoints(grad_high, grad_low, kernel_one, cot, kernel_two)
    return (grad_features, grad_one, grad_flow, grad_two)


def solution(mesh):
    fine = Mesh(mesh.devices.reshape(4, 4, 2, 4, 2), ("x", "zl", "zh", "y", "core"))
    grid = P(None, HA, WA, None)
    share = P(None, None, None, WA, None)
    return jax.shard_map(
        local,
        mesh=fine,
        in_specs=(grid, P(), grid, P(), grid),
        out_specs=(grid, share, grid, share),
        check_vma=False,
    )
```

time: 476 us -> 138 us (0.29)
  the two profiles are of different devices: /device:TPU:97 before, /device:TPU:6 now
where the time goes in v1:
time: 138 us; the launch traced here: 136 us
  waiting for transfers between devices  50.6 us (37%)
  starting transfers between devices  48.5 us (35%)
  Pallas kernels  18 us (13%)
  between operations  8.8 us (6%)
  local copies, waits for them, and re-layouts  6.49 us (5%)
  other arithmetic  3.15 us (2%)
    ppermute x9, waiting for transfers between devices, scatter_sum(): arrived = [lax.ppermute(parts[k], axis, ring(k)) for k in (2, 1, 3)]  35.5 us
    ppermute x9, starting transfers between devices, scatter_sum(): arrived = [lax.ppermute(parts[k], axis, ring(k)) for k in (2, 1, 3)]  22.8 us
    pallas_call x1, Pallas kernels, block_terms(): pl.pallas_call(block_kernel, out_shape=(jax.ShapeDtypeStruct((2, 4, 4, 2,...  8.52 us
    ppermute x1, waiting for transfers between devices, local(): chunk = chunk[0] + lax.ppermute(chunk[1], 'zh', swap)  8.52 us
    pallas_call x1, Pallas kernels, adjoints(): pl.pallas_call(adjoint_kernel, out_shape=(jax.ShapeDtypeStruct((FR, R, W,...  6.85 us
    ppermute x3, starting transfers between devices, local(): lax.ppermute(chunk, 'x', ring(k))  5.9 us
    ppermute x1, starting transfers between devices, local(): lax.ppermute(rows_of(features[:, :2], cotangent[:, :1]), HA, line(16, -1))  4.89 us
    ppermute x2, starting transfers between devices, local(): terms = terms[0] + lax.ppermute(terms[1], 'core', swap)  4.37 us
  transfers between devices with their start and end apart: 22, of which 10 were waited for; matrix products, arithmetic and copies ran while one was open for 3% of the time, Pallas kernels for 11%

profile of v1, /device:TPU:6, one launch (start us, length us, event | category | flops | bytes accessed | tf_op | source)
XLA Modules:
  0.0 135.6 jit_solution(17349105154855113792)
XLA Ops:
  2.3 3.8 %collective-permute-start = (f32[2,80,128]{2,1,0:T(8,128)S(1)}, f32[2,80,128]{2,1,0:T(8,128)S(1)}, u32[]{:S(2)}, u32[]{:S(2)}) collective-permute-start(f32[2,80,128]{2,1,0:T(8,128)S(1)} %pad_maximum_fusion.6), channel_id=1, source_target_pairs={{0,16},{16,32},{32,48},{48,64},{64,80},{80,96},{96,112},{112,128},... | collective-permute-start | bytes 245768 | tf_op jit(solution)/shard_map/ppermute | solution.py:244
  6.2 4.9 %collective-permute-start.1 = (f32[2,80,128]{2,1,0:T(8,128)S(1)}, f32[2,80,128]{2,1,0:T(8,128)S(1)}, u32[]{:S(2)}, u32[]{:S(2)}) collective-permute-start(f32[2,80,128]{2,1,0:T(8,128)S(1)} %pad_maximum_fusion.7), channel_id=1, source_target_pairs={{16,0},{32,16},{48,32},{64,48},{80,64},{96,80},{112,96},{128,112},... | collective-permute-start | bytes 245768 | tf_op jit(solution)/shard_map/ppermute | solution.py:245
  14.2 1.3 collective-permute-start.2
  16.8 3.6 %collective-permute-done.3 = f32[2,50,128]{2,1,0:T(8,128)S(1)} collective-permute-done((f32[2,50,128]{2,1,0:T(8,128)S(1)}, f32[2,50,128]{2,1,0:T(8,128)S(1)}, u32[]{:S(2)}, u32[]{:S(2)}) %collective-permute-start.3) | collective-permute-done | bytes 51232 | tf_op jit(solution)/shard_map/ppermute | solution.py:256
  20.5 2.6 %flow_terms.1 = f32[2,4,4,2,7,16,128]{6,5,4,3,2,1,0:T(8,128)S(1)} custom-call(s32[4]{0:T(128)S(1)} %pad_add_fusion.place_ref, f32[2,8,16,256]{3,2,1,0:T(8,128)S(1)} %copy-done.2, f32[2,10,18,128]{3,2,1,0:T(8,128)S(1)} %pad_maximum_fusion.1.cot_ref), custom_call_target="tpu_custom_call" | custom-call | flops 2000000000 | bytes 5000000 | tf_op jit(solution)/shard_map/flow_terms/pallas_call | solution.py:174
  23.4 2.9 %collective-permute-start.8 = (f32[4,4,2,7,16,128]{5,4,3,2,1,0:T(8,128)S(1)}, f32[4,4,2,7,16,128]{5,4,3,2,1,0:T(8,128)S(1)}, u32[]{:S(2)}, u32[]{:S(2)}) collective-permute-start(f32[4,4,2,7,16,128]{5,4,3,2,1,0:T(8,128)S(1)} %slice_bitcast_fusion), channel_id=1, source_target_pairs={{0,1},{1,0},{2,3},{3,2},{4,5},{5,4},{6,7},{7,6},{8,9},{9,8},{10,11... | collective-permute-start | bytes 5505032 | tf_op jit(solution)/shard_map/ppermute | solution.py:268
  26.3 8.5 %block_terms.1 = (f32[2,4,4,2,7,8,128]{6,5,4,3,2,1,0:T(8,128)}, bf16[3,18,32,256]{3,2,1,0:T(8,128)(2,1)S(1)}, bf16[3,18,32,256]{3,2,1,0:T(8,128)(2,1)S(1)}) custom-call(s32[4]{0:T(128)S(1)} %pad_add_fusion.place_ref, f32[2,16,32,128]{3,2,1,0:T(8,128)S(1)} %copy-done, f32[2,2,32,128]{3,2,1,0:T(8,128)S(1)} %bitcast.105, f32[2,2,32,128]{3,2,1,0:T(8,128)S(1)} %bitcast.107, ...), custom_call_target="tpu_custom_call" | custom-call | flops 5000000000 | bytes 6000000 | tf_op jit(solution)/shard_map/block_terms/pallas_call | solution.py:187
  34.9 1.6 %slice_bitcast_fusion.2 = f32[4,4,2,7,8,128]{5,4,3,2,1,0:T(8,128)S(1)} fusion(f32[2,4,4,2,7,8,128]{6,5,4,3,2,1,0:T(8,128)} %get-tuple-element.12), kind=kLoop, calls=%fused_computation.7 | loop fusion | bytes 1835008 | tf_op jit(solution)/shard_map/squeeze | solution.py:268
  36.5 1.4 %collective-permute-start.4 = (f32[4,4,2,7,8,128]{5,4,3,2,1,0:T(8,128)S(1)}, f32[4,4,2,7,8,128]{5,4,3,2,1,0:T(8,128)S(1)}, u32[]{:S(2)}, u32[]{:S(2)}) collective-permute-start(f32[4,4,2,7,8,128]{5,4,3,2,1,0:T(8,128)S(1)} %slice_bitcast_fusion.2), channel_id=1, source_target_pairs={{0,1},{1,0},{2,3},{3,2},{4,5},{5,4},{6,7},{7,6},{8,9},{9,8},{10,11... | collective-permute-start | bytes 2752520 | tf_op jit(solution)/shard_map/ppermute | solution.py:268
  37.9 2.1 %collective-permute-done.4 = f32[4,4,2,7,8,128]{5,4,3,2,1,0:T(8,128)S(1)} collective-permute-done((f32[4,4,2,7,8,128]{5,4,3,2,1,0:T(8,128)S(1)}, f32[4,4,2,7,8,128]{5,4,3,2,1,0:T(8,128)S(1)}, u32[]{:S(2)}, u32[]{:S(2)}) %collective-permute-start.4) | collective-permute-done | bytes 917536 | tf_op jit(solution)/shard_map/ppermute | solution.py:268
  40.2 14.2 %collective-permute-start.7 = (f32[4,2,7,8,128]{4,3,2,1,0:T(8,128)S(1)}, f32[4,2,7,8,128]{4,3,2,1,0:T(8,128)S(1)}, u32[]{:S(2)}, u32[]{:S(2)}) collective-permute-start(f32[4,2,7,8,128]{4,3,2,1,0:T(8,128)S(1)} %get-tuple-element.17), channel_id=1, source_target_pairs={{0,6},{2,0},{4,2},{6,4},{1,7},{3,1},{5,3},{7,5},{8,14},{10,8},{12,... | collective-permute-start | bytes 688136 | tf_op jit(solution)/shard_map/ppermute | solution.py:233
  54.4 1.6 %collective-permute-start.5 = (f32[4,2,7,8,128]{4,3,2,1,0:T(8,128)S(1)}, f32[4,2,7,8,128]{4,3,2,1,0:T(8,128)S(1)}, u32[]{:S(2)}, u32[]{:S(2)}) collective-permute-start(f32[4,2,7,8,128]{4,3,2,1,0:T(8,128)S(1)} %get-tuple-element.19), channel_id=1, source_target_pairs={{0,4},{2,6},{4,0},{6,2},{1,5},{3,7},{5,1},{7,3},{8,12},{10,14},{12... | collective-permute-start | bytes 688136 | tf_op jit(solution)/shard_map/ppermute | solution.py:233
  56.3 1.9 %collective-permute-start.11 = (f32[4,2,7,16,128]{4,3,2,1,0:T(8,128)S(1)}, f32[4,2,7,16,128]{4,3,2,1,0:T(8,128)S(1)}, u32[]{:S(2)}, u32[]{:S(2)}) collective-permute-start(f32[4,2,7,16,128]{4,3,2,1,0:T(8,128)S(1)} %get-tuple-element.14), channel_id=1, source_target_pairs={{0,6},{2,0},{4,2},{6,4},{1,7},{3,1},{5,3},{7,5},{8,14},{10,8},{12,... | collective-permute-start | bytes 1376264 | tf_op jit(solution)/shard_map/ppermute | solution.py:233
  59.2 5.9 %collective-permute-done.7 = f32[4,2,7,8,128]{4,3,2,1,0:T(8,128)S(1)} collective-permute-done((f32[4,2,7,8,128]{4,3,2,1,0:T(8,128)S(1)}, f32[4,2,7,8,128]{4,3,2,1,0:T(8,128)S(1)}, u32[]{:S(2)}, u32[]{:S(2)}) %collective-permute-start.7) | collective-permute-done | bytes 229408 | tf_op jit(solution)/shard_map/ppermute | solution.py:233
  65.1 3.9 %collective-permute-done.6 = f32[4,2,7,8,128]{4,3,2,1,0:T(8,128)S(1)} collective-permute-done((f32[4,2,7,8,128]{4,3,2,1,0:T(8,128)S(1)}, f32[4,2,7,8,128]{4,3,2,1,0:T(8,128)S(1)}, u32[]{:S(2)}, u32[]{:S(2)}) %collective-permute-start.6) | collective-permute-done | bytes 229408 | tf_op jit(solution)/shard_map/ppermute | solution.py:233
  69.0 15.3 %collective-permute-done.11 = f32[4,2,7,16,128]{4,3,2,1,0:T(8,128)S(1)} collective-permute-done((f32[4,2,7,16,128]{4,3,2,1,0:T(8,128)S(1)}, f32[4,2,7,16,128]{4,3,2,1,0:T(8,128)S(1)}, u32[]{:S(2)}, u32[]{:S(2)}) %collective-permute-start.11) | collective-permute-done | bytes 458784 | tf_op jit(solution)/shard_map/ppermute | solution.py:233
  84.3 3.4 %collective-permute-done.10 = f32[4,2,7,16,128]{4,3,2,1,0:T(8,128)S(1)} collective-permute-done((f32[4,2,7,16,128]{4,3,2,1,0:T(8,128)S(1)}, f32[4,2,7,16,128]{4,3,2,1,0:T(8,128)S(1)}, u32[]{:S(2)}, u32[]{:S(2)}) %collective-permute-start.10) | collective-permute-done | bytes 458784 | tf_op jit(solution)/shard_map/ppermute | solution.py:233
  89.8 2.2 %collective-permute-start.13 = (f32[2,7,24,128]{3,2,1,0:T(8,128)S(1)}, f32[2,7,24,128]{3,2,1,0:T(8,128)S(1)}, u32[]{:S(2)}, u32[]{:S(2)}) collective-permute-start(f32[2,7,24,128]{3,2,1,0:T(8,128)S(1)} %get-tuple-element.22), channel_id=1, source_target_pairs={{0,64},{64,128},{128,192},{192,0},{1,65},{65,129},{129,193},{193,1... | collective-permute-start | bytes 516104 | tf_op jit(solution)/shard_map/ppermute | solution.py:233
  92.0 6.4 %collective-permute-done.14 = f32[2,7,24,128]{3,2,1,0:T(8,128)S(1)} collective-permute-done((f32[2,7,24,128]{3,2,1,0:T(8,128)S(1)}, f32[2,7,24,128]{3,2,1,0:T(8,128)S(1)}, u32[]{:S(2)}, u32[]{:S(2)}) %collective-permute-start.14) | collective-permute-done | bytes 172064 | tf_op jit(solution)/shard_map/ppermute | solution.py:233
  99.2 8.5 %collective-permute-done.15 = f32[7,24,128]{2,1,0:T(8,128)S(1)} collective-permute-done((f32[7,24,128]{2,1,0:T(8,128)S(1)}, f32[7,24,128]{2,1,0:T(8,128)S(1)}, u32[]{:S(2)}, u32[]{:S(2)}) %collective-permute-start.15) | collective-permute-done | bytes 86048 | tf_op jit(solution)/shard_map/ppermute | solution.py:272
  107.7 3.4 %collective-permute-start.18 = (f32[7,24,128]{2,1,0:T(8,128)S(1)}, f32[7,24,128]{2,1,0:T(8,128)S(1)}, u32[]{:S(2)}, u32[]{:S(2)}) collective-permute-start(f32[7,24,128]{2,1,0:T(8,128)S(1)} %fusion.15), channel_id=1, source_target_pairs={{0,48},{16,0},{32,16},{48,32},{1,49},{17,1},{33,17},{49,33},{2,50}... | collective-permute-start | bytes 258056 | tf_op jit(solution)/shard_map/ppermute | solution.py:273
  120.2 2.4 %collective-permute-start.21 = (f32[7,24,128]{2,1,0:T(8,128)S(1)}, f32[7,24,128]{2,1,0:T(8,128)S(1)}, u32[]{:S(2)}, u32[]{:S(2)}) collective-permute-start(f32[7,24,128]{2,1,0:T(8,128)S(1)} %add_add_fusion), channel_id=1, source_target_pairs={{0,192},{64,0},{128,64},{192,128},{1,193},{65,1},{129,65},{193,129... | collective-permute-start | bytes 258056 | tf_op jit(solution)/shard_map/ppermute | solution.py:275
  122.7 2.2 %collective-permute-start.20 = (f32[7,24,128]{2,1,0:T(8,128)S(1)}, f32[7,24,128]{2,1,0:T(8,128)S(1)}, u32[]{:S(2)}, u32[]{:S(2)}) collective-permute-start(f32[7,24,128]{2,1,0:T(8,128)S(1)} %add_add_fusion), channel_id=1, source_target_pairs={{0,128},{64,192},{128,0},{192,64},{1,129},{65,193},{129,1},{193,65... | collective-permute-start | bytes 258056 | tf_op jit(solution)/shard_map/ppermute | solution.py:275
  127.3 6.8 %adjoints.1 = (f32[2,16,32,128]{3,2,1,0:T(8,128)}, f32[2,8,16,256]{3,2,1,0:T(8,128)}) custom-call(bf16[3,18,32,256]{3,2,1,0:T(8,128)(2,1)S(1)} %get-tuple-element.9.grad_high_ref, bf16[3,18,32,256]{3,2,1,0:T(8,128)(2,1)S(1)} %copy-done.4, f32[27,128,128]{2,1,0:T(8,128)S(1)} %bitcast.111, f32[2,10,18,128]{3,2,1,0:T(8,128)S(1)} %pad_maximum_fusion.1.cot_ref, ...), custom_call_target="tpu_custom_call" | custom-call | flops 4000000000 | bytes 10000000 | tf_op jit(solution)/shard_map/adjoints/pallas_call | solution.py:210
  (82 shorter events, 15.7 us)
Async XLA Ops:
  0.6 19.8 %copy-start.6 = (f32[2,8,16,128]{3,2,1,0:T(8,128)S(1)}, f32[2,8,16,128]{3,2,1,0:T(8,128)}, u32[]{:S(2)}) copy-start(f32[2,8,16,128]{3,2,1,0:T(8,128)} %param.9) | copy-start | bytes 393220
  0.6 19.9 %copy-start.2 = (f32[2,8,16,256]{3,2,1,0:T(8,128)S(1)}, f32[2,8,16,256]{3,2,1,0:T(8,128)}, u32[]{:S(2)}) copy-start(f32[2,8,16,256]{3,2,1,0:T(8,128)} %flow_ref.1) | copy-start | bytes 786436
  2.3 9.8 %collective-permute-start = (f32[2,80,128]{2,1,0:T(8,128)S(1)}, f32[2,80,128]{2,1,0:T(8,128)S(1)}, u32[]{:S(2)}, u32[]{:S(2)}) collective-permute-start(f32[2,80,128]{2,1,0:T(8,128)S(1)} %pad_maximum_fusion.6), channel_id=1, source_target_pairs={{0,16},{16,32},{32,48},{48,64},{64,80},{80,96},{96,112},{112,128},... | collective-permute-start | bytes 245768 | tf_op jit(solution)/shard_map/ppermute | solution.py:244
  6.2 6.9 %collective-permute-start.1 = (f32[2,80,128]{2,1,0:T(8,128)S(1)}, f32[2,80,128]{2,1,0:T(8,128)S(1)}, u32[]{:S(2)}, u32[]{:S(2)}) collective-permute-start(f32[2,80,128]{2,1,0:T(8,128)S(1)} %pad_maximum_fusion.7), channel_id=1, source_target_pairs={{16,0},{32,16},{48,32},{64,48},{80,64},{96,80},{112,96},{128,112},... | collective-permute-start | bytes 245768 | tf_op jit(solution)/shard_map/ppermute | solution.py:245
  14.2 2.6 %collective-permute-start.2 = (f32[2,50,128]{2,1,0:T(8,128)S(1)}, f32[2,50,128]{2,1,0:T(8,128)S(1)}, u32[]{:S(2)}, u32[]{:S(2)}) collective-permute-start(f32[2,50,128]{2,1,0:T(8,128)S(1)} %pad_maximum_fusion.8), channel_id=1, source_target_pairs={{0,1},{1,2},{2,3},{3,4},{4,5},{5,6},{6,7},{7,8},{8,9},{9,10},{10,1... | collective-permute-start | bytes 153608 | tf_op jit(solution)/shard_map/ppermute | solution.py:255
  15.5 4.9 %collective-permute-start.3 = (f32[2,50,128]{2,1,0:T(8,128)S(1)}, f32[2,50,128]{2,1,0:T(8,128)S(1)}, u32[]{:S(2)}, u32[]{:S(2)}) collective-permute-start(f32[2,50,128]{2,1,0:T(8,128)S(1)} %pad_maximum_fusion.9), channel_id=1, source_target_pairs={{1,0},{2,1},{3,2},{4,3},{5,4},{6,5},{7,6},{8,7},{9,8},{10,9},{11,1... | collective-permute-start | bytes 153608 | tf_op jit(solution)/shard_map/ppermute | solution.py:256
  23.4 32.6 %collective-permute-start.8 = (f32[4,4,2,7,16,128]{5,4,3,2,1,0:T(8,128)S(1)}, f32[4,4,2,7,16,128]{5,4,3,2,1,0:T(8,128)S(1)}, u32[]{:S(2)}, u32[]{:S(2)}) collective-permute-start(f32[4,4,2,7,16,128]{5,4,3,2,1,0:T(8,128)S(1)} %slice_bitcast_fusion), channel_id=1, source_target_pairs={{0,1},{1,0},{2,3},{3,2},{4,5},{5,4},{6,7},{7,6},{8,9},{9,8},{10,11... | collective-permute-start | bytes 5505032 | tf_op jit(solution)/shard_map/ppermute | solution.py:268
  36.5 3.5 %collective-permute-start.4 = (f32[4,4,2,7,8,128]{5,4,3,2,1,0:T(8,128)S(1)}, f32[4,4,2,7,8,128]{5,4,3,2,1,0:T(8,128)S(1)}, u32[]{:S(2)}, u32[]{:S(2)}) collective-permute-start(f32[4,4,2,7,8,128]{5,4,3,2,1,0:T(8,128)S(1)} %slice_bitcast_fusion.2), channel_id=1, source_target_pairs={{0,1},{1,0},{2,3},{3,2},{4,5},{5,4},{6,7},{7,6},{8,9},{9,8},{10,11... | collective-permute-start | bytes 2752520 | tf_op jit(solution)/shard_map/ppermute | solution.py:268
  40.2 24.9 %collective-permute-start.7 = (f32[4,2,7,8,128]{4,3,2,1,0:T(8,128)S(1)}, f32[4,2,7,8,128]{4,3,2,1,0:T(8,128)S(1)}, u32[]{:S(2)}, u32[]{:S(2)}) collective-permute-start(f32[4,2,7,8,128]{4,3,2,1,0:T(8,128)S(1)} %get-tuple-element.17), channel_id=1, source_target_pairs={{0,6},{2,0},{4,2},{6,4},{1,7},{3,1},{5,3},{7,5},{8,14},{10,8},{12,... | collective-permute-start | bytes 688136 | tf_op jit(solution)/shard_map/ppermute | solution.py:233
  54.4 14.6 %collective-permute-start.6 = (f32[4,2,7,8,128]{4,3,2,1,0:T(8,128)S(1)}, f32[4,2,7,8,128]{4,3,2,1,0:T(8,128)S(1)}, u32[]{:S(2)}, u32[]{:S(2)}) collective-permute-start(f32[4,2,7,8,128]{4,3,2,1,0:T(8,128)S(1)} %get-tuple-element.18), channel_id=1, source_target_pairs={{0,2},{2,4},{4,6},{6,0},{1,3},{3,5},{5,7},{7,1},{8,10},{10,12},{12... | collective-permute-start | bytes 688136 | tf_op jit(solution)/shard_map/ppermute | solution.py:233
  54.4 14.6 %collective-permute-start.5 = (f32[4,2,7,8,128]{4,3,2,1,0:T(8,128)S(1)}, f32[4,2,7,8,128]{4,3,2,1,0:T(8,128)S(1)}, u32[]{:S(2)}, u32[]{:S(2)}) collective-permute-start(f32[4,2,7,8,128]{4,3,2,1,0:T(8,128)S(1)} %get-tuple-element.19), channel_id=1, source_target_pairs={{0,4},{2,6},{4,0},{6,2},{1,5},{3,7},{5,1},{7,3},{8,12},{10,14},{12... | collective-permute-start | bytes 688136 | tf_op jit(solution)/shard_map/ppermute | solution.py:233
  56.3 28.0 %collective-permute-start.11 = (f32[4,2,7,16,128]{4,3,2,1,0:T(8,128)S(1)}, f32[4,2,7,16,128]{4,3,2,1,0:T(8,128)S(1)}, u32[]{:S(2)}, u32[]{:S(2)}) collective-permute-start(f32[4,2,7,16,128]{4,3,2,1,0:T(8,128)S(1)} %get-tuple-element.14), channel_id=1, source_target_pairs={{0,6},{2,0},{4,2},{6,4},{1,7},{3,1},{5,3},{7,5},{8,14},{10,8},{12,... | collective-permute-start | bytes 1376264 | tf_op jit(solution)/shard_map/ppermute | solution.py:233
  58.3 29.5 %collective-permute-start.10 = (f32[4,2,7,16,128]{4,3,2,1,0:T(8,128)S(1)}, f32[4,2,7,16,128]{4,3,2,1,0:T(8,128)S(1)}, u32[]{:S(2)}, u32[]{:S(2)}) collective-permute-start(f32[4,2,7,16,128]{4,3,2,1,0:T(8,128)S(1)} %get-tuple-element.15), channel_id=1, source_target_pairs={{0,2},{2,4},{4,6},{6,0},{1,3},{3,5},{5,7},{7,1},{8,10},{10,12},{12... | collective-permute-start | bytes 1376264 | tf_op jit(solution)/shard_map/ppermute | solution.py:233
  65.1 22.7 %collective-permute-start.9 = (f32[4,2,7,16,128]{4,3,2,1,0:T(8,128)S(1)}, f32[4,2,7,16,128]{4,3,2,1,0:T(8,128)S(1)}, u32[]{:S(2)}, u32[]{:S(2)}) collective-permute-start(f32[4,2,7,16,128]{4,3,2,1,0:T(8,128)S(1)} %get-tuple-element.16), channel_id=1, source_target_pairs={{0,4},{2,6},{4,0},{6,2},{1,5},{3,7},{5,1},{7,3},{8,12},{10,14},{12... | collective-permute-start | bytes 1376264 | tf_op jit(solution)/shard_map/ppermute | solution.py:233
  87.9 10.5 %collective-permute-start.14 = (f32[2,7,24,128]{3,2,1,0:T(8,128)S(1)}, f32[2,7,24,128]{3,2,1,0:T(8,128)S(1)}, u32[]{:S(2)}, u32[]{:S(2)}) collective-permute-start(f32[2,7,24,128]{3,2,1,0:T(8,128)S(1)} %get-tuple-element.20), channel_id=1, source_target_pairs={{0,192},{64,0},{128,64},{192,128},{1,193},{65,1},{129,65},{193,129... | collective-permute-start | bytes 516104 | tf_op jit(solution)/shard_map/ppermute | solution.py:233
  88.8 9.6 %collective-permute-start.12 = (f32[2,7,24,128]{3,2,1,0:T(8,128)S(1)}, f32[2,7,24,128]{3,2,1,0:T(8,128)S(1)}, u32[]{:S(2)}, u32[]{:S(2)}) collective-permute-start(f32[2,7,24,128]{3,2,1,0:T(8,128)S(1)} %get-tuple-element.21), channel_id=1, source_target_pairs={{0,128},{64,192},{128,0},{192,64},{1,129},{65,193},{129,1},{193,65... | collective-permute-start | bytes 516104 | tf_op jit(solution)/shard_map/ppermute | solution.py:233
  89.8 9.2 %collective-permute-start.13 = (f32[2,7,24,128]{3,2,1,0:T(8,128)S(1)}, f32[2,7,24,128]{3,2,1,0:T(8,128)S(1)}, u32[]{:S(2)}, u32[]{:S(2)}) collective-permute-start(f32[2,7,24,128]{3,2,1,0:T(8,128)S(1)} %get-tuple-element.22), channel_id=1, source_target_pairs={{0,64},{64,128},{128,192},{192,0},{1,65},{65,129},{129,193},{193,1... | collective-permute-start | bytes 516104 | tf_op jit(solution)/shard_map/ppermute | solution.py:233
  99.1 8.6 %collective-permute-start.15 = (f32[7,24,128]{2,1,0:T(8,128)S(1)}, f32[7,24,128]{2,1,0:T(8,128)S(1)}, u32[]{:S(2)}, u32[]{:S(2)}) collective-permute-start(f32[7,24,128]{2,1,0:T(8,128)S(1)} %slice_bitcast_fusion.11), channel_id=1, source_target_pairs={{0,8},{8,0},{1,9},{9,1},{2,10},{10,2},{3,11},{11,3},{4,12},{12,4},... | collective-permute-start | bytes 258056 | tf_op jit(solution)/shard_map/ppermute | solution.py:272
  107.7 12.4 %collective-permute-start.18 = (f32[7,24,128]{2,1,0:T(8,128)S(1)}, f32[7,24,128]{2,1,0:T(8,128)S(1)}, u32[]{:S(2)}, u32[]{:S(2)}) collective-permute-start(f32[7,24,128]{2,1,0:T(8,128)S(1)} %fusion.15), channel_id=1, source_target_pairs={{0,48},{16,0},{32,16},{48,32},{1,49},{17,1},{33,17},{49,33},{2,50}... | collective-permute-start | bytes 258056 | tf_op jit(solution)/shard_map/ppermute | solution.py:273
  111.2 9.0 %collective-permute-start.17 = (f32[7,24,128]{2,1,0:T(8,128)S(1)}, f32[7,24,128]{2,1,0:T(8,128)S(1)}, u32[]{:S(2)}, u32[]{:S(2)}) collective-permute-start(f32[7,24,128]{2,1,0:T(8,128)S(1)} %fusion.15), channel_id=1, source_target_pairs={{0,16},{16,32},{32,48},{48,0},{1,17},{17,33},{33,49},{49,1},{2,18}... | collective-permute-start | bytes 258056 | tf_op jit(solution)/shard_map/ppermute | solution.py:273
  111.2 9.0 %collective-permute-start.16 = (f32[7,24,128]{2,1,0:T(8,128)S(1)}, f32[7,24,128]{2,1,0:T(8,128)S(1)}, u32[]{:S(2)}, u32[]{:S(2)}) collective-permute-start(f32[7,24,128]{2,1,0:T(8,128)S(1)} %fusion.15), channel_id=1, source_target_pairs={{0,32},{16,48},{32,0},{48,16},{1,33},{17,49},{33,1},{49,17},{2,34}... | collective-permute-start | bytes 258056 | tf_op jit(solution)/shard_map/ppermute | solution.py:273
  120.2 13.9 %collective-permute-start.21 = (f32[7,24,128]{2,1,0:T(8,128)S(1)}, f32[7,24,128]{2,1,0:T(8,128)S(1)}, u32[]{:S(2)}, u32[]{:S(2)}) collective-permute-start(f32[7,24,128]{2,1,0:T(8,128)S(1)} %add_add_fusion), channel_id=1, source_target_pairs={{0,192},{64,0},{128,64},{192,128},{1,193},{65,1},{129,65},{193,129... | collective-permute-start | bytes 258056 | tf_op jit(solution)/shard_map/ppermute | solution.py:275
  122.7 11.5 %collective-permute-start.20 = (f32[7,24,128]{2,1,0:T(8,128)S(1)}, f32[7,24,128]{2,1,0:T(8,128)S(1)}, u32[]{:S(2)}, u32[]{:S(2)}) collective-permute-start(f32[7,24,128]{2,1,0:T(8,128)S(1)} %add_add_fusion), channel_id=1, source_target_pairs={{0,128},{64,192},{128,0},{192,64},{1,129},{65,193},{129,1},{193,65... | collective-permute-start | bytes 258056 | tf_op jit(solution)/shard_map/ppermute | solution.py:275
  124.9 9.3 %collective-permute-start.19 = (f32[7,24,128]{2,1,0:T(8,128)S(1)}, f32[7,24,128]{2,1,0:T(8,128)S(1)}, u32[]{:S(2)}, u32[]{:S(2)}) collective-permute-start(f32[7,24,128]{2,1,0:T(8,128)S(1)} %add_add_fusion), channel_id=1, source_target_pairs={{0,64},{64,128},{128,192},{192,0},{1,65},{65,129},{129,193},{193,1... | collective-permute-start | bytes 258056 | tf_op jit(solution)/shard_map/ppermute | solution.py:275
  (5 other events, 17.9 us)

commit v2 on v1

--- a/solution.py
+++ b/solution.py
@@ -41,7 +41,7 @@
     return jnp.concatenate([first, second], axis=0)
 
 
-def store_terms(place_ref, out_ref, tap, value, depth):
+def store_terms(place_ref, keep_ref, send_ref, tap, value, depth):
     half = value.shape[0] // 2
     taps = (
         (0, value[:half, C:]),
@@ -52,11 +52,14 @@
     for time_tap, part in taps:
         number = 9 * time_tap + tap
         chunk = lax.rem(number // 7 - x + 4, 4)
-        for owner in range(16):
-            slot_core = lax.rem(owner % 2 - core + 2, 2)
-            slot_y = lax.rem((owner // 2) % 4 - y + 4, 4)
-            slot_zh = lax.rem(owner // 8 - zh + 2, 2)
-            out_ref[slot_core, slot_y, chunk, slot_zh, number % 7] = part[owner * depth : (owner + 1) * depth]
+        for owner in range(8):
+            slot_y = lax.rem(owner % 4 - y + 4, 4)
+            slot_zh = lax.rem(owner // 4 - zh + 2, 2)
+            first = part[2 * owner * depth : (2 * owner + 1) * depth]
+            second = part[(2 * owner + 1) * depth : (2 * owner + 2) * depth]
+            slots = (slot_y, chunk) if depth == 8 else (chunk, slot_y)
+            keep_ref[slots + (slot_zh, number % 7)] = jnp.where(core == 0, first, second)
+            send_ref[slots + (slot_zh, number % 7)] = jnp.where(core == 0, second, first)
 
 
 def shifted_cot(cot_ref, e):
@@ -64,7 +67,7 @@
     return split(both)
 
 
-def flow_terms_kernel(place_ref, flow_ref, cot_ref, out_ref):
+def flow_terms_kernel(place_ref, flow_ref, cot_ref, keep_ref, send_ref):
     flow = jnp.concatenate(
         [flow_ref[0].reshape(R2 * W2, CF).T, flow_ref[1].reshape(R2 * W2, CF).T], axis=0
     )
@@ -73,12 +76,14 @@
         cot = shifted_cot(cot_ref, 2 - col_tap)
         for row_tap in range(3):
             window = [v[2 - row_tap : 2 - row_tap + R2].reshape(R2 * W2, 2 * C) for v in cot]
-            store_terms(place_ref, out_ref, 3 * row_tap + col_tap, product(flow, window, NN), 16)
+            store_terms(
+                place_ref, keep_ref, send_ref, 3 * row_tap + col_tap, product(flow, window, NN), 16
+            )
 
 
 def block_kernel(
-    place_ref, feat_ref, top_ref, bottom_ref, left_ref, right_ref, weight_ref, cot_ref,
-    out_ref, grad_high_ref, grad_low_ref,
+    feat_ref, top_ref, bottom_ref, left_ref, right_ref, weight_ref, cot_ref,
+    grad_high_ref, grad_low_ref,
     ext_ref, wide_ref, taps_high, taps_low, even_high, even_low, odd_high, odd_low, grad_ref,
 ):
     ext_ref[...] = jnp.zeros_like(ext_ref)
@@ -133,6 +138,9 @@
         high, low = split(grad_ref[:, 3 - e : 3 - e + W, :])
         grad_high_ref[e] = high
         grad_low_ref[e] = low
+
+
+def block_terms_kernel(place_ref, feat_ref, grad_high_ref, grad_low_ref, keep_ref, send_ref):
     feat = split(
         jnp.concatenate([feat_ref[t].reshape(R * W, C).T for t in range(FR)], axis=0)
     )
@@ -142,7 +150,9 @@
                 ref[e, 2 - row_tap : 2 - row_tap + R].reshape(R * W, 2 * C)
                 for ref in (grad_high_ref, grad_low_ref)
             ]
-            store_terms(place_ref, out_ref, 3 * row_tap + e, product(feat, window, NN), 8)
+            store_terms(
+                place_ref, keep_ref, send_ref, 3 * row_tap + e, product(feat, window, NN), 8
+            )
 
 
 def adjoint_kernel(grad_high_ref, grad_low_ref, weight_one_ref, cot_ref, weight_two_ref, feat_out, flow_out):
@@ -173,22 +183,21 @@
 def flow_terms(place, flow, cot):
     return pl.pallas_call(
         flow_terms_kernel,
-        out_shape=jax.ShapeDtypeStruct((2, 4, 4, 2, 7, 16, C), f32),
+        out_shape=(jax.ShapeDtypeStruct((4, 4, 2, 7, 16, C), f32),) * 2,
         in_specs=[SMEM, VMEM, VMEM],
-        out_specs=VMEM,
+        out_specs=(VMEM,) * 2,
         compiler_params=params(),
         cost_estimate=pl.CostEstimate(flops=2 * 10**9, bytes_accessed=5 * 10**6, transcendentals=0),
         name="flow_terms",
     )(place, flow, cot)
 
 
-def block_terms(place, feat, top, bottom, left, right, weight, cot):
-    wins = jax.ShapeDtypeStruct((3, R + 2, W, 2 * C), bf16)
+def block_gradient(feat, top, bottom, left, right, weight, cot):
     return pl.pallas_call(
         block_kernel,
-        out_shape=(jax.ShapeDtypeStruct((2, 4, 4, 2, 7, 8, C), f32), wins, wins),
-        in_specs=[SMEM] + [VMEM] * 7,
-        out_specs=(VMEM,) * 3,
+        out_shape=(jax.ShapeDtypeStruct((3, R + 2, W, 2 * C), bf16),) * 2,
+        in_specs=[VMEM] * 7,
+        out_specs=(VMEM,) * 2,
         scratch_shapes=[
             pltpu.VMEM((R + 4, PITCH + 8, 2 * C), f32),
             pltpu.VMEM((FR, R + 2, PITCH, C), f32),
@@ -202,8 +211,20 @@
         ],
         compiler_params=params(),
         cost_estimate=pl.CostEstimate(flops=5 * 10**9, bytes_accessed=6 * 10**6, transcendentals=200000),
+        name="block_gradient",
+    )(feat, top, bottom, left, right, weight, cot)
+
+
+def block_terms(place, feat, grad_high, grad_low):
+    return pl.pallas_call(
+        block_terms_kernel,
+        out_shape=(jax.ShapeDtypeStruct((4, 4, 2, 7, 8, C), f32),) * 2,
+        in_specs=[SMEM] + [VMEM] * 3,
+        out_specs=(VMEM,) * 2,
+        compiler_params=params(),
+        cost_estimate=pl.CostEstimate(flops=10**9, bytes_accessed=10**6, transcendentals=0),
         name="block_terms",
-    )(place, feat, top, bottom, left, right, weight, cot)
+    )(place, feat, grad_high, grad_low)
 
 
 def adjoints(grad_high, grad_low, weight_one, cot, weight_two):
@@ -229,9 +250,12 @@
     return [(i, i + step) for i in range(count) if 0 <= i + step < count]
 
 
-def scatter_sum(parts, axis):
-    arrived = [lax.ppermute(parts[k], axis, ring(k)) for k in (2, 1, 3)]
-    return (parts[0] + arrived[0]) + (arrived[1] + arrived[2])
+def spread(parts, axis):
+    return [lax.ppermute(parts[k], axis, ring(k)) for k in (2, 1, 3)]
+
+
+def summed(own, arrived):
+    return (own + arrived[0]) + (arrived[1] + arrived[2])
 
 
 def local(features, weight_one, flow_feats, weight_two, cotangent):
@@ -258,20 +282,30 @@
     left_feat, right_feat = [v[:, :edge].reshape(FR, R + 4, 2, C) for v in (left, right)]
     cot = jnp.concatenate([left[:, edge:, None], tall, right[:, edge:, None]], axis=2)
 
-    terms_two = flow_terms(place, flow_feats, cot)
-    terms_one, grad_high, grad_low = block_terms(
-        place, features, top_feat, bottom_feat, left_feat, right_feat, kernel_one, cot
-    )
     swap = [(0, 1), (1, 0)]
-    sums = []
-    for terms in (terms_two, terms_one):
-        terms = terms[0] + lax.ppermute(terms[1], "core", swap)
-        sums.append(scatter_sum([terms[k] for k in range(4)], "y"))
-    chunks = jnp.concatenate([sums[1], sums[0]], axis=-2)
-    chunk = scatter_sum([chunks[k] for k in range(4)], "x")
+    keep, send = flow_terms(place, flow_feats, cot)
+    terms_two = keep + lax.ppermute(send, "core", swap)
+    grad_high, grad_low = block_gradient(
+        features, top_feat, bottom_feat, left_feat, right_feat, kernel_one, cot
+    )
+    terms_two, grad_high, grad_low = lax.optimization_barrier((terms_two, grad_high, grad_low))
+    arrived_two = spread(terms_two, "x")
+    keep, send = block_terms(place, features, grad_high, grad_low)
+    terms_one = keep + lax.ppermute(send, "core", swap)
+    arrived_one = spread(terms_one, "y")
+    terms_one, grad_high, grad_low = lax.optimization_barrier((terms_one, grad_high, grad_low))
+    grad_features, grad_flow = adjoints(grad_high, grad_low, kernel_one, cot, kernel_two)
+    arrived_one, arrived_two, grad_features, grad_flow = lax.optimization_barrier(
+        (arrived_one, arrived_two, grad_features, grad_flow)
+    )
+    terms_one = summed(terms_one[0], arrived_one)
+    terms_two = summed(terms_two[0], arrived_two)
+    arrived_one, arrived_two = spread(terms_one, "x"), spread(terms_two, "y")
+    terms_one = summed(terms_one[0], arrived_one)
+    terms_two = summed(terms_two[0], arrived_two)
+    chunk = jnp.concatenate([terms_one, terms_two], axis=-2)
     chunk = chunk[0] + lax.ppermute(chunk[1], "zh", swap)
-    arrived = [lax.ppermute(chunk, "zl", ring(k)) for k in (2, 1, 3)]
-    chunk = (chunk + arrived[0]) + (arrived[1] + arrived[2])
+    chunk = summed(chunk, spread([chunk] * 4, "zl"))
     pieces = jnp.stack([chunk] + [lax.ppermute(chunk, "x", ring(k)) for k in (1, 2, 3)])
     order = lax.rem(place[2] - jnp.arange(4) + 4, 4)
     taps = jnp.concatenate([lax.dynamic_index_in_dim(pieces, order[k], 0, False) for k in range(4)])[:27]
@@ -279,7 +313,6 @@
     scale_two = 1.0 / (FR * R2 * W2 * 256) ** 0.5
     grad_one = (taps[:, :8] * scale_one).reshape(3, 3, 3, 8, C)
     grad_two = (taps[:, 8:] * scale_two).reshape(3, 3, 3, 16, C)
-    grad_features, grad_flow = adjoints(grad_high, grad_low, kernel_one, cot, kernel_two)
     return (grad_features, grad_one, grad_flow, grad_two)
 
 

time: 138 us -> 122 us (0.88)
  the two profiles are of different devices: /device:TPU:6 before, /device:TPU:8 now
where the time goes in v2:
time: 122 us
  starting transfers between devices  66.8 us (55%)
  waiting for transfers between devices  23.9 us (20%)
  Pallas kernels  15.7 us (13%)
  between operations  8.47 us (7%)
  local copies, waits for them, and re-layouts  3.65 us (3%)
  other arithmetic  3.11 us (3%)
    ppermute x15, starting transfers between devices, spread(): return [lax.ppermute(parts[k], axis, ring(k)) for k in (2, 1, 3)]  48.9 us
    ppermute x1, waiting for transfers between devices, local(): chunk = chunk[0] + lax.ppermute(chunk[1], 'zh', swap)  8.93 us
    ppermute x15, waiting for transfers between devices, spread(): return [lax.ppermute(parts[k], axis, ring(k)) for k in (2, 1, 3)]  8.77 us
    pallas_call x1, Pallas kernels, adjoints(): pl.pallas_call(adjoint_kernel, out_shape=(jax.ShapeDtypeStruct((FR, R, W,...  6.85 us
    ppermute x3, starting transfers between devices, local(): lax.ppermute(chunk, 'x', ring(k))  4.94 us
    ppermute x1, waiting for transfers between devices, local(): lax.ppermute(rows_of(features[:, :2], cotangent[:, :1]), HA, line(16, -1))  4.46 us
    ppermute x1, starting transfers between devices, local(): lax.ppermute(rows_of(features[:, R - 2:], cotangent[:, R2 - 1:]), HA, lin...  3.83 us
    ppermute x1, starting transfers between devices, local(): right = lax.ppermute(cols_of(0, 0), WA, line(16, -1))  3.64 us
  transfers between devices with their start and end apart: 25, of which 9 were waited for; matrix products, arithmetic and copies ran while one was open for 2% of the time, Pallas kernels for 9%

profile of v2, /device:TPU:8, one launch (start us, length us, event | category | flops | bytes accessed | tf_op | source)
XLA Modules:
  0.0 121.6 jit_solution(16498072788711919751)
XLA Ops:
  2.3 3.8 %collective-permute-start = (f32[2,80,128]{2,1,0:T(8,128)S(1)}, f32[2,80,128]{2,1,0:T(8,128)S(1)}, u32[]{:S(2)}, u32[]{:S(2)}) collective-permute-start(f32[2,80,128]{2,1,0:T(8,128)S(1)} %pad_maximum_fusion.6), channel_id=1, source_target_pairs={{0,16},{16,32},{32,48},{48,64},{64,80},{80,96},{96,112},{112,128},... | collective-permute-start | bytes 245768 | tf_op jit(solution)/shard_map/ppermute | solution.py:268
  8.6 4.5 %collective-permute-done.1 = f32[2,80,128]{2,1,0:T(8,128)S(1)} collective-permute-done((f32[2,80,128]{2,1,0:T(8,128)S(1)}, f32[2,80,128]{2,1,0:T(8,128)S(1)}, u32[]{:S(2)}, u32[]{:S(2)}) %collective-permute-start.1) | collective-permute-done | bytes 81952 | tf_op jit(solution)/shard_map/ppermute | solution.py:269
  14.1 1.9 %collective-permute-start.2 = (f32[2,50,128]{2,1,0:T(8,128)S(1)}, f32[2,50,128]{2,1,0:T(8,128)S(1)}, u32[]{:S(2)}, u32[]{:S(2)}) collective-permute-start(f32[2,50,128]{2,1,0:T(8,128)S(1)} %pad_maximum_fusion.8), channel_id=1, source_target_pairs={{0,1},{1,2},{2,3},{3,4},{4,5},{5,6},{6,7},{7,8},{8,9},{9,10},{10,1... | collective-permute-start | bytes 153608 | tf_op jit(solution)/shard_map/ppermute | solution.py:279
  16.1 3.6 %collective-permute-start.3 = (f32[2,50,128]{2,1,0:T(8,128)S(1)}, f32[2,50,128]{2,1,0:T(8,128)S(1)}, u32[]{:S(2)}, u32[]{:S(2)}) collective-permute-start(f32[2,50,128]{2,1,0:T(8,128)S(1)} %pad_maximum_fusion.9), channel_id=1, source_target_pairs={{1,0},{2,1},{3,2},{4,3},{5,4},{6,5},{7,6},{8,7},{9,8},{10,9},{11,1... | collective-permute-start | bytes 153608 | tf_op jit(solution)/shard_map/ppermute | solution.py:280
  19.8 1.8 %collective-permute-done.3 = f32[2,50,128]{2,1,0:T(8,128)S(1)} collective-permute-done((f32[2,50,128]{2,1,0:T(8,128)S(1)}, f32[2,50,128]{2,1,0:T(8,128)S(1)}, u32[]{:S(2)}, u32[]{:S(2)}) %collective-permute-start.3) | collective-permute-done | bytes 51232 | tf_op jit(solution)/shard_map/ppermute | solution.py:280
  21.6 2.7 %flow_terms.1 = (f32[4,4,2,7,16,128]{5,4,3,2,1,0:T(8,128)S(1)}, f32[4,4,2,7,16,128]{5,4,3,2,1,0:T(8,128)S(1)}) custom-call(s32[4]{0:T(128)S(1)} %pad_add_fusion.place_ref, f32[2,8,16,256]{3,2,1,0:T(8,128)S(1)} %copy-done.2, f32[2,10,18,128]{3,2,1,0:T(8,128)S(1)} %pad_maximum_fusion.1.cot_ref), custom_call_target="tpu_custom_call" | custom-call | flops 2000000000 | bytes 5000000 | tf_op jit(solution)/shard_map/flow_terms/pallas_call | solution.py:184
  24.3 1.8 %collective-permute-start.4 = (f32[4,4,2,7,16,128]{5,4,3,2,1,0:T(8,128)S(1)}, f32[4,4,2,7,16,128]{5,4,3,2,1,0:T(8,128)S(1)}, u32[]{:S(2)}, u32[]{:S(2)}) collective-permute-start(f32[4,4,2,7,16,128]{5,4,3,2,1,0:T(8,128)S(1)} %get-tuple-element.27), channel_id=1, source_target_pairs={{0,1},{1,0},{2,3},{3,2},{4,5},{5,4},{6,7},{7,6},{8,9},{9,8},{10,11... | collective-permute-start | bytes 5505032 | tf_op jit(solution)/shard_map/ppermute | solution.py:287
  26.2 3.5 %block_gradient.1 = (bf16[3,18,32,256]{3,2,1,0:T(8,128)(2,1)S(1)}, bf16[3,18,32,256]{3,2,1,0:T(8,128)(2,1)S(1)}) custom-call(f32[2,16,32,128]{3,2,1,0:T(8,128)S(1)} %copy-done, f32[2,2,32,128]{3,2,1,0:T(8,128)S(1)} %bitcast.103, f32[2,2,32,128]{3,2,1,0:T(8,128)S(1)} %bitcast.105, f32[2,20,2,128]{3,2,1,0:T(2,128)S(1)} %bitcast.106, ...), custom_call_target="tpu_custom_call" | custom-call | flops 5000000000 | bytes 6000000 | tf_op jit(solution)/shard_map/block_gradient/pallas_call | solution.py:196
  29.9 2.6 %block_terms.1 = (f32[4,4,2,7,8,128]{5,4,3,2,1,0:T(8,128)S(1)}, f32[4,4,2,7,8,128]{5,4,3,2,1,0:T(8,128)S(1)}) custom-call(s32[4]{0:T(128)S(1)} %pad_add_fusion.place_ref, f32[2,16,32,128]{3,2,1,0:T(8,128)S(1)} %copy-done, bf16[3,18,32,256]{3,2,1,0:T(8,128)(2,1)S(1)} %get-tuple-element.35.grad_high_ref, ...), custom_call_target="tpu_custom_call" | custom-call | flops 1000000000 | bytes 1000000 | tf_op jit(solution)/shard_map/block_terms/pallas_call | solution.py:219
  34.5 1.7 %collective-permute-start.11 = (f32[4,2,7,16,128]{4,3,2,1,0:T(8,128)S(1)}, f32[4,2,7,16,128]{4,3,2,1,0:T(8,128)S(1)}, u32[]{:S(2)}, u32[]{:S(2)}) collective-permute-start(f32[4,2,7,16,128]{4,3,2,1,0:T(8,128)S(1)} %get-tuple-element.48), channel_id=1, source_target_pairs={{0,192},{64,0},{128,64},{192,128},{1,193},{65,1},{129,65},{193,129... | collective-permute-start | bytes 1376264 | tf_op jit(solution)/shard_map/ppermute | solution.py:254
  36.3 1.8 %collective-permute-start.9 = (f32[4,2,7,16,128]{4,3,2,1,0:T(8,128)S(1)}, f32[4,2,7,16,128]{4,3,2,1,0:T(8,128)S(1)}, u32[]{:S(2)}, u32[]{:S(2)}) collective-permute-start(f32[4,2,7,16,128]{4,3,2,1,0:T(8,128)S(1)} %get-tuple-element.50), channel_id=1, source_target_pairs={{0,128},{64,192},{128,0},{192,64},{1,129},{65,193},{129,1},{193,65... | collective-permute-start | bytes 1376264 | tf_op jit(solution)/shard_map/ppermute | solution.py:254
  38.3 13.6 %collective-permute-start.6 = (f32[4,2,7,8,128]{4,3,2,1,0:T(8,128)S(1)}, f32[4,2,7,8,128]{4,3,2,1,0:T(8,128)S(1)}, u32[]{:S(2)}, u32[]{:S(2)}) collective-permute-start(f32[4,2,7,8,128]{4,3,2,1,0:T(8,128)S(1)} %get-tuple-element.53), channel_id=1, source_target_pairs={{0,4},{2,6},{4,0},{6,2},{1,5},{3,7},{5,1},{7,3},{8,12},{10,14},{12... | collective-permute-start | bytes 688136 | tf_op jit(solution)/shard_map/ppermute | solution.py:254
  51.8 2.0 %collective-permute-start.8 = (f32[4,2,7,8,128]{4,3,2,1,0:T(8,128)S(1)}, f32[4,2,7,8,128]{4,3,2,1,0:T(8,128)S(1)}, u32[]{:S(2)}, u32[]{:S(2)}) collective-permute-start(f32[4,2,7,8,128]{4,3,2,1,0:T(8,128)S(1)} %get-tuple-element.51), channel_id=1, source_target_pairs={{0,6},{2,0},{4,2},{6,4},{1,7},{3,1},{5,3},{7,5},{8,14},{10,8},{12,... | collective-permute-start | bytes 688136 | tf_op jit(solution)/shard_map/ppermute | solution.py:254
  53.9 6.8 %adjoints.1 = (f32[2,16,32,128]{3,2,1,0:T(8,128)}, f32[2,8,16,256]{3,2,1,0:T(8,128)}) custom-call(bf16[3,18,32,256]{3,2,1,0:T(8,128)(2,1)S(1)} %get-tuple-element.35.grad_high_ref, bf16[3,18,32,256]{3,2,1,0:T(8,128)(2,1)S(1)} %get-tuple-element.36.grad_low_ref, f32[27,128,128]{2,1,0:T(8,128)S(1)} %bitcast.109, ...), custom_call_target="tpu_custom_call" | custom-call | flops 4000000000 | bytes 10000000 | tf_op jit(solution)/shard_map/adjoints/pallas_call | solution.py:231
  62.0 1.7 %collective-permute-start.12 = (f32[2,7,8,128]{3,2,1,0:T(8,128)S(1)}, f32[2,7,8,128]{3,2,1,0:T(8,128)S(1)}, u32[]{:S(2)}, u32[]{:S(2)}) collective-permute-start(f32[2,7,8,128]{3,2,1,0:T(8,128)S(1)} %get-tuple-element.67), channel_id=1, source_target_pairs={{0,128},{64,192},{128,0},{192,64},{1,129},{65,193},{129,1},{193,65... | collective-permute-start | bytes 172040 | tf_op jit(solution)/shard_map/ppermute | solution.py:254
  64.1 2.8 %collective-permute-start.14 = (f32[2,7,8,128]{3,2,1,0:T(8,128)S(1)}, f32[2,7,8,128]{3,2,1,0:T(8,128)S(1)}, u32[]{:S(2)}, u32[]{:S(2)}) collective-permute-start(f32[2,7,8,128]{3,2,1,0:T(8,128)S(1)} %get-tuple-element.65), channel_id=1, source_target_pairs={{0,192},{64,0},{128,64},{192,128},{1,193},{65,1},{129,65},{193,129... | collective-permute-start | bytes 172040 | tf_op jit(solution)/shard_map/ppermute | solution.py:254
  67.1 8.6 %collective-permute-start.15 = (f32[2,7,16,128]{3,2,1,0:T(8,128)S(1)}, f32[2,7,16,128]{3,2,1,0:T(8,128)S(1)}, u32[]{:S(2)}, u32[]{:S(2)}) collective-permute-start(f32[2,7,16,128]{3,2,1,0:T(8,128)S(1)} %get-tuple-element.60), channel_id=1, source_target_pairs={{0,4},{2,6},{4,0},{6,2},{1,5},{3,7},{5,1},{7,3},{8,12},{10,14},{12... | collective-permute-start | bytes 344072 | tf_op jit(solution)/shard_map/ppermute | solution.py:254
  76.1 1.7 %collective-permute-start.17 = (f32[2,7,16,128]{3,2,1,0:T(8,128)S(1)}, f32[2,7,16,128]{3,2,1,0:T(8,128)S(1)}, u32[]{:S(2)}, u32[]{:S(2)}) collective-permute-start(f32[2,7,16,128]{3,2,1,0:T(8,128)S(1)} %get-tuple-element.58), channel_id=1, source_target_pairs={{0,6},{2,0},{4,2},{6,4},{1,7},{3,1},{5,3},{7,5},{8,14},{10,8},{12,... | collective-permute-start | bytes 344072 | tf_op jit(solution)/shard_map/ppermute | solution.py:254
  81.0 8.9 %collective-permute-done.18 = f32[7,24,128]{2,1,0:T(8,128)S(1)} collective-permute-done((f32[7,24,128]{2,1,0:T(8,128)S(1)}, f32[7,24,128]{2,1,0:T(8,128)S(1)}, u32[]{:S(2)}, u32[]{:S(2)}) %collective-permute-start.18) | collective-permute-done | bytes 86048 | tf_op jit(solution)/shard_map/ppermute | solution.py:307
  90.1 12.5 %collective-permute-start.20 = (f32[7,24,128]{2,1,0:T(8,128)S(1)}, f32[7,24,128]{2,1,0:T(8,128)S(1)}, u32[]{:S(2)}, u32[]{:S(2)}) collective-permute-start(f32[7,24,128]{2,1,0:T(8,128)S(1)} %fusion.7), channel_id=1, source_target_pairs={{0,16},{16,32},{32,48},{48,0},{1,17},{17,33},{33,49},{49,1},{2,18}... | collective-permute-start | bytes 258056 | tf_op jit(solution)/shard_map/ppermute | solution.py:254
  102.6 2.8 %collective-permute-done.20 = f32[7,24,128]{2,1,0:T(8,128)S(1)} collective-permute-done((f32[7,24,128]{2,1,0:T(8,128)S(1)}, f32[7,24,128]{2,1,0:T(8,128)S(1)}, u32[]{:S(2)}, u32[]{:S(2)}) %collective-permute-start.20) | collective-permute-done | bytes 86048 | tf_op jit(solution)/shard_map/ppermute | solution.py:254
  105.4 1.7 %collective-permute-done.21 = f32[7,24,128]{2,1,0:T(8,128)S(1)} collective-permute-done((f32[7,24,128]{2,1,0:T(8,128)S(1)}, f32[7,24,128]{2,1,0:T(8,128)S(1)}, u32[]{:S(2)}, u32[]{:S(2)}) %collective-permute-start.21) | collective-permute-done | bytes 86048 | tf_op jit(solution)/shard_map/ppermute | solution.py:254
  107.4 2.2 %collective-permute-start.23 = (f32[7,24,128]{2,1,0:T(8,128)S(1)}, f32[7,24,128]{2,1,0:T(8,128)S(1)}, u32[]{:S(2)}, u32[]{:S(2)}) collective-permute-start(f32[7,24,128]{2,1,0:T(8,128)S(1)} %add_add_fusion), channel_id=1, source_target_pairs={{0,128},{64,192},{128,0},{192,64},{1,129},{65,193},{129,1},{193,65... | collective-permute-start | bytes 258056 | tf_op jit(solution)/shard_map/ppermute | solution.py:309
  109.5 2.5 %collective-permute-start.24 = (f32[7,24,128]{2,1,0:T(8,128)S(1)}, f32[7,24,128]{2,1,0:T(8,128)S(1)}, u32[]{:S(2)}, u32[]{:S(2)}) collective-permute-start(f32[7,24,128]{2,1,0:T(8,128)S(1)} %add_add_fusion), channel_id=1, source_target_pairs={{0,192},{64,0},{128,64},{192,128},{1,193},{65,1},{129,65},{193,129... | collective-permute-start | bytes 258056 | tf_op jit(solution)/shard_map/ppermute | solution.py:309
  (83 shorter events, 15.5 us)
Async XLA Ops:
  2.3 6.2 %collective-permute-start = (f32[2,80,128]{2,1,0:T(8,128)S(1)}, f32[2,80,128]{2,1,0:T(8,128)S(1)}, u32[]{:S(2)}, u32[]{:S(2)}) collective-permute-start(f32[2,80,128]{2,1,0:T(8,128)S(1)} %pad_maximum_fusion.6), channel_id=1, source_target_pairs={{0,16},{16,32},{32,48},{48,64},{64,80},{80,96},{96,112},{112,128},... | collective-permute-start | bytes 245768 | tf_op jit(solution)/shard_map/ppermute | solution.py:268
  6.2 6.9 %collective-permute-start.1 = (f32[2,80,128]{2,1,0:T(8,128)S(1)}, f32[2,80,128]{2,1,0:T(8,128)S(1)}, u32[]{:S(2)}, u32[]{:S(2)}) collective-permute-start(f32[2,80,128]{2,1,0:T(8,128)S(1)} %pad_maximum_fusion.7), channel_id=1, source_target_pairs={{16,0},{32,16},{48,32},{64,48},{80,64},{96,80},{112,96},{128,112},... | collective-permute-start | bytes 245768 | tf_op jit(solution)/shard_map/ppermute | solution.py:269
  14.1 5.6 %collective-permute-start.2 = (f32[2,50,128]{2,1,0:T(8,128)S(1)}, f32[2,50,128]{2,1,0:T(8,128)S(1)}, u32[]{:S(2)}, u32[]{:S(2)}) collective-permute-start(f32[2,50,128]{2,1,0:T(8,128)S(1)} %pad_maximum_fusion.8), channel_id=1, source_target_pairs={{0,1},{1,2},{2,3},{3,4},{4,5},{5,6},{6,7},{7,8},{8,9},{9,10},{10,1... | collective-permute-start | bytes 153608 | tf_op jit(solution)/shard_map/ppermute | solution.py:279
  16.1 5.5 %collective-permute-start.3 = (f32[2,50,128]{2,1,0:T(8,128)S(1)}, f32[2,50,128]{2,1,0:T(8,128)S(1)}, u32[]{:S(2)}, u32[]{:S(2)}) collective-permute-start(f32[2,50,128]{2,1,0:T(8,128)S(1)} %pad_maximum_fusion.9), channel_id=1, source_target_pairs={{1,0},{2,1},{3,2},{4,3},{5,4},{6,5},{7,6},{8,7},{9,8},{10,9},{11,1... | collective-permute-start | bytes 153608 | tf_op jit(solution)/shard_map/ppermute | solution.py:280
  24.3 5.4 %collective-permute-start.4 = (f32[4,4,2,7,16,128]{5,4,3,2,1,0:T(8,128)S(1)}, f32[4,4,2,7,16,128]{5,4,3,2,1,0:T(8,128)S(1)}, u32[]{:S(2)}, u32[]{:S(2)}) collective-permute-start(f32[4,4,2,7,16,128]{5,4,3,2,1,0:T(8,128)S(1)} %get-tuple-element.27), channel_id=1, source_target_pairs={{0,1},{1,0},{2,3},{3,2},{4,5},{5,4},{6,7},{7,6},{8,9},{9,8},{10,11... | collective-permute-start | bytes 5505032 | tf_op jit(solution)/shard_map/ppermute | solution.py:287
  32.6 5.5 %collective-permute-start.5 = (f32[4,4,2,7,8,128]{5,4,3,2,1,0:T(8,128)S(1)}, f32[4,4,2,7,8,128]{5,4,3,2,1,0:T(8,128)S(1)}, u32[]{:S(2)}, u32[]{:S(2)}) collective-permute-start(f32[4,4,2,7,8,128]{5,4,3,2,1,0:T(8,128)S(1)} %get-tuple-element.33), channel_id=1, source_target_pairs={{0,1},{1,0},{2,3},{3,2},{4,5},{5,4},{6,7},{7,6},{8,9},{9,8},{10,11... | collective-permute-start | bytes 2752520 | tf_op jit(solution)/shard_map/ppermute | solution.py:294
  33.0 18.9 %collective-permute-start.10 = (f32[4,2,7,16,128]{4,3,2,1,0:T(8,128)S(1)}, f32[4,2,7,16,128]{4,3,2,1,0:T(8,128)S(1)}, u32[]{:S(2)}, u32[]{:S(2)}) collective-permute-start(f32[4,2,7,16,128]{4,3,2,1,0:T(8,128)S(1)} %get-tuple-element.49), channel_id=1, source_target_pairs={{0,64},{64,128},{128,192},{192,0},{1,65},{65,129},{129,193},{193,1... | collective-permute-start | bytes 1376264 | tf_op jit(solution)/shard_map/ppermute | solution.py:254
  34.5 26.2 %collective-permute-start.11 = (f32[4,2,7,16,128]{4,3,2,1,0:T(8,128)S(1)}, f32[4,2,7,16,128]{4,3,2,1,0:T(8,128)S(1)}, u32[]{:S(2)}, u32[]{:S(2)}) collective-permute-start(f32[4,2,7,16,128]{4,3,2,1,0:T(8,128)S(1)} %get-tuple-element.48), channel_id=1, source_target_pairs={{0,192},{64,0},{128,64},{192,128},{1,193},{65,1},{129,65},{193,129... | collective-permute-start | bytes 1376264 | tf_op jit(solution)/shard_map/ppermute | solution.py:254
  36.3 24.4 %collective-permute-start.9 = (f32[4,2,7,16,128]{4,3,2,1,0:T(8,128)S(1)}, f32[4,2,7,16,128]{4,3,2,1,0:T(8,128)S(1)}, u32[]{:S(2)}, u32[]{:S(2)}) collective-permute-start(f32[4,2,7,16,128]{4,3,2,1,0:T(8,128)S(1)} %get-tuple-element.50), channel_id=1, source_target_pairs={{0,128},{64,192},{128,0},{192,64},{1,129},{65,193},{129,1},{193,65... | collective-permute-start | bytes 1376264 | tf_op jit(solution)/shard_map/ppermute | solution.py:254
  38.3 22.5 %collective-permute-start.6 = (f32[4,2,7,8,128]{4,3,2,1,0:T(8,128)S(1)}, f32[4,2,7,8,128]{4,3,2,1,0:T(8,128)S(1)}, u32[]{:S(2)}, u32[]{:S(2)}) collective-permute-start(f32[4,2,7,8,128]{4,3,2,1,0:T(8,128)S(1)} %get-tuple-element.53), channel_id=1, source_target_pairs={{0,4},{2,6},{4,0},{6,2},{1,5},{3,7},{5,1},{7,3},{8,12},{10,14},{12... | collective-permute-start | bytes 688136 | tf_op jit(solution)/shard_map/ppermute | solution.py:254
  51.8 8.9 %collective-permute-start.7 = (f32[4,2,7,8,128]{4,3,2,1,0:T(8,128)S(1)}, f32[4,2,7,8,128]{4,3,2,1,0:T(8,128)S(1)}, u32[]{:S(2)}, u32[]{:S(2)}) collective-permute-start(f32[4,2,7,8,128]{4,3,2,1,0:T(8,128)S(1)} %get-tuple-element.52), channel_id=1, source_target_pairs={{0,2},{2,4},{4,6},{6,0},{1,3},{3,5},{5,7},{7,1},{8,10},{10,12},{12... | collective-permute-start | bytes 688136 | tf_op jit(solution)/shard_map/ppermute | solution.py:254
  51.8 10.1 %collective-permute-start.8 = (f32[4,2,7,8,128]{4,3,2,1,0:T(8,128)S(1)}, f32[4,2,7,8,128]{4,3,2,1,0:T(8,128)S(1)}, u32[]{:S(2)}, u32[]{:S(2)}) collective-permute-start(f32[4,2,7,8,128]{4,3,2,1,0:T(8,128)S(1)} %get-tuple-element.51), channel_id=1, source_target_pairs={{0,6},{2,0},{4,2},{6,4},{1,7},{3,1},{5,3},{7,5},{8,14},{10,8},{12,... | collective-permute-start | bytes 688136 | tf_op jit(solution)/shard_map/ppermute | solution.py:254
  62.0 14.0 %collective-permute-start.12 = (f32[2,7,8,128]{3,2,1,0:T(8,128)S(1)}, f32[2,7,8,128]{3,2,1,0:T(8,128)S(1)}, u32[]{:S(2)}, u32[]{:S(2)}) collective-permute-start(f32[2,7,8,128]{3,2,1,0:T(8,128)S(1)} %get-tuple-element.67), channel_id=1, source_target_pairs={{0,128},{64,192},{128,0},{192,64},{1,129},{65,193},{129,1},{193,65... | collective-permute-start | bytes 172040 | tf_op jit(solution)/shard_map/ppermute | solution.py:254
  63.7 14.0 %collective-permute-start.13 = (f32[2,7,8,128]{3,2,1,0:T(8,128)S(1)}, f32[2,7,8,128]{3,2,1,0:T(8,128)S(1)}, u32[]{:S(2)}, u32[]{:S(2)}) collective-permute-start(f32[2,7,8,128]{3,2,1,0:T(8,128)S(1)} %get-tuple-element.66), channel_id=1, source_target_pairs={{0,64},{64,128},{128,192},{192,0},{1,65},{65,129},{129,193},{193,1... | collective-permute-start | bytes 172040 | tf_op jit(solution)/shard_map/ppermute | solution.py:254
  64.1 13.7 %collective-permute-start.14 = (f32[2,7,8,128]{3,2,1,0:T(8,128)S(1)}, f32[2,7,8,128]{3,2,1,0:T(8,128)S(1)}, u32[]{:S(2)}, u32[]{:S(2)}) collective-permute-start(f32[2,7,8,128]{3,2,1,0:T(8,128)S(1)} %get-tuple-element.65), channel_id=1, source_target_pairs={{0,192},{64,0},{128,64},{192,128},{1,193},{65,1},{129,65},{193,129... | collective-permute-start | bytes 172040 | tf_op jit(solution)/shard_map/ppermute | solution.py:254
  67.1 12.1 %collective-permute-start.15 = (f32[2,7,16,128]{3,2,1,0:T(8,128)S(1)}, f32[2,7,16,128]{3,2,1,0:T(8,128)S(1)}, u32[]{:S(2)}, u32[]{:S(2)}) collective-permute-start(f32[2,7,16,128]{3,2,1,0:T(8,128)S(1)} %get-tuple-element.60), channel_id=1, source_target_pairs={{0,4},{2,6},{4,0},{6,2},{1,5},{3,7},{5,1},{7,3},{8,12},{10,14},{12... | collective-permute-start | bytes 344072 | tf_op jit(solution)/shard_map/ppermute | solution.py:254
  75.7 4.8 %collective-permute-start.16 = (f32[2,7,16,128]{3,2,1,0:T(8,128)S(1)}, f32[2,7,16,128]{3,2,1,0:T(8,128)S(1)}, u32[]{:S(2)}, u32[]{:S(2)}) collective-permute-start(f32[2,7,16,128]{3,2,1,0:T(8,128)S(1)} %get-tuple-element.59), channel_id=1, source_target_pairs={{0,2},{2,4},{4,6},{6,0},{1,3},{3,5},{5,7},{7,1},{8,10},{10,12},{12... | collective-permute-start | bytes 344072 | tf_op jit(solution)/shard_map/ppermute | solution.py:254
  76.1 4.8 %collective-permute-start.17 = (f32[2,7,16,128]{3,2,1,0:T(8,128)S(1)}, f32[2,7,16,128]{3,2,1,0:T(8,128)S(1)}, u32[]{:S(2)}, u32[]{:S(2)}) collective-permute-start(f32[2,7,16,128]{3,2,1,0:T(8,128)S(1)} %get-tuple-element.58), channel_id=1, source_target_pairs={{0,6},{2,0},{4,2},{6,4},{1,7},{3,1},{5,3},{7,5},{8,14},{10,8},{12,... | collective-permute-start | bytes 344072 | tf_op jit(solution)/shard_map/ppermute | solution.py:254
  80.9 9.0 %collective-permute-start.18 = (f32[7,24,128]{2,1,0:T(8,128)S(1)}, f32[7,24,128]{2,1,0:T(8,128)S(1)}, u32[]{:S(2)}, u32[]{:S(2)}) collective-permute-start(f32[7,24,128]{2,1,0:T(8,128)S(1)} %fusion.8), channel_id=1, source_target_pairs={{0,8},{8,0},{1,9},{9,1},{2,10},{10,2},{3,11},{11,3},{4,12},{12,4},... | collective-permute-start | bytes 258056 | tf_op jit(solution)/shard_map/ppermute | solution.py:307
  90.0 12.7 %collective-permute-start.19 = (f32[7,24,128]{2,1,0:T(8,128)S(1)}, f32[7,24,128]{2,1,0:T(8,128)S(1)}, u32[]{:S(2)}, u32[]{:S(2)}) collective-permute-start(f32[7,24,128]{2,1,0:T(8,128)S(1)} %fusion.7), channel_id=1, source_target_pairs={{0,32},{16,48},{32,0},{48,16},{1,33},{17,49},{33,1},{49,17},{2,34}... | collective-permute-start | bytes 258056 | tf_op jit(solution)/shard_map/ppermute | solution.py:254
  90.1 15.3 %collective-permute-start.20 = (f32[7,24,128]{2,1,0:T(8,128)S(1)}, f32[7,24,128]{2,1,0:T(8,128)S(1)}, u32[]{:S(2)}, u32[]{:S(2)}) collective-permute-start(f32[7,24,128]{2,1,0:T(8,128)S(1)} %fusion.7), channel_id=1, source_target_pairs={{0,16},{16,32},{32,48},{48,0},{1,17},{17,33},{33,49},{49,1},{2,18}... | collective-permute-start | bytes 258056 | tf_op jit(solution)/shard_map/ppermute | solution.py:254
  107.1 13.0 %collective-permute-start.22 = (f32[7,24,128]{2,1,0:T(8,128)S(1)}, f32[7,24,128]{2,1,0:T(8,128)S(1)}, u32[]{:S(2)}, u32[]{:S(2)}) collective-permute-start(f32[7,24,128]{2,1,0:T(8,128)S(1)} %add_add_fusion), channel_id=1, source_target_pairs={{0,64},{64,128},{128,192},{192,0},{1,65},{65,129},{129,193},{193,1... | collective-permute-start | bytes 258056 | tf_op jit(solution)/shard_map/ppermute | solution.py:309
  107.4 12.8 %collective-permute-start.23 = (f32[7,24,128]{2,1,0:T(8,128)S(1)}, f32[7,24,128]{2,1,0:T(8,128)S(1)}, u32[]{:S(2)}, u32[]{:S(2)}) collective-permute-start(f32[7,24,128]{2,1,0:T(8,128)S(1)} %add_add_fusion), channel_id=1, source_target_pairs={{0,128},{64,192},{128,0},{192,64},{1,129},{65,193},{129,1},{193,65... | collective-permute-start | bytes 258056 | tf_op jit(solution)/shard_map/ppermute | solution.py:309
  109.5 10.6 %collective-permute-start.24 = (f32[7,24,128]{2,1,0:T(8,128)S(1)}, f32[7,24,128]{2,1,0:T(8,128)S(1)}, u32[]{:S(2)}, u32[]{:S(2)}) collective-permute-start(f32[7,24,128]{2,1,0:T(8,128)S(1)} %add_add_fusion), channel_id=1, source_target_pairs={{0,192},{64,0},{128,64},{192,128},{1,193},{65,1},{129,65},{193,129... | collective-permute-start | bytes 258056 | tf_op jit(solution)/shard_map/ppermute | solution.py:309
  (5 other events, 55.4 us)

commit v3 on v2

--- a/solution.py
+++ b/solution.py
@@ -12,6 +12,7 @@
 R2, W2, CF = 8, 16, 256
 PITCH = 40
 EXT = (R + 2) * PITCH
+COL = 24
 HA, WA = ("x", "zl"), ("zh", "y", "core")
 
 f32, bf16 = jnp.float32, jnp.bfloat16
@@ -62,12 +63,71 @@
             send_ref[slots + (slot_zh, number % 7)] = jnp.where(core == 0, second, first)
 
 
+def row_edges_kernel(place_ref, feat_ref, cot_ref, first_ref, second_ref):
+    odd = place_ref[4] == 1
+    for t in range(FR):
+        for row in range(2):
+            top, bottom = feat_ref[t, row], feat_ref[t, R - 2 + row]
+            lines = slice(row * W, (row + 1) * W)
+            first_ref[t, lines] = jnp.where(odd, top, bottom)
+            second_ref[t, lines] = jnp.where(odd, bottom, top)
+        top, bottom = cot_ref[t, 0], cot_ref[t, R2 - 1]
+        first_ref[t, 2 * W :] = jnp.where(odd, top, bottom)
+        second_ref[t, 2 * W :] = jnp.where(odd, bottom, top)
+
+
+def row_halo(place_ref, first_ref, second_ref, t, lines):
+    odd = place_ref[4] == 1
+    first, second = first_ref[t, lines], second_ref[t, lines]
+    return jnp.where(odd, first, second), jnp.where(odd, second, first)
+
+
+def col_edges_kernel(place_ref, feat_ref, cot_ref, row_first_ref, row_second_ref, first_ref, second_ref, edge_ref):
+    for t in range(FR):
+        halos = [row_halo(place_ref, row_first_ref, row_second_ref, t, slice(r * W, (r + 1) * W)) for r in range(2)]
+        for side, start in ((0, 0), (1, W - 2)):
+            for col in range(2):
+                at, place = start + col, col * COL
+                for row in range(2):
+                    edge_ref[side, t, place + row : place + row + 1] = halos[row][0][at : at + 1]
+                    low = place + R + 2 + row
+                    edge_ref[side, t, low : low + 1] = halos[row][1][at : at + 1]
+                edge_ref[side, t, place + 2 : place + 2 + R] = feat_ref[t, :, at, :]
+        above, below = row_halo(place_ref, row_first_ref, row_second_ref, t, slice(2 * W, 2 * W + W2))
+        for side, at in ((0, 0), (1, W2 - 1)):
+            place = 2 * COL
+            edge_ref[side, t, place : place + 1] = above[at : at + 1]
+            edge_ref[side, t, place + 1 : place + 1 + R2] = cot_ref[t, :, at, :]
+            edge_ref[side, t, place + 1 + R2 : place + 2 + R2] = below[at : at + 1]
+    odd = place_ref[0] == 1
+    first_ref[...] = jnp.where(odd, edge_ref[0], edge_ref[1])
+    second_ref[...] = jnp.where(odd, edge_ref[1], edge_ref[0])
+
+
+def col_halo(place_ref, first_ref, second_ref, t, lines):
+    odd = place_ref[0] == 1
+    first, second = first_ref[t, lines], second_ref[t, lines]
+    return jnp.where(odd, first, second), jnp.where(odd, second, first)
+
+
 def shifted_cot(cot_ref, e):
     both = jnp.concatenate([cot_ref[0, :, e : e + W2, :], cot_ref[1, :, e : e + W2, :]], axis=-1)
     return split(both)
 
 
-def flow_terms_kernel(place_ref, flow_ref, cot_ref, keep_ref, send_ref):
+def flow_terms_kernel(
+    place_ref, flow_ref, local_ref, row_first_ref, row_second_ref, col_first_ref, col_second_ref,
+    keep_ref, send_ref, cot_ref,
+):
+    for t in range(FR):
+        above, below = row_halo(place_ref, row_first_ref, row_second_ref, t, slice(2 * W, 2 * W + W2))
+        cot_ref[t, 0, 1 : 1 + W2] = above
+        cot_ref[t, 1 : 1 + R2, 1 : 1 + W2] = local_ref[t]
+        cot_ref[t, 1 + R2, 1 : 1 + W2] = below
+        lines = slice(2 * COL, 2 * COL + R2 + 2)
+        left, right = col_halo(place_ref, col_first_ref, col_second_ref, t, lines)
+        cot_ref[t, :, 0] = left
+        cot_ref[t, :, 1 + W2] = right
     flow = jnp.concatenate(
         [flow_ref[0].reshape(R2 * W2, CF).T, flow_ref[1].reshape(R2 * W2, CF).T], axis=0
     )
@@ -82,7 +142,7 @@
 
 
 def block_kernel(
-    feat_ref, top_ref, bottom_ref, left_ref, right_ref, weight_ref, cot_ref,
+    place_ref, feat_ref, row_first_ref, row_second_ref, col_first_ref, col_second_ref, weight_ref, cot_ref,
     grad_high_ref, grad_low_ref,
     ext_ref, wide_ref, taps_high, taps_low, even_high, even_low, odd_high, odd_low, grad_ref,
 ):
@@ -90,10 +150,14 @@
     for t in range(FR):
         lanes = slice(t * C, (t + 1) * C)
         ext_ref[2 : 2 + R, 3 : 3 + W, lanes] = feat_ref[t]
-        ext_ref[0:2, 3 : 3 + W, lanes] = top_ref[t]
-        ext_ref[2 + R : 4 + R, 3 : 3 + W, lanes] = bottom_ref[t]
-        ext_ref[0 : R + 4, 1:3, lanes] = left_ref[t]
-        ext_ref[0 : R + 4, 3 + W : 5 + W, lanes] = right_ref[t]
+        for row in range(2):
+            above, below = row_halo(place_ref, row_first_ref, row_second_ref, t, slice(row * W, (row + 1) * W))
+            ext_ref[row, 3 : 3 + W, lanes] = above
+            ext_ref[R + 2 + row, 3 : 3 + W, lanes] = below
+            place = slice(row * COL, row * COL + R + 4)
+            left, right = col_halo(place_ref, col_first_ref, col_second_ref, t, place)
+            ext_ref[:, 1 + row, lanes] = left
+            ext_ref[:, 3 + W + row, lanes] = right
     for t in range(FR):
         lanes = slice(t * C, (t + 1) * C)
         for row in range(R2 + 2):
@@ -176,27 +240,56 @@
         flow_out[t] = total[:, t * CF : (t + 1) * CF].reshape(R2, W2, CF)
 
 
+def gather_kernel(place_ref, own_ref, one_ref, two_ref, three_ref, grad_one_ref, grad_two_ref):
+    scale_one = 1.0 / (FR * R * W * 256) ** 0.5
+    scale_two = 1.0 / (FR * R2 * W2 * 256) ** 0.5
+    for k, ref in enumerate((own_ref, one_ref, two_ref, three_ref)):
+        first = 7 * lax.rem(place_ref[2] - k + 4, 4)
+
+        def put(j, ref=ref, first=first):
+            grad_one_ref[first + j] = ref[j, :8] * scale_one
+            grad_two_ref[first + j] = ref[j, 8:] * scale_two
+
+        for j in range(6):
+            put(j)
+        pl.when(first < 21)(functools.partial(put, 6))
+
+
 def params():
     return pltpu.CompilerParams(vmem_limit_bytes=48 * 2**20)
 
 
-def flow_terms(place, flow, cot):
+def small(kernel, name, out_shape, count, scratch=()):
+    return pl.pallas_call(
+        kernel,
+        out_shape=out_shape,
+        in_specs=[SMEM] + [VMEM] * count,
+        out_specs=(VMEM,) * len(out_shape),
+        scratch_shapes=scratch,
+        compiler_params=params(),
+        cost_estimate=pl.CostEstimate(flops=10**6, bytes_accessed=10**6, transcendentals=0),
+        name=name,
+    )
+
+
+def flow_terms(*args):
     return pl.pallas_call(
         flow_terms_kernel,
-        out_shape=(jax.ShapeDtypeStruct((4, 4, 2, 7, 16, C), f32),) * 2,
-        in_specs=[SMEM, VMEM, VMEM],
-        out_specs=(VMEM,) * 2,
+        out_shape=(jax.ShapeDtypeStruct((4, 4, 2, 7, 16, C), f32),) * 2
+        + (jax.ShapeDtypeStruct((FR, R2 + 2, W2 + 2, C), f32),),
+        in_specs=[SMEM] + [VMEM] * 6,
+        out_specs=(VMEM,) * 3,
         compiler_params=params(),
         cost_estimate=pl.CostEstimate(flops=2 * 10**9, bytes_accessed=5 * 10**6, transcendentals=0),
         name="flow_terms",
-    )(place, flow, cot)
-
-
-def block_gradient(feat, top, bottom, left, right, weight, cot):
+    )(*args)
+
+
+def block_gradient(*args):
     return pl.pallas_call(
         block_kernel,
         out_shape=(jax.ShapeDtypeStruct((3, R + 2, W, 2 * C), bf16),) * 2,
-        in_specs=[VMEM] * 7,
+        in_specs=[SMEM] + [VMEM] * 7,
         out_specs=(VMEM,) * 2,
         scratch_shapes=[
             pltpu.VMEM((R + 4, PITCH + 8, 2 * C), f32),
@@ -212,7 +305,7 @@
         compiler_params=params(),
         cost_estimate=pl.CostEstimate(flops=5 * 10**9, bytes_accessed=6 * 10**6, transcendentals=200000),
         name="block_gradient",
-    )(feat, top, bottom, left, right, weight, cot)
+    )(*args)
 
 
 def block_terms(place, feat, grad_high, grad_low):
@@ -246,8 +339,8 @@
     return [(i, (i + steps) % count) for i in range(count)]
 
 
-def line(count, step):
-    return [(i, i + step) for i in range(count) if 0 <= i + step < count]
+def pairs(start, count=16):
+    return [p for i in range(start, count - 1, 2) for p in ((i, i + 1), (i + 1, i))]
 
 
 def spread(parts, axis):
@@ -259,35 +352,26 @@
 
 
 def local(features, weight_one, flow_feats, weight_two, cotangent):
-    place = jnp.stack([lax.axis_index(a) for a in ("core", "y", "x", "zh")]).astype(jnp.int32)
+    place = [lax.axis_index(a) for a in ("core", "y", "x", "zh")] + [lax.axis_index("zl") % 2]
+    place = jnp.stack(place).astype(jnp.int32)
     kernel_one = weight_one.reshape(27, C, C)
     kernel_two = weight_two.reshape(27, CF, C)
-    def rows_of(feat, cot):
-        return jnp.concatenate([feat.reshape(FR, 2 * W, C), cot.reshape(FR, W2, C)], axis=1)
-
-    top = lax.ppermute(rows_of(features[:, R - 2 :], cotangent[:, R2 - 1 :]), HA, line(16, 1))
-    bottom = lax.ppermute(rows_of(features[:, :2], cotangent[:, :1]), HA, line(16, -1))
-    top_feat, top_cot = top[:, : 2 * W].reshape(FR, 2, W, C), top[:, 2 * W :][:, None]
-    bottom_feat, bottom_cot = bottom[:, : 2 * W].reshape(FR, 2, W, C), bottom[:, 2 * W :][:, None]
-    tall = jnp.concatenate([top_cot, cotangent, bottom_cot], axis=1)
-
-    def cols_of(place, cot_place):
-        cols = [v[:, :, place : place + 2] for v in (top_feat, features, bottom_feat)]
-        cols = jnp.concatenate(cols, axis=1).reshape(FR, (R + 4) * 2, C)
-        return jnp.concatenate([cols, tall[:, :, cot_place]], axis=1)
-
-    left = lax.ppermute(cols_of(W - 2, W2 - 1), WA, line(16, 1))
-    right = lax.ppermute(cols_of(0, 0), WA, line(16, -1))
-    edge = 2 * (R + 4)
-    left_feat, right_feat = [v[:, :edge].reshape(FR, R + 4, 2, C) for v in (left, right)]
-    cot = jnp.concatenate([left[:, edge:, None], tall, right[:, edge:, None]], axis=2)
-
+    edges = (jax.ShapeDtypeStruct((FR, 2 * W + W2, C), f32),) * 2
+    edges = small(row_edges_kernel, "row_edges", edges, 2)(place, features, cotangent)
+    rows = [lax.ppermute(edges[k], HA, pairs(k)) for k in range(2)]
+    shape = (FR, 2 * COL + 16, C)
+    edges = small(
+        col_edges_kernel,
+        "col_edges",
+        (jax.ShapeDtypeStruct(shape, f32),) * 2,
+        4,
+        [pltpu.VMEM((2,) + shape, f32)],
+    )(place, features, cotangent, *rows)
+    cols = [lax.ppermute(edges[k], WA, pairs(k)) for k in range(2)]
     swap = [(0, 1), (1, 0)]
-    keep, send = flow_terms(place, flow_feats, cot)
+    keep, send, cot = flow_terms(place, flow_feats, cotangent, *rows, *cols)
     terms_two = keep + lax.ppermute(send, "core", swap)
-    grad_high, grad_low = block_gradient(
-        features, top_feat, bottom_feat, left_feat, right_feat, kernel_one, cot
-    )
+    grad_high, grad_low = block_gradient(place, features, *rows, *cols, kernel_one, cot)
     terms_two, grad_high, grad_low = lax.optimization_barrier((terms_two, grad_high, grad_low))
     arrived_two = spread(terms_two, "x")
     keep, send = block_terms(place, features, grad_high, grad_low)
@@ -306,13 +390,11 @@
     chunk = jnp.concatenate([terms_one, terms_two], axis=-2)
     chunk = chunk[0] + lax.ppermute(chunk[1], "zh", swap)
     chunk = summed(chunk, spread([chunk] * 4, "zl"))
-    pieces = jnp.stack([chunk] + [lax.ppermute(chunk, "x", ring(k)) for k in (1, 2, 3)])
-    order = lax.rem(place[2] - jnp.arange(4) + 4, 4)
-    taps = jnp.concatenate([lax.dynamic_index_in_dim(pieces, order[k], 0, False) for k in range(4)])[:27]
-    scale_one = 1.0 / (FR * R * W * 256) ** 0.5
-    scale_two = 1.0 / (FR * R2 * W2 * 256) ** 0.5
-    grad_one = (taps[:, :8] * scale_one).reshape(3, 3, 3, 8, C)
-    grad_two = (taps[:, 8:] * scale_two).reshape(3, 3, 3, 16, C)
+    pieces = [chunk] + [lax.ppermute(chunk, "x", ring(k)) for k in (1, 2, 3)]
+    shares = tuple(jax.ShapeDtypeStruct((27, depth, C), f32) for depth in (8, 16))
+    grad_one, grad_two = small(gather_kernel, "gather", shares, 4)(place, *pieces)
+    grad_one = grad_one.reshape(3, 3, 3, 8, C)
+    grad_two = grad_two.reshape(3, 3, 3, 16, C)
     return (grad_features, grad_one, grad_flow, grad_two)
 
 

time: 122 us -> 107 us (0.88)
  the two profiles are of different devices: /device:TPU:8 before, /device:TPU:6 now
where the time goes in v3:
time: 107 us; the launch traced here: 106 us
  starting transfers between devices  60.6 us (57%)
  waiting for transfers between devices  21.4 us (20%)
  Pallas kernels  18.8 us (18%)
  local copies, waits for them, and re-layouts  4.1 us (4%)
    ppermute x15, starting transfers between devices, spread(): return [lax.ppermute(parts[k], axis, ring(k)) for k in (2, 1, 3)]  38.6 us
    ppermute x15, waiting for transfers between devices, spread(): return [lax.ppermute(parts[k], axis, ring(k)) for k in (2, 1, 3)]  7.03 us
    ppermute x2, starting transfers between devices, local(): rows = [lax.ppermute(edges[k], HA, pairs(k)) for k in range(2)]  6.98 us
    pallas_call x1, Pallas kernels, adjoints(): pl.pallas_call(adjoint_kernel, out_shape=(jax.ShapeDtypeStruct((FR, R, W,...  6.9 us
    ppermute x3, waiting for transfers between devices, local(): pieces = [chunk] + [lax.ppermute(chunk, 'x', ring(k)) for k in (1, 2, 3)]  5.66 us
    ppermute x1, starting transfers between devices, local(): terms_two = keep + lax.ppermute(send, 'core', swap)  5.04 us
    ppermute x3, starting transfers between devices, local(): pieces = [chunk] + [lax.ppermute(chunk, 'x', ring(k)) for k in (1, 2, 3)]  4.53 us
    ppermute x1, starting transfers between devices, local(): chunk = chunk[0] + lax.ppermute(chunk[1], 'zh', swap)  4.44 us
  transfers between devices with their start and end apart: 25, of which 10 were waited for; matrix products, arithmetic and copies ran while one was open for 0% of the time, Pallas kernels for 10%

profile of v3, /device:TPU:6, one launch (start us, length us, event | category | flops | bytes accessed | tf_op | source)
XLA Modules:
  0.0 106.4 jit_solution(10916889876205831967)
XLA Ops:
  3.2 2.0 %collective-permute-start = (f32[2,80,128]{2,1,0:T(8,128)S(1)}, f32[2,80,128]{2,1,0:T(8,128)S(1)}, u32[]{:S(2)}, u32[]{:S(2)}) collective-permute-start(f32[2,80,128]{2,1,0:T(8,128)S(1)} %get-tuple-element.33), channel_id=1, source_target_pairs={{0,16},{16,0},{32,48},{48,32},{64,80},{80,64},{96,112},{112,96},{1... | collective-permute-start | bytes 245768 | tf_op jit(solution)/shard_map/ppermute | solution.py:361
  5.2 5.0 %collective-permute-start.1 = (f32[2,80,128]{2,1,0:T(8,128)S(1)}, f32[2,80,128]{2,1,0:T(8,128)S(1)}, u32[]{:S(2)}, u32[]{:S(2)}) collective-permute-start(f32[2,80,128]{2,1,0:T(8,128)S(1)} %get-tuple-element.34), channel_id=1, source_target_pairs={{16,32},{32,16},{48,64},{64,48},{80,96},{96,80},{112,128},{128,112... | collective-permute-start | bytes 245768 | tf_op jit(solution)/shard_map/ppermute | solution.py:361
  10.2 4.1 %collective-permute-done.1.row_second_ref = f32[2,80,128]{2,1,0:T(8,128)S(1)} collective-permute-done((f32[2,80,128]{2,1,0:T(8,128)S(1)}, f32[2,80,128]{2,1,0:T(8,128)S(1)}, u32[]{:S(2)}, u32[]{:S(2)}) %collective-permute-start.1) | collective-permute-done | bytes 81952 | tf_op jit(solution)/shard_map/ppermute | solution.py:361
  18.2 2.7 %flow_terms.1 = (f32[4,4,2,7,16,128]{5,4,3,2,1,0:T(8,128)S(1)}, f32[4,4,2,7,16,128]{5,4,3,2,1,0:T(8,128)S(1)}, f32[2,10,18,128]{3,2,1,0:T(8,128)S(1)}) custom-call(s32[5]{0:T(128)S(1)} %stack.23.place_ref, f32[2,8,16,256]{3,2,1,0:T(8,128)S(1)} %copy-done.5, f32[2,8,16,128]{3,2,1,0:T(8,128)S(1)} %copy-done.3, ...), custom_call_target="tpu_custom_call" | custom-call | flops 2000000000 | bytes 5000000 | tf_op jit(solution)/shard_map/flow_terms/pallas_call | solution.py:276
  20.9 5.0 %collective-permute-start.4 = (f32[4,4,2,7,16,128]{5,4,3,2,1,0:T(8,128)S(1)}, f32[4,4,2,7,16,128]{5,4,3,2,1,0:T(8,128)S(1)}, u32[]{:S(2)}, u32[]{:S(2)}) collective-permute-start(f32[4,4,2,7,16,128]{5,4,3,2,1,0:T(8,128)S(1)} %get-tuple-element.38), channel_id=1, source_target_pairs={{0,1},{1,0},{2,3},{3,2},{4,5},{5,4},{6,7},{7,6},{8,9},{9,8},{10,11... | collective-permute-start | bytes 5505032 | tf_op jit(solution)/shard_map/ppermute | solution.py:373
  25.9 4.1 %block_gradient.1 = (bf16[3,18,32,256]{3,2,1,0:T(8,128)(2,1)S(1)}, bf16[3,18,32,256]{3,2,1,0:T(8,128)(2,1)S(1)}) custom-call(s32[5]{0:T(128)S(1)} %stack.23.place_ref, f32[2,16,32,128]{3,2,1,0:T(8,128)S(1)} %copy-done.1, f32[2,80,128]{2,1,0:T(8,128)S(1)} %collective-permute-done.row_first_ref, f32[2,80,128]{2,1,0:T(8,128)S(1)} %collective-permute-done.1.row_second_ref, ...), custom_call_target="tpu_custom_call" | custom-call | flops 5000000000 | bytes 6000000 | tf_op jit(solution)/shard_map/block_gradient/pallas_call | solution.py:289
  30.3 2.7 %block_terms.1 = (f32[4,4,2,7,8,128]{5,4,3,2,1,0:T(8,128)S(1)}, f32[4,4,2,7,8,128]{5,4,3,2,1,0:T(8,128)S(1)}) custom-call(s32[5]{0:T(128)S(1)} %stack.23.place_ref, f32[2,16,32,128]{3,2,1,0:T(8,128)S(1)} %copy-done.1, bf16[3,18,32,256]{3,2,1,0:T(8,128)(2,1)S(1)} %get-tuple-element.47.grad_high_ref, bf16[3,18,32,256]{3,2,1,0:T(8,128)(2,1)S(1)} %get-tuple-element.48.grad_low_ref), custom_call_target="tpu_custom_call" | custom-call | flops 1000000000 | bytes 1000000 | tf_op jit(solution)/shard_map/block_terms/pallas_call | solution.py:312
  33.3 2.0 %collective-permute-start.11 = (f32[4,2,7,16,128]{4,3,2,1,0:T(8,128)S(1)}, f32[4,2,7,16,128]{4,3,2,1,0:T(8,128)S(1)}, u32[]{:S(2)}, u32[]{:S(2)}) collective-permute-start(f32[4,2,7,16,128]{4,3,2,1,0:T(8,128)S(1)} %get-tuple-element.62), channel_id=1, source_target_pairs={{0,192},{64,0},{128,64},{192,128},{1,193},{65,1},{129,65},{193,129... | collective-permute-start | bytes 1376264 | tf_op jit(solution)/shard_map/ppermute | solution.py:347
  36.8 3.5 %collective-permute-start.6 = (f32[4,2,7,8,128]{4,3,2,1,0:T(8,128)S(1)}, f32[4,2,7,8,128]{4,3,2,1,0:T(8,128)S(1)}, u32[]{:S(2)}, u32[]{:S(2)}) collective-permute-start(f32[4,2,7,8,128]{4,3,2,1,0:T(8,128)S(1)} %get-tuple-element.67), channel_id=1, source_target_pairs={{0,4},{2,6},{4,0},{6,2},{1,5},{3,7},{5,1},{7,3},{8,12},{10,14},{12... | collective-permute-start | bytes 688136 | tf_op jit(solution)/shard_map/ppermute | solution.py:347
  40.3 6.8 %collective-permute-start.7 = (f32[4,2,7,8,128]{4,3,2,1,0:T(8,128)S(1)}, f32[4,2,7,8,128]{4,3,2,1,0:T(8,128)S(1)}, u32[]{:S(2)}, u32[]{:S(2)}) collective-permute-start(f32[4,2,7,8,128]{4,3,2,1,0:T(8,128)S(1)} %get-tuple-element.66), channel_id=1, source_target_pairs={{0,2},{2,4},{4,6},{6,0},{1,3},{3,5},{5,7},{7,1},{8,10},{10,12},{12... | collective-permute-start | bytes 688136 | tf_op jit(solution)/shard_map/ppermute | solution.py:347
  47.1 8.6 %collective-permute-start.8 = (f32[4,2,7,8,128]{4,3,2,1,0:T(8,128)S(1)}, f32[4,2,7,8,128]{4,3,2,1,0:T(8,128)S(1)}, u32[]{:S(2)}, u32[]{:S(2)}) collective-permute-start(f32[4,2,7,8,128]{4,3,2,1,0:T(8,128)S(1)} %get-tuple-element.65), channel_id=1, source_target_pairs={{0,6},{2,0},{4,2},{6,4},{1,7},{3,1},{5,3},{7,5},{8,14},{10,8},{12,... | collective-permute-start | bytes 688136 | tf_op jit(solution)/shard_map/ppermute | solution.py:347
  55.7 6.9 %adjoints.1 = (f32[2,16,32,128]{3,2,1,0:T(8,128)}, f32[2,8,16,256]{3,2,1,0:T(8,128)}) custom-call(bf16[3,18,32,256]{3,2,1,0:T(8,128)(2,1)S(1)} %get-tuple-element.47.grad_high_ref, bf16[3,18,32,256]{3,2,1,0:T(8,128)(2,1)S(1)} %get-tuple-element.48.grad_low_ref, f32[27,128,128]{2,1,0:T(8,128)S(1)} %bitcast.60, ...), custom_call_target="tpu_custom_call" | custom-call | flops 4000000000 | bytes 10000000 | tf_op jit(solution)/shard_map/adjoints/pallas_call | solution.py:324
  62.7 1.5 %collective-permute-start.12 = (f32[2,7,8,128]{3,2,1,0:T(8,128)S(1)}, f32[2,7,8,128]{3,2,1,0:T(8,128)S(1)}, u32[]{:S(2)}, u32[]{:S(2)}) collective-permute-start(f32[2,7,8,128]{3,2,1,0:T(8,128)S(1)} %get-tuple-element.73), channel_id=1, source_target_pairs={{0,128},{64,192},{128,0},{192,64},{1,129},{65,193},{129,1},{193,65... | collective-permute-start | bytes 172040 | tf_op jit(solution)/shard_map/ppermute | solution.py:347
  64.2 2.1 %collective-permute-start.13 = (f32[2,7,8,128]{3,2,1,0:T(8,128)S(1)}, f32[2,7,8,128]{3,2,1,0:T(8,128)S(1)}, u32[]{:S(2)}, u32[]{:S(2)}) collective-permute-start(f32[2,7,8,128]{3,2,1,0:T(8,128)S(1)} %get-tuple-element.72), channel_id=1, source_target_pairs={{0,64},{64,128},{128,192},{192,0},{1,65},{65,129},{129,193},{193,1... | collective-permute-start | bytes 172040 | tf_op jit(solution)/shard_map/ppermute | solution.py:347
  66.6 5.1 %collective-permute-start.16 = (f32[2,7,16,128]{3,2,1,0:T(8,128)S(1)}, f32[2,7,16,128]{3,2,1,0:T(8,128)S(1)}, u32[]{:S(2)}, u32[]{:S(2)}) collective-permute-start(f32[2,7,16,128]{3,2,1,0:T(8,128)S(1)} %get-tuple-element.69), channel_id=1, source_target_pairs={{0,2},{2,4},{4,6},{6,0},{1,3},{3,5},{5,7},{7,1},{8,10},{10,12},{12... | collective-permute-start | bytes 344072 | tf_op jit(solution)/shard_map/ppermute | solution.py:347
  74.5 2.0 %collective-permute-done.17 = f32[2,7,16,128]{3,2,1,0:T(8,128)S(1)} collective-permute-done((f32[2,7,16,128]{3,2,1,0:T(8,128)S(1)}, f32[2,7,16,128]{3,2,1,0:T(8,128)S(1)}, u32[]{:S(2)}, u32[]{:S(2)}) %collective-permute-start.17) | collective-permute-done | bytes 114720 | tf_op jit(solution)/shard_map/ppermute | solution.py:347
  76.5 4.4 %collective-permute-start.18 = (f32[7,24,128]{2,1,0:T(8,128)S(1)}, f32[7,24,128]{2,1,0:T(8,128)S(1)}, u32[]{:S(2)}, u32[]{:S(2)}) collective-permute-start(f32[7,24,128]{2,1,0:T(8,128)S(1)} %fusion.7), channel_id=1, source_target_pairs={{0,8},{8,0},{1,9},{9,1},{2,10},{10,2},{3,11},{11,3},{4,12},{12,4},... | collective-permute-start | bytes 258056 | tf_op jit(solution)/shard_map/ppermute | solution.py:391
  81.0 4.1 %collective-permute-done.18 = f32[7,24,128]{2,1,0:T(8,128)S(1)} collective-permute-done((f32[7,24,128]{2,1,0:T(8,128)S(1)}, f32[7,24,128]{2,1,0:T(8,128)S(1)}, u32[]{:S(2)}, u32[]{:S(2)}) %collective-permute-start.18) | collective-permute-done | bytes 86048 | tf_op jit(solution)/shard_map/ppermute | solution.py:391
  85.1 2.7 %collective-permute-start.19 = (f32[7,24,128]{2,1,0:T(8,128)S(1)}, f32[7,24,128]{2,1,0:T(8,128)S(1)}, u32[]{:S(2)}, u32[]{:S(2)}) collective-permute-start(f32[7,24,128]{2,1,0:T(8,128)S(1)} %fusion.6), channel_id=1, source_target_pairs={{0,32},{16,48},{32,0},{48,16},{1,33},{17,49},{33,1},{49,17},{2,34}... | collective-permute-start | bytes 258056 | tf_op jit(solution)/shard_map/ppermute | solution.py:347
  89.1 2.5 %collective-permute-start.21 = (f32[7,24,128]{2,1,0:T(8,128)S(1)}, f32[7,24,128]{2,1,0:T(8,128)S(1)}, u32[]{:S(2)}, u32[]{:S(2)}) collective-permute-start(f32[7,24,128]{2,1,0:T(8,128)S(1)} %fusion.6), channel_id=1, source_target_pairs={{0,48},{16,0},{32,16},{48,32},{1,49},{17,1},{33,17},{49,33},{2,50}... | collective-permute-start | bytes 258056 | tf_op jit(solution)/shard_map/ppermute | solution.py:347
  91.6 3.3 %collective-permute-done.20 = f32[7,24,128]{2,1,0:T(8,128)S(1)} collective-permute-done((f32[7,24,128]{2,1,0:T(8,128)S(1)}, f32[7,24,128]{2,1,0:T(8,128)S(1)}, u32[]{:S(2)}, u32[]{:S(2)}) %collective-permute-start.20) | collective-permute-done | bytes 86048 | tf_op jit(solution)/shard_map/ppermute | solution.py:347
  94.9 3.6 %collective-permute-start.22 = (f32[7,24,128]{2,1,0:T(8,128)S(1)}, f32[7,24,128]{2,1,0:T(8,128)S(1)}, u32[]{:S(2)}, u32[]{:S(2)}) collective-permute-start(f32[7,24,128]{2,1,0:T(8,128)S(1)} %add_add_fusion.own_ref), channel_id=1, source_target_pairs={{0,64},{64,128},{128,192},{192,0},{1,65},{65,129},{129,193},{193,1... | collective-permute-start | bytes 258056 | tf_op jit(solution)/shard_map/ppermute | solution.py:393
  99.5 2.0 %collective-permute-done.22.one_ref = f32[7,24,128]{2,1,0:T(8,128)S(1)} collective-permute-done((f32[7,24,128]{2,1,0:T(8,128)S(1)}, f32[7,24,128]{2,1,0:T(8,128)S(1)}, u32[]{:S(2)}, u32[]{:S(2)}) %collective-permute-start.22) | collective-permute-done | bytes 86048 | tf_op jit(solution)/shard_map/ppermute | solution.py:393
  101.5 3.1 %collective-permute-done.23.two_ref = f32[7,24,128]{2,1,0:T(8,128)S(1)} collective-permute-done((f32[7,24,128]{2,1,0:T(8,128)S(1)}, f32[7,24,128]{2,1,0:T(8,128)S(1)}, u32[]{:S(2)}, u32[]{:S(2)}) %collective-permute-start.23) | collective-permute-done | bytes 86048 | tf_op jit(solution)/shard_map/ppermute | solution.py:393
  (59 shorter events, 15.8 us)
Async XLA Ops:
  3.2 7.0 %collective-permute-start = (f32[2,80,128]{2,1,0:T(8,128)S(1)}, f32[2,80,128]{2,1,0:T(8,128)S(1)}, u32[]{:S(2)}, u32[]{:S(2)}) collective-permute-start(f32[2,80,128]{2,1,0:T(8,128)S(1)} %get-tuple-element.33), channel_id=1, source_target_pairs={{0,16},{16,0},{32,48},{48,32},{64,80},{80,64},{96,112},{112,96},{1... | collective-permute-start | bytes 245768 | tf_op jit(solution)/shard_map/ppermute | solution.py:361
  5.2 9.1 %collective-permute-start.1 = (f32[2,80,128]{2,1,0:T(8,128)S(1)}, f32[2,80,128]{2,1,0:T(8,128)S(1)}, u32[]{:S(2)}, u32[]{:S(2)}) collective-permute-start(f32[2,80,128]{2,1,0:T(8,128)S(1)} %get-tuple-element.34), channel_id=1, source_target_pairs={{16,32},{32,16},{48,64},{64,48},{80,96},{96,80},{112,128},{128,112... | collective-permute-start | bytes 245768 | tf_op jit(solution)/shard_map/ppermute | solution.py:361
  15.0 1.3 %collective-permute-start.2 = (f32[2,64,128]{2,1,0:T(8,128)S(1)}, f32[2,64,128]{2,1,0:T(8,128)S(1)}, u32[]{:S(2)}, u32[]{:S(2)}) collective-permute-start(f32[2,64,128]{2,1,0:T(8,128)S(1)} %get-tuple-element.35), channel_id=1, source_target_pairs={{0,1},{1,0},{2,3},{3,2},{4,5},{5,4},{6,7},{7,6},{8,9},{9,8},{10,11... | collective-permute-start | bytes 196616 | tf_op jit(solution)/shard_map/ppermute | solution.py:370
  20.9 9.2 %collective-permute-start.4 = (f32[4,4,2,7,16,128]{5,4,3,2,1,0:T(8,128)S(1)}, f32[4,4,2,7,16,128]{5,4,3,2,1,0:T(8,128)S(1)}, u32[]{:S(2)}, u32[]{:S(2)}) collective-permute-start(f32[4,4,2,7,16,128]{5,4,3,2,1,0:T(8,128)S(1)} %get-tuple-element.38), channel_id=1, source_target_pairs={{0,1},{1,0},{2,3},{3,2},{4,5},{5,4},{6,7},{7,6},{8,9},{9,8},{10,11... | collective-permute-start | bytes 5505032 | tf_op jit(solution)/shard_map/ppermute | solution.py:373
  33.0 3.7 %collective-permute-start.5 = (f32[4,4,2,7,8,128]{5,4,3,2,1,0:T(8,128)S(1)}, f32[4,4,2,7,8,128]{5,4,3,2,1,0:T(8,128)S(1)}, u32[]{:S(2)}, u32[]{:S(2)}) collective-permute-start(f32[4,4,2,7,8,128]{5,4,3,2,1,0:T(8,128)S(1)} %get-tuple-element.45), channel_id=1, source_target_pairs={{0,1},{1,0},{2,3},{3,2},{4,5},{5,4},{6,7},{7,6},{8,9},{9,8},{10,11... | collective-permute-start | bytes 2752520 | tf_op jit(solution)/shard_map/ppermute | solution.py:378
  33.2 13.9 %collective-permute-start.10 = (f32[4,2,7,16,128]{4,3,2,1,0:T(8,128)S(1)}, f32[4,2,7,16,128]{4,3,2,1,0:T(8,128)S(1)}, u32[]{:S(2)}, u32[]{:S(2)}) collective-permute-start(f32[4,2,7,16,128]{4,3,2,1,0:T(8,128)S(1)} %get-tuple-element.63), channel_id=1, source_target_pairs={{0,64},{64,128},{128,192},{192,0},{1,65},{65,129},{129,193},{193,1... | collective-permute-start | bytes 1376264 | tf_op jit(solution)/shard_map/ppermute | solution.py:347
  33.3 29.3 %collective-permute-start.11 = (f32[4,2,7,16,128]{4,3,2,1,0:T(8,128)S(1)}, f32[4,2,7,16,128]{4,3,2,1,0:T(8,128)S(1)}, u32[]{:S(2)}, u32[]{:S(2)}) collective-permute-start(f32[4,2,7,16,128]{4,3,2,1,0:T(8,128)S(1)} %get-tuple-element.62), channel_id=1, source_target_pairs={{0,192},{64,0},{128,64},{192,128},{1,193},{65,1},{129,65},{193,129... | collective-permute-start | bytes 1376264 | tf_op jit(solution)/shard_map/ppermute | solution.py:347
  35.3 27.3 %collective-permute-start.9 = (f32[4,2,7,16,128]{4,3,2,1,0:T(8,128)S(1)}, f32[4,2,7,16,128]{4,3,2,1,0:T(8,128)S(1)}, u32[]{:S(2)}, u32[]{:S(2)}) collective-permute-start(f32[4,2,7,16,128]{4,3,2,1,0:T(8,128)S(1)} %get-tuple-element.64), channel_id=1, source_target_pairs={{0,128},{64,192},{128,0},{192,64},{1,129},{65,193},{129,1},{193,65... | collective-permute-start | bytes 1376264 | tf_op jit(solution)/shard_map/ppermute | solution.py:347
  36.8 25.8 %collective-permute-start.6 = (f32[4,2,7,8,128]{4,3,2,1,0:T(8,128)S(1)}, f32[4,2,7,8,128]{4,3,2,1,0:T(8,128)S(1)}, u32[]{:S(2)}, u32[]{:S(2)}) collective-permute-start(f32[4,2,7,8,128]{4,3,2,1,0:T(8,128)S(1)} %get-tuple-element.67), channel_id=1, source_target_pairs={{0,4},{2,6},{4,0},{6,2},{1,5},{3,7},{5,1},{7,3},{8,12},{10,14},{12... | collective-permute-start | bytes 688136 | tf_op jit(solution)/shard_map/ppermute | solution.py:347
  40.3 22.3 %collective-permute-start.7 = (f32[4,2,7,8,128]{4,3,2,1,0:T(8,128)S(1)}, f32[4,2,7,8,128]{4,3,2,1,0:T(8,128)S(1)}, u32[]{:S(2)}, u32[]{:S(2)}) collective-permute-start(f32[4,2,7,8,128]{4,3,2,1,0:T(8,128)S(1)} %get-tuple-element.66), channel_id=1, source_target_pairs={{0,2},{2,4},{4,6},{6,0},{1,3},{3,5},{5,7},{7,1},{8,10},{10,12},{12... | collective-permute-start | bytes 688136 | tf_op jit(solution)/shard_map/ppermute | solution.py:347
  47.1 15.6 %collective-permute-start.8 = (f32[4,2,7,8,128]{4,3,2,1,0:T(8,128)S(1)}, f32[4,2,7,8,128]{4,3,2,1,0:T(8,128)S(1)}, u32[]{:S(2)}, u32[]{:S(2)}) collective-permute-start(f32[4,2,7,8,128]{4,3,2,1,0:T(8,128)S(1)} %get-tuple-element.65), channel_id=1, source_target_pairs={{0,6},{2,0},{4,2},{6,4},{1,7},{3,1},{5,3},{7,5},{8,14},{10,8},{12,... | collective-permute-start | bytes 688136 | tf_op jit(solution)/shard_map/ppermute | solution.py:347
  62.7 9.0 %collective-permute-start.12 = (f32[2,7,8,128]{3,2,1,0:T(8,128)S(1)}, f32[2,7,8,128]{3,2,1,0:T(8,128)S(1)}, u32[]{:S(2)}, u32[]{:S(2)}) collective-permute-start(f32[2,7,8,128]{3,2,1,0:T(8,128)S(1)} %get-tuple-element.73), channel_id=1, source_target_pairs={{0,128},{64,192},{128,0},{192,64},{1,129},{65,193},{129,1},{193,65... | collective-permute-start | bytes 172040 | tf_op jit(solution)/shard_map/ppermute | solution.py:347
  64.2 8.5 %collective-permute-start.13 = (f32[2,7,8,128]{3,2,1,0:T(8,128)S(1)}, f32[2,7,8,128]{3,2,1,0:T(8,128)S(1)}, u32[]{:S(2)}, u32[]{:S(2)}) collective-permute-start(f32[2,7,8,128]{3,2,1,0:T(8,128)S(1)} %get-tuple-element.72), channel_id=1, source_target_pairs={{0,64},{64,128},{128,192},{192,0},{1,65},{65,129},{129,193},{193,1... | collective-permute-start | bytes 172040 | tf_op jit(solution)/shard_map/ppermute | solution.py:347
  66.3 6.4 %collective-permute-start.14 = (f32[2,7,8,128]{3,2,1,0:T(8,128)S(1)}, f32[2,7,8,128]{3,2,1,0:T(8,128)S(1)}, u32[]{:S(2)}, u32[]{:S(2)}) collective-permute-start(f32[2,7,8,128]{3,2,1,0:T(8,128)S(1)} %get-tuple-element.71), channel_id=1, source_target_pairs={{0,192},{64,0},{128,64},{192,128},{1,193},{65,1},{129,65},{193,129... | collective-permute-start | bytes 172040 | tf_op jit(solution)/shard_map/ppermute | solution.py:347
  66.5 7.6 %collective-permute-start.15 = (f32[2,7,16,128]{3,2,1,0:T(8,128)S(1)}, f32[2,7,16,128]{3,2,1,0:T(8,128)S(1)}, u32[]{:S(2)}, u32[]{:S(2)}) collective-permute-start(f32[2,7,16,128]{3,2,1,0:T(8,128)S(1)} %get-tuple-element.70), channel_id=1, source_target_pairs={{0,4},{2,6},{4,0},{6,2},{1,5},{3,7},{5,1},{7,3},{8,12},{10,14},{12... | collective-permute-start | bytes 344072 | tf_op jit(solution)/shard_map/ppermute | solution.py:347
  66.6 7.9 %collective-permute-start.16 = (f32[2,7,16,128]{3,2,1,0:T(8,128)S(1)}, f32[2,7,16,128]{3,2,1,0:T(8,128)S(1)}, u32[]{:S(2)}, u32[]{:S(2)}) collective-permute-start(f32[2,7,16,128]{3,2,1,0:T(8,128)S(1)} %get-tuple-element.69), channel_id=1, source_target_pairs={{0,2},{2,4},{4,6},{6,0},{1,3},{3,5},{5,7},{7,1},{8,10},{10,12},{12... | collective-permute-start | bytes 344072 | tf_op jit(solution)/shard_map/ppermute | solution.py:347
  71.7 4.8 %collective-permute-start.17 = (f32[2,7,16,128]{3,2,1,0:T(8,128)S(1)}, f32[2,7,16,128]{3,2,1,0:T(8,128)S(1)}, u32[]{:S(2)}, u32[]{:S(2)}) collective-permute-start(f32[2,7,16,128]{3,2,1,0:T(8,128)S(1)} %get-tuple-element.68), channel_id=1, source_target_pairs={{0,6},{2,0},{4,2},{6,4},{1,7},{3,1},{5,3},{7,5},{8,14},{10,8},{12,... | collective-permute-start | bytes 344072 | tf_op jit(solution)/shard_map/ppermute | solution.py:347
  76.5 8.6 %collective-permute-start.18 = (f32[7,24,128]{2,1,0:T(8,128)S(1)}, f32[7,24,128]{2,1,0:T(8,128)S(1)}, u32[]{:S(2)}, u32[]{:S(2)}) collective-permute-start(f32[7,24,128]{2,1,0:T(8,128)S(1)} %fusion.7), channel_id=1, source_target_pairs={{0,8},{8,0},{1,9},{9,1},{2,10},{10,2},{3,11},{11,3},{4,12},{12,4},... | collective-permute-start | bytes 258056 | tf_op jit(solution)/shard_map/ppermute | solution.py:391
  85.1 6.5 %collective-permute-start.19 = (f32[7,24,128]{2,1,0:T(8,128)S(1)}, f32[7,24,128]{2,1,0:T(8,128)S(1)}, u32[]{:S(2)}, u32[]{:S(2)}) collective-permute-start(f32[7,24,128]{2,1,0:T(8,128)S(1)} %fusion.6), channel_id=1, source_target_pairs={{0,32},{16,48},{32,0},{48,16},{1,33},{17,49},{33,1},{49,17},{2,34}... | collective-permute-start | bytes 258056 | tf_op jit(solution)/shard_map/ppermute | solution.py:347
  87.8 7.1 %collective-permute-start.20 = (f32[7,24,128]{2,1,0:T(8,128)S(1)}, f32[7,24,128]{2,1,0:T(8,128)S(1)}, u32[]{:S(2)}, u32[]{:S(2)}) collective-permute-start(f32[7,24,128]{2,1,0:T(8,128)S(1)} %fusion.6), channel_id=1, source_target_pairs={{0,16},{16,32},{32,48},{48,0},{1,17},{17,33},{33,49},{49,1},{2,18}... | collective-permute-start | bytes 258056 | tf_op jit(solution)/shard_map/ppermute | solution.py:347
  89.1 5.8 %collective-permute-start.21 = (f32[7,24,128]{2,1,0:T(8,128)S(1)}, f32[7,24,128]{2,1,0:T(8,128)S(1)}, u32[]{:S(2)}, u32[]{:S(2)}) collective-permute-start(f32[7,24,128]{2,1,0:T(8,128)S(1)} %fusion.6), channel_id=1, source_target_pairs={{0,48},{16,0},{32,16},{48,32},{1,49},{17,1},{33,17},{49,33},{2,50}... | collective-permute-start | bytes 258056 | tf_op jit(solution)/shard_map/ppermute | solution.py:347
  94.9 6.5 %collective-permute-start.22 = (f32[7,24,128]{2,1,0:T(8,128)S(1)}, f32[7,24,128]{2,1,0:T(8,128)S(1)}, u32[]{:S(2)}, u32[]{:S(2)}) collective-permute-start(f32[7,24,128]{2,1,0:T(8,128)S(1)} %add_add_fusion.own_ref), channel_id=1, source_target_pairs={{0,64},{64,128},{128,192},{192,0},{1,65},{65,129},{129,193},{193,1... | collective-permute-start | bytes 258056 | tf_op jit(solution)/shard_map/ppermute | solution.py:393
  98.5 6.1 %collective-permute-start.23 = (f32[7,24,128]{2,1,0:T(8,128)S(1)}, f32[7,24,128]{2,1,0:T(8,128)S(1)}, u32[]{:S(2)}, u32[]{:S(2)}) collective-permute-start(f32[7,24,128]{2,1,0:T(8,128)S(1)} %add_add_fusion.own_ref), channel_id=1, source_target_pairs={{0,128},{64,192},{128,0},{192,64},{1,129},{65,193},{129,1},{193,65... | collective-permute-start | bytes 258056 | tf_op jit(solution)/shard_map/ppermute | solution.py:393
  98.5 6.6 %collective-permute-start.24 = (f32[7,24,128]{2,1,0:T(8,128)S(1)}, f32[7,24,128]{2,1,0:T(8,128)S(1)}, u32[]{:S(2)}, u32[]{:S(2)}) collective-permute-start(f32[7,24,128]{2,1,0:T(8,128)S(1)} %add_add_fusion.own_ref), channel_id=1, source_target_pairs={{0,192},{64,0},{128,64},{192,128},{1,193},{65,1},{129,65},{193,129... | collective-permute-start | bytes 258056 | tf_op jit(solution)/shard_map/ppermute | solution.py:393
  (7 other events, 23.6 us)

commit v4 on v3

--- a/solution.py
+++ b/solution.py
@@ -18,6 +18,7 @@
 f32, bf16 = jnp.float32, jnp.bfloat16
 VMEM = pl.BlockSpec(memory_space=pltpu.VMEM)
 SMEM = pl.BlockSpec(memory_space=pltpu.SMEM)
+HBM = pl.BlockSpec(memory_space=pltpu.HBM)
 
 
 def split(values):
@@ -52,28 +53,54 @@
     core, y, x, zh = place_ref[0], place_ref[1], place_ref[2], place_ref[3]
     for time_tap, part in taps:
         number = 9 * time_tap + tap
-        chunk = lax.rem(number // 7 - x + 4, 4)
+        slot_x = lax.rem(number // 7 - x + 4, 4)
         for owner in range(8):
             slot_y = lax.rem(owner % 4 - y + 4, 4)
             slot_zh = lax.rem(owner // 4 - zh + 2, 2)
+            slots = [jnp.where(core == 0, slot_x, slot_y), jnp.where(core == 0, slot_y, slot_x)]
             first = part[2 * owner * depth : (2 * owner + 1) * depth]
             second = part[(2 * owner + 1) * depth : (2 * owner + 2) * depth]
-            slots = (slot_y, chunk) if depth == 8 else (chunk, slot_y)
-            keep_ref[slots + (slot_zh, number % 7)] = jnp.where(core == 0, first, second)
-            send_ref[slots + (slot_zh, number % 7)] = jnp.where(core == 0, second, first)
-
-
-def row_edges_kernel(place_ref, feat_ref, cot_ref, first_ref, second_ref):
+            keep_ref[slots[0], slots[1], slot_zh, number % 7] = jnp.where(core == 0, first, second)
+            send_ref[slots[1], slots[0], slot_zh, number % 7] = jnp.where(core == 0, second, first)
+
+
+def row_edges_kernel(
+    place_ref, feat_ref, cot_ref, first_ref, second_ref, feat_top, feat_bottom, cot_top, cot_bottom, sems
+):
+    copies = [
+        pltpu.make_async_copy(feat_ref.at[:, 0:2], feat_top, sems.at[0]),
+        pltpu.make_async_copy(feat_ref.at[:, R - 2 : R], feat_bottom, sems.at[1]),
+        pltpu.make_async_copy(cot_ref.at[:, 0:1], cot_top, sems.at[2]),
+        pltpu.make_async_copy(cot_ref.at[:, R2 - 1 : R2], cot_bottom, sems.at[3]),
+    ]
+    for copy in copies:
+        copy.start()
+    for copy in copies:
+        copy.wait()
     odd = place_ref[4] == 1
     for t in range(FR):
         for row in range(2):
-            top, bottom = feat_ref[t, row], feat_ref[t, R - 2 + row]
+            top, bottom = feat_top[t, row], feat_bottom[t, row]
             lines = slice(row * W, (row + 1) * W)
             first_ref[t, lines] = jnp.where(odd, top, bottom)
             second_ref[t, lines] = jnp.where(odd, bottom, top)
-        top, bottom = cot_ref[t, 0], cot_ref[t, R2 - 1]
+        top, bottom = cot_top[t, 0], cot_bottom[t, 0]
         first_ref[t, 2 * W :] = jnp.where(odd, top, bottom)
         second_ref[t, 2 * W :] = jnp.where(odd, bottom, top)
+
+
+def prepare_kernel(place_ref, weight_ref, feat_ref, taps_high, taps_low, feat_high, feat_low):
+    for tap in range(9):
+        taps_high[tap], taps_low[tap] = split(both_frames(weight_ref, tap))
+    for t in range(FR):
+        lines = slice(t * C, (t + 1) * C)
+        feat_high[lines], feat_low[lines] = split(feat_ref[t].reshape(R * W, C).T)
+
+
+def prepare_flow_kernel(place_ref, flow_ref, flow_high, flow_low):
+    for t in range(FR):
+        lines = slice(t * CF, (t + 1) * CF)
+        flow_high[lines], flow_low[lines] = split(flow_ref[t].reshape(R2 * W2, CF).T)
 
 
 def row_halo(place_ref, first_ref, second_ref, t, lines):
@@ -116,7 +143,7 @@
 
 
 def flow_terms_kernel(
-    place_ref, flow_ref, local_ref, row_first_ref, row_second_ref, col_first_ref, col_second_ref,
+    place_ref, flow_high, flow_low, local_ref, row_first_ref, row_second_ref, col_first_ref, col_second_ref,
     keep_ref, send_ref, cot_ref,
 ):
     for t in range(FR):
@@ -128,10 +155,7 @@
         left, right = col_halo(place_ref, col_first_ref, col_second_ref, t, lines)
         cot_ref[t, :, 0] = left
         cot_ref[t, :, 1 + W2] = right
-    flow = jnp.concatenate(
-        [flow_ref[0].reshape(R2 * W2, CF).T, flow_ref[1].reshape(R2 * W2, CF).T], axis=0
-    )
-    flow = split(flow)
+    flow = flow_high[...], flow_low[...]
     for col_tap in range(3):
         cot = shifted_cot(cot_ref, 2 - col_tap)
         for row_tap in range(3):
@@ -142,9 +166,9 @@
 
 
 def block_kernel(
-    place_ref, feat_ref, row_first_ref, row_second_ref, col_first_ref, col_second_ref, weight_ref, cot_ref,
-    grad_high_ref, grad_low_ref,
-    ext_ref, wide_ref, taps_high, taps_low, even_high, even_low, odd_high, odd_low, grad_ref,
+    place_ref, feat_ref, row_first_ref, row_second_ref, col_first_ref, col_second_ref,
+    taps_high, taps_low, cot_ref, grad_high_ref, grad_low_ref,
+    ext_ref, wide_ref, even_high, even_low, odd_high, odd_low, grad_ref,
 ):
     ext_ref[...] = jnp.zeros_like(ext_ref)
     for t in range(FR):
@@ -166,10 +190,6 @@
                 if 0 <= target < R + 2:
                     wide_ref[t, target, pl.ds(0, W2 + 2, stride=2), :] = line
                     wide_ref[t, target, pl.ds(1, W2 + 2, stride=2), :] = line
-    for tap in range(9):
-        high, low = split(both_frames(weight_ref, tap))
-        taps_high[tap] = high
-        taps_low[tap] = low
     rows = R + 4
     for e in range(3):
         shifted = ext_ref[:, e : e + PITCH, :].reshape(rows * PITCH, 2 * C)
@@ -204,10 +224,8 @@
         grad_low_ref[e] = low
 
 
-def block_terms_kernel(place_ref, feat_ref, grad_high_ref, grad_low_ref, keep_ref, send_ref):
-    feat = split(
-        jnp.concatenate([feat_ref[t].reshape(R * W, C).T for t in range(FR)], axis=0)
-    )
+def block_terms_kernel(place_ref, feat_high, feat_low, grad_high_ref, grad_low_ref, keep_ref, send_ref):
+    feat = feat_high[...], feat_low[...]
     for row_tap in range(3):
         for e in range(3):
             window = [
@@ -219,7 +237,7 @@
             )
 
 
-def adjoint_kernel(grad_high_ref, grad_low_ref, weight_one_ref, cot_ref, weight_two_ref, feat_out, flow_out):
+def adjoint_kernel(grad_high_ref, grad_low_ref, taps_high, taps_low, cot_ref, weight_two_ref, feat_out, flow_out):
     total = jnp.zeros((R * W, 2 * C), f32)
     for row_tap in range(3):
         for e in range(3):
@@ -227,7 +245,8 @@
                 ref[e, 2 - row_tap : 2 - row_tap + R].reshape(R * W, 2 * C)
                 for ref in (grad_high_ref, grad_low_ref)
             ]
-            total = total + product(window, split(both_frames(weight_one_ref, 3 * row_tap + e)), NT)
+            tap = 3 * row_tap + e
+            total = total + product(window, (taps_high[tap], taps_low[tap]), NT)
     for t in range(FR):
         feat_out[t] = total[:, t * C : (t + 1) * C].reshape(R, W, C)
     total = jnp.zeros((R2 * W2, 2 * CF), f32)
@@ -255,18 +274,18 @@
         pl.when(first < 21)(functools.partial(put, 6))
 
 
-def params():
-    return pltpu.CompilerParams(vmem_limit_bytes=48 * 2**20)
-
-
-def small(kernel, name, out_shape, count, scratch=()):
+def params(mebibytes=48):
+    return pltpu.CompilerParams(vmem_limit_bytes=mebibytes * 2**20)
+
+
+def small(kernel, name, out_shape, count, scratch=(), space=VMEM):
     return pl.pallas_call(
         kernel,
         out_shape=out_shape,
-        in_specs=[SMEM] + [VMEM] * count,
+        in_specs=[SMEM] + [space] * count,
         out_specs=(VMEM,) * len(out_shape),
         scratch_shapes=scratch,
-        compiler_params=params(),
+        compiler_params=params(48 if space is VMEM else 64),
         cost_estimate=pl.CostEstimate(flops=10**6, bytes_accessed=10**6, transcendentals=0),
         name=name,
     )
@@ -277,7 +296,7 @@
         flow_terms_kernel,
         out_shape=(jax.ShapeDtypeStruct((4, 4, 2, 7, 16, C), f32),) * 2
         + (jax.ShapeDtypeStruct((FR, R2 + 2, W2 + 2, C), f32),),
-        in_specs=[SMEM] + [VMEM] * 6,
+        in_specs=[SMEM] + [VMEM] * 7,
         out_specs=(VMEM,) * 3,
         compiler_params=params(),
         cost_estimate=pl.CostEstimate(flops=2 * 10**9, bytes_accessed=5 * 10**6, transcendentals=0),
@@ -289,13 +308,11 @@
     return pl.pallas_call(
         block_kernel,
         out_shape=(jax.ShapeDtypeStruct((3, R + 2, W, 2 * C), bf16),) * 2,
-        in_specs=[SMEM] + [VMEM] * 7,
+        in_specs=[SMEM] + [VMEM] * 8,
         out_specs=(VMEM,) * 2,
         scratch_shapes=[
             pltpu.VMEM((R + 4, PITCH + 8, 2 * C), f32),
             pltpu.VMEM((FR, R + 2, PITCH, C), f32),
-            pltpu.VMEM((9, 2 * C, 2 * C), bf16),
-            pltpu.VMEM((9, 2 * C, 2 * C), bf16),
             pltpu.VMEM((3, (R + 4) * PITCH, 2 * C), bf16),
             pltpu.VMEM((3, (R + 4) * PITCH, 2 * C), bf16),
             pltpu.VMEM((3, EXT, 2 * C), bf16),
@@ -308,43 +325,56 @@
     )(*args)
 
 
-def block_terms(place, feat, grad_high, grad_low):
+def block_terms(*args):
     return pl.pallas_call(
         block_terms_kernel,
         out_shape=(jax.ShapeDtypeStruct((4, 4, 2, 7, 8, C), f32),) * 2,
-        in_specs=[SMEM] + [VMEM] * 3,
+        in_specs=[SMEM] + [VMEM] * 4,
         out_specs=(VMEM,) * 2,
         compiler_params=params(),
         cost_estimate=pl.CostEstimate(flops=10**9, bytes_accessed=10**6, transcendentals=0),
         name="block_terms",
-    )(place, feat, grad_high, grad_low)
-
-
-def adjoints(grad_high, grad_low, weight_one, cot, weight_two):
+    )(*args)
+
+
+def adjoints(*args):
     return pl.pallas_call(
         adjoint_kernel,
         out_shape=(
             jax.ShapeDtypeStruct((FR, R, W, C), f32),
             jax.ShapeDtypeStruct((FR, R2, W2, CF), f32),
         ),
-        in_specs=[VMEM] * 5,
+        in_specs=[VMEM] * 6,
         out_specs=(VMEM,) * 2,
         compiler_params=params(),
         cost_estimate=pl.CostEstimate(flops=4 * 10**9, bytes_accessed=10**7, transcendentals=0),
         name="adjoints",
-    )(grad_high, grad_low, weight_one, cot, weight_two)
+    )(*args)
 
 
 def ring(steps, count=4):
     return [(i, (i + steps) % count) for i in range(count)]
 
 
+def crossed(steps, axes):
+    both = []
+    for x in range(4):
+        for y in range(4):
+            for core in range(2):
+                along_x = axes[core] == "x"
+                x_to, y_to = ((x + steps) % 4, y) if along_x else (x, (y + steps) % 4)
+                both.append((8 * x + 2 * y + core, 8 * x_to + 2 * y_to + core))
+    return both
+
+
 def pairs(start, count=16):
     return [p for i in range(start, count - 1, 2) for p in ((i, i + 1), (i + 1, i))]
 
 
-def spread(parts, axis):
-    return [lax.ppermute(parts[k], axis, ring(k)) for k in (2, 1, 3)]
+def spread(parts, axes):
+    if axes == "zl":
+        return [lax.ppermute(parts[k], "zl", ring(k)) for k in (2, 1, 3)]
+    return [lax.ppermute(parts[k], ("x", "y", "core"), crossed(k, axes)) for k in (2, 1, 3)]
 
 
 def summed(own, arrived):
@@ -357,8 +387,22 @@
     kernel_one = weight_one.reshape(27, C, C)
     kernel_two = weight_two.reshape(27, CF, C)
     edges = (jax.ShapeDtypeStruct((FR, 2 * W + W2, C), f32),) * 2
-    edges = small(row_edges_kernel, "row_edges", edges, 2)(place, features, cotangent)
+    edges = small(
+        row_edges_kernel,
+        "row_edges",
+        edges,
+        2,
+        [pltpu.VMEM((FR, 2, W, C), f32)] * 2
+        + [pltpu.VMEM((FR, 1, W2, C), f32)] * 2
+        + [pltpu.SemaphoreType.DMA((4,))],
+        HBM,
+    )(place, features, cotangent)
+    edges, kernel_one = lax.optimization_barrier((edges, kernel_one))
     rows = [lax.ppermute(edges[k], HA, pairs(k)) for k in range(2)]
+    taps = jax.ShapeDtypeStruct((9, 2 * C, 2 * C), bf16)
+    feats = jax.ShapeDtypeStruct((2 * C, R * W), bf16)
+    prepared = small(prepare_kernel, "prepare", (taps, taps, feats, feats), 2)(place, kernel_one, features)
+    rows, prepared = lax.optimization_barrier((rows, prepared))
     shape = (FR, 2 * COL + 16, C)
     edges = small(
         col_edges_kernel,
@@ -367,27 +411,30 @@
         4,
         [pltpu.VMEM((2,) + shape, f32)],
     )(place, features, cotangent, *rows)
+    edges, flow_feats = lax.optimization_barrier((edges, flow_feats))
     cols = [lax.ppermute(edges[k], WA, pairs(k)) for k in range(2)]
+    flows = (jax.ShapeDtypeStruct((2 * CF, R2 * W2), bf16),) * 2
+    flows = small(prepare_flow_kernel, "prepare_flow", flows, 1)(place, flow_feats)
+    cols, flows = lax.optimization_barrier((cols, flows))
     swap = [(0, 1), (1, 0)]
-    keep, send, cot = flow_terms(place, flow_feats, cotangent, *rows, *cols)
+    taps, feats = prepared[:2], prepared[2:]
+    keep, send, cot = flow_terms(place, *flows, cotangent, *rows, *cols)
     terms_two = keep + lax.ppermute(send, "core", swap)
-    grad_high, grad_low = block_gradient(place, features, *rows, *cols, kernel_one, cot)
+    grad_high, grad_low = block_gradient(place, features, *rows, *cols, *taps, cot)
     terms_two, grad_high, grad_low = lax.optimization_barrier((terms_two, grad_high, grad_low))
-    arrived_two = spread(terms_two, "x")
-    keep, send = block_terms(place, features, grad_high, grad_low)
+    arrived_two = spread(terms_two, ("x", "y"))
+    keep, send = block_terms(place, *feats, grad_high, grad_low)
     terms_one = keep + lax.ppermute(send, "core", swap)
-    arrived_one = spread(terms_one, "y")
+    arrived_one = spread(terms_one, ("x", "y"))
     terms_one, grad_high, grad_low = lax.optimization_barrier((terms_one, grad_high, grad_low))
-    grad_features, grad_flow = adjoints(grad_high, grad_low, kernel_one, cot, kernel_two)
+    grad_features, grad_flow = adjoints(grad_high, grad_low, *taps, cot, kernel_two)
     arrived_one, arrived_two, grad_features, grad_flow = lax.optimization_barrier(
         (arrived_one, arrived_two, grad_features, grad_flow)
     )
     terms_one = summed(terms_one[0], arrived_one)
     terms_two = summed(terms_two[0], arrived_two)
-    arrived_one, arrived_two = spread(terms_one, "x"), spread(terms_two, "y")
-    terms_one = summed(terms_one[0], arrived_one)
-    terms_two = summed(terms_two[0], arrived_two)
-    chunk = jnp.concatenate([terms_one, terms_two], axis=-2)
+    terms = jnp.concatenate([terms_one, terms_two], axis=-2)
+    chunk = summed(terms[0], spread(terms, ("y", "x")))
     chunk = chunk[0] + lax.ppermute(chunk[1], "zh", swap)
     chunk = summed(chunk, spread([chunk] * 4, "zl"))
     pieces = [chunk] + [lax.ppermute(chunk, "x", ring(k)) for k in (1, 2, 3)]

time: 107 us -> 97.2 us (0.908)
  starting transfers between devices: 60.6 us -> 41.9 us
  waiting for transfers between devices: 21.4 us -> 26.9 us
  Pallas kernels: 18.8 us -> 22.2 us
    ppermute x15 -> x12, starting transfers between devices: 38.6 us -> 21.7 us  [the longest x9 17.8 us: spread(): lax.ppermute(parts[k], ('x', 'y', 'core'), crossed(k, axes))]
    ppermute x15 -> x12, waiting for transfers between devices: 7.03 us -> 17.3 us  [the longest x9 10.5 us: spread(): lax.ppermute(parts[k], ('x', 'y', 'core'), crossed(k, axes))]
    ppermute x2, waiting for transfers between devices: 4.13 us -> 0.1 us  [local(): rows = [lax.ppermute(edges[k], HA, pairs(k)) for k in range(2)]]
    pallas_call x1 -> x3, Pallas kernels: 0.56 us -> 4.01 us  [the longest x1 2.25 us: local(): small(row_edges_kernel, 'row_edges', edges, 2, [pltpu.VMEM((FR, 2, W, C),...]
    ppermute x3, starting transfers between devices: 4.53 us -> 2.1 us  [local(): pieces = [chunk] + [lax.ppermute(chunk, 'x', ring(k)) for k in (1, 2, 3)]]
    ppermute x1, starting transfers between devices: 4.44 us -> 5.51 us  [local(): chunk = chunk[0] + lax.ppermute(chunk[1], 'zh', swap)]
    unnamed x12 -> x14, local copies, waits for them, and re-layouts: 3.81 us -> 3.16 us
  transfers between devices with their start and end apart: 25 -> 22, of which waited for: 10 -> 11; matrix products, arithmetic and copies ran while one was open for 0% -> 0% of each run, Pallas kernels for 10% -> 13%
where the time goes in v4:
time: 97.2 us; the launch traced here: 96.4 us
  starting transfers between devices  41.9 us (43%)
  waiting for transfers between devices  26.9 us (28%)
  Pallas kernels  22.2 us (23%)
  local copies, waits for them, and re-layouts  3.95 us (4%)
    ppermute x9, starting transfers between devices, spread(): lax.ppermute(parts[k], ('x', 'y', 'core'), crossed(k, axes))  17.8 us
    ppermute x9, waiting for transfers between devices, spread(): lax.ppermute(parts[k], ('x', 'y', 'core'), crossed(k, axes))  10.5 us
    ppermute x2, starting transfers between devices, local(): rows = [lax.ppermute(edges[k], HA, pairs(k)) for k in range(2)]  6.98 us
    pallas_call x1, Pallas kernels, adjoints(): pl.pallas_call(adjoint_kernel, out_shape=(jax.ShapeDtypeStruct((FR, R, W,...  6.89 us
    ppermute x3, waiting for transfers between devices, spread(): return [lax.ppermute(parts[k], 'zl', ring(k)) for k in (2, 1, 3)]  6.85 us
    ppermute x3, waiting for transfers between devices, local(): pieces = [chunk] + [lax.ppermute(chunk, 'x', ring(k)) for k in (1, 2, 3)]  5.52 us
    ppermute x1, starting transfers between devices, local(): chunk = chunk[0] + lax.ppermute(chunk[1], 'zh', swap)  5.51 us
    ppermute x1, starting transfers between devices, local(): terms_two = keep + lax.ppermute(send, 'core', swap)  4.76 us
  transfers between devices with their start and end apart: 22, of which 11 were waited for; matrix products, arithmetic and copies ran while one was open for 0% of the time, Pallas kernels for 13%

profile of v4, /device:TPU:6, one launch (start us, length us, event | category | flops | bytes accessed | tf_op | source)
XLA Modules:
  0.0 96.4 jit_solution(14005338201438467486)
XLA Ops:
  1.3 2.2 %row_edges.1 = (f32[2,80,128]{2,1,0:T(8,128)}, f32[2,80,128]{2,1,0:T(8,128)}) custom-call(s32[5]{0:T(128)} %stack.23.place_ref, f32[2,16,32,128]{3,2,1,0:T(8,128)} %feat_ref.7, f32[2,8,16,128]{3,2,1,0:T(8,128)} %local_ref.1), custom_call_target="tpu_custom_call" | custom-call | flops 1000000 | bytes 1000000 | tf_op jit(solution)/shard_map/row_edges/pallas_call | solution.py:390
  3.5 2.0 %collective-permute-start = (f32[2,80,128]{2,1,0:T(8,128)}, f32[2,80,128]{2,1,0:T(8,128)S(1)}, u32[]{:S(2)}, u32[]{:S(2)}) collective-permute-start(f32[2,80,128]{2,1,0:T(8,128)} %get-tuple-element.57), channel_id=1, source_target_pairs={{0,16},{16,0},{32,48},{48,32},{64,80},{80,64},{96,112},{112,96},{1... | collective-permute-start | bytes 245768 | tf_op jit(solution)/shard_map/ppermute | solution.py:401
  5.5 5.0 %collective-permute-start.1 = (f32[2,80,128]{2,1,0:T(8,128)}, f32[2,80,128]{2,1,0:T(8,128)S(1)}, u32[]{:S(2)}, u32[]{:S(2)}) collective-permute-start(f32[2,80,128]{2,1,0:T(8,128)} %get-tuple-element.58), channel_id=1, source_target_pairs={{16,32},{32,16},{48,64},{64,48},{80,96},{96,80},{112,128},{128,112... | collective-permute-start | bytes 245768 | tf_op jit(solution)/shard_map/ppermute | solution.py:401
  11.6 1.5 %copy-done.2 = f32[3,3,3,128,128]{4,3,2,1,0:T(8,128)S(1)} copy-done((f32[3,3,3,128,128]{4,3,2,1,0:T(8,128)S(1)}, f32[3,3,3,128,128]{4,3,2,1,0:T(8,128)}, u32[]{:S(2)}) %copy-start.2) | copy-done | bytes 1769496
  17.0 2.7 %flow_terms.1 = (f32[4,4,2,7,16,128]{5,4,3,2,1,0:T(8,128)S(1)}, f32[4,4,2,7,16,128]{5,4,3,2,1,0:T(8,128)S(1)}, f32[2,10,18,128]{3,2,1,0:T(8,128)S(1)}) custom-call(s32[5]{0:T(128)S(1)} %copy-done.5, bf16[512,128]{1,0:T(8,128)(2,1)S(1)} %get-tuple-element.75.flow_high, bf16[512,128]{1,0:T(8,128)(2,1)S(1)} %get-tuple-element.76.flow_low, ...), custom_call_target="tpu_custom_call" | custom-call | flops 2000000000 | bytes 5000000 | tf_op jit(solution)/shard_map/flow_terms/pallas_call | solution.py:295
  19.7 4.8 %collective-permute-start.4 = (f32[4,4,2,7,16,128]{5,4,3,2,1,0:T(8,128)S(1)}, f32[4,4,2,7,16,128]{5,4,3,2,1,0:T(8,128)S(1)}, u32[]{:S(2)}, u32[]{:S(2)}) collective-permute-start(f32[4,4,2,7,16,128]{5,4,3,2,1,0:T(8,128)S(1)} %get-tuple-element.80), channel_id=1, source_target_pairs={{0,1},{1,0},{2,3},{3,2},{4,5},{5,4},{6,7},{7,6},{8,9},{9,8},{10,11... | collective-permute-start | bytes 5505032 | tf_op jit(solution)/shard_map/ppermute | solution.py:422
  24.5 4.0 %block_gradient.1 = (bf16[3,18,32,256]{3,2,1,0:T(8,128)(2,1)S(1)}, bf16[3,18,32,256]{3,2,1,0:T(8,128)(2,1)S(1)}) custom-call(s32[5]{0:T(128)S(1)} %copy-done.5, f32[2,16,32,128]{3,2,1,0:T(8,128)S(1)} %copy-done.1, f32[2,80,128]{2,1,0:T(8,128)S(1)} %collective-permute-done.row_first_ref, f32[2,80,128]{2,1,0:T(8,128)S(1)} %collective-permute-done.1.row_second_ref, ...), custom_call_target="tpu_custom_call" | custom-call | flops 5000000000 | bytes 6000000 | tf_op jit(solution)/shard_map/block_gradient/pallas_call | solution.py:308
  28.7 2.7 %block_terms.1 = (f32[4,4,2,7,8,128]{5,4,3,2,1,0:T(8,128)S(1)}, f32[4,4,2,7,8,128]{5,4,3,2,1,0:T(8,128)S(1)}) custom-call(s32[5]{0:T(128)S(1)} %copy-done.5, bf16[256,512]{1,0:T(8,128)(2,1)S(1)} %get-tuple-element.64.feat_high, bf16[256,512]{1,0:T(8,128)(2,1)S(1)} %get-tuple-element.65.feat_low, ...), custom_call_target="tpu_custom_call" | custom-call | flops 1000000000 | bytes 1000000 | tf_op jit(solution)/shard_map/block_terms/pallas_call | solution.py:329
  33.1 2.1 %collective-permute-start.10 = (f32[4,2,7,16,128]{4,3,2,1,0:T(8,128)S(1)}, f32[4,2,7,16,128]{4,3,2,1,0:T(8,128)S(1)}, u32[]{:S(2)}, u32[]{:S(2)}) collective-permute-start(f32[4,2,7,16,128]{4,3,2,1,0:T(8,128)S(1)} %get-tuple-element.107), channel_id=1, source_target_pairs={{0,64},{1,3},{2,66},{3,5},{4,68},{5,7},{6,70},{7,1},{64,128},{65,6... | collective-permute-start | bytes 1376264 | tf_op jit(solution)/shard_map/ppermute | solution.py:377
  35.4 2.2 %collective-permute-start.6 = (f32[4,2,7,8,128]{4,3,2,1,0:T(8,128)S(1)}, f32[4,2,7,8,128]{4,3,2,1,0:T(8,128)S(1)}, u32[]{:S(2)}, u32[]{:S(2)}) collective-permute-start(f32[4,2,7,8,128]{4,3,2,1,0:T(8,128)S(1)} %get-tuple-element.111), channel_id=1, source_target_pairs={{0,128},{1,5},{2,130},{3,7},{4,132},{5,1},{6,134},{7,3},{64,192},{... | collective-permute-start | bytes 688136 | tf_op jit(solution)/shard_map/ppermute | solution.py:377
  38.8 3.1 %collective-permute-done.9 = f32[4,2,7,16,128]{4,3,2,1,0:T(8,128)S(1)} collective-permute-done((f32[4,2,7,16,128]{4,3,2,1,0:T(8,128)S(1)}, f32[4,2,7,16,128]{4,3,2,1,0:T(8,128)S(1)}, u32[]{:S(2)}, u32[]{:S(2)}) %collective-permute-start.9) | collective-permute-done | bytes 458784 | tf_op jit(solution)/shard_map/ppermute | solution.py:377
  42.6 6.9 %adjoints.1 = (f32[2,16,32,128]{3,2,1,0:T(8,128)}, f32[2,8,16,256]{3,2,1,0:T(8,128)}) custom-call(bf16[3,18,32,256]{3,2,1,0:T(8,128)(2,1)S(1)} %get-tuple-element.91.grad_high_ref, bf16[3,18,32,256]{3,2,1,0:T(8,128)(2,1)S(1)} %get-tuple-element.92.grad_low_ref, bf16[9,256,256]{2,1,0:T(8,128)(2,1)S(1)} %get-tuple-element.81.taps_high, ...), custom_call_target="tpu_custom_call" | custom-call | flops 4000000000 | bytes 10000000 | tf_op jit(solution)/shard_map/adjoints/pallas_call | solution.py:341
  49.5 2.0 %collective-permute-done.8 = f32[4,2,7,8,128]{4,3,2,1,0:T(8,128)S(1)} collective-permute-done((f32[4,2,7,8,128]{4,3,2,1,0:T(8,128)S(1)}, f32[4,2,7,8,128]{4,3,2,1,0:T(8,128)S(1)}, u32[]{:S(2)}, u32[]{:S(2)}) %collective-permute-start.8) | collective-permute-done | bytes 229408 | tf_op jit(solution)/shard_map/ppermute | solution.py:377
  51.8 3.3 %collective-permute-start.12 = (f32[2,7,24,128]{3,2,1,0:T(8,128)S(1)}, f32[2,7,24,128]{3,2,1,0:T(8,128)S(1)}, u32[]{:S(2)}, u32[]{:S(2)}) collective-permute-start(f32[2,7,24,128]{3,2,1,0:T(8,128)S(1)} %get-tuple-element.113), channel_id=1, source_target_pairs={{0,4},{1,129},{2,6},{3,131},{4,0},{5,133},{6,2},{7,135},{64,68},{6... | collective-permute-start | bytes 516104 | tf_op jit(solution)/shard_map/ppermute | solution.py:377
  55.1 6.7 %collective-permute-start.13 = (f32[2,7,24,128]{3,2,1,0:T(8,128)S(1)}, f32[2,7,24,128]{3,2,1,0:T(8,128)S(1)}, u32[]{:S(2)}, u32[]{:S(2)}) collective-permute-start(f32[2,7,24,128]{3,2,1,0:T(8,128)S(1)} %get-tuple-element.114), channel_id=1, source_target_pairs={{0,2},{1,65},{2,4},{3,67},{4,6},{5,69},{6,0},{7,71},{64,66},{65,12... | collective-permute-start | bytes 516104 | tf_op jit(solution)/shard_map/ppermute | solution.py:377
  61.8 2.9 %collective-permute-done.13 = f32[2,7,24,128]{3,2,1,0:T(8,128)S(1)} collective-permute-done((f32[2,7,24,128]{3,2,1,0:T(8,128)S(1)}, f32[2,7,24,128]{3,2,1,0:T(8,128)S(1)}, u32[]{:S(2)}, u32[]{:S(2)}) %collective-permute-start.13) | collective-permute-done | bytes 172064 | tf_op jit(solution)/shard_map/ppermute | solution.py:377
  64.7 2.5 %collective-permute-done.14 = f32[2,7,24,128]{3,2,1,0:T(8,128)S(1)} collective-permute-done((f32[2,7,24,128]{3,2,1,0:T(8,128)S(1)}, f32[2,7,24,128]{3,2,1,0:T(8,128)S(1)}, u32[]{:S(2)}, u32[]{:S(2)}) %collective-permute-start.14) | collective-permute-done | bytes 172064 | tf_op jit(solution)/shard_map/ppermute | solution.py:377
  67.3 5.5 %collective-permute-start.15 = (f32[7,24,128]{2,1,0:T(8,128)S(1)}, f32[7,24,128]{2,1,0:T(8,128)S(1)}, u32[]{:S(2)}, u32[]{:S(2)}) collective-permute-start(f32[7,24,128]{2,1,0:T(8,128)S(1)} %slice_bitcast_fusion.6), channel_id=1, source_target_pairs={{0,8},{8,0},{1,9},{9,1},{2,10},{10,2},{3,11},{11,3},{4,12},{12,4},... | collective-permute-start | bytes 258056 | tf_op jit(solution)/shard_map/ppermute | solution.py:438
  72.8 3.9 %collective-permute-done.15 = f32[7,24,128]{2,1,0:T(8,128)S(1)} collective-permute-done((f32[7,24,128]{2,1,0:T(8,128)S(1)}, f32[7,24,128]{2,1,0:T(8,128)S(1)}, u32[]{:S(2)}, u32[]{:S(2)}) %collective-permute-start.15) | collective-permute-done | bytes 86048 | tf_op jit(solution)/shard_map/ppermute | solution.py:438
  77.5 3.1 %collective-permute-start.18 = (f32[7,24,128]{2,1,0:T(8,128)S(1)}, f32[7,24,128]{2,1,0:T(8,128)S(1)}, u32[]{:S(2)}, u32[]{:S(2)}) collective-permute-start(f32[7,24,128]{2,1,0:T(8,128)S(1)} %fusion.11), channel_id=1, source_target_pairs={{0,48},{16,0},{32,16},{48,32},{1,49},{17,1},{33,17},{49,33},{2,50}... | collective-permute-start | bytes 258056 | tf_op jit(solution)/shard_map/ppermute | solution.py:376
  80.6 3.3 %collective-permute-done.17 = f32[7,24,128]{2,1,0:T(8,128)S(1)} collective-permute-done((f32[7,24,128]{2,1,0:T(8,128)S(1)}, f32[7,24,128]{2,1,0:T(8,128)S(1)}, u32[]{:S(2)}, u32[]{:S(2)}) %collective-permute-start.17) | collective-permute-done | bytes 86048 | tf_op jit(solution)/shard_map/ppermute | solution.py:376
  83.9 3.6 %collective-permute-done.16 = f32[7,24,128]{2,1,0:T(8,128)S(1)} collective-permute-done((f32[7,24,128]{2,1,0:T(8,128)S(1)}, f32[7,24,128]{2,1,0:T(8,128)S(1)}, u32[]{:S(2)}, u32[]{:S(2)}) %collective-permute-start.16) | collective-permute-done | bytes 86048 | tf_op jit(solution)/shard_map/ppermute | solution.py:376
  89.6 2.5 %collective-permute-done.19.one_ref = f32[7,24,128]{2,1,0:T(8,128)S(1)} collective-permute-done((f32[7,24,128]{2,1,0:T(8,128)S(1)}, f32[7,24,128]{2,1,0:T(8,128)S(1)}, u32[]{:S(2)}, u32[]{:S(2)}) %collective-permute-start.19) | collective-permute-done | bytes 86048 | tf_op jit(solution)/shard_map/ppermute | solution.py:440
  92.0 2.5 %collective-permute-done.20.two_ref = f32[7,24,128]{2,1,0:T(8,128)S(1)} collective-permute-done((f32[7,24,128]{2,1,0:T(8,128)S(1)}, f32[7,24,128]{2,1,0:T(8,128)S(1)}, u32[]{:S(2)}, u32[]{:S(2)}) %collective-permute-start.20) | collective-permute-done | bytes 86048 | tf_op jit(solution)/shard_map/ppermute | solution.py:440
  (55 shorter events, 14.7 us)
Async XLA Ops:
  3.5 11.2 %collective-permute-start = (f32[2,80,128]{2,1,0:T(8,128)}, f32[2,80,128]{2,1,0:T(8,128)S(1)}, u32[]{:S(2)}, u32[]{:S(2)}) collective-permute-start(f32[2,80,128]{2,1,0:T(8,128)} %get-tuple-element.57), channel_id=1, source_target_pairs={{0,16},{16,0},{32,48},{48,32},{64,80},{80,64},{96,112},{112,96},{1... | collective-permute-start | bytes 245768 | tf_op jit(solution)/shard_map/ppermute | solution.py:401
  5.5 9.3 %collective-permute-start.1 = (f32[2,80,128]{2,1,0:T(8,128)}, f32[2,80,128]{2,1,0:T(8,128)S(1)}, u32[]{:S(2)}, u32[]{:S(2)}) collective-permute-start(f32[2,80,128]{2,1,0:T(8,128)} %get-tuple-element.58), channel_id=1, source_target_pairs={{16,32},{32,16},{48,64},{64,48},{80,96},{96,80},{112,128},{128,112... | collective-permute-start | bytes 245768 | tf_op jit(solution)/shard_map/ppermute | solution.py:401
  15.5 1.5 %collective-permute-start.2 = (f32[2,64,128]{2,1,0:T(8,128)S(1)}, f32[2,64,128]{2,1,0:T(8,128)S(1)}, u32[]{:S(2)}, u32[]{:S(2)}) collective-permute-start(f32[2,64,128]{2,1,0:T(8,128)S(1)} %get-tuple-element.70), channel_id=1, source_target_pairs={{0,1},{1,0},{2,3},{3,2},{4,5},{5,4},{6,7},{7,6},{8,9},{9,8},{10,11... | collective-permute-start | bytes 196616 | tf_op jit(solution)/shard_map/ppermute | solution.py:415
  15.6 1.4 %collective-permute-start.3 = (f32[2,64,128]{2,1,0:T(8,128)S(1)}, f32[2,64,128]{2,1,0:T(8,128)S(1)}, u32[]{:S(2)}, u32[]{:S(2)}) collective-permute-start(f32[2,64,128]{2,1,0:T(8,128)S(1)} %get-tuple-element.71), channel_id=1, source_target_pairs={{1,2},{2,1},{3,4},{4,3},{5,6},{6,5},{7,8},{8,7},{9,10},{10,9},{11,... | collective-permute-start | bytes 196616 | tf_op jit(solution)/shard_map/ppermute | solution.py:415
  17.0 7.5 %copy-start.1 = (f32[2,16,32,128]{3,2,1,0:T(8,128)S(1)}, f32[2,16,32,128]{3,2,1,0:T(8,128)}, u32[]{:S(2)}) copy-start(f32[2,16,32,128]{3,2,1,0:T(8,128)} %feat_ref.7) | copy-start | bytes 1572868
  19.7 8.8 %collective-permute-start.4 = (f32[4,4,2,7,16,128]{5,4,3,2,1,0:T(8,128)S(1)}, f32[4,4,2,7,16,128]{5,4,3,2,1,0:T(8,128)S(1)}, u32[]{:S(2)}, u32[]{:S(2)}) collective-permute-start(f32[4,4,2,7,16,128]{5,4,3,2,1,0:T(8,128)S(1)} %get-tuple-element.80), channel_id=1, source_target_pairs={{0,1},{1,0},{2,3},{3,2},{4,5},{5,4},{6,7},{7,6},{8,9},{9,8},{10,11... | collective-permute-start | bytes 5505032 | tf_op jit(solution)/shard_map/ppermute | solution.py:422
  31.4 3.8 %collective-permute-start.5 = (f32[4,4,2,7,8,128]{5,4,3,2,1,0:T(8,128)S(1)}, f32[4,4,2,7,8,128]{5,4,3,2,1,0:T(8,128)S(1)}, u32[]{:S(2)}, u32[]{:S(2)}) collective-permute-start(f32[4,4,2,7,8,128]{5,4,3,2,1,0:T(8,128)S(1)} %get-tuple-element.89), channel_id=1, source_target_pairs={{0,1},{1,0},{2,3},{3,2},{4,5},{5,4},{6,7},{7,6},{8,9},{9,8},{10,11... | collective-permute-start | bytes 2752520 | tf_op jit(solution)/shard_map/ppermute | solution.py:427
  31.7 10.2 %collective-permute-start.9 = (f32[4,2,7,16,128]{4,3,2,1,0:T(8,128)S(1)}, f32[4,2,7,16,128]{4,3,2,1,0:T(8,128)S(1)}, u32[]{:S(2)}, u32[]{:S(2)}) collective-permute-start(f32[4,2,7,16,128]{4,3,2,1,0:T(8,128)S(1)} %get-tuple-element.108), channel_id=1, source_target_pairs={{0,128},{1,5},{2,130},{3,7},{4,132},{5,1},{6,134},{7,3},{64,192},{... | collective-permute-start | bytes 1376264 | tf_op jit(solution)/shard_map/ppermute | solution.py:377
  33.1 16.4 %collective-permute-start.10 = (f32[4,2,7,16,128]{4,3,2,1,0:T(8,128)S(1)}, f32[4,2,7,16,128]{4,3,2,1,0:T(8,128)S(1)}, u32[]{:S(2)}, u32[]{:S(2)}) collective-permute-start(f32[4,2,7,16,128]{4,3,2,1,0:T(8,128)S(1)} %get-tuple-element.107), channel_id=1, source_target_pairs={{0,64},{1,3},{2,66},{3,5},{4,68},{5,7},{6,70},{7,1},{64,128},{65,6... | collective-permute-start | bytes 1376264 | tf_op jit(solution)/shard_map/ppermute | solution.py:377
  35.2 14.3 %collective-permute-start.11 = (f32[4,2,7,16,128]{4,3,2,1,0:T(8,128)S(1)}, f32[4,2,7,16,128]{4,3,2,1,0:T(8,128)S(1)}, u32[]{:S(2)}, u32[]{:S(2)}) collective-permute-start(f32[4,2,7,16,128]{4,3,2,1,0:T(8,128)S(1)} %get-tuple-element.106), channel_id=1, source_target_pairs={{0,192},{1,7},{2,194},{3,1},{4,196},{5,3},{6,198},{7,5},{64,0},{65... | collective-permute-start | bytes 1376264 | tf_op jit(solution)/shard_map/ppermute | solution.py:377
  35.4 14.2 %collective-permute-start.6 = (f32[4,2,7,8,128]{4,3,2,1,0:T(8,128)S(1)}, f32[4,2,7,8,128]{4,3,2,1,0:T(8,128)S(1)}, u32[]{:S(2)}, u32[]{:S(2)}) collective-permute-start(f32[4,2,7,8,128]{4,3,2,1,0:T(8,128)S(1)} %get-tuple-element.111), channel_id=1, source_target_pairs={{0,128},{1,5},{2,130},{3,7},{4,132},{5,1},{6,134},{7,3},{64,192},{... | collective-permute-start | bytes 688136 | tf_op jit(solution)/shard_map/ppermute | solution.py:377
  37.5 12.0 %collective-permute-start.7 = (f32[4,2,7,8,128]{4,3,2,1,0:T(8,128)S(1)}, f32[4,2,7,8,128]{4,3,2,1,0:T(8,128)S(1)}, u32[]{:S(2)}, u32[]{:S(2)}) collective-permute-start(f32[4,2,7,8,128]{4,3,2,1,0:T(8,128)S(1)} %get-tuple-element.110), channel_id=1, source_target_pairs={{0,64},{1,3},{2,66},{3,5},{4,68},{5,7},{6,70},{7,1},{64,128},{65,6... | collective-permute-start | bytes 688136 | tf_op jit(solution)/shard_map/ppermute | solution.py:377
  41.8 9.7 %collective-permute-start.8 = (f32[4,2,7,8,128]{4,3,2,1,0:T(8,128)S(1)}, f32[4,2,7,8,128]{4,3,2,1,0:T(8,128)S(1)}, u32[]{:S(2)}, u32[]{:S(2)}) collective-permute-start(f32[4,2,7,8,128]{4,3,2,1,0:T(8,128)S(1)} %get-tuple-element.109), channel_id=1, source_target_pairs={{0,192},{1,7},{2,194},{3,1},{4,196},{5,3},{6,198},{7,5},{64,0},{65... | collective-permute-start | bytes 688136 | tf_op jit(solution)/shard_map/ppermute | solution.py:377
  51.7 43.4 %copy-start.6 = (s32[5]{0:T(128)S(1)}, s32[5]{0:T(128)}, u32[]{:S(2)}) copy-start(s32[5]{0:T(128)} %stack.23.place_ref) | copy-start | bytes 64
  51.8 10.0 %collective-permute-start.12 = (f32[2,7,24,128]{3,2,1,0:T(8,128)S(1)}, f32[2,7,24,128]{3,2,1,0:T(8,128)S(1)}, u32[]{:S(2)}, u32[]{:S(2)}) collective-permute-start(f32[2,7,24,128]{3,2,1,0:T(8,128)S(1)} %get-tuple-element.113), channel_id=1, source_target_pairs={{0,4},{1,129},{2,6},{3,131},{4,0},{5,133},{6,2},{7,135},{64,68},{6... | collective-permute-start | bytes 516104 | tf_op jit(solution)/shard_map/ppermute | solution.py:377
  55.1 9.7 %collective-permute-start.13 = (f32[2,7,24,128]{3,2,1,0:T(8,128)S(1)}, f32[2,7,24,128]{3,2,1,0:T(8,128)S(1)}, u32[]{:S(2)}, u32[]{:S(2)}) collective-permute-start(f32[2,7,24,128]{3,2,1,0:T(8,128)S(1)} %get-tuple-element.114), channel_id=1, source_target_pairs={{0,2},{1,65},{2,4},{3,67},{4,6},{5,69},{6,0},{7,71},{64,66},{65,12... | collective-permute-start | bytes 516104 | tf_op jit(solution)/shard_map/ppermute | solution.py:377
  61.8 5.4 %collective-permute-start.14 = (f32[2,7,24,128]{3,2,1,0:T(8,128)S(1)}, f32[2,7,24,128]{3,2,1,0:T(8,128)S(1)}, u32[]{:S(2)}, u32[]{:S(2)}) collective-permute-start(f32[2,7,24,128]{3,2,1,0:T(8,128)S(1)} %get-tuple-element.112), channel_id=1, source_target_pairs={{0,6},{1,193},{2,0},{3,195},{4,2},{5,197},{6,4},{7,199},{64,70},{6... | collective-permute-start | bytes 516104 | tf_op jit(solution)/shard_map/ppermute | solution.py:377
  67.3 9.4 %collective-permute-start.15 = (f32[7,24,128]{2,1,0:T(8,128)S(1)}, f32[7,24,128]{2,1,0:T(8,128)S(1)}, u32[]{:S(2)}, u32[]{:S(2)}) collective-permute-start(f32[7,24,128]{2,1,0:T(8,128)S(1)} %slice_bitcast_fusion.6), channel_id=1, source_target_pairs={{0,8},{8,0},{1,9},{9,1},{2,10},{10,2},{3,11},{11,3},{4,12},{12,4},... | collective-permute-start | bytes 258056 | tf_op jit(solution)/shard_map/ppermute | solution.py:438
  76.7 7.2 %collective-permute-start.17 = (f32[7,24,128]{2,1,0:T(8,128)S(1)}, f32[7,24,128]{2,1,0:T(8,128)S(1)}, u32[]{:S(2)}, u32[]{:S(2)}) collective-permute-start(f32[7,24,128]{2,1,0:T(8,128)S(1)} %fusion.11), channel_id=1, source_target_pairs={{0,16},{16,32},{32,48},{48,0},{1,17},{17,33},{33,49},{49,1},{2,18}... | collective-permute-start | bytes 258056 | tf_op jit(solution)/shard_map/ppermute | solution.py:376
  77.5 6.3 %collective-permute-start.18 = (f32[7,24,128]{2,1,0:T(8,128)S(1)}, f32[7,24,128]{2,1,0:T(8,128)S(1)}, u32[]{:S(2)}, u32[]{:S(2)}) collective-permute-start(f32[7,24,128]{2,1,0:T(8,128)S(1)} %fusion.11), channel_id=1, source_target_pairs={{0,48},{16,0},{32,16},{48,32},{1,49},{17,1},{33,17},{49,33},{2,50}... | collective-permute-start | bytes 258056 | tf_op jit(solution)/shard_map/ppermute | solution.py:376
  80.6 6.9 %collective-permute-start.16 = (f32[7,24,128]{2,1,0:T(8,128)S(1)}, f32[7,24,128]{2,1,0:T(8,128)S(1)}, u32[]{:S(2)}, u32[]{:S(2)}) collective-permute-start(f32[7,24,128]{2,1,0:T(8,128)S(1)} %fusion.11), channel_id=1, source_target_pairs={{0,32},{16,48},{32,0},{48,16},{1,33},{17,49},{33,1},{49,17},{2,34}... | collective-permute-start | bytes 258056 | tf_op jit(solution)/shard_map/ppermute | solution.py:376
  87.5 4.6 %collective-permute-start.19 = (f32[7,24,128]{2,1,0:T(8,128)S(1)}, f32[7,24,128]{2,1,0:T(8,128)S(1)}, u32[]{:S(2)}, u32[]{:S(2)}) collective-permute-start(f32[7,24,128]{2,1,0:T(8,128)S(1)} %add_add_fusion.own_ref), channel_id=1, source_target_pairs={{0,64},{64,128},{128,192},{192,0},{1,65},{65,129},{129,193},{193,1... | collective-permute-start | bytes 258056 | tf_op jit(solution)/shard_map/ppermute | solution.py:440
  87.6 7.0 %collective-permute-start.20 = (f32[7,24,128]{2,1,0:T(8,128)S(1)}, f32[7,24,128]{2,1,0:T(8,128)S(1)}, u32[]{:S(2)}, u32[]{:S(2)}) collective-permute-start(f32[7,24,128]{2,1,0:T(8,128)S(1)} %add_add_fusion.own_ref), channel_id=1, source_target_pairs={{0,128},{64,192},{128,0},{192,64},{1,129},{65,193},{129,1},{193,65... | collective-permute-start | bytes 258056 | tf_op jit(solution)/shard_map/ppermute | solution.py:440
  88.1 7.0 %collective-permute-start.21 = (f32[7,24,128]{2,1,0:T(8,128)S(1)}, f32[7,24,128]{2,1,0:T(8,128)S(1)}, u32[]{:S(2)}, u32[]{:S(2)}) collective-permute-start(f32[7,24,128]{2,1,0:T(8,128)S(1)} %add_add_fusion.own_ref), channel_id=1, source_target_pairs={{0,192},{64,0},{128,64},{192,128},{1,193},{65,1},{129,65},{193,129... | collective-permute-start | bytes 258056 | tf_op jit(solution)/shard_map/ppermute | solution.py:440
  (5 other events, 6.9 us)

commit v5 on v4

--- a/solution.py
+++ b/solution.py
@@ -12,12 +12,11 @@
 R2, W2, CF = 8, 16, 256
 PITCH = 40
 EXT = (R + 2) * PITCH
-COL = 24
+COL = 20
 HA, WA = ("x", "zl"), ("zh", "y", "core")
 
 f32, bf16 = jnp.float32, jnp.bfloat16
 VMEM = pl.BlockSpec(memory_space=pltpu.VMEM)
-SMEM = pl.BlockSpec(memory_space=pltpu.SMEM)
 HBM = pl.BlockSpec(memory_space=pltpu.HBM)
 
 
@@ -26,11 +25,18 @@
     return high, (values - high.astype(f32)).astype(bf16)
 
 
+def dot(left, right, dims):
+    return lax.dot_general(left, right, (dims, ((), ())), preferred_element_type=f32)
+
+
 def product(left, right, dims):
-    dot = functools.partial(
-        lax.dot_general, dimension_numbers=(dims, ((), ())), preferred_element_type=f32
-    )
-    return dot(left[0], right[0]) + (dot(left[0], right[1]) + dot(left[1], right[0]))
+    return dot(left[0], right[0], dims) + (dot(left[0], right[1], dims) + dot(left[1], right[0], dims))
+
+
+def tall_product(left, right, dims):
+    rows = left[0].shape[0]
+    both = dot(jnp.concatenate(left, axis=0), right[0], dims)
+    return both[:rows] + (both[rows:] + dot(left[0], right[1], dims))
 
 
 NN = ((1,), (0,))
@@ -43,14 +49,14 @@
     return jnp.concatenate([first, second], axis=0)
 
 
-def store_terms(place_ref, keep_ref, send_ref, tap, value, depth):
+def store_terms(keep_ref, send_ref, tap, value, depth):
     half = value.shape[0] // 2
     taps = (
         (0, value[:half, C:]),
         (1, value[:half, :C] + value[half:, C:]),
         (2, value[half:, :C]),
     )
-    core, y, x, zh = place_ref[0], place_ref[1], place_ref[2], place_ref[3]
+    core, y, x, zh = [lax.axis_index(a) for a in ("core", "y", "x", "zh")]
     for time_tap, part in taps:
         number = 9 * time_tap + tap
         slot_x = lax.rem(number // 7 - x + 4, 4)
@@ -65,7 +71,7 @@
 
 
 def row_edges_kernel(
-    place_ref, feat_ref, cot_ref, first_ref, second_ref, feat_top, feat_bottom, cot_top, cot_bottom, sems
+    feat_ref, cot_ref, first_ref, second_ref, feat_top, feat_bottom, cot_top, cot_bottom, sems
 ):
     copies = [
         pltpu.make_async_copy(feat_ref.at[:, 0:2], feat_top, sems.at[0]),
@@ -77,7 +83,7 @@
         copy.start()
     for copy in copies:
         copy.wait()
-    odd = place_ref[4] == 1
+    odd = lax.rem(lax.axis_index("zl"), 2) == 1
     for t in range(FR):
         for row in range(2):
             top, bottom = feat_top[t, row], feat_bottom[t, row]
@@ -89,29 +95,30 @@
         second_ref[t, 2 * W :] = jnp.where(odd, bottom, top)
 
 
-def prepare_kernel(place_ref, weight_ref, feat_ref, taps_high, taps_low, feat_high, feat_low):
+def prepare_features_kernel(feat_ref, cot_ref, feat_high, feat_low, near_cot_ref):
+    near_cot_ref[...] = cot_ref[...]
+    for t in range(FR):
+        lines = slice(t * C, (t + 1) * C)
+        feat_high[lines], feat_low[lines] = split(feat_ref[t].reshape(R * W, C).T)
+
+
+def prepare_kernel(weight_ref, flow_ref, taps_high, taps_low, flow_high, flow_low):
     for tap in range(9):
         taps_high[tap], taps_low[tap] = split(both_frames(weight_ref, tap))
     for t in range(FR):
-        lines = slice(t * C, (t + 1) * C)
-        feat_high[lines], feat_low[lines] = split(feat_ref[t].reshape(R * W, C).T)
-
-
-def prepare_flow_kernel(place_ref, flow_ref, flow_high, flow_low):
-    for t in range(FR):
         lines = slice(t * CF, (t + 1) * CF)
         flow_high[lines], flow_low[lines] = split(flow_ref[t].reshape(R2 * W2, CF).T)
 
 
-def row_halo(place_ref, first_ref, second_ref, t, lines):
-    odd = place_ref[4] == 1
+def row_halo(first_ref, second_ref, t, lines):
+    odd = lax.rem(lax.axis_index("zl"), 2) == 1
     first, second = first_ref[t, lines], second_ref[t, lines]
     return jnp.where(odd, first, second), jnp.where(odd, second, first)
 
 
-def col_edges_kernel(place_ref, feat_ref, cot_ref, row_first_ref, row_second_ref, first_ref, second_ref, edge_ref):
-    for t in range(FR):
-        halos = [row_halo(place_ref, row_first_ref, row_second_ref, t, slice(r * W, (r + 1) * W)) for r in range(2)]
+def col_edges_kernel(feat_ref, cot_ref, row_first_ref, row_second_ref, first_ref, second_ref, edge_ref):
+    for t in range(FR):
+        halos = [row_halo(row_first_ref, row_second_ref, t, slice(r * W, (r + 1) * W)) for r in range(2)]
         for side, start in ((0, 0), (1, W - 2)):
             for col in range(2):
                 at, place = start + col, col * COL
@@ -120,19 +127,19 @@
                     low = place + R + 2 + row
                     edge_ref[side, t, low : low + 1] = halos[row][1][at : at + 1]
                 edge_ref[side, t, place + 2 : place + 2 + R] = feat_ref[t, :, at, :]
-        above, below = row_halo(place_ref, row_first_ref, row_second_ref, t, slice(2 * W, 2 * W + W2))
+        above, below = row_halo(row_first_ref, row_second_ref, t, slice(2 * W, 2 * W + W2))
         for side, at in ((0, 0), (1, W2 - 1)):
             place = 2 * COL
             edge_ref[side, t, place : place + 1] = above[at : at + 1]
             edge_ref[side, t, place + 1 : place + 1 + R2] = cot_ref[t, :, at, :]
             edge_ref[side, t, place + 1 + R2 : place + 2 + R2] = below[at : at + 1]
-    odd = place_ref[0] == 1
+    odd = lax.axis_index("core") == 1
     first_ref[...] = jnp.where(odd, edge_ref[0], edge_ref[1])
     second_ref[...] = jnp.where(odd, edge_ref[1], edge_ref[0])
 
 
-def col_halo(place_ref, first_ref, second_ref, t, lines):
-    odd = place_ref[0] == 1
+def col_halo(first_ref, second_ref, t, lines):
+    odd = lax.axis_index("core") == 1
     first, second = first_ref[t, lines], second_ref[t, lines]
     return jnp.where(odd, first, second), jnp.where(odd, second, first)
 
@@ -143,30 +150,29 @@
 
 
 def flow_terms_kernel(
-    place_ref, flow_high, flow_low, local_ref, row_first_ref, row_second_ref, col_first_ref, col_second_ref,
+    flow_high, flow_low, local_ref, row_first_ref, row_second_ref, col_first_ref, col_second_ref,
     keep_ref, send_ref, cot_ref,
 ):
     for t in range(FR):
-        above, below = row_halo(place_ref, row_first_ref, row_second_ref, t, slice(2 * W, 2 * W + W2))
+        above, below = row_halo(row_first_ref, row_second_ref, t, slice(2 * W, 2 * W + W2))
         cot_ref[t, 0, 1 : 1 + W2] = above
         cot_ref[t, 1 : 1 + R2, 1 : 1 + W2] = local_ref[t]
         cot_ref[t, 1 + R2, 1 : 1 + W2] = below
         lines = slice(2 * COL, 2 * COL + R2 + 2)
-        left, right = col_halo(place_ref, col_first_ref, col_second_ref, t, lines)
+        left, right = col_halo(col_first_ref, col_second_ref, t, lines)
         cot_ref[t, :, 0] = left
         cot_ref[t, :, 1 + W2] = right
-    flow = flow_high[...], flow_low[...]
+    flow = jnp.concatenate([flow_high[...], flow_high[...], flow_low[...]], axis=1)
     for col_tap in range(3):
         cot = shifted_cot(cot_ref, 2 - col_tap)
         for row_tap in range(3):
             window = [v[2 - row_tap : 2 - row_tap + R2].reshape(R2 * W2, 2 * C) for v in cot]
-            store_terms(
-                place_ref, keep_ref, send_ref, 3 * row_tap + col_tap, product(flow, window, NN), 16
-            )
+            window = jnp.concatenate([window[0], window[1], window[0]], axis=0)
+            store_terms(keep_ref, send_ref, 3 * row_tap + col_tap, dot(flow, window, NN), 16)
 
 
 def block_kernel(
-    place_ref, feat_ref, row_first_ref, row_second_ref, col_first_ref, col_second_ref,
+    feat_ref, row_first_ref, row_second_ref, col_first_ref, col_second_ref,
     taps_high, taps_low, cot_ref, grad_high_ref, grad_low_ref,
     ext_ref, wide_ref, even_high, even_low, odd_high, odd_low, grad_ref,
 ):
@@ -175,11 +181,11 @@
         lanes = slice(t * C, (t + 1) * C)
         ext_ref[2 : 2 + R, 3 : 3 + W, lanes] = feat_ref[t]
         for row in range(2):
-            above, below = row_halo(place_ref, row_first_ref, row_second_ref, t, slice(row * W, (row + 1) * W))
+            above, below = row_halo(row_first_ref, row_second_ref, t, slice(row * W, (row + 1) * W))
             ext_ref[row, 3 : 3 + W, lanes] = above
             ext_ref[R + 2 + row, 3 : 3 + W, lanes] = below
             place = slice(row * COL, row * COL + R + 4)
-            left, right = col_halo(place_ref, col_first_ref, col_second_ref, t, place)
+            left, right = col_halo(col_first_ref, col_second_ref, t, place)
             ext_ref[:, 1 + row, lanes] = left
             ext_ref[:, 3 + W + row, lanes] = right
     for t in range(FR):
@@ -224,7 +230,7 @@
         grad_low_ref[e] = low
 
 
-def block_terms_kernel(place_ref, feat_high, feat_low, grad_high_ref, grad_low_ref, keep_ref, send_ref):
+def block_terms_kernel(feat_high, feat_low, grad_high_ref, grad_low_ref, keep_ref, send_ref):
     feat = feat_high[...], feat_low[...]
     for row_tap in range(3):
         for e in range(3):
@@ -232,12 +238,10 @@
                 ref[e, 2 - row_tap : 2 - row_tap + R].reshape(R * W, 2 * C)
                 for ref in (grad_high_ref, grad_low_ref)
             ]
-            store_terms(
-                place_ref, keep_ref, send_ref, 3 * row_tap + e, product(feat, window, NN), 8
-            )
-
-
-def adjoint_kernel(grad_high_ref, grad_low_ref, taps_high, taps_low, cot_ref, weight_two_ref, feat_out, flow_out):
+            store_terms(keep_ref, send_ref, 3 * row_tap + e, tall_product(feat, window, NN), 8)
+
+
+def feature_adjoint_kernel(grad_high_ref, grad_low_ref, taps_high, taps_low, feat_out):
     total = jnp.zeros((R * W, 2 * C), f32)
     for row_tap in range(3):
         for e in range(3):
@@ -246,24 +250,40 @@
                 for ref in (grad_high_ref, grad_low_ref)
             ]
             tap = 3 * row_tap + e
-            total = total + product(window, (taps_high[tap], taps_low[tap]), NT)
+            total = total + tall_product(window, (taps_high[tap], taps_low[tap]), NT)
     for t in range(FR):
         feat_out[t] = total[:, t * C : (t + 1) * C].reshape(R, W, C)
+
+
+def flow_adjoint_kernel(cot_ref, weight_two_ref, flow_out):
     total = jnp.zeros((R2 * W2, 2 * CF), f32)
     for e in range(3):
         cot = shifted_cot(cot_ref, 2 - e)
         for row_tap in range(3):
             window = [v[2 - row_tap : 2 - row_tap + R2].reshape(R2 * W2, 2 * C) for v in cot]
-            total = total + product(window, split(both_frames(weight_two_ref, 3 * row_tap + e)), NT)
+            total = total + tall_product(window, split(both_frames(weight_two_ref, 3 * row_tap + e)), NT)
     for t in range(FR):
         flow_out[t] = total[:, t * CF : (t + 1) * CF].reshape(R2, W2, CF)
 
 
-def gather_kernel(place_ref, own_ref, one_ref, two_ref, three_ref, grad_one_ref, grad_two_ref):
+def first_sum_kernel(*refs):
+    ones, twos, outs = refs[:4], refs[4:8], refs[8:]
+    for slot, out in enumerate(outs):
+        for depth, parts in ((slice(0, 8), ones), (slice(8, 24), twos)):
+            own, second, first, third = parts
+            out[:, :, depth] = (own[0, slot] + second[slot]) + (first[slot] + third[slot])
+
+
+def second_sum_kernel(own, second, first, third, keep, send):
+    keep[...] = (own[0] + second[0]) + (first[0] + third[0])
+    send[...] = (own[1] + second[1]) + (first[1] + third[1])
+
+
+def gather_kernel(own_ref, one_ref, two_ref, three_ref, grad_one_ref, grad_two_ref):
     scale_one = 1.0 / (FR * R * W * 256) ** 0.5
     scale_two = 1.0 / (FR * R2 * W2 * 256) ** 0.5
     for k, ref in enumerate((own_ref, one_ref, two_ref, three_ref)):
-        first = 7 * lax.rem(place_ref[2] - k + 4, 4)
+        first = 7 * lax.rem(lax.axis_index("x") - k + 4, 4)
 
         def put(j, ref=ref, first=first):
             grad_one_ref[first + j] = ref[j, :8] * scale_one
@@ -282,7 +302,7 @@
     return pl.pallas_call(
         kernel,
         out_shape=out_shape,
-        in_specs=[SMEM] + [space] * count,
+        in_specs=[space] * count,
         out_specs=(VMEM,) * len(out_shape),
         scratch_shapes=scratch,
         compiler_params=params(48 if space is VMEM else 64),
@@ -296,7 +316,7 @@
         flow_terms_kernel,
         out_shape=(jax.ShapeDtypeStruct((4, 4, 2, 7, 16, C), f32),) * 2
         + (jax.ShapeDtypeStruct((FR, R2 + 2, W2 + 2, C), f32),),
-        in_specs=[SMEM] + [VMEM] * 7,
+        in_specs=[VMEM] * 7,
         out_specs=(VMEM,) * 3,
         compiler_params=params(),
         cost_estimate=pl.CostEstimate(flops=2 * 10**9, bytes_accessed=5 * 10**6, transcendentals=0),
@@ -308,7 +328,7 @@
     return pl.pallas_call(
         block_kernel,
         out_shape=(jax.ShapeDtypeStruct((3, R + 2, W, 2 * C), bf16),) * 2,
-        in_specs=[SMEM] + [VMEM] * 8,
+        in_specs=[VMEM] * 8,
         out_specs=(VMEM,) * 2,
         scratch_shapes=[
             pltpu.VMEM((R + 4, PITCH + 8, 2 * C), f32),
@@ -329,7 +349,7 @@
     return pl.pallas_call(
         block_terms_kernel,
         out_shape=(jax.ShapeDtypeStruct((4, 4, 2, 7, 8, C), f32),) * 2,
-        in_specs=[SMEM] + [VMEM] * 4,
+        in_specs=[VMEM] * 4,
         out_specs=(VMEM,) * 2,
         compiler_params=params(),
         cost_estimate=pl.CostEstimate(flops=10**9, bytes_accessed=10**6, transcendentals=0),
@@ -337,18 +357,15 @@
     )(*args)
 
 
-def adjoints(*args):
+def adjoint(kernel, name, shape, *args):
     return pl.pallas_call(
-        adjoint_kernel,
-        out_shape=(
-            jax.ShapeDtypeStruct((FR, R, W, C), f32),
-            jax.ShapeDtypeStruct((FR, R2, W2, CF), f32),
-        ),
-        in_specs=[VMEM] * 6,
-        out_specs=(VMEM,) * 2,
+        kernel,
+        out_shape=jax.ShapeDtypeStruct(shape, f32),
+        in_specs=[VMEM] * len(args),
+        out_specs=VMEM,
         compiler_params=params(),
-        cost_estimate=pl.CostEstimate(flops=4 * 10**9, bytes_accessed=10**7, transcendentals=0),
-        name="adjoints",
+        cost_estimate=pl.CostEstimate(flops=2 * 10**9, bytes_accessed=5 * 10**6, transcendentals=0),
+        name=name,
     )(*args)
 
 
@@ -382,8 +399,6 @@
 
 
 def local(features, weight_one, flow_feats, weight_two, cotangent):
-    place = [lax.axis_index(a) for a in ("core", "y", "x", "zh")] + [lax.axis_index("zl") % 2]
-    place = jnp.stack(place).astype(jnp.int32)
     kernel_one = weight_one.reshape(27, C, C)
     kernel_two = weight_two.reshape(27, CF, C)
     edges = (jax.ShapeDtypeStruct((FR, 2 * W + W2, C), f32),) * 2
@@ -396,50 +411,54 @@
         + [pltpu.VMEM((FR, 1, W2, C), f32)] * 2
         + [pltpu.SemaphoreType.DMA((4,))],
         HBM,
-    )(place, features, cotangent)
-    edges, kernel_one = lax.optimization_barrier((edges, kernel_one))
-    rows = [lax.ppermute(edges[k], HA, pairs(k)) for k in range(2)]
-    taps = jax.ShapeDtypeStruct((9, 2 * C, 2 * C), bf16)
-    feats = jax.ShapeDtypeStruct((2 * C, R * W), bf16)
-    prepared = small(prepare_kernel, "prepare", (taps, taps, feats, feats), 2)(place, kernel_one, features)
-    rows, prepared = lax.optimization_barrier((rows, prepared))
-    shape = (FR, 2 * COL + 16, C)
+    )(features, cotangent)
+    rows = [lax.ppermute(edges[k], HA, pairs(k)) for k in (1, 0)][::-1]
+    feats = (jax.ShapeDtypeStruct((2 * C, R * W), bf16),) * 2
+    near = (jax.ShapeDtypeStruct((FR, R2, W2, C), f32),)
+    *feats, near = small(prepare_features_kernel, "prepare_features", feats + near, 2)(features, cotangent)
+    rows, feats, near = lax.optimization_barrier((rows, feats, near))
+    shape = (FR, 56, C)
     edges = small(
         col_edges_kernel,
         "col_edges",
         (jax.ShapeDtypeStruct(shape, f32),) * 2,
         4,
         [pltpu.VMEM((2,) + shape, f32)],
-    )(place, features, cotangent, *rows)
+    )(features, near, *rows)
     edges, flow_feats = lax.optimization_barrier((edges, flow_feats))
-    cols = [lax.ppermute(edges[k], WA, pairs(k)) for k in range(2)]
+    cols = [lax.ppermute(edges[k], WA, pairs(k)) for k in (1, 0)][::-1]
+    taps = (jax.ShapeDtypeStruct((9, 2 * C, 2 * C), bf16),) * 2
     flows = (jax.ShapeDtypeStruct((2 * CF, R2 * W2), bf16),) * 2
-    flows = small(prepare_flow_kernel, "prepare_flow", flows, 1)(place, flow_feats)
-    cols, flows = lax.optimization_barrier((cols, flows))
+    prepared = small(prepare_kernel, "prepare", taps + flows, 2)(kernel_one, flow_feats)
+    cols, prepared = lax.optimization_barrier((cols, prepared))
     swap = [(0, 1), (1, 0)]
-    taps, feats = prepared[:2], prepared[2:]
-    keep, send, cot = flow_terms(place, *flows, cotangent, *rows, *cols)
+    taps, flows = prepared[:2], prepared[2:]
+    keep, send, cot = flow_terms(*flows, near, *rows, *cols)
     terms_two = keep + lax.ppermute(send, "core", swap)
-    grad_high, grad_low = block_gradient(place, features, *rows, *cols, *taps, cot)
+    grad_high, grad_low = block_gradient(features, *rows, *cols, *taps, cot)
     terms_two, grad_high, grad_low = lax.optimization_barrier((terms_two, grad_high, grad_low))
     arrived_two = spread(terms_two, ("x", "y"))
-    keep, send = block_terms(place, *feats, grad_high, grad_low)
+    keep, send = block_terms(*feats, grad_high, grad_low)
     terms_one = keep + lax.ppermute(send, "core", swap)
     arrived_one = spread(terms_one, ("x", "y"))
-    terms_one, grad_high, grad_low = lax.optimization_barrier((terms_one, grad_high, grad_low))
-    grad_features, grad_flow = adjoints(grad_high, grad_low, *taps, cot, kernel_two)
-    arrived_one, arrived_two, grad_features, grad_flow = lax.optimization_barrier(
-        (arrived_one, arrived_two, grad_features, grad_flow)
+    terms_one, cot, kernel_two = lax.optimization_barrier((terms_one, cot, kernel_two))
+    grad_flow = adjoint(flow_adjoint_kernel, "flow_adjoint", (FR, R2, W2, CF), cot, kernel_two)
+    arrived_one, arrived_two, grad_flow = lax.optimization_barrier((arrived_one, arrived_two, grad_flow))
+    parts = (jax.ShapeDtypeStruct((2, 7, 24, C), f32),) * 4
+    parts = small(first_sum_kernel, "first_sum", parts, 8)(terms_one, *arrived_one, terms_two, *arrived_two)
+    chunk = (jax.ShapeDtypeStruct((7, 24, C), f32),) * 2
+    keep, send = small(second_sum_kernel, "second_sum", chunk, 4)(parts[0], *spread(parts, ("y", "x")))
+    arrived = lax.ppermute(send, "zh", swap)
+    keep, grad_high, grad_low = lax.optimization_barrier((keep, grad_high, grad_low))
+    grad_features = adjoint(
+        feature_adjoint_kernel, "feature_adjoint", (FR, R, W, C), grad_high, grad_low, *taps
     )
-    terms_one = summed(terms_one[0], arrived_one)
-    terms_two = summed(terms_two[0], arrived_two)
-    terms = jnp.concatenate([terms_one, terms_two], axis=-2)
-    chunk = summed(terms[0], spread(terms, ("y", "x")))
-    chunk = chunk[0] + lax.ppermute(chunk[1], "zh", swap)
+    arrived, grad_features = lax.optimization_barrier((arrived, grad_features))
+    chunk = keep + arrived
     chunk = summed(chunk, spread([chunk] * 4, "zl"))
     pieces = [chunk] + [lax.ppermute(chunk, "x", ring(k)) for k in (1, 2, 3)]
     shares = tuple(jax.ShapeDtypeStruct((27, depth, C), f32) for depth in (8, 16))
-    grad_one, grad_two = small(gather_kernel, "gather", shares, 4)(place, *pieces)
+    grad_one, grad_two = small(gather_kernel, "gather", shares, 4)(*pieces)
     grad_one = grad_one.reshape(3, 3, 3, 8, C)
     grad_two = grad_two.reshape(3, 3, 3, 16, C)
     return (grad_features, grad_one, grad_flow, grad_two)

time: 97.2 us -> 94.1 us (0.968)
  Pallas kernels: 22.2 us -> 15.4 us
  waiting for transfers between devices: 26.9 us -> 29.8 us
  starting transfers between devices: 41.9 us -> 40.6 us
  other arithmetic: 0.62 us -> 1.89 us
    ppermute x9, waiting for transfers between devices: 10.5 us -> 14.9 us  [spread(): lax.ppermute(parts[k], ('x', 'y', 'core'), crossed(k, axes))]
    pallas_call x4 -> x7, Pallas kernels: 9.96 us -> 6.73 us  [the longest x2 5.12 us: adjoint(): pl.pallas_call(kernel, out_shape=jax.ShapeDtypeStruct(shape, f32), in_spe...]
    ppermute x1, starting transfers between devices: 4.76 us -> 3.02 us  [local(): terms_two = keep + lax.ppermute(send, 'core', swap)]
    add x1, other arithmetic: 0.24 us -> 1.76 us  [local(): terms_two = keep + lax.ppermute(send, 'core', swap)]
    pallas_call x1, Pallas kernels: 2.72 us -> 1.46 us  [flow_terms(): pl.pallas_call(flow_terms_kernel, out_shape=(jax.ShapeDtypeStruct((4, 4,...]
    ppermute x5, waiting for transfers between devices: 3.99 us -> 2.74 us  [the longest x2 2.18 us: local(): rows = [lax.ppermute(edges[k], HA, pairs(k)) for k in (1, 0)][::-1]]
    unnamed x14 -> x12, local copies, waits for them, and re-layouts: 3.16 us -> 4.37 us
  transfers between devices with their start and end apart: 22 -> 22, of which waited for: 11 -> 14; matrix products, arithmetic and copies ran while one was open for 0% -> 0% of each run, Pallas kernels for 13% -> 10%
where the time goes in v5:
time: 94.1 us; the launch traced here: 93 us
  starting transfers between devices  40.6 us (43%)
  waiting for transfers between devices  29.8 us (32%)
  Pallas kernels  15.4 us (16%)
  local copies, waits for them, and re-layouts  4.53 us (5%)
  other arithmetic  1.89 us (2%)
    ppermute x9, starting transfers between devices, spread(): lax.ppermute(parts[k], ('x', 'y', 'core'), crossed(k, axes))  17.3 us
    ppermute x9, waiting for transfers between devices, spread(): lax.ppermute(parts[k], ('x', 'y', 'core'), crossed(k, axes))  14.9 us
    ppermute x2, starting transfers between devices, local(): rows = [lax.ppermute(edges[k], HA, pairs(k)) for k in (1, 0)][::-1]  6.98 us
    ppermute x3, waiting for transfers between devices, spread(): return [lax.ppermute(parts[k], 'zl', ring(k)) for k in (2, 1, 3)]  6.65 us
    ppermute x3, waiting for transfers between devices, local(): pieces = [chunk] + [lax.ppermute(chunk, 'x', ring(k)) for k in (1, 2, 3)]  5.38 us
    ppermute x1, starting transfers between devices, local(): arrived = lax.ppermute(send, 'zh', swap)  5.2 us
    pallas_call x2, Pallas kernels, adjoint(): pl.pallas_call(kernel, out_shape=jax.ShapeDtypeStruct(shape, f32), in_spe...  5.12 us
    ppermute x3, starting transfers between devices, spread(): return [lax.ppermute(parts[k], 'zl', ring(k)) for k in (2, 1, 3)]  4.73 us
  transfers between devices with their start and end apart: 22, of which 14 were waited for; matrix products, arithmetic and copies ran while one was open for 0% of the time, Pallas kernels for 10%

profile of v5, /device:TPU:6, one launch (start us, length us, event | category | flops | bytes accessed | tf_op | source)
XLA Modules:
  0.0 93.0 jit_solution(9476920960169563021)
XLA Ops:
  2.2 2.0 %collective-permute-start = (f32[2,80,128]{2,1,0:T(8,128)}, f32[2,80,128]{2,1,0:T(8,128)S(1)}, u32[]{:S(2)}, u32[]{:S(2)}) collective-permute-start(f32[2,80,128]{2,1,0:T(8,128)} %get-tuple-element.62), channel_id=1, source_target_pairs={{0,16},{16,0},{32,48},{48,32},{64,80},{80,64},{96,112},{112,96},{1... | collective-permute-start | bytes 245768 | tf_op jit(solution)/shard_map/ppermute | solution.py:415
  4.2 5.0 %collective-permute-start.1 = (f32[2,80,128]{2,1,0:T(8,128)}, f32[2,80,128]{2,1,0:T(8,128)S(1)}, u32[]{:S(2)}, u32[]{:S(2)}) collective-permute-start(f32[2,80,128]{2,1,0:T(8,128)} %get-tuple-element.63), channel_id=1, source_target_pairs={{16,32},{32,16},{48,64},{64,48},{80,96},{96,80},{112,128},{128,112... | collective-permute-start | bytes 245768 | tf_op jit(solution)/shard_map/ppermute | solution.py:415
  11.4 2.2 %collective-permute-done.1.row_second_ref = f32[2,80,128]{2,1,0:T(8,128)S(1)} collective-permute-done((f32[2,80,128]{2,1,0:T(8,128)}, f32[2,80,128]{2,1,0:T(8,128)S(1)}, u32[]{:S(2)}, u32[]{:S(2)}) %collective-permute-start.1) | collective-permute-done | bytes 81952 | tf_op jit(solution)/shard_map/ppermute | solution.py:415
  18.8 3.0 %collective-permute-start.4 = (f32[4,4,2,7,16,128]{5,4,3,2,1,0:T(8,128)S(1)}, f32[4,4,2,7,16,128]{5,4,3,2,1,0:T(8,128)}, u32[]{:S(2)}, u32[]{:S(2)}) collective-permute-start(f32[4,4,2,7,16,128]{5,4,3,2,1,0:T(8,128)S(1)} %get-tuple-element.86), channel_id=1, source_target_pairs={{0,1},{1,0},{2,3},{3,2},{4,5},{5,4},{6,7},{7,6},{8,9},{9,8},{10,11... | collective-permute-start | bytes 5505032 | tf_op jit(solution)/shard_map/ppermute | solution.py:437
  21.8 3.5 %block_gradient.1 = (bf16[3,18,32,256]{3,2,1,0:T(8,128)(2,1)S(1)}, bf16[3,18,32,256]{3,2,1,0:T(8,128)(2,1)S(1)}) custom-call(f32[2,16,32,128]{3,2,1,0:T(8,128)S(1)} %copy-done.1, f32[2,80,128]{2,1,0:T(8,128)S(1)} %collective-permute-done.row_first_ref, f32[2,80,128]{2,1,0:T(8,128)S(1)} %collective-permute-done.1.row_second_ref, ...), custom_call_target="tpu_custom_call" | custom-call | flops 5000000000 | bytes 6000000 | tf_op jit(solution)/shard_map/block_gradient/pallas_call | solution.py:328
  25.4 1.8 %add.18.refs_4_ = f32[4,4,2,7,16,128]{5,4,3,2,1,0:T(8,128)S(1)} add(f32[4,4,2,7,16,128]{5,4,3,2,1,0:T(8,128)S(1)} %get-tuple-element.85, f32[4,4,2,7,16,128]{5,4,3,2,1,0:T(8,128)} %collective-permute-done.4) | non-fusion elementwise | flops 458752 | bytes 5505024 | tf_op jit(solution)/shard_map/add | solution.py:437
  27.2 2.1 %block_terms.1 = (f32[4,4,2,7,8,128]{5,4,3,2,1,0:T(8,128)S(1)}, f32[4,4,2,7,8,128]{5,4,3,2,1,0:T(8,128)S(1)}) custom-call(bf16[256,512]{1,0:T(8,128)(2,1)S(1)} %get-tuple-element.67.feat_high, bf16[256,512]{1,0:T(8,128)(2,1)S(1)} %get-tuple-element.68.feat_low, bf16[3,18,32,256]{3,2,1,0:T(8,128)(2,1)S(1)} %get-tuple-element.112.grad_high_ref, ...), custom_call_target="tpu_custom_call" | custom-call | flops 1000000000 | bytes 1000000 | tf_op jit(solution)/shard_map/block_terms/pallas_call | solution.py:349
  31.3 2.1 %collective-permute-start.10 = (f32[4,2,7,16,128]{4,3,2,1,0:T(8,128)S(1)}, f32[4,2,7,16,128]{4,3,2,1,0:T(8,128)S(1)}, u32[]{:S(2)}, u32[]{:S(2)}) collective-permute-start(f32[4,2,7,16,128]{4,3,2,1,0:T(8,128)S(1)} %get-tuple-element.121), channel_id=1, source_target_pairs={{0,64},{1,3},{2,66},{3,5},{4,68},{5,7},{6,70},{7,1},{64,128},{65,6... | collective-permute-start | bytes 1376264 | tf_op jit(solution)/shard_map/ppermute | solution.py:394
  33.5 2.4 %collective-permute-start.6 = (f32[4,2,7,8,128]{4,3,2,1,0:T(8,128)S(1)}, f32[4,2,7,8,128]{4,3,2,1,0:T(8,128)S(1)}, u32[]{:S(2)}, u32[]{:S(2)}) collective-permute-start(f32[4,2,7,8,128]{4,3,2,1,0:T(8,128)S(1)} %get-tuple-element.125), channel_id=1, source_target_pairs={{0,128},{1,5},{2,130},{3,7},{4,132},{5,1},{6,134},{7,3},{64,192},{... | collective-permute-start | bytes 688136 | tf_op jit(solution)/shard_map/ppermute | solution.py:394
  37.1 2.9 %collective-permute-done.9.refs_5_ = f32[4,2,7,16,128]{4,3,2,1,0:T(8,128)S(1)} collective-permute-done((f32[4,2,7,16,128]{4,3,2,1,0:T(8,128)S(1)}, f32[4,2,7,16,128]{4,3,2,1,0:T(8,128)S(1)}, u32[]{:S(2)}, u32[]{:S(2)}) %collective-permute-start.9) | collective-permute-done | bytes 458784 | tf_op jit(solution)/shard_map/ppermute | solution.py:394
  40.8 2.3 %flow_adjoint.1 = f32[2,8,16,256]{3,2,1,0:T(8,128)} custom-call(f32[2,10,18,128]{3,2,1,0:T(8,128)S(1)} %get-tuple-element.98.cot_ref, f32[27,256,128]{2,1,0:T(8,128)S(1)} %bitcast.17), custom_call_target="tpu_custom_call" | custom-call | flops 2000000000 | bytes 5000000 | tf_op jit(solution)/shard_map/flow_adjoint/pallas_call | solution.py:361
  44.8 2.6 %collective-permute-done.6.refs_1_ = f32[4,2,7,8,128]{4,3,2,1,0:T(8,128)S(1)} collective-permute-done((f32[4,2,7,8,128]{4,3,2,1,0:T(8,128)S(1)}, f32[4,2,7,8,128]{4,3,2,1,0:T(8,128)S(1)}, u32[]{:S(2)}, u32[]{:S(2)}) %collective-permute-start.6) | collective-permute-done | bytes 229408 | tf_op jit(solution)/shard_map/ppermute | solution.py:394
  47.4 2.3 %collective-permute-done.8.refs_3_ = f32[4,2,7,8,128]{4,3,2,1,0:T(8,128)S(1)} collective-permute-done((f32[4,2,7,8,128]{4,3,2,1,0:T(8,128)S(1)}, f32[4,2,7,8,128]{4,3,2,1,0:T(8,128)S(1)}, u32[]{:S(2)}, u32[]{:S(2)}) %collective-permute-start.8) | collective-permute-done | bytes 229408 | tf_op jit(solution)/shard_map/ppermute | solution.py:394
  49.8 3.0 %collective-permute-start.12 = (f32[2,7,24,128]{3,2,1,0:T(8,128)S(1)}, f32[2,7,24,128]{3,2,1,0:T(8,128)S(1)}, u32[]{:S(2)}, u32[]{:S(2)}) collective-permute-start(f32[2,7,24,128]{3,2,1,0:T(8,128)S(1)} %get-tuple-element.107), channel_id=1, source_target_pairs={{0,4},{1,129},{2,6},{3,131},{4,0},{5,133},{6,2},{7,135},{64,68},{6... | collective-permute-start | bytes 516104 | tf_op jit(solution)/shard_map/ppermute | solution.py:394
  52.8 6.4 %collective-permute-start.13 = (f32[2,7,24,128]{3,2,1,0:T(8,128)S(1)}, f32[2,7,24,128]{3,2,1,0:T(8,128)S(1)}, u32[]{:S(2)}, u32[]{:S(2)}) collective-permute-start(f32[2,7,24,128]{3,2,1,0:T(8,128)S(1)} %get-tuple-element.108), channel_id=1, source_target_pairs={{0,2},{1,65},{2,4},{3,67},{4,6},{5,69},{6,0},{7,71},{64,66},{65,12... | collective-permute-start | bytes 516104 | tf_op jit(solution)/shard_map/ppermute | solution.py:394
  59.3 2.9 %collective-permute-done.13.first = f32[2,7,24,128]{3,2,1,0:T(8,128)S(1)} collective-permute-done((f32[2,7,24,128]{3,2,1,0:T(8,128)S(1)}, f32[2,7,24,128]{3,2,1,0:T(8,128)S(1)}, u32[]{:S(2)}, u32[]{:S(2)}) %collective-permute-start.13) | collective-permute-done | bytes 172064 | tf_op jit(solution)/shard_map/ppermute | solution.py:394
  62.2 2.5 %collective-permute-done.14.third = f32[2,7,24,128]{3,2,1,0:T(8,128)S(1)} collective-permute-done((f32[2,7,24,128]{3,2,1,0:T(8,128)S(1)}, f32[2,7,24,128]{3,2,1,0:T(8,128)S(1)}, u32[]{:S(2)}, u32[]{:S(2)}) %collective-permute-start.14) | collective-permute-done | bytes 172064 | tf_op jit(solution)/shard_map/ppermute | solution.py:394
  64.7 5.2 %collective-permute-start.15 = (f32[7,24,128]{2,1,0:T(8,128)S(1)}, f32[7,24,128]{2,1,0:T(8,128)S(1)}, u32[]{:S(2)}, u32[]{:S(2)}) collective-permute-start(f32[7,24,128]{2,1,0:T(8,128)S(1)} %get-tuple-element.110), channel_id=1, source_target_pairs={{0,8},{8,0},{1,9},{9,1},{2,10},{10,2},{3,11},{11,3},{4,12},{12,4},... | collective-permute-start | bytes 258056 | tf_op jit(solution)/shard_map/ppermute | solution.py:451
  69.9 2.8 %feature_adjoint.1 = f32[2,16,32,128]{3,2,1,0:T(8,128)} custom-call(bf16[3,18,32,256]{3,2,1,0:T(8,128)(2,1)S(1)} %get-tuple-element.112.grad_high_ref, bf16[3,18,32,256]{3,2,1,0:T(8,128)(2,1)S(1)} %get-tuple-element.113.grad_low_ref, bf16[9,256,256]{2,1,0:T(8,128)(2,1)S(1)} %get-tuple-element.87.taps_high, bf16[9,256,256]{2,1,0:T(8,128)(2,1)S(1)} %get-tuple-element.88.taps_low), custom_call_target="tpu_custom_call" | custom-call | flops 2000000000 | bytes 5000000 | tf_op jit(solution)/shard_map/feature_adjoint/pallas_call | solution.py:361
  74.7 2.5 %collective-permute-start.18 = (f32[7,24,128]{2,1,0:T(8,128)S(1)}, f32[7,24,128]{2,1,0:T(8,128)S(1)}, u32[]{:S(2)}, u32[]{:S(2)}) collective-permute-start(f32[7,24,128]{2,1,0:T(8,128)S(1)} %add.20), channel_id=1, source_target_pairs={{0,48},{16,0},{32,16},{48,32},{1,49},{17,1},{33,17},{49,33},{2,50}... | collective-permute-start | bytes 258056 | tf_op jit(solution)/shard_map/ppermute | solution.py:393
  78.0 2.5 %collective-permute-done.17 = f32[7,24,128]{2,1,0:T(8,128)S(1)} collective-permute-done((f32[7,24,128]{2,1,0:T(8,128)S(1)}, f32[7,24,128]{2,1,0:T(8,128)S(1)}, u32[]{:S(2)}, u32[]{:S(2)}) %collective-permute-start.17) | collective-permute-done | bytes 86048 | tf_op jit(solution)/shard_map/ppermute | solution.py:393
  80.6 4.1 %collective-permute-done.16 = f32[7,24,128]{2,1,0:T(8,128)S(1)} collective-permute-done((f32[7,24,128]{2,1,0:T(8,128)S(1)}, f32[7,24,128]{2,1,0:T(8,128)S(1)}, u32[]{:S(2)}, u32[]{:S(2)}) %collective-permute-start.16) | collective-permute-done | bytes 86048 | tf_op jit(solution)/shard_map/ppermute | solution.py:393
  86.8 2.6 %collective-permute-done.19.one_ref = f32[7,24,128]{2,1,0:T(8,128)S(1)} collective-permute-done((f32[7,24,128]{2,1,0:T(8,128)S(1)}, f32[7,24,128]{2,1,0:T(8,128)S(1)}, u32[]{:S(2)}, u32[]{:S(2)}) %collective-permute-start.19) | collective-permute-done | bytes 86048 | tf_op jit(solution)/shard_map/ppermute | solution.py:459
  89.4 2.1 %collective-permute-done.20.two_ref = f32[7,24,128]{2,1,0:T(8,128)S(1)} collective-permute-done((f32[7,24,128]{2,1,0:T(8,128)S(1)}, f32[7,24,128]{2,1,0:T(8,128)S(1)}, u32[]{:S(2)}, u32[]{:S(2)}) %collective-permute-start.20) | collective-permute-done | bytes 86048 | tf_op jit(solution)/shard_map/ppermute | solution.py:459
  (50 shorter events, 21.4 us)
Async XLA Ops:
  2.2 9.2 %collective-permute-start = (f32[2,80,128]{2,1,0:T(8,128)}, f32[2,80,128]{2,1,0:T(8,128)S(1)}, u32[]{:S(2)}, u32[]{:S(2)}) collective-permute-start(f32[2,80,128]{2,1,0:T(8,128)} %get-tuple-element.62), channel_id=1, source_target_pairs={{0,16},{16,0},{32,48},{48,32},{64,80},{80,64},{96,112},{112,96},{1... | collective-permute-start | bytes 245768 | tf_op jit(solution)/shard_map/ppermute | solution.py:415
  4.2 9.3 %collective-permute-start.1 = (f32[2,80,128]{2,1,0:T(8,128)}, f32[2,80,128]{2,1,0:T(8,128)S(1)}, u32[]{:S(2)}, u32[]{:S(2)}) collective-permute-start(f32[2,80,128]{2,1,0:T(8,128)} %get-tuple-element.63), channel_id=1, source_target_pairs={{16,32},{32,16},{48,64},{64,48},{80,96},{96,80},{112,128},{128,112... | collective-permute-start | bytes 245768 | tf_op jit(solution)/shard_map/ppermute | solution.py:415
  13.6 3.7 %collective-permute-start.2 = (f32[2,56,128]{2,1,0:T(8,128)S(1)}, f32[2,56,128]{2,1,0:T(8,128)S(1)}, u32[]{:S(2)}, u32[]{:S(2)}) collective-permute-start(f32[2,56,128]{2,1,0:T(8,128)S(1)} %get-tuple-element.74), channel_id=1, source_target_pairs={{0,1},{1,0},{2,3},{3,2},{4,5},{5,4},{6,7},{7,6},{8,9},{9,8},{10,11... | collective-permute-start | bytes 172040 | tf_op jit(solution)/shard_map/ppermute | solution.py:429
  13.7 3.6 %collective-permute-start.3 = (f32[2,56,128]{2,1,0:T(8,128)S(1)}, f32[2,56,128]{2,1,0:T(8,128)S(1)}, u32[]{:S(2)}, u32[]{:S(2)}) collective-permute-start(f32[2,56,128]{2,1,0:T(8,128)S(1)} %get-tuple-element.75), channel_id=1, source_target_pairs={{1,2},{2,1},{3,4},{4,3},{5,6},{6,5},{7,8},{8,7},{9,10},{10,9},{11,... | collective-permute-start | bytes 172040 | tf_op jit(solution)/shard_map/ppermute | solution.py:429
  17.3 4.5 %copy-start.1 = (f32[2,16,32,128]{3,2,1,0:T(8,128)S(1)}, f32[2,16,32,128]{3,2,1,0:T(8,128)}, u32[]{:S(2)}) copy-start(f32[2,16,32,128]{3,2,1,0:T(8,128)} %feat_ref.7) | copy-start | bytes 1572868
  18.8 6.6 %collective-permute-start.4 = (f32[4,4,2,7,16,128]{5,4,3,2,1,0:T(8,128)S(1)}, f32[4,4,2,7,16,128]{5,4,3,2,1,0:T(8,128)}, u32[]{:S(2)}, u32[]{:S(2)}) collective-permute-start(f32[4,4,2,7,16,128]{5,4,3,2,1,0:T(8,128)S(1)} %get-tuple-element.86), channel_id=1, source_target_pairs={{0,1},{1,0},{2,3},{3,2},{4,5},{5,4},{6,7},{7,6},{8,9},{9,8},{10,11... | collective-permute-start | bytes 5505032 | tf_op jit(solution)/shard_map/ppermute | solution.py:437
  29.2 4.1 %collective-permute-start.5 = (f32[4,4,2,7,8,128]{5,4,3,2,1,0:T(8,128)S(1)}, f32[4,4,2,7,8,128]{5,4,3,2,1,0:T(8,128)S(1)}, u32[]{:S(2)}, u32[]{:S(2)}) collective-permute-start(f32[4,4,2,7,8,128]{5,4,3,2,1,0:T(8,128)S(1)} %get-tuple-element.95), channel_id=1, source_target_pairs={{0,1},{1,0},{2,3},{3,2},{4,5},{5,4},{6,7},{7,6},{8,9},{9,8},{10,11... | collective-permute-start | bytes 2752520 | tf_op jit(solution)/shard_map/ppermute | solution.py:442
  29.8 10.2 %collective-permute-start.9 = (f32[4,2,7,16,128]{4,3,2,1,0:T(8,128)S(1)}, f32[4,2,7,16,128]{4,3,2,1,0:T(8,128)S(1)}, u32[]{:S(2)}, u32[]{:S(2)}) collective-permute-start(f32[4,2,7,16,128]{4,3,2,1,0:T(8,128)S(1)} %get-tuple-element.122), channel_id=1, source_target_pairs={{0,128},{1,5},{2,130},{3,7},{4,132},{5,1},{6,134},{7,3},{64,192},{... | collective-permute-start | bytes 1376264 | tf_op jit(solution)/shard_map/ppermute | solution.py:394
  31.3 11.8 %collective-permute-start.10 = (f32[4,2,7,16,128]{4,3,2,1,0:T(8,128)S(1)}, f32[4,2,7,16,128]{4,3,2,1,0:T(8,128)S(1)}, u32[]{:S(2)}, u32[]{:S(2)}) collective-permute-start(f32[4,2,7,16,128]{4,3,2,1,0:T(8,128)S(1)} %get-tuple-element.121), channel_id=1, source_target_pairs={{0,64},{1,3},{2,66},{3,5},{4,68},{5,7},{6,70},{7,1},{64,128},{65,6... | collective-permute-start | bytes 1376264 | tf_op jit(solution)/shard_map/ppermute | solution.py:394
  33.3 11.4 %collective-permute-start.11 = (f32[4,2,7,16,128]{4,3,2,1,0:T(8,128)S(1)}, f32[4,2,7,16,128]{4,3,2,1,0:T(8,128)S(1)}, u32[]{:S(2)}, u32[]{:S(2)}) collective-permute-start(f32[4,2,7,16,128]{4,3,2,1,0:T(8,128)S(1)} %get-tuple-element.120), channel_id=1, source_target_pairs={{0,192},{1,7},{2,194},{3,1},{4,196},{5,3},{6,198},{7,5},{64,0},{65... | collective-permute-start | bytes 1376264 | tf_op jit(solution)/shard_map/ppermute | solution.py:394
  33.4 7.4 %copy-start.5 = (f32[3,3,3,256,128]{4,3,2,1,0:T(8,128)S(1)}, f32[3,3,3,256,128]{4,3,2,1,0:T(8,128)}, u32[]{:S(2)}) copy-start(f32[3,3,3,256,128]{4,3,2,1,0:T(8,128)} %param.8) | copy-start | bytes 10616836
  33.5 13.9 %collective-permute-start.6 = (f32[4,2,7,8,128]{4,3,2,1,0:T(8,128)S(1)}, f32[4,2,7,8,128]{4,3,2,1,0:T(8,128)S(1)}, u32[]{:S(2)}, u32[]{:S(2)}) collective-permute-start(f32[4,2,7,8,128]{4,3,2,1,0:T(8,128)S(1)} %get-tuple-element.125), channel_id=1, source_target_pairs={{0,128},{1,5},{2,130},{3,7},{4,132},{5,1},{6,134},{7,3},{64,192},{... | collective-permute-start | bytes 688136 | tf_op jit(solution)/shard_map/ppermute | solution.py:394
  35.9 11.5 %collective-permute-start.7 = (f32[4,2,7,8,128]{4,3,2,1,0:T(8,128)S(1)}, f32[4,2,7,8,128]{4,3,2,1,0:T(8,128)S(1)}, u32[]{:S(2)}, u32[]{:S(2)}) collective-permute-start(f32[4,2,7,8,128]{4,3,2,1,0:T(8,128)S(1)} %get-tuple-element.124), channel_id=1, source_target_pairs={{0,64},{1,3},{2,66},{3,5},{4,68},{5,7},{6,70},{7,1},{64,128},{65,6... | collective-permute-start | bytes 688136 | tf_op jit(solution)/shard_map/ppermute | solution.py:394
  40.0 9.7 %collective-permute-start.8 = (f32[4,2,7,8,128]{4,3,2,1,0:T(8,128)S(1)}, f32[4,2,7,8,128]{4,3,2,1,0:T(8,128)S(1)}, u32[]{:S(2)}, u32[]{:S(2)}) collective-permute-start(f32[4,2,7,8,128]{4,3,2,1,0:T(8,128)S(1)} %get-tuple-element.123), channel_id=1, source_target_pairs={{0,192},{1,7},{2,194},{3,1},{4,196},{5,3},{6,198},{7,5},{64,0},{65... | collective-permute-start | bytes 688136 | tf_op jit(solution)/shard_map/ppermute | solution.py:394
  49.8 9.4 %collective-permute-start.12 = (f32[2,7,24,128]{3,2,1,0:T(8,128)S(1)}, f32[2,7,24,128]{3,2,1,0:T(8,128)S(1)}, u32[]{:S(2)}, u32[]{:S(2)}) collective-permute-start(f32[2,7,24,128]{3,2,1,0:T(8,128)S(1)} %get-tuple-element.107), channel_id=1, source_target_pairs={{0,4},{1,129},{2,6},{3,131},{4,0},{5,133},{6,2},{7,135},{64,68},{6... | collective-permute-start | bytes 516104 | tf_op jit(solution)/shard_map/ppermute | solution.py:394
  52.8 9.3 %collective-permute-start.13 = (f32[2,7,24,128]{3,2,1,0:T(8,128)S(1)}, f32[2,7,24,128]{3,2,1,0:T(8,128)S(1)}, u32[]{:S(2)}, u32[]{:S(2)}) collective-permute-start(f32[2,7,24,128]{3,2,1,0:T(8,128)S(1)} %get-tuple-element.108), channel_id=1, source_target_pairs={{0,2},{1,65},{2,4},{3,67},{4,6},{5,69},{6,0},{7,71},{64,66},{65,12... | collective-permute-start | bytes 516104 | tf_op jit(solution)/shard_map/ppermute | solution.py:394
  59.3 5.4 %collective-permute-start.14 = (f32[2,7,24,128]{3,2,1,0:T(8,128)S(1)}, f32[2,7,24,128]{3,2,1,0:T(8,128)S(1)}, u32[]{:S(2)}, u32[]{:S(2)}) collective-permute-start(f32[2,7,24,128]{3,2,1,0:T(8,128)S(1)} %get-tuple-element.109), channel_id=1, source_target_pairs={{0,6},{1,193},{2,0},{3,195},{4,2},{5,197},{6,4},{7,199},{64,70},{6... | collective-permute-start | bytes 516104 | tf_op jit(solution)/shard_map/ppermute | solution.py:394
  64.7 8.6 %collective-permute-start.15 = (f32[7,24,128]{2,1,0:T(8,128)S(1)}, f32[7,24,128]{2,1,0:T(8,128)S(1)}, u32[]{:S(2)}, u32[]{:S(2)}) collective-permute-start(f32[7,24,128]{2,1,0:T(8,128)S(1)} %get-tuple-element.110), channel_id=1, source_target_pairs={{0,8},{8,0},{1,9},{9,1},{2,10},{10,2},{3,11},{11,3},{4,12},{12,4},... | collective-permute-start | bytes 258056 | tf_op jit(solution)/shard_map/ppermute | solution.py:451
  73.3 7.3 %collective-permute-start.17 = (f32[7,24,128]{2,1,0:T(8,128)S(1)}, f32[7,24,128]{2,1,0:T(8,128)S(1)}, u32[]{:S(2)}, u32[]{:S(2)}) collective-permute-start(f32[7,24,128]{2,1,0:T(8,128)S(1)} %add.20), channel_id=1, source_target_pairs={{0,16},{16,32},{32,48},{48,0},{1,17},{17,33},{33,49},{49,1},{2,18}... | collective-permute-start | bytes 258056 | tf_op jit(solution)/shard_map/ppermute | solution.py:393
  74.7 5.8 %collective-permute-start.18 = (f32[7,24,128]{2,1,0:T(8,128)S(1)}, f32[7,24,128]{2,1,0:T(8,128)S(1)}, u32[]{:S(2)}, u32[]{:S(2)}) collective-permute-start(f32[7,24,128]{2,1,0:T(8,128)S(1)} %add.20), channel_id=1, source_target_pairs={{0,48},{16,0},{32,16},{48,32},{1,49},{17,1},{33,17},{49,33},{2,50}... | collective-permute-start | bytes 258056 | tf_op jit(solution)/shard_map/ppermute | solution.py:393
  77.2 7.5 %collective-permute-start.16 = (f32[7,24,128]{2,1,0:T(8,128)S(1)}, f32[7,24,128]{2,1,0:T(8,128)S(1)}, u32[]{:S(2)}, u32[]{:S(2)}) collective-permute-start(f32[7,24,128]{2,1,0:T(8,128)S(1)} %add.20), channel_id=1, source_target_pairs={{0,32},{16,48},{32,0},{48,16},{1,33},{17,49},{33,1},{49,17},{2,34}... | collective-permute-start | bytes 258056 | tf_op jit(solution)/shard_map/ppermute | solution.py:393
  84.7 4.7 %collective-permute-start.19 = (f32[7,24,128]{2,1,0:T(8,128)S(1)}, f32[7,24,128]{2,1,0:T(8,128)S(1)}, u32[]{:S(2)}, u32[]{:S(2)}) collective-permute-start(f32[7,24,128]{2,1,0:T(8,128)S(1)} %add_add_fusion.own_ref), channel_id=1, source_target_pairs={{0,64},{64,128},{128,192},{192,0},{1,65},{65,129},{129,193},{193,1... | collective-permute-start | bytes 258056 | tf_op jit(solution)/shard_map/ppermute | solution.py:459
  84.8 6.7 %collective-permute-start.20 = (f32[7,24,128]{2,1,0:T(8,128)S(1)}, f32[7,24,128]{2,1,0:T(8,128)S(1)}, u32[]{:S(2)}, u32[]{:S(2)}) collective-permute-start(f32[7,24,128]{2,1,0:T(8,128)S(1)} %add_add_fusion.own_ref), channel_id=1, source_target_pairs={{0,128},{64,192},{128,0},{192,64},{1,129},{65,193},{129,1},{193,65... | collective-permute-start | bytes 258056 | tf_op jit(solution)/shard_map/ppermute | solution.py:459
  85.5 6.6 %collective-permute-start.21 = (f32[7,24,128]{2,1,0:T(8,128)S(1)}, f32[7,24,128]{2,1,0:T(8,128)S(1)}, u32[]{:S(2)}, u32[]{:S(2)}) collective-permute-start(f32[7,24,128]{2,1,0:T(8,128)S(1)} %add_add_fusion.own_ref), channel_id=1, source_target_pairs={{0,192},{64,0},{128,64},{192,128},{1,193},{65,1},{129,65},{193,129... | collective-permute-start | bytes 258056 | tf_op jit(solution)/shard_map/ppermute | solution.py:459
  (4 other events, 4.4 us)

commit v6 on v5

--- a/solution.py
+++ b/solution.py
@@ -59,10 +59,10 @@
     core, y, x, zh = [lax.axis_index(a) for a in ("core", "y", "x", "zh")]
     for time_tap, part in taps:
         number = 9 * time_tap + tap
-        slot_x = lax.rem(number // 7 - x + 4, 4)
+        slot_x = x ^ (number // 7)
         for owner in range(8):
-            slot_y = lax.rem(owner % 4 - y + 4, 4)
-            slot_zh = lax.rem(owner // 4 - zh + 2, 2)
+            slot_y = y ^ (owner % 4)
+            slot_zh = zh ^ (owner // 4)
             slots = [jnp.where(core == 0, slot_x, slot_y), jnp.where(core == 0, slot_y, slot_x)]
             first = part[2 * owner * depth : (2 * owner + 1) * depth]
             second = part[(2 * owner + 1) * depth : (2 * owner + 2) * depth]
@@ -283,7 +283,7 @@
     scale_one = 1.0 / (FR * R * W * 256) ** 0.5
     scale_two = 1.0 / (FR * R2 * W2 * 256) ** 0.5
     for k, ref in enumerate((own_ref, one_ref, two_ref, three_ref)):
-        first = 7 * lax.rem(lax.axis_index("x") - k + 4, 4)
+        first = 7 * (lax.axis_index("x") ^ k)
 
         def put(j, ref=ref, first=first):
             grad_one_ref[first + j] = ref[j, :8] * scale_one
@@ -294,7 +294,7 @@
         pl.when(first < 21)(functools.partial(put, 6))
 
 
-def params(mebibytes=48):
+def params(mebibytes=24):
     return pltpu.CompilerParams(vmem_limit_bytes=mebibytes * 2**20)
 
 
@@ -305,7 +305,7 @@
         in_specs=[space] * count,
         out_specs=(VMEM,) * len(out_shape),
         scratch_shapes=scratch,
-        compiler_params=params(48 if space is VMEM else 64),
+        compiler_params=params(24 if space is VMEM else 64),
         cost_estimate=pl.CostEstimate(flops=10**6, bytes_accessed=10**6, transcendentals=0),
         name=name,
     )
@@ -369,17 +369,16 @@
     )(*args)
 
 
-def ring(steps, count=4):
-    return [(i, (i + steps) % count) for i in range(count)]
-
-
-def crossed(steps, axes):
+def swaps(mask, count=4):
+    return [(i, i ^ mask) for i in range(count)]
+
+
+def crossed(mask, axes):
     both = []
     for x in range(4):
         for y in range(4):
             for core in range(2):
-                along_x = axes[core] == "x"
-                x_to, y_to = ((x + steps) % 4, y) if along_x else (x, (y + steps) % 4)
+                x_to, y_to = (x ^ mask, y) if axes[core] == "x" else (x, y ^ mask)
                 both.append((8 * x + 2 * y + core, 8 * x_to + 2 * y_to + core))
     return both
 
@@ -390,12 +389,13 @@
 
 def spread(parts, axes):
     if axes == "zl":
-        return [lax.ppermute(parts[k], "zl", ring(k)) for k in (2, 1, 3)]
+        return [lax.ppermute(parts[k], "zl", swaps(k)) for k in (3, 2, 1)]
     return [lax.ppermute(parts[k], ("x", "y", "core"), crossed(k, axes)) for k in (2, 1, 3)]
 
 
 def summed(own, arrived):
-    return (own + arrived[0]) + (arrived[1] + arrived[2])
+    third, second, first = arrived
+    return (own + first) + (second + third)
 
 
 def local(features, weight_one, flow_feats, weight_two, cotangent):
@@ -448,7 +448,7 @@
     parts = small(first_sum_kernel, "first_sum", parts, 8)(terms_one, *arrived_one, terms_two, *arrived_two)
     chunk = (jax.ShapeDtypeStruct((7, 24, C), f32),) * 2
     keep, send = small(second_sum_kernel, "second_sum", chunk, 4)(parts[0], *spread(parts, ("y", "x")))
-    arrived = lax.ppermute(send, "zh", swap)
+    arrived = lax.ppermute(send, ("zl", "zh"), [(i, 7 - i) for i in range(8)])
     keep, grad_high, grad_low = lax.optimization_barrier((keep, grad_high, grad_low))
     grad_features = adjoint(
         feature_adjoint_kernel, "feature_adjoint", (FR, R, W, C), grad_high, grad_low, *taps
@@ -456,7 +456,7 @@
     arrived, grad_features = lax.optimization_barrier((arrived, grad_features))
     chunk = keep + arrived
     chunk = summed(chunk, spread([chunk] * 4, "zl"))
-    pieces = [chunk] + [lax.ppermute(chunk, "x", ring(k)) for k in (1, 2, 3)]
+    pieces = [chunk] + [lax.ppermute(chunk, "x", swaps(k)) for k in (1, 2, 3)]
     shares = tuple(jax.ShapeDtypeStruct((27, depth, C), f32) for depth in (8, 16))
     grad_one, grad_two = small(gather_kernel, "gather", shares, 4)(*pieces)
     grad_one = grad_one.reshape(3, 3, 3, 8, C)

time: 94.1 us -> 89.4 us (0.950)
  starting transfers between devices: 40.6 us -> 35.5 us
  waiting for transfers between devices: 29.8 us -> 32.4 us
  other arithmetic: 1.89 us -> 0.39 us
    ppermute x9, waiting for transfers between devices: 14.9 us -> 18.4 us  [spread(): lax.ppermute(parts[k], ('x', 'y', 'core'), crossed(k, axes))]
    ppermute x7, starting transfers between devices: 12 us -> 9.3 us  [the longest x3 4.79 us: local(): pieces = [chunk] + [lax.ppermute(chunk, 'x', swaps(k)) for k in (1, 2, 3)]]
    ppermute x9, starting transfers between devices: 17.3 us -> 15 us  [spread(): lax.ppermute(parts[k], ('x', 'y', 'core'), crossed(k, axes))]
    add x1, other arithmetic: 1.76 us -> 0.26 us  [local(): terms_two = keep + lax.ppermute(send, 'core', swap)]
  transfers between devices with their start and end apart: 22 -> 22, of which waited for: 14 -> 12; matrix products, arithmetic and copies ran while one was open for 0% -> 0% of each run, Pallas kernels for 10% -> 10%
where the time goes in v6:
time: 89.4 us; the launch traced here: 89 us
  starting transfers between devices  35.5 us (40%)
  waiting for transfers between devices  32.4 us (36%)
  Pallas kernels  15.4 us (17%)
  local copies, waits for them, and re-layouts  4.53 us (5%)
    ppermute x9, waiting for transfers between devices, spread(): lax.ppermute(parts[k], ('x', 'y', 'core'), crossed(k, axes))  18.4 us
    ppermute x9, starting transfers between devices, spread(): lax.ppermute(parts[k], ('x', 'y', 'core'), crossed(k, axes))  15 us
    ppermute x2, starting transfers between devices, local(): rows = [lax.ppermute(edges[k], HA, pairs(k)) for k in (1, 0)][::-1]  6.98 us
    ppermute x3, waiting for transfers between devices, spread(): return [lax.ppermute(parts[k], 'zl', swaps(k)) for k in (3, 2, 1)]  5.46 us
    pallas_call x2, Pallas kernels, adjoint(): pl.pallas_call(kernel, out_shape=jax.ShapeDtypeStruct(shape, f32), in_spe...  5.11 us
    ppermute x3, starting transfers between devices, local(): pieces = [chunk] + [lax.ppermute(chunk, 'x', swaps(k)) for k in (1, 2, 3)]  4.79 us
    unnamed x12, local copies, waits for them, and re-layouts  4.37 us
    ppermute x3, starting transfers between devices, spread(): return [lax.ppermute(parts[k], 'zl', swaps(k)) for k in (3, 2, 1)]  3.58 us
  transfers between devices with their start and end apart: 22, of which 12 were waited for; matrix products, arithmetic and copies ran while one was open for 0% of the time, Pallas kernels for 10%

profile of v6, /device:TPU:6, one launch (start us, length us, event | category | flops | bytes accessed | tf_op | source)
XLA Modules:
  0.0 89.0 jit_solution(17230940548636340644)
XLA Ops:
  0.6 1.6 %row_edges.1 = (f32[2,80,128]{2,1,0:T(8,128)}, f32[2,80,128]{2,1,0:T(8,128)}) custom-call(f32[2,16,32,128]{3,2,1,0:T(8,128)} %feat_ref.7, f32[2,8,16,128]{3,2,1,0:T(8,128)} %cot_ref.3), custom_call_target="tpu_custom_call" | custom-call | flops 1000000 | bytes 1000000 | tf_op jit(solution)/shard_map/row_edges/pallas_call | solution.py:405
  2.2 2.0 %collective-permute-start = (f32[2,80,128]{2,1,0:T(8,128)}, f32[2,80,128]{2,1,0:T(8,128)S(1)}, u32[]{:S(2)}, u32[]{:S(2)}) collective-permute-start(f32[2,80,128]{2,1,0:T(8,128)} %get-tuple-element.62), channel_id=1, source_target_pairs={{0,16},{16,0},{32,48},{48,32},{64,80},{80,64},{96,112},{112,96},{1... | collective-permute-start | bytes 245768 | tf_op jit(solution)/shard_map/ppermute | solution.py:415
  4.2 5.0 %collective-permute-start.1 = (f32[2,80,128]{2,1,0:T(8,128)}, f32[2,80,128]{2,1,0:T(8,128)S(1)}, u32[]{:S(2)}, u32[]{:S(2)}) collective-permute-start(f32[2,80,128]{2,1,0:T(8,128)} %get-tuple-element.63), channel_id=1, source_target_pairs={{16,32},{32,16},{48,64},{64,48},{80,96},{96,80},{112,128},{128,112... | collective-permute-start | bytes 245768 | tf_op jit(solution)/shard_map/ppermute | solution.py:415
  11.4 2.2 %collective-permute-done.1.row_second_ref = f32[2,80,128]{2,1,0:T(8,128)S(1)} collective-permute-done((f32[2,80,128]{2,1,0:T(8,128)}, f32[2,80,128]{2,1,0:T(8,128)S(1)}, u32[]{:S(2)}, u32[]{:S(2)}) %collective-permute-start.1) | collective-permute-done | bytes 81952 | tf_op jit(solution)/shard_map/ppermute | solution.py:415
  14.4 1.5 %copy-done.2 = f32[3,3,3,128,128]{4,3,2,1,0:T(8,128)S(1)} copy-done((f32[3,3,3,128,128]{4,3,2,1,0:T(8,128)S(1)}, f32[3,3,3,128,128]{4,3,2,1,0:T(8,128)}, u32[]{:S(2)}) %copy-start.2) | copy-done | bytes 1769496
  18.8 3.0 %collective-permute-start.4 = (f32[4,4,2,7,16,128]{5,4,3,2,1,0:T(8,128)S(1)}, f32[4,4,2,7,16,128]{5,4,3,2,1,0:T(8,128)S(1)}, u32[]{:S(2)}, u32[]{:S(2)}) collective-permute-start(f32[4,4,2,7,16,128]{5,4,3,2,1,0:T(8,128)S(1)} %get-tuple-element.86), channel_id=1, source_target_pairs={{0,1},{1,0},{2,3},{3,2},{4,5},{5,4},{6,7},{7,6},{8,9},{9,8},{10,11... | collective-permute-start | bytes 5505032 | tf_op jit(solution)/shard_map/ppermute | solution.py:437
  21.9 3.5 %block_gradient.1 = (bf16[3,18,32,256]{3,2,1,0:T(8,128)(2,1)S(1)}, bf16[3,18,32,256]{3,2,1,0:T(8,128)(2,1)S(1)}) custom-call(f32[2,16,32,128]{3,2,1,0:T(8,128)S(1)} %copy-done.1, f32[2,80,128]{2,1,0:T(8,128)S(1)} %collective-permute-done.row_first_ref, f32[2,80,128]{2,1,0:T(8,128)S(1)} %collective-permute-done.1.row_second_ref, ...), custom_call_target="tpu_custom_call" | custom-call | flops 5000000000 | bytes 6000000 | tf_op jit(solution)/shard_map/block_gradient/pallas_call | solution.py:328
  25.6 2.1 %block_terms.1 = (f32[4,4,2,7,8,128]{5,4,3,2,1,0:T(8,128)S(1)}, f32[4,4,2,7,8,128]{5,4,3,2,1,0:T(8,128)S(1)}) custom-call(bf16[256,512]{1,0:T(8,128)(2,1)S(1)} %get-tuple-element.67.feat_high, bf16[256,512]{1,0:T(8,128)(2,1)S(1)} %get-tuple-element.68.feat_low, bf16[3,18,32,256]{3,2,1,0:T(8,128)(2,1)S(1)} %get-tuple-element.112.grad_high_ref, ...), custom_call_target="tpu_custom_call" | custom-call | flops 1000000000 | bytes 1000000 | tf_op jit(solution)/shard_map/block_terms/pallas_call | solution.py:349
  29.6 2.7 %collective-permute-start.11 = (f32[4,2,7,16,128]{4,3,2,1,0:T(8,128)S(1)}, f32[4,2,7,16,128]{4,3,2,1,0:T(8,128)S(1)}, u32[]{:S(2)}, u32[]{:S(2)}) collective-permute-start(f32[4,2,7,16,128]{4,3,2,1,0:T(8,128)S(1)} %get-tuple-element.120), channel_id=1, source_target_pairs={{0,192},{1,7},{2,194},{3,5},{4,196},{5,3},{6,198},{7,1},{64,128},{... | collective-permute-start | bytes 1376264 | tf_op jit(solution)/shard_map/ppermute | solution.py:393
  34.0 4.4 %collective-permute-done.9.refs_5_ = f32[4,2,7,16,128]{4,3,2,1,0:T(8,128)S(1)} collective-permute-done((f32[4,2,7,16,128]{4,3,2,1,0:T(8,128)S(1)}, f32[4,2,7,16,128]{4,3,2,1,0:T(8,128)S(1)}, u32[]{:S(2)}, u32[]{:S(2)}) %collective-permute-start.9) | collective-permute-done | bytes 458784 | tf_op jit(solution)/shard_map/ppermute | solution.py:393
  38.4 2.3 %flow_adjoint.1 = f32[2,8,16,256]{3,2,1,0:T(8,128)} custom-call(f32[2,10,18,128]{3,2,1,0:T(8,128)S(1)} %get-tuple-element.98.cot_ref, f32[27,256,128]{2,1,0:T(8,128)S(1)} %bitcast.17), custom_call_target="tpu_custom_call" | custom-call | flops 2000000000 | bytes 5000000 | tf_op jit(solution)/shard_map/flow_adjoint/pallas_call | solution.py:361
  40.6 2.5 %collective-permute-done.11.refs_7_ = f32[4,2,7,16,128]{4,3,2,1,0:T(8,128)S(1)} collective-permute-done((f32[4,2,7,16,128]{4,3,2,1,0:T(8,128)S(1)}, f32[4,2,7,16,128]{4,3,2,1,0:T(8,128)S(1)}, u32[]{:S(2)}, u32[]{:S(2)}) %collective-permute-start.11) | collective-permute-done | bytes 458784 | tf_op jit(solution)/shard_map/ppermute | solution.py:393
  43.2 2.6 %collective-permute-done.6.refs_1_ = f32[4,2,7,8,128]{4,3,2,1,0:T(8,128)S(1)} collective-permute-done((f32[4,2,7,8,128]{4,3,2,1,0:T(8,128)S(1)}, f32[4,2,7,8,128]{4,3,2,1,0:T(8,128)S(1)}, u32[]{:S(2)}, u32[]{:S(2)}) %collective-permute-start.6) | collective-permute-done | bytes 229408 | tf_op jit(solution)/shard_map/ppermute | solution.py:393
  45.8 2.3 %collective-permute-done.8.refs_3_ = f32[4,2,7,8,128]{4,3,2,1,0:T(8,128)S(1)} collective-permute-done((f32[4,2,7,8,128]{4,3,2,1,0:T(8,128)S(1)}, f32[4,2,7,8,128]{4,3,2,1,0:T(8,128)S(1)}, u32[]{:S(2)}, u32[]{:S(2)}) %collective-permute-start.8) | collective-permute-done | bytes 229408 | tf_op jit(solution)/shard_map/ppermute | solution.py:393
  48.2 3.0 %collective-permute-start.12 = (f32[2,7,24,128]{3,2,1,0:T(8,128)S(1)}, f32[2,7,24,128]{3,2,1,0:T(8,128)S(1)}, u32[]{:S(2)}, u32[]{:S(2)}) collective-permute-start(f32[2,7,24,128]{3,2,1,0:T(8,128)S(1)} %get-tuple-element.107), channel_id=1, source_target_pairs={{0,4},{1,129},{2,6},{3,131},{4,0},{5,133},{6,2},{7,135},{64,68},{6... | collective-permute-start | bytes 516104 | tf_op jit(solution)/shard_map/ppermute | solution.py:393
  51.2 6.4 %collective-permute-start.13 = (f32[2,7,24,128]{3,2,1,0:T(8,128)S(1)}, f32[2,7,24,128]{3,2,1,0:T(8,128)S(1)}, u32[]{:S(2)}, u32[]{:S(2)}) collective-permute-start(f32[2,7,24,128]{3,2,1,0:T(8,128)S(1)} %get-tuple-element.108), channel_id=1, source_target_pairs={{0,2},{1,65},{2,0},{3,67},{4,6},{5,69},{6,4},{7,71},{64,66},{65,1}... | collective-permute-start | bytes 516104 | tf_op jit(solution)/shard_map/ppermute | solution.py:393
  57.6 5.2 %collective-permute-done.13.first = f32[2,7,24,128]{3,2,1,0:T(8,128)S(1)} collective-permute-done((f32[2,7,24,128]{3,2,1,0:T(8,128)S(1)}, f32[2,7,24,128]{3,2,1,0:T(8,128)S(1)}, u32[]{:S(2)}, u32[]{:S(2)}) %collective-permute-start.13) | collective-permute-done | bytes 172064 | tf_op jit(solution)/shard_map/ppermute | solution.py:393
  65.2 2.8 %feature_adjoint.1 = f32[2,16,32,128]{3,2,1,0:T(8,128)} custom-call(bf16[3,18,32,256]{3,2,1,0:T(8,128)(2,1)S(1)} %get-tuple-element.112.grad_high_ref, bf16[3,18,32,256]{3,2,1,0:T(8,128)(2,1)S(1)} %get-tuple-element.113.grad_low_ref, bf16[9,256,256]{2,1,0:T(8,128)(2,1)S(1)} %get-tuple-element.87.taps_high, bf16[9,256,256]{2,1,0:T(8,128)(2,1)S(1)} %get-tuple-element.88.taps_low), custom_call_target="tpu_custom_call" | custom-call | flops 2000000000 | bytes 5000000 | tf_op jit(solution)/shard_map/feature_adjoint/pallas_call | solution.py:361
  68.1 2.9 %collective-permute-done.15 = f32[7,24,128]{2,1,0:T(8,128)S(1)} collective-permute-done((f32[7,24,128]{2,1,0:T(8,128)S(1)}, f32[7,24,128]{2,1,0:T(8,128)S(1)}, u32[]{:S(2)}, u32[]{:S(2)}) %collective-permute-start.15) | collective-permute-done | bytes 86048 | tf_op jit(solution)/shard_map/ppermute | solution.py:451
  71.0 2.7 %collective-permute-start.17 = (f32[7,24,128]{2,1,0:T(8,128)S(1)}, f32[7,24,128]{2,1,0:T(8,128)S(1)}, u32[]{:S(2)}, u32[]{:S(2)}) collective-permute-start(f32[7,24,128]{2,1,0:T(8,128)S(1)} %add.20), channel_id=1, source_target_pairs={{0,32},{16,48},{32,0},{48,16},{1,33},{17,49},{33,1},{49,17},{2,34}... | collective-permute-start | bytes 258056 | tf_op jit(solution)/shard_map/ppermute | solution.py:392
  74.6 2.8 %collective-permute-done.17 = f32[7,24,128]{2,1,0:T(8,128)S(1)} collective-permute-done((f32[7,24,128]{2,1,0:T(8,128)S(1)}, f32[7,24,128]{2,1,0:T(8,128)S(1)}, u32[]{:S(2)}, u32[]{:S(2)}) %collective-permute-start.17) | collective-permute-done | bytes 86048 | tf_op jit(solution)/shard_map/ppermute | solution.py:392
  77.4 2.6 %collective-permute-done.18 = f32[7,24,128]{2,1,0:T(8,128)S(1)} collective-permute-done((f32[7,24,128]{2,1,0:T(8,128)S(1)}, f32[7,24,128]{2,1,0:T(8,128)S(1)}, u32[]{:S(2)}, u32[]{:S(2)}) %collective-permute-start.18) | collective-permute-done | bytes 86048 | tf_op jit(solution)/shard_map/ppermute | solution.py:392
  82.6 2.3 %collective-permute-start.21 = (f32[7,24,128]{2,1,0:T(8,128)S(1)}, f32[7,24,128]{2,1,0:T(8,128)S(1)}, u32[]{:S(2)}, u32[]{:S(2)}) collective-permute-start(f32[7,24,128]{2,1,0:T(8,128)S(1)} %add_add_fusion.own_ref), channel_id=1, source_target_pairs={{0,192},{64,128},{128,64},{192,0},{1,193},{65,129},{129,65},{193,1... | collective-permute-start | bytes 258056 | tf_op jit(solution)/shard_map/ppermute | solution.py:459
  84.9 2.4 %collective-permute-done.20.two_ref = f32[7,24,128]{2,1,0:T(8,128)S(1)} collective-permute-done((f32[7,24,128]{2,1,0:T(8,128)S(1)}, f32[7,24,128]{2,1,0:T(8,128)S(1)}, u32[]{:S(2)}, u32[]{:S(2)}) %collective-permute-start.20) | collective-permute-done | bytes 86048 | tf_op jit(solution)/shard_map/ppermute | solution.py:459
  (50 shorter events, 17.3 us)
Async XLA Ops:
  2.2 9.2 %collective-permute-start = (f32[2,80,128]{2,1,0:T(8,128)}, f32[2,80,128]{2,1,0:T(8,128)S(1)}, u32[]{:S(2)}, u32[]{:S(2)}) collective-permute-start(f32[2,80,128]{2,1,0:T(8,128)} %get-tuple-element.62), channel_id=1, source_target_pairs={{0,16},{16,0},{32,48},{48,32},{64,80},{80,64},{96,112},{112,96},{1... | collective-permute-start | bytes 245768 | tf_op jit(solution)/shard_map/ppermute | solution.py:415
  4.2 9.3 %collective-permute-start.1 = (f32[2,80,128]{2,1,0:T(8,128)}, f32[2,80,128]{2,1,0:T(8,128)S(1)}, u32[]{:S(2)}, u32[]{:S(2)}) collective-permute-start(f32[2,80,128]{2,1,0:T(8,128)} %get-tuple-element.63), channel_id=1, source_target_pairs={{16,32},{32,16},{48,64},{64,48},{80,96},{96,80},{112,128},{128,112... | collective-permute-start | bytes 245768 | tf_op jit(solution)/shard_map/ppermute | solution.py:415
  13.6 3.7 %collective-permute-start.2 = (f32[2,56,128]{2,1,0:T(8,128)S(1)}, f32[2,56,128]{2,1,0:T(8,128)S(1)}, u32[]{:S(2)}, u32[]{:S(2)}) collective-permute-start(f32[2,56,128]{2,1,0:T(8,128)S(1)} %get-tuple-element.74), channel_id=1, source_target_pairs={{0,1},{1,0},{2,3},{3,2},{4,5},{5,4},{6,7},{7,6},{8,9},{9,8},{10,11... | collective-permute-start | bytes 172040 | tf_op jit(solution)/shard_map/ppermute | solution.py:429
  13.7 3.6 %collective-permute-start.3 = (f32[2,56,128]{2,1,0:T(8,128)S(1)}, f32[2,56,128]{2,1,0:T(8,128)S(1)}, u32[]{:S(2)}, u32[]{:S(2)}) collective-permute-start(f32[2,56,128]{2,1,0:T(8,128)S(1)} %get-tuple-element.75), channel_id=1, source_target_pairs={{1,2},{2,1},{3,4},{4,3},{5,6},{6,5},{7,8},{8,7},{9,10},{10,9},{11,... | collective-permute-start | bytes 172040 | tf_op jit(solution)/shard_map/ppermute | solution.py:429
  17.3 4.5 %copy-start.1 = (f32[2,16,32,128]{3,2,1,0:T(8,128)S(1)}, f32[2,16,32,128]{3,2,1,0:T(8,128)}, u32[]{:S(2)}) copy-start(f32[2,16,32,128]{3,2,1,0:T(8,128)} %feat_ref.7) | copy-start | bytes 1572868
  18.8 6.5 %collective-permute-start.4 = (f32[4,4,2,7,16,128]{5,4,3,2,1,0:T(8,128)S(1)}, f32[4,4,2,7,16,128]{5,4,3,2,1,0:T(8,128)S(1)}, u32[]{:S(2)}, u32[]{:S(2)}) collective-permute-start(f32[4,4,2,7,16,128]{5,4,3,2,1,0:T(8,128)S(1)} %get-tuple-element.86), channel_id=1, source_target_pairs={{0,1},{1,0},{2,3},{3,2},{4,5},{5,4},{6,7},{7,6},{8,9},{9,8},{10,11... | collective-permute-start | bytes 5505032 | tf_op jit(solution)/shard_map/ppermute | solution.py:437
  27.7 4.7 %collective-permute-start.5 = (f32[4,4,2,7,8,128]{5,4,3,2,1,0:T(8,128)S(1)}, f32[4,4,2,7,8,128]{5,4,3,2,1,0:T(8,128)S(1)}, u32[]{:S(2)}, u32[]{:S(2)}) collective-permute-start(f32[4,4,2,7,8,128]{5,4,3,2,1,0:T(8,128)S(1)} %get-tuple-element.95), channel_id=1, source_target_pairs={{0,1},{1,0},{2,3},{3,2},{4,5},{5,4},{6,7},{7,6},{8,9},{9,8},{10,11... | collective-permute-start | bytes 2752520 | tf_op jit(solution)/shard_map/ppermute | solution.py:442
  28.2 10.2 %collective-permute-start.9 = (f32[4,2,7,16,128]{4,3,2,1,0:T(8,128)S(1)}, f32[4,2,7,16,128]{4,3,2,1,0:T(8,128)S(1)}, u32[]{:S(2)}, u32[]{:S(2)}) collective-permute-start(f32[4,2,7,16,128]{4,3,2,1,0:T(8,128)S(1)} %get-tuple-element.122), channel_id=1, source_target_pairs={{0,128},{1,5},{2,130},{3,7},{4,132},{5,1},{6,134},{7,3},{64,192},{... | collective-permute-start | bytes 1376264 | tf_op jit(solution)/shard_map/ppermute | solution.py:393
  29.6 11.0 %collective-permute-start.10 = (f32[4,2,7,16,128]{4,3,2,1,0:T(8,128)S(1)}, f32[4,2,7,16,128]{4,3,2,1,0:T(8,128)S(1)}, u32[]{:S(2)}, u32[]{:S(2)}) collective-permute-start(f32[4,2,7,16,128]{4,3,2,1,0:T(8,128)S(1)} %get-tuple-element.121), channel_id=1, source_target_pairs={{0,64},{1,3},{2,66},{3,1},{4,68},{5,7},{6,70},{7,5},{64,0},{65,67}... | collective-permute-start | bytes 1376264 | tf_op jit(solution)/shard_map/ppermute | solution.py:393
  29.6 13.5 %collective-permute-start.11 = (f32[4,2,7,16,128]{4,3,2,1,0:T(8,128)S(1)}, f32[4,2,7,16,128]{4,3,2,1,0:T(8,128)S(1)}, u32[]{:S(2)}, u32[]{:S(2)}) collective-permute-start(f32[4,2,7,16,128]{4,3,2,1,0:T(8,128)S(1)} %get-tuple-element.120), channel_id=1, source_target_pairs={{0,192},{1,7},{2,194},{3,5},{4,196},{5,3},{6,198},{7,1},{64,128},{... | collective-permute-start | bytes 1376264 | tf_op jit(solution)/shard_map/ppermute | solution.py:393
  32.4 6.0 %copy-start.5 = (f32[3,3,3,256,128]{4,3,2,1,0:T(8,128)S(1)}, f32[3,3,3,256,128]{4,3,2,1,0:T(8,128)}, u32[]{:S(2)}) copy-start(f32[3,3,3,256,128]{4,3,2,1,0:T(8,128)} %param.8) | copy-start | bytes 10616836
  32.5 13.2 %collective-permute-start.6 = (f32[4,2,7,8,128]{4,3,2,1,0:T(8,128)S(1)}, f32[4,2,7,8,128]{4,3,2,1,0:T(8,128)S(1)}, u32[]{:S(2)}, u32[]{:S(2)}) collective-permute-start(f32[4,2,7,8,128]{4,3,2,1,0:T(8,128)S(1)} %get-tuple-element.125), channel_id=1, source_target_pairs={{0,128},{1,5},{2,130},{3,7},{4,132},{5,1},{6,134},{7,3},{64,192},{... | collective-permute-start | bytes 688136 | tf_op jit(solution)/shard_map/ppermute | solution.py:393
  34.0 11.8 %collective-permute-start.7 = (f32[4,2,7,8,128]{4,3,2,1,0:T(8,128)S(1)}, f32[4,2,7,8,128]{4,3,2,1,0:T(8,128)S(1)}, u32[]{:S(2)}, u32[]{:S(2)}) collective-permute-start(f32[4,2,7,8,128]{4,3,2,1,0:T(8,128)S(1)} %get-tuple-element.124), channel_id=1, source_target_pairs={{0,64},{1,3},{2,66},{3,1},{4,68},{5,7},{6,70},{7,5},{64,0},{65,67}... | collective-permute-start | bytes 688136 | tf_op jit(solution)/shard_map/ppermute | solution.py:393
  38.4 9.7 %collective-permute-start.8 = (f32[4,2,7,8,128]{4,3,2,1,0:T(8,128)S(1)}, f32[4,2,7,8,128]{4,3,2,1,0:T(8,128)S(1)}, u32[]{:S(2)}, u32[]{:S(2)}) collective-permute-start(f32[4,2,7,8,128]{4,3,2,1,0:T(8,128)S(1)} %get-tuple-element.123), channel_id=1, source_target_pairs={{0,192},{1,7},{2,194},{3,5},{4,196},{5,3},{6,198},{7,1},{64,128},{... | collective-permute-start | bytes 688136 | tf_op jit(solution)/shard_map/ppermute | solution.py:393
  48.2 9.4 %collective-permute-start.12 = (f32[2,7,24,128]{3,2,1,0:T(8,128)S(1)}, f32[2,7,24,128]{3,2,1,0:T(8,128)S(1)}, u32[]{:S(2)}, u32[]{:S(2)}) collective-permute-start(f32[2,7,24,128]{3,2,1,0:T(8,128)S(1)} %get-tuple-element.107), channel_id=1, source_target_pairs={{0,4},{1,129},{2,6},{3,131},{4,0},{5,133},{6,2},{7,135},{64,68},{6... | collective-permute-start | bytes 516104 | tf_op jit(solution)/shard_map/ppermute | solution.py:393
  51.2 11.6 %collective-permute-start.13 = (f32[2,7,24,128]{3,2,1,0:T(8,128)S(1)}, f32[2,7,24,128]{3,2,1,0:T(8,128)S(1)}, u32[]{:S(2)}, u32[]{:S(2)}) collective-permute-start(f32[2,7,24,128]{3,2,1,0:T(8,128)S(1)} %get-tuple-element.108), channel_id=1, source_target_pairs={{0,2},{1,65},{2,0},{3,67},{4,6},{5,69},{6,4},{7,71},{64,66},{65,1}... | collective-permute-start | bytes 516104 | tf_op jit(solution)/shard_map/ppermute | solution.py:393
  57.6 6.6 %collective-permute-start.14 = (f32[2,7,24,128]{3,2,1,0:T(8,128)S(1)}, f32[2,7,24,128]{3,2,1,0:T(8,128)S(1)}, u32[]{:S(2)}, u32[]{:S(2)}) collective-permute-start(f32[2,7,24,128]{3,2,1,0:T(8,128)S(1)} %get-tuple-element.109), channel_id=1, source_target_pairs={{0,6},{1,193},{2,4},{3,195},{4,2},{5,197},{6,0},{7,199},{64,70},{6... | collective-permute-start | bytes 516104 | tf_op jit(solution)/shard_map/ppermute | solution.py:393
  64.3 6.7 %collective-permute-start.15 = (f32[7,24,128]{2,1,0:T(8,128)S(1)}, f32[7,24,128]{2,1,0:T(8,128)S(1)}, u32[]{:S(2)}, u32[]{:S(2)}) collective-permute-start(f32[7,24,128]{2,1,0:T(8,128)S(1)} %get-tuple-element.110), channel_id=1, source_target_pairs={{0,56},{8,48},{16,40},{24,32},{32,24},{40,16},{48,8},{56,0},{1,57}... | collective-permute-start | bytes 258056 | tf_op jit(solution)/shard_map/ppermute | solution.py:451
  71.0 6.4 %collective-permute-start.17 = (f32[7,24,128]{2,1,0:T(8,128)S(1)}, f32[7,24,128]{2,1,0:T(8,128)S(1)}, u32[]{:S(2)}, u32[]{:S(2)}) collective-permute-start(f32[7,24,128]{2,1,0:T(8,128)S(1)} %add.20), channel_id=1, source_target_pairs={{0,32},{16,48},{32,0},{48,16},{1,33},{17,49},{33,1},{49,17},{2,34}... | collective-permute-start | bytes 258056 | tf_op jit(solution)/shard_map/ppermute | solution.py:392
  73.8 6.3 %collective-permute-start.18 = (f32[7,24,128]{2,1,0:T(8,128)S(1)}, f32[7,24,128]{2,1,0:T(8,128)S(1)}, u32[]{:S(2)}, u32[]{:S(2)}) collective-permute-start(f32[7,24,128]{2,1,0:T(8,128)S(1)} %add.20), channel_id=1, source_target_pairs={{0,48},{16,32},{32,16},{48,0},{1,49},{17,33},{33,17},{49,1},{2,50}... | collective-permute-start | bytes 258056 | tf_op jit(solution)/shard_map/ppermute | solution.py:392
  74.4 5.7 %collective-permute-start.16 = (f32[7,24,128]{2,1,0:T(8,128)S(1)}, f32[7,24,128]{2,1,0:T(8,128)S(1)}, u32[]{:S(2)}, u32[]{:S(2)}) collective-permute-start(f32[7,24,128]{2,1,0:T(8,128)S(1)} %add.20), channel_id=1, source_target_pairs={{0,16},{16,0},{32,48},{48,32},{1,17},{17,1},{33,49},{49,33},{2,18}... | collective-permute-start | bytes 258056 | tf_op jit(solution)/shard_map/ppermute | solution.py:392
  80.1 4.8 %collective-permute-start.19 = (f32[7,24,128]{2,1,0:T(8,128)S(1)}, f32[7,24,128]{2,1,0:T(8,128)S(1)}, u32[]{:S(2)}, u32[]{:S(2)}) collective-permute-start(f32[7,24,128]{2,1,0:T(8,128)S(1)} %add_add_fusion.own_ref), channel_id=1, source_target_pairs={{0,64},{64,0},{128,192},{192,128},{1,65},{65,1},{129,193},{193,129... | collective-permute-start | bytes 258056 | tf_op jit(solution)/shard_map/ppermute | solution.py:459
  81.2 6.0 %collective-permute-start.20 = (f32[7,24,128]{2,1,0:T(8,128)S(1)}, f32[7,24,128]{2,1,0:T(8,128)S(1)}, u32[]{:S(2)}, u32[]{:S(2)}) collective-permute-start(f32[7,24,128]{2,1,0:T(8,128)S(1)} %add_add_fusion.own_ref), channel_id=1, source_target_pairs={{0,128},{64,192},{128,0},{192,64},{1,129},{65,193},{129,1},{193,65... | collective-permute-start | bytes 258056 | tf_op jit(solution)/shard_map/ppermute | solution.py:459
  82.6 5.7 %collective-permute-start.21 = (f32[7,24,128]{2,1,0:T(8,128)S(1)}, f32[7,24,128]{2,1,0:T(8,128)S(1)}, u32[]{:S(2)}, u32[]{:S(2)}) collective-permute-start(f32[7,24,128]{2,1,0:T(8,128)S(1)} %add_add_fusion.own_ref), channel_id=1, source_target_pairs={{0,192},{64,128},{128,64},{192,0},{1,193},{65,129},{129,65},{193,1... | collective-permute-start | bytes 258056 | tf_op jit(solution)/shard_map/ppermute | solution.py:459
  (4 other events, 4.4 us)

commit v7 on v6

--- a/solution.py
+++ b/solution.py
@@ -116,7 +116,7 @@
     return jnp.where(odd, first, second), jnp.where(odd, second, first)
 
 
-def col_edges_kernel(feat_ref, cot_ref, row_first_ref, row_second_ref, first_ref, second_ref, edge_ref):
+def col_edges_kernel(feat_ref, cot_ref, row_second_ref, row_first_ref, first_ref, second_ref, edge_ref):
     for t in range(FR):
         halos = [row_halo(row_first_ref, row_second_ref, t, slice(r * W, (r + 1) * W)) for r in range(2)]
         for side, start in ((0, 0), (1, W - 2)):
@@ -150,7 +150,7 @@
 
 
 def flow_terms_kernel(
-    flow_high, flow_low, local_ref, row_first_ref, row_second_ref, col_first_ref, col_second_ref,
+    flow_high, flow_low, local_ref, row_second_ref, row_first_ref, col_second_ref, col_first_ref,
     keep_ref, send_ref, cot_ref,
 ):
     for t in range(FR):
@@ -172,7 +172,7 @@
 
 
 def block_kernel(
-    feat_ref, row_first_ref, row_second_ref, col_first_ref, col_second_ref,
+    feat_ref, row_second_ref, row_first_ref, col_second_ref, col_first_ref,
     taps_high, taps_low, cot_ref, grad_high_ref, grad_low_ref,
     ext_ref, wide_ref, even_high, even_low, odd_high, odd_low, grad_ref,
 ):
@@ -412,7 +412,7 @@
         + [pltpu.SemaphoreType.DMA((4,))],
         HBM,
     )(features, cotangent)
-    rows = [lax.ppermute(edges[k], HA, pairs(k)) for k in (1, 0)][::-1]
+    rows = [lax.ppermute(edges[k], HA, pairs(k)) for k in (1, 0)]
     feats = (jax.ShapeDtypeStruct((2 * C, R * W), bf16),) * 2
     near = (jax.ShapeDtypeStruct((FR, R2, W2, C), f32),)
     *feats, near = small(prepare_features_kernel, "prepare_features", feats + near, 2)(features, cotangent)
@@ -426,7 +426,7 @@
         [pltpu.VMEM((2,) + shape, f32)],
     )(features, near, *rows)
     edges, flow_feats = lax.optimization_barrier((edges, flow_feats))
-    cols = [lax.ppermute(edges[k], WA, pairs(k)) for k in (1, 0)][::-1]
+    cols = [lax.ppermute(edges[k], WA, pairs(k)) for k in (1, 0)]
     taps = (jax.ShapeDtypeStruct((9, 2 * C, 2 * C), bf16),) * 2
     flows = (jax.ShapeDtypeStruct((2 * CF, R2 * W2), bf16),) * 2
     prepared = small(prepare_kernel, "prepare", taps + flows, 2)(kernel_one, flow_feats)

time: 89.4 us -> 88.6 us (level)
  waiting for transfers between devices: 32.4 us -> 30.8 us
    ppermute x1, starting transfers between devices: 3.02 us -> 0.11 us  [local(): terms_two = keep + lax.ppermute(send, 'core', swap)]
    ppermute x4, starting transfers between devices: 7.74 us -> 10.6 us  [the longest x2 6.89 us: local(): rows = [lax.ppermute(edges[k], HA, pairs(k)) for k in (1, 0)]]
    ppermute x9, starting transfers between devices: 15 us -> 13 us  [spread(): lax.ppermute(parts[k], ('x', 'y', 'core'), crossed(k, axes))]
    ppermute x3, starting transfers between devices: 3.58 us -> 5.35 us  [spread(): return [lax.ppermute(parts[k], 'zl', swaps(k)) for k in (3, 2, 1)]]
    ppermute x1, waiting for transfers between devices: 2.94 us -> 1.22 us  [local(): arrived = lax.ppermute(send, ('zl', 'zh'), [(i, 7 - i) for i in range(8)])]
    ppermute x3, waiting for transfers between devices: 5.46 us -> 4.55 us  [spread(): return [lax.ppermute(parts[k], 'zl', swaps(k)) for k in (3, 2, 1)]]
  transfers between devices with their start and end apart: 22 -> 22, of which waited for: 12 -> 15; matrix products, arithmetic and copies ran while one was open for 0% -> 0% of each run, Pallas kernels for 10% -> 11%
where the time goes in v7:
time: 88.6 us; the launch traced here: 87.8 us
  starting transfers between devices  35.9 us (41%)
  waiting for transfers between devices  30.8 us (35%)
  Pallas kernels  15.4 us (17%)
  local copies, waits for them, and re-layouts  4.53 us (5%)
    ppermute x9, waiting for transfers between devices, spread(): lax.ppermute(parts[k], ('x', 'y', 'core'), crossed(k, axes))  18.6 us
    ppermute x9, starting transfers between devices, spread(): lax.ppermute(parts[k], ('x', 'y', 'core'), crossed(k, axes))  13 us
    ppermute x2, starting transfers between devices, local(): rows = [lax.ppermute(edges[k], HA, pairs(k)) for k in (1, 0)]  6.89 us
    ppermute x3, starting transfers between devices, spread(): return [lax.ppermute(parts[k], 'zl', swaps(k)) for k in (3, 2, 1)]  5.35 us
    pallas_call x2, Pallas kernels, adjoint(): pl.pallas_call(kernel, out_shape=jax.ShapeDtypeStruct(shape, f32), in_spe...  5.12 us
    ppermute x3, starting transfers between devices, local(): pieces = [chunk] + [lax.ppermute(chunk, 'x', swaps(k)) for k in (1, 2, 3)]  4.79 us
    ppermute x3, waiting for transfers between devices, spread(): return [lax.ppermute(parts[k], 'zl', swaps(k)) for k in (3, 2, 1)]  4.55 us
    unnamed x12, local copies, waits for them, and re-layouts  4.38 us
  transfers between devices with their start and end apart: 22, of which 15 were waited for; matrix products, arithmetic and copies ran while one was open for 0% of the time, Pallas kernels for 11%

profile of v7, /device:TPU:6, one launch (start us, length us, event | category | flops | bytes accessed | tf_op | source)
XLA Modules:
  0.0 87.8 jit_solution(13538881495130980702)
XLA Ops:
  0.6 1.6 %row_edges.1 = (f32[2,80,128]{2,1,0:T(8,128)}, f32[2,80,128]{2,1,0:T(8,128)}) custom-call(f32[2,16,32,128]{3,2,1,0:T(8,128)} %feat_ref.7, f32[2,8,16,128]{3,2,1,0:T(8,128)} %cot_ref.3), custom_call_target="tpu_custom_call" | custom-call | flops 1000000 | bytes 1000000 | tf_op jit(solution)/shard_map/row_edges/pallas_call | solution.py:405
  2.2 6.8 %collective-permute-start = (f32[2,80,128]{2,1,0:T(8,128)}, f32[2,80,128]{2,1,0:T(8,128)S(1)}, u32[]{:S(2)}, u32[]{:S(2)}) collective-permute-start(f32[2,80,128]{2,1,0:T(8,128)} %get-tuple-element.62), channel_id=1, source_target_pairs={{16,32},{32,16},{48,64},{64,48},{80,96},{96,80},{112,128},{128,112... | collective-permute-start | bytes 245768 | tf_op jit(solution)/shard_map/ppermute | solution.py:415
  14.5 3.0 %collective-permute-start.3 = (f32[2,56,128]{2,1,0:T(8,128)S(1)}, f32[2,56,128]{2,1,0:T(8,128)S(1)}, u32[]{:S(2)}, u32[]{:S(2)}) collective-permute-start(f32[2,56,128]{2,1,0:T(8,128)S(1)} %get-tuple-element.75), channel_id=1, source_target_pairs={{0,1},{1,0},{2,3},{3,2},{4,5},{5,4},{6,7},{7,6},{8,9},{9,8},{10,11... | collective-permute-start | bytes 172040 | tf_op jit(solution)/shard_map/ppermute | solution.py:429
  17.5 1.5 %copy-done.2 = f32[3,3,3,128,128]{4,3,2,1,0:T(8,128)S(1)} copy-done((f32[3,3,3,128,128]{4,3,2,1,0:T(8,128)S(1)}, f32[3,3,3,128,128]{4,3,2,1,0:T(8,128)}, u32[]{:S(2)}) %copy-start.2) | copy-done | bytes 1769496
  20.5 1.5 %flow_terms.1 = (f32[4,4,2,7,16,128]{5,4,3,2,1,0:T(8,128)S(1)}, f32[4,4,2,7,16,128]{5,4,3,2,1,0:T(8,128)S(1)}, f32[2,10,18,128]{3,2,1,0:T(8,128)S(1)}) custom-call(bf16[512,128]{1,0:T(8,128)(2,1)S(1)} %get-tuple-element.81.flow_high, bf16[512,128]{1,0:T(8,128)(2,1)S(1)} %get-tuple-element.82.flow_low, ...), custom_call_target="tpu_custom_call" | custom-call | flops 2000000000 | bytes 5000000 | tf_op jit(solution)/shard_map/flow_terms/pallas_call | solution.py:315
  22.1 3.5 %block_gradient.1 = (bf16[3,18,32,256]{3,2,1,0:T(8,128)(2,1)S(1)}, bf16[3,18,32,256]{3,2,1,0:T(8,128)(2,1)S(1)}) custom-call(f32[2,16,32,128]{3,2,1,0:T(8,128)S(1)} %copy-done.1, f32[2,80,128]{2,1,0:T(8,128)S(1)} %collective-permute-done.row_second_ref, f32[2,80,128]{2,1,0:T(8,128)S(1)} %collective-permute-done.1.row_first_ref, ...), custom_call_target="tpu_custom_call" | custom-call | flops 5000000000 | bytes 6000000 | tf_op jit(solution)/shard_map/block_gradient/pallas_call | solution.py:328
  26.1 2.1 %block_terms.1 = (f32[4,4,2,7,8,128]{5,4,3,2,1,0:T(8,128)S(1)}, f32[4,4,2,7,8,128]{5,4,3,2,1,0:T(8,128)S(1)}) custom-call(bf16[256,512]{1,0:T(8,128)(2,1)S(1)} %get-tuple-element.67.feat_high, bf16[256,512]{1,0:T(8,128)(2,1)S(1)} %get-tuple-element.68.feat_low, bf16[3,18,32,256]{3,2,1,0:T(8,128)(2,1)S(1)} %get-tuple-element.112.grad_high_ref, ...), custom_call_target="tpu_custom_call" | custom-call | flops 1000000000 | bytes 1000000 | tf_op jit(solution)/shard_map/block_terms/pallas_call | solution.py:349
  29.9 2.9 %collective-permute-start.11 = (f32[4,2,7,16,128]{4,3,2,1,0:T(8,128)S(1)}, f32[4,2,7,16,128]{4,3,2,1,0:T(8,128)S(1)}, u32[]{:S(2)}, u32[]{:S(2)}) collective-permute-start(f32[4,2,7,16,128]{4,3,2,1,0:T(8,128)S(1)} %get-tuple-element.120), channel_id=1, source_target_pairs={{0,192},{1,7},{2,194},{3,5},{4,196},{5,3},{6,198},{7,1},{64,128},{... | collective-permute-start | bytes 1376264 | tf_op jit(solution)/shard_map/ppermute | solution.py:393
  34.2 4.6 %collective-permute-done.9.refs_5_ = f32[4,2,7,16,128]{4,3,2,1,0:T(8,128)S(1)} collective-permute-done((f32[4,2,7,16,128]{4,3,2,1,0:T(8,128)S(1)}, f32[4,2,7,16,128]{4,3,2,1,0:T(8,128)S(1)}, u32[]{:S(2)}, u32[]{:S(2)}) %collective-permute-start.9) | collective-permute-done | bytes 458784 | tf_op jit(solution)/shard_map/ppermute | solution.py:393
  38.8 2.3 %flow_adjoint.1 = f32[2,8,16,256]{3,2,1,0:T(8,128)} custom-call(f32[2,10,18,128]{3,2,1,0:T(8,128)S(1)} %get-tuple-element.98.cot_ref, f32[27,256,128]{2,1,0:T(8,128)S(1)} %bitcast.17), custom_call_target="tpu_custom_call" | custom-call | flops 2000000000 | bytes 5000000 | tf_op jit(solution)/shard_map/flow_adjoint/pallas_call | solution.py:361
  41.1 2.5 %collective-permute-done.11.refs_7_ = f32[4,2,7,16,128]{4,3,2,1,0:T(8,128)S(1)} collective-permute-done((f32[4,2,7,16,128]{4,3,2,1,0:T(8,128)S(1)}, f32[4,2,7,16,128]{4,3,2,1,0:T(8,128)S(1)}, u32[]{:S(2)}, u32[]{:S(2)}) %collective-permute-start.11) | collective-permute-done | bytes 458784 | tf_op jit(solution)/shard_map/ppermute | solution.py:393
  43.6 2.6 %collective-permute-done.6.refs_1_ = f32[4,2,7,8,128]{4,3,2,1,0:T(8,128)S(1)} collective-permute-done((f32[4,2,7,8,128]{4,3,2,1,0:T(8,128)S(1)}, f32[4,2,7,8,128]{4,3,2,1,0:T(8,128)S(1)}, u32[]{:S(2)}, u32[]{:S(2)}) %collective-permute-start.6) | collective-permute-done | bytes 229408 | tf_op jit(solution)/shard_map/ppermute | solution.py:393
  46.2 2.3 %collective-permute-done.8.refs_3_ = f32[4,2,7,8,128]{4,3,2,1,0:T(8,128)S(1)} collective-permute-done((f32[4,2,7,8,128]{4,3,2,1,0:T(8,128)S(1)}, f32[4,2,7,8,128]{4,3,2,1,0:T(8,128)S(1)}, u32[]{:S(2)}, u32[]{:S(2)}) %collective-permute-start.8) | collective-permute-done | bytes 229408 | tf_op jit(solution)/shard_map/ppermute | solution.py:393
  48.6 3.0 %collective-permute-start.12 = (f32[2,7,24,128]{3,2,1,0:T(8,128)S(1)}, f32[2,7,24,128]{3,2,1,0:T(8,128)S(1)}, u32[]{:S(2)}, u32[]{:S(2)}) collective-permute-start(f32[2,7,24,128]{3,2,1,0:T(8,128)S(1)} %get-tuple-element.107), channel_id=1, source_target_pairs={{0,4},{1,129},{2,6},{3,131},{4,0},{5,133},{6,2},{7,135},{64,68},{6... | collective-permute-start | bytes 516104 | tf_op jit(solution)/shard_map/ppermute | solution.py:393
  51.6 4.6 %collective-permute-start.13 = (f32[2,7,24,128]{3,2,1,0:T(8,128)S(1)}, f32[2,7,24,128]{3,2,1,0:T(8,128)S(1)}, u32[]{:S(2)}, u32[]{:S(2)}) collective-permute-start(f32[2,7,24,128]{3,2,1,0:T(8,128)S(1)} %get-tuple-element.108), channel_id=1, source_target_pairs={{0,2},{1,65},{2,0},{3,67},{4,6},{5,69},{6,4},{7,71},{64,66},{65,1}... | collective-permute-start | bytes 516104 | tf_op jit(solution)/shard_map/ppermute | solution.py:393
  56.2 5.2 %collective-permute-done.13.first = f32[2,7,24,128]{3,2,1,0:T(8,128)S(1)} collective-permute-done((f32[2,7,24,128]{3,2,1,0:T(8,128)S(1)}, f32[2,7,24,128]{3,2,1,0:T(8,128)S(1)}, u32[]{:S(2)}, u32[]{:S(2)}) %collective-permute-start.13) | collective-permute-done | bytes 172064 | tf_op jit(solution)/shard_map/ppermute | solution.py:393
  62.9 1.7 %collective-permute-start.15 = (f32[7,24,128]{2,1,0:T(8,128)S(1)}, f32[7,24,128]{2,1,0:T(8,128)S(1)}, u32[]{:S(2)}, u32[]{:S(2)}) collective-permute-start(f32[7,24,128]{2,1,0:T(8,128)S(1)} %get-tuple-element.110), channel_id=1, source_target_pairs={{0,56},{8,48},{16,40},{24,32},{32,24},{40,16},{48,8},{56,0},{1,57}... | collective-permute-start | bytes 258056 | tf_op jit(solution)/shard_map/ppermute | solution.py:451
  64.6 2.8 %feature_adjoint.1 = f32[2,16,32,128]{3,2,1,0:T(8,128)} custom-call(bf16[3,18,32,256]{3,2,1,0:T(8,128)(2,1)S(1)} %get-tuple-element.112.grad_high_ref, bf16[3,18,32,256]{3,2,1,0:T(8,128)(2,1)S(1)} %get-tuple-element.113.grad_low_ref, bf16[9,256,256]{2,1,0:T(8,128)(2,1)S(1)} %get-tuple-element.87.taps_high, bf16[9,256,256]{2,1,0:T(8,128)(2,1)S(1)} %get-tuple-element.88.taps_low), custom_call_target="tpu_custom_call" | custom-call | flops 2000000000 | bytes 5000000 | tf_op jit(solution)/shard_map/feature_adjoint/pallas_call | solution.py:361
  68.7 2.6 %collective-permute-start.17 = (f32[7,24,128]{2,1,0:T(8,128)S(1)}, f32[7,24,128]{2,1,0:T(8,128)S(1)}, u32[]{:S(2)}, u32[]{:S(2)}) collective-permute-start(f32[7,24,128]{2,1,0:T(8,128)S(1)} %add.20), channel_id=1, source_target_pairs={{0,32},{16,48},{32,0},{48,16},{1,33},{17,49},{33,1},{49,17},{2,34}... | collective-permute-start | bytes 258056 | tf_op jit(solution)/shard_map/ppermute | solution.py:392
  71.3 2.7 %collective-permute-start.18 = (f32[7,24,128]{2,1,0:T(8,128)S(1)}, f32[7,24,128]{2,1,0:T(8,128)S(1)}, u32[]{:S(2)}, u32[]{:S(2)}) collective-permute-start(f32[7,24,128]{2,1,0:T(8,128)S(1)} %add.20), channel_id=1, source_target_pairs={{0,48},{16,32},{32,16},{48,0},{1,49},{17,33},{33,17},{49,1},{2,50}... | collective-permute-start | bytes 258056 | tf_op jit(solution)/shard_map/ppermute | solution.py:392
  75.2 2.4 %collective-permute-done.18 = f32[7,24,128]{2,1,0:T(8,128)S(1)} collective-permute-done((f32[7,24,128]{2,1,0:T(8,128)S(1)}, f32[7,24,128]{2,1,0:T(8,128)S(1)}, u32[]{:S(2)}, u32[]{:S(2)}) %collective-permute-start.18) | collective-permute-done | bytes 86048 | tf_op jit(solution)/shard_map/ppermute | solution.py:392
  78.6 1.5 %collective-permute-start.19 = (f32[7,24,128]{2,1,0:T(8,128)S(1)}, f32[7,24,128]{2,1,0:T(8,128)S(1)}, u32[]{:S(2)}, u32[]{:S(2)}) collective-permute-start(f32[7,24,128]{2,1,0:T(8,128)S(1)} %add_add_fusion.own_ref), channel_id=1, source_target_pairs={{0,64},{64,0},{128,192},{192,128},{1,65},{65,1},{129,193},{193,129... | collective-permute-start | bytes 258056 | tf_op jit(solution)/shard_map/ppermute | solution.py:459
  81.4 2.0 %collective-permute-start.21 = (f32[7,24,128]{2,1,0:T(8,128)S(1)}, f32[7,24,128]{2,1,0:T(8,128)S(1)}, u32[]{:S(2)}, u32[]{:S(2)}) collective-permute-start(f32[7,24,128]{2,1,0:T(8,128)S(1)} %add_add_fusion.own_ref), channel_id=1, source_target_pairs={{0,192},{64,128},{128,64},{192,0},{1,193},{65,129},{129,65},{193,1... | collective-permute-start | bytes 258056 | tf_op jit(solution)/shard_map/ppermute | solution.py:459
  83.4 2.7 %collective-permute-done.20.two_ref = f32[7,24,128]{2,1,0:T(8,128)S(1)} collective-permute-done((f32[7,24,128]{2,1,0:T(8,128)S(1)}, f32[7,24,128]{2,1,0:T(8,128)S(1)}, u32[]{:S(2)}, u32[]{:S(2)}) %collective-permute-start.20) | collective-permute-done | bytes 86048 | tf_op jit(solution)/shard_map/ppermute | solution.py:459
  (50 shorter events, 18.7 us)
Async XLA Ops:
  2.2 10.3 %collective-permute-start = (f32[2,80,128]{2,1,0:T(8,128)}, f32[2,80,128]{2,1,0:T(8,128)S(1)}, u32[]{:S(2)}, u32[]{:S(2)}) collective-permute-start(f32[2,80,128]{2,1,0:T(8,128)} %get-tuple-element.62), channel_id=1, source_target_pairs={{16,32},{32,16},{48,64},{64,48},{80,96},{96,80},{112,128},{128,112... | collective-permute-start | bytes 245768 | tf_op jit(solution)/shard_map/ppermute | solution.py:415
  9.0 4.7 %collective-permute-start.1 = (f32[2,80,128]{2,1,0:T(8,128)}, f32[2,80,128]{2,1,0:T(8,128)S(1)}, u32[]{:S(2)}, u32[]{:S(2)}) collective-permute-start(f32[2,80,128]{2,1,0:T(8,128)} %get-tuple-element.63), channel_id=1, source_target_pairs={{0,16},{16,0},{32,48},{48,32},{64,80},{80,64},{96,112},{112,96},{1... | collective-permute-start | bytes 245768 | tf_op jit(solution)/shard_map/ppermute | solution.py:415
  13.8 6.6 %collective-permute-start.2 = (f32[2,56,128]{2,1,0:T(8,128)S(1)}, f32[2,56,128]{2,1,0:T(8,128)S(1)}, u32[]{:S(2)}, u32[]{:S(2)}) collective-permute-start(f32[2,56,128]{2,1,0:T(8,128)S(1)} %get-tuple-element.74), channel_id=1, source_target_pairs={{1,2},{2,1},{3,4},{4,3},{5,6},{6,5},{7,8},{8,7},{9,10},{10,9},{11,... | collective-permute-start | bytes 172040 | tf_op jit(solution)/shard_map/ppermute | solution.py:429
  14.5 5.9 %collective-permute-start.3 = (f32[2,56,128]{2,1,0:T(8,128)S(1)}, f32[2,56,128]{2,1,0:T(8,128)S(1)}, u32[]{:S(2)}, u32[]{:S(2)}) collective-permute-start(f32[2,56,128]{2,1,0:T(8,128)S(1)} %get-tuple-element.75), channel_id=1, source_target_pairs={{0,1},{1,0},{2,3},{3,2},{4,5},{5,4},{6,7},{7,6},{8,9},{9,8},{10,11... | collective-permute-start | bytes 172040 | tf_op jit(solution)/shard_map/ppermute | solution.py:429
  20.5 1.6 %copy-start.1 = (f32[2,16,32,128]{3,2,1,0:T(8,128)S(1)}, f32[2,16,32,128]{3,2,1,0:T(8,128)}, u32[]{:S(2)}) copy-start(f32[2,16,32,128]{3,2,1,0:T(8,128)} %feat_ref.7) | copy-start | bytes 1572868
  22.0 3.9 %collective-permute-start.4 = (f32[4,4,2,7,16,128]{5,4,3,2,1,0:T(8,128)S(1)}, f32[4,4,2,7,16,128]{5,4,3,2,1,0:T(8,128)S(1)}, u32[]{:S(2)}, u32[]{:S(2)}) collective-permute-start(f32[4,4,2,7,16,128]{5,4,3,2,1,0:T(8,128)S(1)} %get-tuple-element.86), channel_id=1, source_target_pairs={{0,1},{1,0},{2,3},{3,2},{4,5},{5,4},{6,7},{7,6},{8,9},{9,8},{10,11... | collective-permute-start | bytes 5505032 | tf_op jit(solution)/shard_map/ppermute | solution.py:437
  28.2 4.6 %collective-permute-start.5 = (f32[4,4,2,7,8,128]{5,4,3,2,1,0:T(8,128)S(1)}, f32[4,4,2,7,8,128]{5,4,3,2,1,0:T(8,128)S(1)}, u32[]{:S(2)}, u32[]{:S(2)}) collective-permute-start(f32[4,4,2,7,8,128]{5,4,3,2,1,0:T(8,128)S(1)} %get-tuple-element.95), channel_id=1, source_target_pairs={{0,1},{1,0},{2,3},{3,2},{4,5},{5,4},{6,7},{7,6},{8,9},{9,8},{10,11... | collective-permute-start | bytes 2752520 | tf_op jit(solution)/shard_map/ppermute | solution.py:442
  28.6 10.2 %collective-permute-start.9 = (f32[4,2,7,16,128]{4,3,2,1,0:T(8,128)S(1)}, f32[4,2,7,16,128]{4,3,2,1,0:T(8,128)S(1)}, u32[]{:S(2)}, u32[]{:S(2)}) collective-permute-start(f32[4,2,7,16,128]{4,3,2,1,0:T(8,128)S(1)} %get-tuple-element.122), channel_id=1, source_target_pairs={{0,128},{1,5},{2,130},{3,7},{4,132},{5,1},{6,134},{7,3},{64,192},{... | collective-permute-start | bytes 1376264 | tf_op jit(solution)/shard_map/ppermute | solution.py:393
  29.8 11.2 %collective-permute-start.10 = (f32[4,2,7,16,128]{4,3,2,1,0:T(8,128)S(1)}, f32[4,2,7,16,128]{4,3,2,1,0:T(8,128)S(1)}, u32[]{:S(2)}, u32[]{:S(2)}) collective-permute-start(f32[4,2,7,16,128]{4,3,2,1,0:T(8,128)S(1)} %get-tuple-element.121), channel_id=1, source_target_pairs={{0,64},{1,3},{2,66},{3,1},{4,68},{5,7},{6,70},{7,5},{64,0},{65,67}... | collective-permute-start | bytes 1376264 | tf_op jit(solution)/shard_map/ppermute | solution.py:393
  29.9 13.7 %collective-permute-start.11 = (f32[4,2,7,16,128]{4,3,2,1,0:T(8,128)S(1)}, f32[4,2,7,16,128]{4,3,2,1,0:T(8,128)S(1)}, u32[]{:S(2)}, u32[]{:S(2)}) collective-permute-start(f32[4,2,7,16,128]{4,3,2,1,0:T(8,128)S(1)} %get-tuple-element.120), channel_id=1, source_target_pairs={{0,192},{1,7},{2,194},{3,5},{4,196},{5,3},{6,198},{7,1},{64,128},{... | collective-permute-start | bytes 1376264 | tf_op jit(solution)/shard_map/ppermute | solution.py:393
  32.8 6.0 %copy-start.5 = (f32[3,3,3,256,128]{4,3,2,1,0:T(8,128)S(1)}, f32[3,3,3,256,128]{4,3,2,1,0:T(8,128)}, u32[]{:S(2)}) copy-start(f32[3,3,3,256,128]{4,3,2,1,0:T(8,128)} %param.8) | copy-start | bytes 10616836
  32.9 13.2 %collective-permute-start.6 = (f32[4,2,7,8,128]{4,3,2,1,0:T(8,128)S(1)}, f32[4,2,7,8,128]{4,3,2,1,0:T(8,128)S(1)}, u32[]{:S(2)}, u32[]{:S(2)}) collective-permute-start(f32[4,2,7,8,128]{4,3,2,1,0:T(8,128)S(1)} %get-tuple-element.125), channel_id=1, source_target_pairs={{0,128},{1,5},{2,130},{3,7},{4,132},{5,1},{6,134},{7,3},{64,192},{... | collective-permute-start | bytes 688136 | tf_op jit(solution)/shard_map/ppermute | solution.py:393
  34.2 12.0 %collective-permute-start.7 = (f32[4,2,7,8,128]{4,3,2,1,0:T(8,128)S(1)}, f32[4,2,7,8,128]{4,3,2,1,0:T(8,128)S(1)}, u32[]{:S(2)}, u32[]{:S(2)}) collective-permute-start(f32[4,2,7,8,128]{4,3,2,1,0:T(8,128)S(1)} %get-tuple-element.124), channel_id=1, source_target_pairs={{0,64},{1,3},{2,66},{3,1},{4,68},{5,7},{6,70},{7,5},{64,0},{65,67}... | collective-permute-start | bytes 688136 | tf_op jit(solution)/shard_map/ppermute | solution.py:393
  38.8 9.7 %collective-permute-start.8 = (f32[4,2,7,8,128]{4,3,2,1,0:T(8,128)S(1)}, f32[4,2,7,8,128]{4,3,2,1,0:T(8,128)S(1)}, u32[]{:S(2)}, u32[]{:S(2)}) collective-permute-start(f32[4,2,7,8,128]{4,3,2,1,0:T(8,128)S(1)} %get-tuple-element.123), channel_id=1, source_target_pairs={{0,192},{1,7},{2,194},{3,5},{4,196},{5,3},{6,198},{7,1},{64,128},{... | collective-permute-start | bytes 688136 | tf_op jit(solution)/shard_map/ppermute | solution.py:393
  48.6 7.6 %collective-permute-start.12 = (f32[2,7,24,128]{3,2,1,0:T(8,128)S(1)}, f32[2,7,24,128]{3,2,1,0:T(8,128)S(1)}, u32[]{:S(2)}, u32[]{:S(2)}) collective-permute-start(f32[2,7,24,128]{3,2,1,0:T(8,128)S(1)} %get-tuple-element.107), channel_id=1, source_target_pairs={{0,4},{1,129},{2,6},{3,131},{4,0},{5,133},{6,2},{7,135},{64,68},{6... | collective-permute-start | bytes 516104 | tf_op jit(solution)/shard_map/ppermute | solution.py:393
  51.6 9.8 %collective-permute-start.13 = (f32[2,7,24,128]{3,2,1,0:T(8,128)S(1)}, f32[2,7,24,128]{3,2,1,0:T(8,128)S(1)}, u32[]{:S(2)}, u32[]{:S(2)}) collective-permute-start(f32[2,7,24,128]{3,2,1,0:T(8,128)S(1)} %get-tuple-element.108), channel_id=1, source_target_pairs={{0,2},{1,65},{2,0},{3,67},{4,6},{5,69},{6,4},{7,71},{64,66},{65,1}... | collective-permute-start | bytes 516104 | tf_op jit(solution)/shard_map/ppermute | solution.py:393
  56.2 6.6 %collective-permute-start.14 = (f32[2,7,24,128]{3,2,1,0:T(8,128)S(1)}, f32[2,7,24,128]{3,2,1,0:T(8,128)S(1)}, u32[]{:S(2)}, u32[]{:S(2)}) collective-permute-start(f32[2,7,24,128]{3,2,1,0:T(8,128)S(1)} %get-tuple-element.109), channel_id=1, source_target_pairs={{0,6},{1,193},{2,4},{3,195},{4,2},{5,197},{6,0},{7,199},{64,70},{6... | collective-permute-start | bytes 516104 | tf_op jit(solution)/shard_map/ppermute | solution.py:393
  62.9 5.8 %collective-permute-start.15 = (f32[7,24,128]{2,1,0:T(8,128)S(1)}, f32[7,24,128]{2,1,0:T(8,128)S(1)}, u32[]{:S(2)}, u32[]{:S(2)}) collective-permute-start(f32[7,24,128]{2,1,0:T(8,128)S(1)} %get-tuple-element.110), channel_id=1, source_target_pairs={{0,56},{8,48},{16,40},{24,32},{32,24},{40,16},{48,8},{56,0},{1,57}... | collective-permute-start | bytes 258056 | tf_op jit(solution)/shard_map/ppermute | solution.py:451
  68.7 6.6 %collective-permute-start.17 = (f32[7,24,128]{2,1,0:T(8,128)S(1)}, f32[7,24,128]{2,1,0:T(8,128)S(1)}, u32[]{:S(2)}, u32[]{:S(2)}) collective-permute-start(f32[7,24,128]{2,1,0:T(8,128)S(1)} %add.20), channel_id=1, source_target_pairs={{0,32},{16,48},{32,0},{48,16},{1,33},{17,49},{33,1},{49,17},{2,34}... | collective-permute-start | bytes 258056 | tf_op jit(solution)/shard_map/ppermute | solution.py:392
  71.3 6.3 %collective-permute-start.18 = (f32[7,24,128]{2,1,0:T(8,128)S(1)}, f32[7,24,128]{2,1,0:T(8,128)S(1)}, u32[]{:S(2)}, u32[]{:S(2)}) collective-permute-start(f32[7,24,128]{2,1,0:T(8,128)S(1)} %add.20), channel_id=1, source_target_pairs={{0,48},{16,32},{32,16},{48,0},{1,49},{17,33},{33,17},{49,1},{2,50}... | collective-permute-start | bytes 258056 | tf_op jit(solution)/shard_map/ppermute | solution.py:392
  74.0 4.6 %collective-permute-start.16 = (f32[7,24,128]{2,1,0:T(8,128)S(1)}, f32[7,24,128]{2,1,0:T(8,128)S(1)}, u32[]{:S(2)}, u32[]{:S(2)}) collective-permute-start(f32[7,24,128]{2,1,0:T(8,128)S(1)} %add.20), channel_id=1, source_target_pairs={{0,16},{16,0},{32,48},{48,32},{1,17},{17,1},{33,49},{49,33},{2,18}... | collective-permute-start | bytes 258056 | tf_op jit(solution)/shard_map/ppermute | solution.py:392
  78.6 4.8 %collective-permute-start.19 = (f32[7,24,128]{2,1,0:T(8,128)S(1)}, f32[7,24,128]{2,1,0:T(8,128)S(1)}, u32[]{:S(2)}, u32[]{:S(2)}) collective-permute-start(f32[7,24,128]{2,1,0:T(8,128)S(1)} %add_add_fusion.own_ref), channel_id=1, source_target_pairs={{0,64},{64,0},{128,192},{192,128},{1,65},{65,1},{129,193},{193,129... | collective-permute-start | bytes 258056 | tf_op jit(solution)/shard_map/ppermute | solution.py:459
  80.1 6.0 %collective-permute-start.20 = (f32[7,24,128]{2,1,0:T(8,128)S(1)}, f32[7,24,128]{2,1,0:T(8,128)S(1)}, u32[]{:S(2)}, u32[]{:S(2)}) collective-permute-start(f32[7,24,128]{2,1,0:T(8,128)S(1)} %add_add_fusion.own_ref), channel_id=1, source_target_pairs={{0,128},{64,192},{128,0},{192,64},{1,129},{65,193},{129,1},{193,65... | collective-permute-start | bytes 258056 | tf_op jit(solution)/shard_map/ppermute | solution.py:459
  81.4 5.7 %collective-permute-start.21 = (f32[7,24,128]{2,1,0:T(8,128)S(1)}, f32[7,24,128]{2,1,0:T(8,128)S(1)}, u32[]{:S(2)}, u32[]{:S(2)}) collective-permute-start(f32[7,24,128]{2,1,0:T(8,128)S(1)} %add_add_fusion.own_ref), channel_id=1, source_target_pairs={{0,192},{64,128},{128,64},{192,0},{1,193},{65,129},{129,65},{193,1... | collective-permute-start | bytes 258056 | tf_op jit(solution)/shard_map/ppermute | solution.py:459
  (4 other events, 4.4 us)

commit v8 on v7

--- a/solution.py
+++ b/solution.py
@@ -266,12 +266,18 @@
         flow_out[t] = total[:, t * CF : (t + 1) * CF].reshape(R2, W2, CF)
 
 
-def first_sum_kernel(*refs):
-    ones, twos, outs = refs[:4], refs[4:8], refs[8:]
+def halving_kernel(own, first_half, second_half, keep, first_send, second_send):
+    keep[:2] = own[0, :2] + first_half[0]
+    first_send[...] = own[3, :2] + first_half[1]
+    keep[2:] = own[0, 2:] + second_half[1]
+    second_send[...] = own[1, 2:] + second_half[0]
+
+
+def first_sum_kernel(keep_one, ones_first, ones_second, keep_two, twos_first, twos_second, *outs):
     for slot, out in enumerate(outs):
-        for depth, parts in ((slice(0, 8), ones), (slice(8, 24), twos)):
-            own, second, first, third = parts
-            out[:, :, depth] = (own[0, slot] + second[slot]) + (first[slot] + third[slot])
+        ones, twos = (ones_first, twos_first) if slot < 2 else (ones_second, twos_second)
+        out[:, :, :8] = keep_one[slot] + ones[slot % 2]
+        out[:, :, 8:] = keep_two[slot] + twos[slot % 2]
 
 
 def second_sum_kernel(own, second, first, third, keep, send):
@@ -390,7 +396,17 @@
 def spread(parts, axes):
     if axes == "zl":
         return [lax.ppermute(parts[k], "zl", swaps(k)) for k in (3, 2, 1)]
-    return [lax.ppermute(parts[k], ("x", "y", "core"), crossed(k, axes)) for k in (2, 1, 3)]
+    return cross([parts[k] for k in (2, 1, 3)], axes, (2, 1, 3))
+
+
+def cross(parts, axes, masks):
+    return [lax.ppermute(v, ("x", "y", "core"), crossed(k, axes)) for v, k in zip(parts, masks)]
+
+
+def halved(terms, arrived):
+    slots, _, *rest = terms.shape
+    shapes = [jax.ShapeDtypeStruct((count, *rest), f32) for count in (4, 2, 2)]
+    return small(halving_kernel, "halving", tuple(shapes), 3)(terms, *arrived)
 
 
 def summed(own, arrived):
@@ -437,15 +453,20 @@
     terms_two = keep + lax.ppermute(send, "core", swap)
     grad_high, grad_low = block_gradient(features, *rows, *cols, *taps, cot)
     terms_two, grad_high, grad_low = lax.optimization_barrier((terms_two, grad_high, grad_low))
-    arrived_two = spread(terms_two, ("x", "y"))
+    axes = ("x", "y")
+    arrived_two = cross((terms_two[1:3, :2], terms_two[2:4, 2:]), axes, (1, 3))
     keep, send = block_terms(*feats, grad_high, grad_low)
     terms_one = keep + lax.ppermute(send, "core", swap)
-    arrived_one = spread(terms_one, ("x", "y"))
+    arrived_one = cross((terms_one[1:3, :2], terms_one[2:4, 2:]), axes, (1, 3))
     terms_one, cot, kernel_two = lax.optimization_barrier((terms_one, cot, kernel_two))
     grad_flow = adjoint(flow_adjoint_kernel, "flow_adjoint", (FR, R2, W2, CF), cot, kernel_two)
-    arrived_one, arrived_two, grad_flow = lax.optimization_barrier((arrived_one, arrived_two, grad_flow))
+    arrived_two, grad_flow = lax.optimization_barrier((arrived_two, grad_flow))
+    keep_two, *sends = halved(terms_two, arrived_two)
+    arrived_two = cross(sends, axes, (3, 1))
+    keep_one, *sends = halved(terms_one, arrived_one)
+    arrived_one = cross(sends, axes, (3, 1))
     parts = (jax.ShapeDtypeStruct((2, 7, 24, C), f32),) * 4
-    parts = small(first_sum_kernel, "first_sum", parts, 8)(terms_one, *arrived_one, terms_two, *arrived_two)
+    parts = small(first_sum_kernel, "first_sum", parts, 6)(keep_one, *arrived_one, keep_two, *arrived_two)
     chunk = (jax.ShapeDtypeStruct((7, 24, C), f32),) * 2
     keep, send = small(second_sum_kernel, "second_sum", chunk, 4)(parts[0], *spread(parts, ("y", "x")))
     arrived = lax.ppermute(send, ("zl", "zh"), [(i, 7 - i) for i in range(8)])

time: 88.6 us -> 90.6 us (1.023)
  starting transfers between devices: 35.9 us -> 41.2 us
  waiting for transfers between devices: 30.8 us -> 27.9 us
    ppermute x9 -> x11, waiting for transfers between devices: 18.6 us -> 14.4 us  [cross(): lax.ppermute(v, ('x', 'y', 'core'), crossed(k, axes))]
    ppermute x9 -> x11, starting transfers between devices: 13 us -> 16.8 us  [cross(): lax.ppermute(v, ('x', 'y', 'core'), crossed(k, axes))]
    ppermute x3, waiting for transfers between devices: 3.7 us -> 5.69 us  [local(): pieces = [chunk] + [lax.ppermute(chunk, 'x', swaps(k)) for k in (1, 2, 3)]]
    ppermute x1, starting transfers between devices: 1.73 us -> 3.41 us  [local(): arrived = lax.ppermute(send, ('zl', 'zh'), [(i, 7 - i) for i in range(8)])]
    ppermute x1, waiting for transfers between devices: 1.22 us -> 0.01 us  [local(): arrived = lax.ppermute(send, ('zl', 'zh'), [(i, 7 - i) for i in range(8)])]
  transfers between devices with their start and end apart: 22 -> 24, of which waited for: 15 -> 16; matrix products, arithmetic and copies ran while one was open for 0% -> 0% of each run, Pallas kernels for 11% -> 10%
where the time goes in v8:
time: 90.6 us; the launch traced here: 90.3 us
  starting transfers between devices  41.2 us (45%)
  waiting for transfers between devices  27.9 us (31%)
  Pallas kernels  15.5 us (17%)
  local copies, waits for them, and re-layouts  4.48 us (5%)
    ppermute x11, starting transfers between devices, cross(): lax.ppermute(v, ('x', 'y', 'core'), crossed(k, axes))  16.8 us
    ppermute x11, waiting for transfers between devices, cross(): lax.ppermute(v, ('x', 'y', 'core'), crossed(k, axes))  14.4 us
    ppermute x2, starting transfers between devices, local(): rows = [lax.ppermute(edges[k], HA, pairs(k)) for k in (1, 0)]  6.89 us
    ppermute x3, waiting for transfers between devices, local(): pieces = [chunk] + [lax.ppermute(chunk, 'x', swaps(k)) for k in (1, 2, 3)]  5.69 us
    ppermute x3, starting transfers between devices, local(): pieces = [chunk] + [lax.ppermute(chunk, 'x', swaps(k)) for k in (1, 2, 3)]  5.25 us
    pallas_call x2, Pallas kernels, adjoint(): pl.pallas_call(kernel, out_shape=jax.ShapeDtypeStruct(shape, f32), in_spe...  5.12 us
    ppermute x3, starting transfers between devices, spread(): return [lax.ppermute(parts[k], 'zl', swaps(k)) for k in (3, 2, 1)]  4.77 us
    ppermute x3, waiting for transfers between devices, spread(): return [lax.ppermute(parts[k], 'zl', swaps(k)) for k in (3, 2, 1)]  4.72 us
  transfers between devices with their start and end apart: 24, of which 16 were waited for; matrix products, arithmetic and copies ran while one was open for 0% of the time, Pallas kernels for 10%

profile of v8, /device:TPU:6, one launch (start us, length us, event | category | flops | bytes accessed | tf_op | source)
XLA Modules:
  0.0 90.3 jit_solution(14318292514154726930)
XLA Ops:
  0.6 1.6 %row_edges.1 = (f32[2,80,128]{2,1,0:T(8,128)}, f32[2,80,128]{2,1,0:T(8,128)}) custom-call(f32[2,16,32,128]{3,2,1,0:T(8,128)} %feat_ref.7, f32[2,8,16,128]{3,2,1,0:T(8,128)} %cot_ref.3), custom_call_target="tpu_custom_call" | custom-call | flops 1000000 | bytes 1000000 | tf_op jit(solution)/shard_map/row_edges/pallas_call | solution.py:421
  2.2 6.8 %collective-permute-start = (f32[2,80,128]{2,1,0:T(8,128)}, f32[2,80,128]{2,1,0:T(8,128)S(1)}, u32[]{:S(2)}, u32[]{:S(2)}) collective-permute-start(f32[2,80,128]{2,1,0:T(8,128)} %get-tuple-element.64), channel_id=1, source_target_pairs={{16,32},{32,16},{48,64},{64,48},{80,96},{96,80},{112,128},{128,112... | collective-permute-start | bytes 245768 | tf_op jit(solution)/shard_map/ppermute | solution.py:431
  14.5 3.0 %collective-permute-start.3 = (f32[2,56,128]{2,1,0:T(8,128)S(1)}, f32[2,56,128]{2,1,0:T(8,128)S(1)}, u32[]{:S(2)}, u32[]{:S(2)}) collective-permute-start(f32[2,56,128]{2,1,0:T(8,128)S(1)} %get-tuple-element.77), channel_id=1, source_target_pairs={{0,1},{1,0},{2,3},{3,2},{4,5},{5,4},{6,7},{7,6},{8,9},{9,8},{10,11... | collective-permute-start | bytes 172040 | tf_op jit(solution)/shard_map/ppermute | solution.py:445
  17.5 1.5 %copy-done.2 = f32[3,3,3,128,128]{4,3,2,1,0:T(8,128)S(1)} copy-done((f32[3,3,3,128,128]{4,3,2,1,0:T(8,128)S(1)}, f32[3,3,3,128,128]{4,3,2,1,0:T(8,128)}, u32[]{:S(2)}) %copy-start.2) | copy-done | bytes 1769496
  20.5 1.5 %flow_terms.1 = (f32[4,4,2,7,16,128]{5,4,3,2,1,0:T(8,128)S(1)}, f32[4,4,2,7,16,128]{5,4,3,2,1,0:T(8,128)S(1)}, f32[2,10,18,128]{3,2,1,0:T(8,128)S(1)}) custom-call(bf16[512,128]{1,0:T(8,128)(2,1)S(1)} %get-tuple-element.83.flow_high, bf16[512,128]{1,0:T(8,128)(2,1)S(1)} %get-tuple-element.84.flow_low, ...), custom_call_target="tpu_custom_call" | custom-call | flops 2000000000 | bytes 5000000 | tf_op jit(solution)/shard_map/flow_terms/pallas_call | solution.py:321
  22.1 3.5 %block_gradient.1 = (bf16[3,18,32,256]{3,2,1,0:T(8,128)(2,1)S(1)}, bf16[3,18,32,256]{3,2,1,0:T(8,128)(2,1)S(1)}) custom-call(f32[2,16,32,128]{3,2,1,0:T(8,128)S(1)} %copy-done.1, f32[2,80,128]{2,1,0:T(8,128)S(1)} %collective-permute-done.row_second_ref, f32[2,80,128]{2,1,0:T(8,128)S(1)} %collective-permute-done.1.row_first_ref, ...), custom_call_target="tpu_custom_call" | custom-call | flops 5000000000 | bytes 6000000 | tf_op jit(solution)/shard_map/block_gradient/pallas_call | solution.py:334
  26.1 2.1 %block_terms.1 = (f32[4,4,2,7,8,128]{5,4,3,2,1,0:T(8,128)S(1)}, f32[4,4,2,7,8,128]{5,4,3,2,1,0:T(8,128)S(1)}) custom-call(bf16[256,512]{1,0:T(8,128)(2,1)S(1)} %get-tuple-element.69.feat_high, bf16[256,512]{1,0:T(8,128)(2,1)S(1)} %get-tuple-element.70.feat_low, bf16[3,18,32,256]{3,2,1,0:T(8,128)(2,1)S(1)} %get-tuple-element.116.grad_high_ref, ...), custom_call_target="tpu_custom_call" | custom-call | flops 1000000000 | bytes 1000000 | tf_op jit(solution)/shard_map/block_terms/pallas_call | solution.py:355
  31.5 2.1 %collective-permute-start.7 = (f32[2,2,2,7,8,128]{5,4,3,2,1,0:T(8,128)S(1)}, f32[2,2,2,7,8,128]{5,4,3,2,1,0:T(8,128)S(1)}, u32[]{:S(2)}, u32[]{:S(2)}) collective-permute-start(f32[2,2,2,7,8,128]{5,4,3,2,1,0:T(8,128)S(1)} %get-tuple-element.126), channel_id=1, source_target_pairs={{0,192},{1,7},{2,194},{3,5},{4,196},{5,3},{6,198},{7,1},{64,128},{... | collective-permute-start | bytes 688136 | tf_op jit(solution)/shard_map/ppermute | solution.py:403
  33.5 2.3 %flow_adjoint.1 = f32[2,8,16,256]{3,2,1,0:T(8,128)} custom-call(f32[2,10,18,128]{3,2,1,0:T(8,128)S(1)} %get-tuple-element.103.cot_ref, f32[27,256,128]{2,1,0:T(8,128)S(1)} %bitcast.5), custom_call_target="tpu_custom_call" | custom-call | flops 2000000000 | bytes 5000000 | tf_op jit(solution)/shard_map/flow_adjoint/pallas_call | solution.py:367
  35.8 1.3 %collective-permute-done.10.first_half = f32[2,2,2,7,16,128]{5,4,3,2,1,0:T(8,128)S(1)} collective-permute-done((f32[2,2,2,7,16,128]{5,4,3,2,1,0:T(8,128)S(1)}, f32[2,2,2,7,16,128]{5,4,3,2,1,0:T(8,128)S(1)}, u32[]{:S(2)}, u32[]{:S(2)}) %collective-permute-start.10) | collective-permute-done | bytes 458784 | tf_op jit(solution)/shard_map/ppermute | solution.py:403
  37.1 1.7 %collective-permute-done.11.second_half = f32[2,2,2,7,16,128]{5,4,3,2,1,0:T(8,128)S(1)} collective-permute-done((f32[2,2,2,7,16,128]{5,4,3,2,1,0:T(8,128)S(1)}, f32[2,2,2,7,16,128]{5,4,3,2,1,0:T(8,128)S(1)}, u32[]{:S(2)}, u32[]{:S(2)}) %collective-permute-start.11) | collective-permute-done | bytes 458784 | tf_op jit(solution)/shard_map/ppermute | solution.py:403
  43.8 2.4 %collective-permute-done.12.twos_first = f32[2,2,7,16,128]{4,3,2,1,0:T(8,128)S(1)} collective-permute-done((f32[2,2,7,16,128]{4,3,2,1,0:T(8,128)S(1)}, f32[2,2,7,16,128]{4,3,2,1,0:T(8,128)S(1)}, u32[]{:S(2)}, u32[]{:S(2)}) %collective-permute-start.12) | collective-permute-done | bytes 229408 | tf_op jit(solution)/shard_map/ppermute | solution.py:403
  47.6 3.0 %collective-permute-start.14 = (f32[2,7,24,128]{3,2,1,0:T(8,128)S(1)}, f32[2,7,24,128]{3,2,1,0:T(8,128)S(1)}, u32[]{:S(2)}, u32[]{:S(2)}) collective-permute-start(f32[2,7,24,128]{3,2,1,0:T(8,128)S(1)} %get-tuple-element.111), channel_id=1, source_target_pairs={{0,4},{1,129},{2,6},{3,131},{4,0},{5,133},{6,2},{7,135},{64,68},{6... | collective-permute-start | bytes 516104 | tf_op jit(solution)/shard_map/ppermute | solution.py:403
  50.6 5.5 %collective-permute-start.15 = (f32[2,7,24,128]{3,2,1,0:T(8,128)S(1)}, f32[2,7,24,128]{3,2,1,0:T(8,128)S(1)}, u32[]{:S(2)}, u32[]{:S(2)}) collective-permute-start(f32[2,7,24,128]{3,2,1,0:T(8,128)S(1)} %get-tuple-element.112), channel_id=1, source_target_pairs={{0,2},{1,65},{2,0},{3,67},{4,6},{5,69},{6,4},{7,71},{64,66},{65,1}... | collective-permute-start | bytes 516104 | tf_op jit(solution)/shard_map/ppermute | solution.py:403
  56.1 5.2 %collective-permute-done.15.first = f32[2,7,24,128]{3,2,1,0:T(8,128)S(1)} collective-permute-done((f32[2,7,24,128]{3,2,1,0:T(8,128)S(1)}, f32[2,7,24,128]{3,2,1,0:T(8,128)S(1)}, u32[]{:S(2)}, u32[]{:S(2)}) %collective-permute-start.15) | collective-permute-done | bytes 172064 | tf_op jit(solution)/shard_map/ppermute | solution.py:403
  61.3 1.4 %collective-permute-done.16.third = f32[2,7,24,128]{3,2,1,0:T(8,128)S(1)} collective-permute-done((f32[2,7,24,128]{3,2,1,0:T(8,128)S(1)}, f32[2,7,24,128]{3,2,1,0:T(8,128)S(1)}, u32[]{:S(2)}, u32[]{:S(2)}) %collective-permute-start.16) | collective-permute-done | bytes 172064 | tf_op jit(solution)/shard_map/ppermute | solution.py:403
  62.8 3.4 %collective-permute-start.17 = (f32[7,24,128]{2,1,0:T(8,128)S(1)}, f32[7,24,128]{2,1,0:T(8,128)S(1)}, u32[]{:S(2)}, u32[]{:S(2)}) collective-permute-start(f32[7,24,128]{2,1,0:T(8,128)S(1)} %get-tuple-element.114), channel_id=1, source_target_pairs={{0,56},{8,48},{16,40},{24,32},{32,24},{40,16},{48,8},{56,0},{1,57}... | collective-permute-start | bytes 258056 | tf_op jit(solution)/shard_map/ppermute | solution.py:472
  66.2 2.8 %feature_adjoint.1 = f32[2,16,32,128]{3,2,1,0:T(8,128)} custom-call(bf16[3,18,32,256]{3,2,1,0:T(8,128)(2,1)S(1)} %get-tuple-element.116.grad_high_ref, bf16[3,18,32,256]{3,2,1,0:T(8,128)(2,1)S(1)} %get-tuple-element.117.grad_low_ref, bf16[9,256,256]{2,1,0:T(8,128)(2,1)S(1)} %get-tuple-element.89.taps_high, bf16[9,256,256]{2,1,0:T(8,128)(2,1)S(1)} %get-tuple-element.90.taps_low), custom_call_target="tpu_custom_call" | custom-call | flops 2000000000 | bytes 5000000 | tf_op jit(solution)/shard_map/feature_adjoint/pallas_call | solution.py:367
  69.0 2.2 %collective-permute-start.19 = (f32[7,24,128]{2,1,0:T(8,128)S(1)}, f32[7,24,128]{2,1,0:T(8,128)S(1)}, u32[]{:S(2)}, u32[]{:S(2)}) collective-permute-start(f32[7,24,128]{2,1,0:T(8,128)S(1)} %add.20), channel_id=1, source_target_pairs={{0,32},{16,48},{32,0},{48,16},{1,33},{17,49},{33,1},{49,17},{2,34}... | collective-permute-start | bytes 258056 | tf_op jit(solution)/shard_map/ppermute | solution.py:398
  71.3 2.5 %collective-permute-start.20 = (f32[7,24,128]{2,1,0:T(8,128)S(1)}, f32[7,24,128]{2,1,0:T(8,128)S(1)}, u32[]{:S(2)}, u32[]{:S(2)}) collective-permute-start(f32[7,24,128]{2,1,0:T(8,128)S(1)} %add.20), channel_id=1, source_target_pairs={{0,48},{16,32},{32,16},{48,0},{1,49},{17,33},{33,17},{49,1},{2,50}... | collective-permute-start | bytes 258056 | tf_op jit(solution)/shard_map/ppermute | solution.py:398
  74.5 3.1 %collective-permute-done.20 = f32[7,24,128]{2,1,0:T(8,128)S(1)} collective-permute-done((f32[7,24,128]{2,1,0:T(8,128)S(1)}, f32[7,24,128]{2,1,0:T(8,128)S(1)}, u32[]{:S(2)}, u32[]{:S(2)}) %collective-permute-start.20) | collective-permute-done | bytes 86048 | tf_op jit(solution)/shard_map/ppermute | solution.py:398
  79.6 4.2 %collective-permute-start.22 = (f32[7,24,128]{2,1,0:T(8,128)S(1)}, f32[7,24,128]{2,1,0:T(8,128)S(1)}, u32[]{:S(2)}, u32[]{:S(2)}) collective-permute-start(f32[7,24,128]{2,1,0:T(8,128)S(1)} %add_add_fusion.own_ref), channel_id=1, source_target_pairs={{0,128},{64,192},{128,0},{192,64},{1,129},{65,193},{129,1},{193,65... | collective-permute-start | bytes 258056 | tf_op jit(solution)/shard_map/ppermute | solution.py:480
  83.8 3.4 %collective-permute-done.22.two_ref = f32[7,24,128]{2,1,0:T(8,128)S(1)} collective-permute-done((f32[7,24,128]{2,1,0:T(8,128)S(1)}, f32[7,24,128]{2,1,0:T(8,128)S(1)}, u32[]{:S(2)}, u32[]{:S(2)}) %collective-permute-start.22) | collective-permute-done | bytes 86048 | tf_op jit(solution)/shard_map/ppermute | solution.py:480
  87.2 2.3 %collective-permute-done.23.three_ref = f32[7,24,128]{2,1,0:T(8,128)S(1)} collective-permute-done((f32[7,24,128]{2,1,0:T(8,128)S(1)}, f32[7,24,128]{2,1,0:T(8,128)S(1)}, u32[]{:S(2)}, u32[]{:S(2)}) %collective-permute-start.23) | collective-permute-done | bytes 86048 | tf_op jit(solution)/shard_map/ppermute | solution.py:480
  (56 shorter events, 20.6 us)
Async XLA Ops:
  2.2 10.3 %collective-permute-start = (f32[2,80,128]{2,1,0:T(8,128)}, f32[2,80,128]{2,1,0:T(8,128)S(1)}, u32[]{:S(2)}, u32[]{:S(2)}) collective-permute-start(f32[2,80,128]{2,1,0:T(8,128)} %get-tuple-element.64), channel_id=1, source_target_pairs={{16,32},{32,16},{48,64},{64,48},{80,96},{96,80},{112,128},{128,112... | collective-permute-start | bytes 245768 | tf_op jit(solution)/shard_map/ppermute | solution.py:431
  9.0 4.7 %collective-permute-start.1 = (f32[2,80,128]{2,1,0:T(8,128)}, f32[2,80,128]{2,1,0:T(8,128)S(1)}, u32[]{:S(2)}, u32[]{:S(2)}) collective-permute-start(f32[2,80,128]{2,1,0:T(8,128)} %get-tuple-element.65), channel_id=1, source_target_pairs={{0,16},{16,0},{32,48},{48,32},{64,80},{80,64},{96,112},{112,96},{1... | collective-permute-start | bytes 245768 | tf_op jit(solution)/shard_map/ppermute | solution.py:431
  13.8 6.6 %collective-permute-start.2 = (f32[2,56,128]{2,1,0:T(8,128)S(1)}, f32[2,56,128]{2,1,0:T(8,128)S(1)}, u32[]{:S(2)}, u32[]{:S(2)}) collective-permute-start(f32[2,56,128]{2,1,0:T(8,128)S(1)} %get-tuple-element.76), channel_id=1, source_target_pairs={{1,2},{2,1},{3,4},{4,3},{5,6},{6,5},{7,8},{8,7},{9,10},{10,9},{11,... | collective-permute-start | bytes 172040 | tf_op jit(solution)/shard_map/ppermute | solution.py:445
  14.5 5.9 %collective-permute-start.3 = (f32[2,56,128]{2,1,0:T(8,128)S(1)}, f32[2,56,128]{2,1,0:T(8,128)S(1)}, u32[]{:S(2)}, u32[]{:S(2)}) collective-permute-start(f32[2,56,128]{2,1,0:T(8,128)S(1)} %get-tuple-element.77), channel_id=1, source_target_pairs={{0,1},{1,0},{2,3},{3,2},{4,5},{5,4},{6,7},{7,6},{8,9},{9,8},{10,11... | collective-permute-start | bytes 172040 | tf_op jit(solution)/shard_map/ppermute | solution.py:445
  22.0 3.9 %collective-permute-start.4 = (f32[4,4,2,7,16,128]{5,4,3,2,1,0:T(8,128)S(1)}, f32[4,4,2,7,16,128]{5,4,3,2,1,0:T(8,128)S(1)}, u32[]{:S(2)}, u32[]{:S(2)}) collective-permute-start(f32[4,4,2,7,16,128]{5,4,3,2,1,0:T(8,128)S(1)} %get-tuple-element.88), channel_id=1, source_target_pairs={{0,1},{1,0},{2,3},{3,2},{4,5},{5,4},{6,7},{7,6},{8,9},{9,8},{10,11... | collective-permute-start | bytes 5505032 | tf_op jit(solution)/shard_map/ppermute | solution.py:453
  28.1 2.6 %collective-permute-start.5 = (f32[4,4,2,7,8,128]{5,4,3,2,1,0:T(8,128)S(1)}, f32[4,4,2,7,8,128]{5,4,3,2,1,0:T(8,128)S(1)}, u32[]{:S(2)}, u32[]{:S(2)}) collective-permute-start(f32[4,4,2,7,8,128]{5,4,3,2,1,0:T(8,128)S(1)} %get-tuple-element.97), channel_id=1, source_target_pairs={{0,1},{1,0},{2,3},{3,2},{4,5},{5,4},{6,7},{7,6},{8,9},{9,8},{10,11... | collective-permute-start | bytes 2752520 | tf_op jit(solution)/shard_map/ppermute | solution.py:459
  28.5 8.6 %collective-permute-start.10 = (f32[2,2,2,7,16,128]{5,4,3,2,1,0:T(8,128)S(1)}, f32[2,2,2,7,16,128]{5,4,3,2,1,0:T(8,128)S(1)}, u32[]{:S(2)}, u32[]{:S(2)}) collective-permute-start(f32[2,2,2,7,16,128]{5,4,3,2,1,0:T(8,128)S(1)} %get-tuple-element.125), channel_id=1, source_target_pairs={{0,64},{1,3},{2,66},{3,1},{4,68},{5,7},{6,70},{7,5},{64,0},{65,67}... | collective-permute-start | bytes 1376264 | tf_op jit(solution)/shard_map/ppermute | solution.py:403
  29.2 9.7 %collective-permute-start.11 = (f32[2,2,2,7,16,128]{5,4,3,2,1,0:T(8,128)S(1)}, f32[2,2,2,7,16,128]{5,4,3,2,1,0:T(8,128)S(1)}, u32[]{:S(2)}, u32[]{:S(2)}) collective-permute-start(f32[2,2,2,7,16,128]{5,4,3,2,1,0:T(8,128)S(1)} %get-tuple-element.124), channel_id=1, source_target_pairs={{0,192},{1,7},{2,194},{3,5},{4,196},{5,3},{6,198},{7,1},{64,128},{... | collective-permute-start | bytes 1376264 | tf_op jit(solution)/shard_map/ppermute | solution.py:403
  30.8 9.4 %collective-permute-start.6 = (f32[2,2,2,7,8,128]{5,4,3,2,1,0:T(8,128)S(1)}, f32[2,2,2,7,8,128]{5,4,3,2,1,0:T(8,128)S(1)}, u32[]{:S(2)}, u32[]{:S(2)}) collective-permute-start(f32[2,2,2,7,8,128]{5,4,3,2,1,0:T(8,128)S(1)} %get-tuple-element.127), channel_id=1, source_target_pairs={{0,64},{1,3},{2,66},{3,1},{4,68},{5,7},{6,70},{7,5},{64,0},{65,67}... | collective-permute-start | bytes 688136 | tf_op jit(solution)/shard_map/ppermute | solution.py:403
  31.5 9.8 %collective-permute-start.7 = (f32[2,2,2,7,8,128]{5,4,3,2,1,0:T(8,128)S(1)}, f32[2,2,2,7,8,128]{5,4,3,2,1,0:T(8,128)S(1)}, u32[]{:S(2)}, u32[]{:S(2)}) collective-permute-start(f32[2,2,2,7,8,128]{5,4,3,2,1,0:T(8,128)S(1)} %get-tuple-element.126), channel_id=1, source_target_pairs={{0,192},{1,7},{2,194},{3,5},{4,196},{5,3},{6,198},{7,1},{64,128},{... | collective-permute-start | bytes 688136 | tf_op jit(solution)/shard_map/ppermute | solution.py:403
  38.9 7.3 %collective-permute-start.12 = (f32[2,2,7,16,128]{4,3,2,1,0:T(8,128)S(1)}, f32[2,2,7,16,128]{4,3,2,1,0:T(8,128)S(1)}, u32[]{:S(2)}, u32[]{:S(2)}) collective-permute-start(f32[2,2,7,16,128]{4,3,2,1,0:T(8,128)S(1)} %get-tuple-element.108), channel_id=1, source_target_pairs={{0,192},{1,7},{2,194},{3,5},{4,196},{5,3},{6,198},{7,1},{64,128},{... | collective-permute-start | bytes 688136 | tf_op jit(solution)/shard_map/ppermute | solution.py:403
  40.2 6.0 %collective-permute-start.13 = (f32[2,2,7,16,128]{4,3,2,1,0:T(8,128)S(1)}, f32[2,2,7,16,128]{4,3,2,1,0:T(8,128)S(1)}, u32[]{:S(2)}, u32[]{:S(2)}) collective-permute-start(f32[2,2,7,16,128]{4,3,2,1,0:T(8,128)S(1)} %get-tuple-element.109), channel_id=1, source_target_pairs={{0,64},{1,3},{2,66},{3,1},{4,68},{5,7},{6,70},{7,5},{64,0},{65,67}... | collective-permute-start | bytes 688136 | tf_op jit(solution)/shard_map/ppermute | solution.py:403
  41.4 6.1 %collective-permute-start.8 = (f32[2,2,7,8,128]{4,3,2,1,0:T(8,128)S(1)}, f32[2,2,7,8,128]{4,3,2,1,0:T(8,128)S(1)}, u32[]{:S(2)}, u32[]{:S(2)}) collective-permute-start(f32[2,2,7,8,128]{4,3,2,1,0:T(8,128)S(1)} %get-tuple-element.100), channel_id=1, source_target_pairs={{0,192},{1,7},{2,194},{3,5},{4,196},{5,3},{6,198},{7,1},{64,128},{... | collective-permute-start | bytes 344072 | tf_op jit(solution)/shard_map/ppermute | solution.py:403
  42.6 4.9 %collective-permute-start.9 = (f32[2,2,7,8,128]{4,3,2,1,0:T(8,128)S(1)}, f32[2,2,7,8,128]{4,3,2,1,0:T(8,128)S(1)}, u32[]{:S(2)}, u32[]{:S(2)}) collective-permute-start(f32[2,2,7,8,128]{4,3,2,1,0:T(8,128)S(1)} %get-tuple-element.101), channel_id=1, source_target_pairs={{0,64},{1,3},{2,66},{3,1},{4,68},{5,7},{6,70},{7,5},{64,0},{65,67}... | collective-permute-start | bytes 344072 | tf_op jit(solution)/shard_map/ppermute | solution.py:403
  47.6 8.5 %collective-permute-start.14 = (f32[2,7,24,128]{3,2,1,0:T(8,128)S(1)}, f32[2,7,24,128]{3,2,1,0:T(8,128)S(1)}, u32[]{:S(2)}, u32[]{:S(2)}) collective-permute-start(f32[2,7,24,128]{3,2,1,0:T(8,128)S(1)} %get-tuple-element.111), channel_id=1, source_target_pairs={{0,4},{1,129},{2,6},{3,131},{4,0},{5,133},{6,2},{7,135},{64,68},{6... | collective-permute-start | bytes 516104 | tf_op jit(solution)/shard_map/ppermute | solution.py:403
  50.6 10.8 %collective-permute-start.15 = (f32[2,7,24,128]{3,2,1,0:T(8,128)S(1)}, f32[2,7,24,128]{3,2,1,0:T(8,128)S(1)}, u32[]{:S(2)}, u32[]{:S(2)}) collective-permute-start(f32[2,7,24,128]{3,2,1,0:T(8,128)S(1)} %get-tuple-element.112), channel_id=1, source_target_pairs={{0,2},{1,65},{2,0},{3,67},{4,6},{5,69},{6,4},{7,71},{64,66},{65,1}... | collective-permute-start | bytes 516104 | tf_op jit(solution)/shard_map/ppermute | solution.py:403
  56.1 6.6 %collective-permute-start.16 = (f32[2,7,24,128]{3,2,1,0:T(8,128)S(1)}, f32[2,7,24,128]{3,2,1,0:T(8,128)S(1)}, u32[]{:S(2)}, u32[]{:S(2)}) collective-permute-start(f32[2,7,24,128]{3,2,1,0:T(8,128)S(1)} %get-tuple-element.113), channel_id=1, source_target_pairs={{0,6},{1,193},{2,4},{3,195},{4,2},{5,197},{6,0},{7,199},{64,70},{6... | collective-permute-start | bytes 516104 | tf_op jit(solution)/shard_map/ppermute | solution.py:403
  62.8 6.2 %collective-permute-start.17 = (f32[7,24,128]{2,1,0:T(8,128)S(1)}, f32[7,24,128]{2,1,0:T(8,128)S(1)}, u32[]{:S(2)}, u32[]{:S(2)}) collective-permute-start(f32[7,24,128]{2,1,0:T(8,128)S(1)} %get-tuple-element.114), channel_id=1, source_target_pairs={{0,56},{8,48},{16,40},{24,32},{32,24},{40,16},{48,8},{56,0},{1,57}... | collective-permute-start | bytes 258056 | tf_op jit(solution)/shard_map/ppermute | solution.py:472
  69.0 5.5 %collective-permute-start.19 = (f32[7,24,128]{2,1,0:T(8,128)S(1)}, f32[7,24,128]{2,1,0:T(8,128)S(1)}, u32[]{:S(2)}, u32[]{:S(2)}) collective-permute-start(f32[7,24,128]{2,1,0:T(8,128)S(1)} %add.20), channel_id=1, source_target_pairs={{0,32},{16,48},{32,0},{48,16},{1,33},{17,49},{33,1},{49,17},{2,34}... | collective-permute-start | bytes 258056 | tf_op jit(solution)/shard_map/ppermute | solution.py:398
  71.3 6.4 %collective-permute-start.20 = (f32[7,24,128]{2,1,0:T(8,128)S(1)}, f32[7,24,128]{2,1,0:T(8,128)S(1)}, u32[]{:S(2)}, u32[]{:S(2)}) collective-permute-start(f32[7,24,128]{2,1,0:T(8,128)S(1)} %add.20), channel_id=1, source_target_pairs={{0,48},{16,32},{32,16},{48,0},{1,49},{17,33},{33,17},{49,1},{2,50}... | collective-permute-start | bytes 258056 | tf_op jit(solution)/shard_map/ppermute | solution.py:398
  73.8 4.7 %collective-permute-start.18 = (f32[7,24,128]{2,1,0:T(8,128)S(1)}, f32[7,24,128]{2,1,0:T(8,128)S(1)}, u32[]{:S(2)}, u32[]{:S(2)}) collective-permute-start(f32[7,24,128]{2,1,0:T(8,128)S(1)} %add.20), channel_id=1, source_target_pairs={{0,16},{16,0},{32,48},{48,32},{1,17},{17,1},{33,49},{49,33},{2,18}... | collective-permute-start | bytes 258056 | tf_op jit(solution)/shard_map/ppermute | solution.py:398
  78.6 5.3 %collective-permute-start.21 = (f32[7,24,128]{2,1,0:T(8,128)S(1)}, f32[7,24,128]{2,1,0:T(8,128)S(1)}, u32[]{:S(2)}, u32[]{:S(2)}) collective-permute-start(f32[7,24,128]{2,1,0:T(8,128)S(1)} %add_add_fusion.own_ref), channel_id=1, source_target_pairs={{0,64},{64,0},{128,192},{192,128},{1,65},{65,1},{129,193},{193,129... | collective-permute-start | bytes 258056 | tf_op jit(solution)/shard_map/ppermute | solution.py:480
  79.6 7.6 %collective-permute-start.22 = (f32[7,24,128]{2,1,0:T(8,128)S(1)}, f32[7,24,128]{2,1,0:T(8,128)S(1)}, u32[]{:S(2)}, u32[]{:S(2)}) collective-permute-start(f32[7,24,128]{2,1,0:T(8,128)S(1)} %add_add_fusion.own_ref), channel_id=1, source_target_pairs={{0,128},{64,192},{128,0},{192,64},{1,129},{65,193},{129,1},{193,65... | collective-permute-start | bytes 258056 | tf_op jit(solution)/shard_map/ppermute | solution.py:480
  83.8 5.7 %collective-permute-start.23 = (f32[7,24,128]{2,1,0:T(8,128)S(1)}, f32[7,24,128]{2,1,0:T(8,128)S(1)}, u32[]{:S(2)}, u32[]{:S(2)}) collective-permute-start(f32[7,24,128]{2,1,0:T(8,128)S(1)} %add_add_fusion.own_ref), channel_id=1, source_target_pairs={{0,192},{64,128},{128,64},{192,0},{1,193},{65,129},{129,65},{193,1... | collective-permute-start | bytes 258056 | tf_op jit(solution)/shard_map/ppermute | solution.py:480
  (6 other events, 8.8 us)

commit v9 on v7

--- a/solution.py
+++ b/solution.py
@@ -270,13 +270,13 @@
     ones, twos, outs = refs[:4], refs[4:8], refs[8:]
     for slot, out in enumerate(outs):
         for depth, parts in ((slice(0, 8), ones), (slice(8, 24), twos)):
-            own, second, first, third = parts
-            out[:, :, depth] = (own[0, slot] + second[slot]) + (first[slot] + third[slot])
-
-
-def second_sum_kernel(own, second, first, third, keep, send):
-    keep[...] = (own[0] + second[0]) + (first[0] + third[0])
-    send[...] = (own[1] + second[1]) + (first[1] + third[1])
+            own, first, third, second = parts
+            out[:, :, depth] = (own[0, slot] + first[slot]) + (second[slot] + third[slot])
+
+
+def second_sum_kernel(own, first, third, second, keep, send):
+    keep[...] = (own[0] + first[0]) + (second[0] + third[0])
+    send[...] = (own[1] + first[1]) + (second[1] + third[1])
 
 
 def gather_kernel(own_ref, one_ref, two_ref, three_ref, grad_one_ref, grad_two_ref):
@@ -390,7 +390,7 @@
 def spread(parts, axes):
     if axes == "zl":
         return [lax.ppermute(parts[k], "zl", swaps(k)) for k in (3, 2, 1)]
-    return [lax.ppermute(parts[k], ("x", "y", "core"), crossed(k, axes)) for k in (2, 1, 3)]
+    return [lax.ppermute(parts[k], ("x", "y", "core"), crossed(k, axes)) for k in (1, 3, 2)]
 
 
 def summed(own, arrived):

time: 88.6 us -> 89.9 us (1.015)
  starting transfers between devices: 35.9 us -> 39.1 us
  waiting for transfers between devices: 30.8 us -> 28.4 us
    ppermute x9, starting transfers between devices: 13 us -> 15.6 us  [spread(): lax.ppermute(parts[k], ('x', 'y', 'core'), crossed(k, axes))]
    ppermute x9, waiting for transfers between devices: 18.6 us -> 16.1 us  [spread(): lax.ppermute(parts[k], ('x', 'y', 'core'), crossed(k, axes))]
    ppermute x1, starting transfers between devices: 1.73 us -> 4.14 us  [local(): arrived = lax.ppermute(send, ('zl', 'zh'), [(i, 7 - i) for i in range(8)])]
    ppermute x3, starting transfers between devices: 5.35 us -> 3.58 us  [spread(): return [lax.ppermute(parts[k], 'zl', swaps(k)) for k in (3, 2, 1)]]
  transfers between devices with their start and end apart: 22 -> 22, of which waited for: 15 -> 15; matrix products, arithmetic and copies ran while one was open for 0% -> 0% of each run, Pallas kernels for 11% -> 10%
where the time goes in v9:
time: 89.9 us; the launch traced here: 88.7 us
  starting transfers between devices  39.1 us (43%)
  waiting for transfers between devices  28.4 us (32%)
  Pallas kernels  15.4 us (17%)
  local copies, waits for them, and re-layouts  4.53 us (5%)
    ppermute x9, waiting for transfers between devices, spread(): lax.ppermute(parts[k], ('x', 'y', 'core'), crossed(k, axes))  16.1 us
    ppermute x9, starting transfers between devices, spread(): lax.ppermute(parts[k], ('x', 'y', 'core'), crossed(k, axes))  15.6 us
    ppermute x2, starting transfers between devices, local(): rows = [lax.ppermute(edges[k], HA, pairs(k)) for k in (1, 0)]  6.89 us
    ppermute x3, waiting for transfers between devices, spread(): return [lax.ppermute(parts[k], 'zl', swaps(k)) for k in (3, 2, 1)]  5.15 us
    pallas_call x2, Pallas kernels, adjoint(): pl.pallas_call(kernel, out_shape=jax.ShapeDtypeStruct(shape, f32), in_spe...  5.11 us
    ppermute x3, starting transfers between devices, local(): pieces = [chunk] + [lax.ppermute(chunk, 'x', swaps(k)) for k in (1, 2, 3)]  4.78 us
    unnamed x12, local copies, waits for them, and re-layouts  4.38 us
    ppermute x1, starting transfers between devices, local(): arrived = lax.ppermute(send, ('zl', 'zh'), [(i, 7 - i) for i in range(8)])  4.14 us
  transfers between devices with their start and end apart: 22, of which 15 were waited for; matrix products, arithmetic and copies ran while one was open for 0% of the time, Pallas kernels for 10%

profile of v9, /device:TPU:6, one launch (start us, length us, event | category | flops | bytes accessed | tf_op | source)
XLA Modules:
  0.0 88.7 jit_solution(8358693370300203097)
XLA Ops:
  0.6 1.6 %row_edges.1 = (f32[2,80,128]{2,1,0:T(8,128)}, f32[2,80,128]{2,1,0:T(8,128)}) custom-call(f32[2,16,32,128]{3,2,1,0:T(8,128)} %feat_ref.7, f32[2,8,16,128]{3,2,1,0:T(8,128)} %cot_ref.3), custom_call_target="tpu_custom_call" | custom-call | flops 1000000 | bytes 1000000 | tf_op jit(solution)/shard_map/row_edges/pallas_call | solution.py:405
  2.2 6.8 %collective-permute-start = (f32[2,80,128]{2,1,0:T(8,128)}, f32[2,80,128]{2,1,0:T(8,128)S(1)}, u32[]{:S(2)}, u32[]{:S(2)}) collective-permute-start(f32[2,80,128]{2,1,0:T(8,128)} %get-tuple-element.62), channel_id=1, source_target_pairs={{16,32},{32,16},{48,64},{64,48},{80,96},{96,80},{112,128},{128,112... | collective-permute-start | bytes 245768 | tf_op jit(solution)/shard_map/ppermute | solution.py:415
  14.5 3.0 %collective-permute-start.3 = (f32[2,56,128]{2,1,0:T(8,128)S(1)}, f32[2,56,128]{2,1,0:T(8,128)S(1)}, u32[]{:S(2)}, u32[]{:S(2)}) collective-permute-start(f32[2,56,128]{2,1,0:T(8,128)S(1)} %get-tuple-element.75), channel_id=1, source_target_pairs={{0,1},{1,0},{2,3},{3,2},{4,5},{5,4},{6,7},{7,6},{8,9},{9,8},{10,11... | collective-permute-start | bytes 172040 | tf_op jit(solution)/shard_map/ppermute | solution.py:429
  17.5 1.5 %copy-done.2 = f32[3,3,3,128,128]{4,3,2,1,0:T(8,128)S(1)} copy-done((f32[3,3,3,128,128]{4,3,2,1,0:T(8,128)S(1)}, f32[3,3,3,128,128]{4,3,2,1,0:T(8,128)}, u32[]{:S(2)}) %copy-start.2) | copy-done | bytes 1769496
  22.1 3.5 %block_gradient.1 = (bf16[3,18,32,256]{3,2,1,0:T(8,128)(2,1)S(1)}, bf16[3,18,32,256]{3,2,1,0:T(8,128)(2,1)S(1)}) custom-call(f32[2,16,32,128]{3,2,1,0:T(8,128)S(1)} %copy-done.1, f32[2,80,128]{2,1,0:T(8,128)S(1)} %collective-permute-done.row_second_ref, f32[2,80,128]{2,1,0:T(8,128)S(1)} %collective-permute-done.1.row_first_ref, ...), custom_call_target="tpu_custom_call" | custom-call | flops 5000000000 | bytes 6000000 | tf_op jit(solution)/shard_map/block_gradient/pallas_call | solution.py:328
  26.1 2.1 %block_terms.1 = (f32[4,4,2,7,8,128]{5,4,3,2,1,0:T(8,128)S(1)}, f32[4,4,2,7,8,128]{5,4,3,2,1,0:T(8,128)S(1)}) custom-call(bf16[256,512]{1,0:T(8,128)(2,1)S(1)} %get-tuple-element.67.feat_high, bf16[256,512]{1,0:T(8,128)(2,1)S(1)} %get-tuple-element.68.feat_low, bf16[3,18,32,256]{3,2,1,0:T(8,128)(2,1)S(1)} %get-tuple-element.112.grad_high_ref, ...), custom_call_target="tpu_custom_call" | custom-call | flops 1000000000 | bytes 1000000 | tf_op jit(solution)/shard_map/block_terms/pallas_call | solution.py:349
  30.4 2.4 %collective-permute-start.11 = (f32[4,2,7,16,128]{4,3,2,1,0:T(8,128)S(1)}, f32[4,2,7,16,128]{4,3,2,1,0:T(8,128)S(1)}, u32[]{:S(2)}, u32[]{:S(2)}) collective-permute-start(f32[4,2,7,16,128]{4,3,2,1,0:T(8,128)S(1)} %get-tuple-element.120), channel_id=1, source_target_pairs={{0,128},{1,5},{2,130},{3,7},{4,132},{5,1},{6,134},{7,3},{64,192},{... | collective-permute-start | bytes 1376264 | tf_op jit(solution)/shard_map/ppermute | solution.py:393
  34.8 2.4 %collective-permute-done.9.refs_5_ = f32[4,2,7,16,128]{4,3,2,1,0:T(8,128)S(1)} collective-permute-done((f32[4,2,7,16,128]{4,3,2,1,0:T(8,128)S(1)}, f32[4,2,7,16,128]{4,3,2,1,0:T(8,128)S(1)}, u32[]{:S(2)}, u32[]{:S(2)}) %collective-permute-start.9) | collective-permute-done | bytes 458784 | tf_op jit(solution)/shard_map/ppermute | solution.py:393
  38.3 2.3 %flow_adjoint.1 = f32[2,8,16,256]{3,2,1,0:T(8,128)} custom-call(f32[2,10,18,128]{3,2,1,0:T(8,128)S(1)} %get-tuple-element.98.cot_ref, f32[27,256,128]{2,1,0:T(8,128)S(1)} %bitcast.17), custom_call_target="tpu_custom_call" | custom-call | flops 2000000000 | bytes 5000000 | tf_op jit(solution)/shard_map/flow_adjoint/pallas_call | solution.py:361
  40.6 3.2 %collective-permute-done.10.refs_6_ = f32[4,2,7,16,128]{4,3,2,1,0:T(8,128)S(1)} collective-permute-done((f32[4,2,7,16,128]{4,3,2,1,0:T(8,128)S(1)}, f32[4,2,7,16,128]{4,3,2,1,0:T(8,128)S(1)}, u32[]{:S(2)}, u32[]{:S(2)}) %collective-permute-start.10) | collective-permute-done | bytes 458784 | tf_op jit(solution)/shard_map/ppermute | solution.py:393
  44.6 4.2 %collective-permute-done.7.refs_2_ = f32[4,2,7,8,128]{4,3,2,1,0:T(8,128)S(1)} collective-permute-done((f32[4,2,7,8,128]{4,3,2,1,0:T(8,128)S(1)}, f32[4,2,7,8,128]{4,3,2,1,0:T(8,128)S(1)}, u32[]{:S(2)}, u32[]{:S(2)}) %collective-permute-start.7) | collective-permute-done | bytes 229408 | tf_op jit(solution)/shard_map/ppermute | solution.py:393
  48.9 1.7 %collective-permute-start.12 = (f32[2,7,24,128]{3,2,1,0:T(8,128)S(1)}, f32[2,7,24,128]{3,2,1,0:T(8,128)S(1)}, u32[]{:S(2)}, u32[]{:S(2)}) collective-permute-start(f32[2,7,24,128]{3,2,1,0:T(8,128)S(1)} %get-tuple-element.107), channel_id=1, source_target_pairs={{0,2},{1,65},{2,0},{3,67},{4,6},{5,69},{6,4},{7,71},{64,66},{65,1}... | collective-permute-start | bytes 516104 | tf_op jit(solution)/shard_map/ppermute | solution.py:393
  50.5 5.4 %collective-permute-start.13 = (f32[2,7,24,128]{3,2,1,0:T(8,128)S(1)}, f32[2,7,24,128]{3,2,1,0:T(8,128)S(1)}, u32[]{:S(2)}, u32[]{:S(2)}) collective-permute-start(f32[2,7,24,128]{3,2,1,0:T(8,128)S(1)} %get-tuple-element.108), channel_id=1, source_target_pairs={{0,6},{1,193},{2,4},{3,195},{4,2},{5,197},{6,0},{7,199},{64,70},{6... | collective-permute-start | bytes 516104 | tf_op jit(solution)/shard_map/ppermute | solution.py:393
  57.3 3.4 %collective-permute-done.13.third = f32[2,7,24,128]{3,2,1,0:T(8,128)S(1)} collective-permute-done((f32[2,7,24,128]{3,2,1,0:T(8,128)S(1)}, f32[2,7,24,128]{3,2,1,0:T(8,128)S(1)}, u32[]{:S(2)}, u32[]{:S(2)}) %collective-permute-start.13) | collective-permute-done | bytes 172064 | tf_op jit(solution)/shard_map/ppermute | solution.py:393
  60.8 2.1 %collective-permute-done.14.second = f32[2,7,24,128]{3,2,1,0:T(8,128)S(1)} collective-permute-done((f32[2,7,24,128]{3,2,1,0:T(8,128)S(1)}, f32[2,7,24,128]{3,2,1,0:T(8,128)S(1)}, u32[]{:S(2)}, u32[]{:S(2)}) %collective-permute-start.14) | collective-permute-done | bytes 172064 | tf_op jit(solution)/shard_map/ppermute | solution.py:393
  62.9 4.1 %collective-permute-start.15 = (f32[7,24,128]{2,1,0:T(8,128)S(1)}, f32[7,24,128]{2,1,0:T(8,128)S(1)}, u32[]{:S(2)}, u32[]{:S(2)}) collective-permute-start(f32[7,24,128]{2,1,0:T(8,128)S(1)} %get-tuple-element.110), channel_id=1, source_target_pairs={{0,56},{8,48},{16,40},{24,32},{32,24},{40,16},{48,8},{56,0},{1,57}... | collective-permute-start | bytes 258056 | tf_op jit(solution)/shard_map/ppermute | solution.py:451
  67.1 2.8 %feature_adjoint.1 = f32[2,16,32,128]{3,2,1,0:T(8,128)} custom-call(bf16[3,18,32,256]{3,2,1,0:T(8,128)(2,1)S(1)} %get-tuple-element.112.grad_high_ref, bf16[3,18,32,256]{3,2,1,0:T(8,128)(2,1)S(1)} %get-tuple-element.113.grad_low_ref, bf16[9,256,256]{2,1,0:T(8,128)(2,1)S(1)} %get-tuple-element.87.taps_high, bf16[9,256,256]{2,1,0:T(8,128)(2,1)S(1)} %get-tuple-element.88.taps_low), custom_call_target="tpu_custom_call" | custom-call | flops 2000000000 | bytes 5000000 | tf_op jit(solution)/shard_map/feature_adjoint/pallas_call | solution.py:361
  71.9 2.0 %collective-permute-start.18 = (f32[7,24,128]{2,1,0:T(8,128)S(1)}, f32[7,24,128]{2,1,0:T(8,128)S(1)}, u32[]{:S(2)}, u32[]{:S(2)}) collective-permute-start(f32[7,24,128]{2,1,0:T(8,128)S(1)} %add.20), channel_id=1, source_target_pairs={{0,48},{16,32},{32,16},{48,0},{1,49},{17,33},{33,17},{49,1},{2,50}... | collective-permute-start | bytes 258056 | tf_op jit(solution)/shard_map/ppermute | solution.py:392
  74.0 2.8 %collective-permute-done.17 = f32[7,24,128]{2,1,0:T(8,128)S(1)} collective-permute-done((f32[7,24,128]{2,1,0:T(8,128)S(1)}, f32[7,24,128]{2,1,0:T(8,128)S(1)}, u32[]{:S(2)}, u32[]{:S(2)}) %collective-permute-start.17) | collective-permute-done | bytes 86048 | tf_op jit(solution)/shard_map/ppermute | solution.py:392
  76.9 1.5 %collective-permute-done.18 = f32[7,24,128]{2,1,0:T(8,128)S(1)} collective-permute-done((f32[7,24,128]{2,1,0:T(8,128)S(1)}, f32[7,24,128]{2,1,0:T(8,128)S(1)}, u32[]{:S(2)}, u32[]{:S(2)}) %collective-permute-start.18) | collective-permute-done | bytes 86048 | tf_op jit(solution)/shard_map/ppermute | solution.py:392
  79.3 2.9 %collective-permute-start.20 = (f32[7,24,128]{2,1,0:T(8,128)S(1)}, f32[7,24,128]{2,1,0:T(8,128)S(1)}, u32[]{:S(2)}, u32[]{:S(2)}) collective-permute-start(f32[7,24,128]{2,1,0:T(8,128)S(1)} %add_add_fusion.own_ref), channel_id=1, source_target_pairs={{0,128},{64,192},{128,0},{192,64},{1,129},{65,193},{129,1},{193,65... | collective-permute-start | bytes 258056 | tf_op jit(solution)/shard_map/ppermute | solution.py:459
  82.2 1.8 %collective-permute-start.21 = (f32[7,24,128]{2,1,0:T(8,128)S(1)}, f32[7,24,128]{2,1,0:T(8,128)S(1)}, u32[]{:S(2)}, u32[]{:S(2)}) collective-permute-start(f32[7,24,128]{2,1,0:T(8,128)S(1)} %add_add_fusion.own_ref), channel_id=1, source_target_pairs={{0,192},{64,128},{128,64},{192,0},{1,193},{65,129},{129,65},{193,1... | collective-permute-start | bytes 258056 | tf_op jit(solution)/shard_map/ppermute | solution.py:459
  84.0 1.6 %collective-permute-done.20.two_ref = f32[7,24,128]{2,1,0:T(8,128)S(1)} collective-permute-done((f32[7,24,128]{2,1,0:T(8,128)S(1)}, f32[7,24,128]{2,1,0:T(8,128)S(1)}, u32[]{:S(2)}, u32[]{:S(2)}) %collective-permute-start.20) | collective-permute-done | bytes 86048 | tf_op jit(solution)/shard_map/ppermute | solution.py:459
  85.6 2.3 %collective-permute-done.21.three_ref = f32[7,24,128]{2,1,0:T(8,128)S(1)} collective-permute-done((f32[7,24,128]{2,1,0:T(8,128)S(1)}, f32[7,24,128]{2,1,0:T(8,128)S(1)}, u32[]{:S(2)}, u32[]{:S(2)}) %collective-permute-start.21) | collective-permute-done | bytes 86048 | tf_op jit(solution)/shard_map/ppermute | solution.py:459
  (50 shorter events, 20.5 us)
Async XLA Ops:
  2.2 10.3 %collective-permute-start = (f32[2,80,128]{2,1,0:T(8,128)}, f32[2,80,128]{2,1,0:T(8,128)S(1)}, u32[]{:S(2)}, u32[]{:S(2)}) collective-permute-start(f32[2,80,128]{2,1,0:T(8,128)} %get-tuple-element.62), channel_id=1, source_target_pairs={{16,32},{32,16},{48,64},{64,48},{80,96},{96,80},{112,128},{128,112... | collective-permute-start | bytes 245768 | tf_op jit(solution)/shard_map/ppermute | solution.py:415
  9.0 4.7 %collective-permute-start.1 = (f32[2,80,128]{2,1,0:T(8,128)}, f32[2,80,128]{2,1,0:T(8,128)S(1)}, u32[]{:S(2)}, u32[]{:S(2)}) collective-permute-start(f32[2,80,128]{2,1,0:T(8,128)} %get-tuple-element.63), channel_id=1, source_target_pairs={{0,16},{16,0},{32,48},{48,32},{64,80},{80,64},{96,112},{112,96},{1... | collective-permute-start | bytes 245768 | tf_op jit(solution)/shard_map/ppermute | solution.py:415
  13.8 6.6 %collective-permute-start.2 = (f32[2,56,128]{2,1,0:T(8,128)S(1)}, f32[2,56,128]{2,1,0:T(8,128)S(1)}, u32[]{:S(2)}, u32[]{:S(2)}) collective-permute-start(f32[2,56,128]{2,1,0:T(8,128)S(1)} %get-tuple-element.74), channel_id=1, source_target_pairs={{1,2},{2,1},{3,4},{4,3},{5,6},{6,5},{7,8},{8,7},{9,10},{10,9},{11,... | collective-permute-start | bytes 172040 | tf_op jit(solution)/shard_map/ppermute | solution.py:429
  14.5 5.9 %collective-permute-start.3 = (f32[2,56,128]{2,1,0:T(8,128)S(1)}, f32[2,56,128]{2,1,0:T(8,128)S(1)}, u32[]{:S(2)}, u32[]{:S(2)}) collective-permute-start(f32[2,56,128]{2,1,0:T(8,128)S(1)} %get-tuple-element.75), channel_id=1, source_target_pairs={{0,1},{1,0},{2,3},{3,2},{4,5},{5,4},{6,7},{7,6},{8,9},{9,8},{10,11... | collective-permute-start | bytes 172040 | tf_op jit(solution)/shard_map/ppermute | solution.py:429
  20.5 1.6 %copy-start.1 = (f32[2,16,32,128]{3,2,1,0:T(8,128)S(1)}, f32[2,16,32,128]{3,2,1,0:T(8,128)}, u32[]{:S(2)}) copy-start(f32[2,16,32,128]{3,2,1,0:T(8,128)} %feat_ref.7) | copy-start | bytes 1572868
  22.0 3.9 %collective-permute-start.4 = (f32[4,4,2,7,16,128]{5,4,3,2,1,0:T(8,128)S(1)}, f32[4,4,2,7,16,128]{5,4,3,2,1,0:T(8,128)S(1)}, u32[]{:S(2)}, u32[]{:S(2)}) collective-permute-start(f32[4,4,2,7,16,128]{5,4,3,2,1,0:T(8,128)S(1)} %get-tuple-element.86), channel_id=1, source_target_pairs={{0,1},{1,0},{2,3},{3,2},{4,5},{5,4},{6,7},{7,6},{8,9},{9,8},{10,11... | collective-permute-start | bytes 5505032 | tf_op jit(solution)/shard_map/ppermute | solution.py:437
  28.2 4.6 %collective-permute-start.5 = (f32[4,4,2,7,8,128]{5,4,3,2,1,0:T(8,128)S(1)}, f32[4,4,2,7,8,128]{5,4,3,2,1,0:T(8,128)S(1)}, u32[]{:S(2)}, u32[]{:S(2)}) collective-permute-start(f32[4,4,2,7,8,128]{5,4,3,2,1,0:T(8,128)S(1)} %get-tuple-element.95), channel_id=1, source_target_pairs={{0,1},{1,0},{2,3},{3,2},{4,5},{5,4},{6,7},{7,6},{8,9},{9,8},{10,11... | collective-permute-start | bytes 2752520 | tf_op jit(solution)/shard_map/ppermute | solution.py:442
  28.6 8.6 %collective-permute-start.9 = (f32[4,2,7,16,128]{4,3,2,1,0:T(8,128)S(1)}, f32[4,2,7,16,128]{4,3,2,1,0:T(8,128)S(1)}, u32[]{:S(2)}, u32[]{:S(2)}) collective-permute-start(f32[4,2,7,16,128]{4,3,2,1,0:T(8,128)S(1)} %get-tuple-element.122), channel_id=1, source_target_pairs={{0,64},{1,3},{2,66},{3,1},{4,68},{5,7},{6,70},{7,5},{64,0},{65,67}... | collective-permute-start | bytes 1376264 | tf_op jit(solution)/shard_map/ppermute | solution.py:393
  29.2 14.6 %collective-permute-start.10 = (f32[4,2,7,16,128]{4,3,2,1,0:T(8,128)S(1)}, f32[4,2,7,16,128]{4,3,2,1,0:T(8,128)S(1)}, u32[]{:S(2)}, u32[]{:S(2)}) collective-permute-start(f32[4,2,7,16,128]{4,3,2,1,0:T(8,128)S(1)} %get-tuple-element.121), channel_id=1, source_target_pairs={{0,192},{1,7},{2,194},{3,5},{4,196},{5,3},{6,198},{7,1},{64,128},{... | collective-permute-start | bytes 1376264 | tf_op jit(solution)/shard_map/ppermute | solution.py:393
  30.4 13.4 %collective-permute-start.11 = (f32[4,2,7,16,128]{4,3,2,1,0:T(8,128)S(1)}, f32[4,2,7,16,128]{4,3,2,1,0:T(8,128)S(1)}, u32[]{:S(2)}, u32[]{:S(2)}) collective-permute-start(f32[4,2,7,16,128]{4,3,2,1,0:T(8,128)S(1)} %get-tuple-element.120), channel_id=1, source_target_pairs={{0,128},{1,5},{2,130},{3,7},{4,132},{5,1},{6,134},{7,3},{64,192},{... | collective-permute-start | bytes 1376264 | tf_op jit(solution)/shard_map/ppermute | solution.py:393
  32.8 5.6 %copy-start.5 = (f32[3,3,3,256,128]{4,3,2,1,0:T(8,128)S(1)}, f32[3,3,3,256,128]{4,3,2,1,0:T(8,128)}, u32[]{:S(2)}) copy-start(f32[3,3,3,256,128]{4,3,2,1,0:T(8,128)} %param.8) | copy-start | bytes 10616836
  32.9 11.6 %collective-permute-start.6 = (f32[4,2,7,8,128]{4,3,2,1,0:T(8,128)S(1)}, f32[4,2,7,8,128]{4,3,2,1,0:T(8,128)S(1)}, u32[]{:S(2)}, u32[]{:S(2)}) collective-permute-start(f32[4,2,7,8,128]{4,3,2,1,0:T(8,128)S(1)} %get-tuple-element.125), channel_id=1, source_target_pairs={{0,64},{1,3},{2,66},{3,1},{4,68},{5,7},{6,70},{7,5},{64,0},{65,67}... | collective-permute-start | bytes 688136 | tf_op jit(solution)/shard_map/ppermute | solution.py:393
  33.6 15.2 %collective-permute-start.7 = (f32[4,2,7,8,128]{4,3,2,1,0:T(8,128)S(1)}, f32[4,2,7,8,128]{4,3,2,1,0:T(8,128)S(1)}, u32[]{:S(2)}, u32[]{:S(2)}) collective-permute-start(f32[4,2,7,8,128]{4,3,2,1,0:T(8,128)S(1)} %get-tuple-element.124), channel_id=1, source_target_pairs={{0,192},{1,7},{2,194},{3,5},{4,196},{5,3},{6,198},{7,1},{64,128},{... | collective-permute-start | bytes 688136 | tf_op jit(solution)/shard_map/ppermute | solution.py:393
  37.2 11.6 %collective-permute-start.8 = (f32[4,2,7,8,128]{4,3,2,1,0:T(8,128)S(1)}, f32[4,2,7,8,128]{4,3,2,1,0:T(8,128)S(1)}, u32[]{:S(2)}, u32[]{:S(2)}) collective-permute-start(f32[4,2,7,8,128]{4,3,2,1,0:T(8,128)S(1)} %get-tuple-element.123), channel_id=1, source_target_pairs={{0,128},{1,5},{2,130},{3,7},{4,132},{5,1},{6,134},{7,3},{64,192},{... | collective-permute-start | bytes 688136 | tf_op jit(solution)/shard_map/ppermute | solution.py:393
  48.9 8.5 %collective-permute-start.12 = (f32[2,7,24,128]{3,2,1,0:T(8,128)S(1)}, f32[2,7,24,128]{3,2,1,0:T(8,128)S(1)}, u32[]{:S(2)}, u32[]{:S(2)}) collective-permute-start(f32[2,7,24,128]{3,2,1,0:T(8,128)S(1)} %get-tuple-element.107), channel_id=1, source_target_pairs={{0,2},{1,65},{2,0},{3,67},{4,6},{5,69},{6,4},{7,71},{64,66},{65,1}... | collective-permute-start | bytes 516104 | tf_op jit(solution)/shard_map/ppermute | solution.py:393
  50.5 10.2 %collective-permute-start.13 = (f32[2,7,24,128]{3,2,1,0:T(8,128)S(1)}, f32[2,7,24,128]{3,2,1,0:T(8,128)S(1)}, u32[]{:S(2)}, u32[]{:S(2)}) collective-permute-start(f32[2,7,24,128]{3,2,1,0:T(8,128)S(1)} %get-tuple-element.108), channel_id=1, source_target_pairs={{0,6},{1,193},{2,4},{3,195},{4,2},{5,197},{6,0},{7,199},{64,70},{6... | collective-permute-start | bytes 516104 | tf_op jit(solution)/shard_map/ppermute | solution.py:393
  56.0 6.9 %collective-permute-start.14 = (f32[2,7,24,128]{3,2,1,0:T(8,128)S(1)}, f32[2,7,24,128]{3,2,1,0:T(8,128)S(1)}, u32[]{:S(2)}, u32[]{:S(2)}) collective-permute-start(f32[2,7,24,128]{3,2,1,0:T(8,128)S(1)} %get-tuple-element.109), channel_id=1, source_target_pairs={{0,4},{1,129},{2,6},{3,131},{4,0},{5,133},{6,2},{7,135},{64,68},{6... | collective-permute-start | bytes 516104 | tf_op jit(solution)/shard_map/ppermute | solution.py:393
  62.9 7.5 %collective-permute-start.15 = (f32[7,24,128]{2,1,0:T(8,128)S(1)}, f32[7,24,128]{2,1,0:T(8,128)S(1)}, u32[]{:S(2)}, u32[]{:S(2)}) collective-permute-start(f32[7,24,128]{2,1,0:T(8,128)S(1)} %get-tuple-element.110), channel_id=1, source_target_pairs={{0,56},{8,48},{16,40},{24,32},{32,24},{40,16},{48,8},{56,0},{1,57}... | collective-permute-start | bytes 258056 | tf_op jit(solution)/shard_map/ppermute | solution.py:451
  70.5 6.4 %collective-permute-start.17 = (f32[7,24,128]{2,1,0:T(8,128)S(1)}, f32[7,24,128]{2,1,0:T(8,128)S(1)}, u32[]{:S(2)}, u32[]{:S(2)}) collective-permute-start(f32[7,24,128]{2,1,0:T(8,128)S(1)} %add.20), channel_id=1, source_target_pairs={{0,32},{16,48},{32,0},{48,16},{1,33},{17,49},{33,1},{49,17},{2,34}... | collective-permute-start | bytes 258056 | tf_op jit(solution)/shard_map/ppermute | solution.py:392
  71.9 6.5 %collective-permute-start.18 = (f32[7,24,128]{2,1,0:T(8,128)S(1)}, f32[7,24,128]{2,1,0:T(8,128)S(1)}, u32[]{:S(2)}, u32[]{:S(2)}) collective-permute-start(f32[7,24,128]{2,1,0:T(8,128)S(1)} %add.20), channel_id=1, source_target_pairs={{0,48},{16,32},{32,16},{48,0},{1,49},{17,33},{33,17},{49,1},{2,50}... | collective-permute-start | bytes 258056 | tf_op jit(solution)/shard_map/ppermute | solution.py:392
  73.9 5.3 %collective-permute-start.16 = (f32[7,24,128]{2,1,0:T(8,128)S(1)}, f32[7,24,128]{2,1,0:T(8,128)S(1)}, u32[]{:S(2)}, u32[]{:S(2)}) collective-permute-start(f32[7,24,128]{2,1,0:T(8,128)S(1)} %add.20), channel_id=1, source_target_pairs={{0,16},{16,0},{32,48},{48,32},{1,17},{17,1},{33,49},{49,33},{2,18}... | collective-permute-start | bytes 258056 | tf_op jit(solution)/shard_map/ppermute | solution.py:392
  79.2 4.8 %collective-permute-start.19 = (f32[7,24,128]{2,1,0:T(8,128)S(1)}, f32[7,24,128]{2,1,0:T(8,128)S(1)}, u32[]{:S(2)}, u32[]{:S(2)}) collective-permute-start(f32[7,24,128]{2,1,0:T(8,128)S(1)} %add_add_fusion.own_ref), channel_id=1, source_target_pairs={{0,64},{64,0},{128,192},{192,128},{1,65},{65,1},{129,193},{193,129... | collective-permute-start | bytes 258056 | tf_op jit(solution)/shard_map/ppermute | solution.py:459
  79.3 6.3 %collective-permute-start.20 = (f32[7,24,128]{2,1,0:T(8,128)S(1)}, f32[7,24,128]{2,1,0:T(8,128)S(1)}, u32[]{:S(2)}, u32[]{:S(2)}) collective-permute-start(f32[7,24,128]{2,1,0:T(8,128)S(1)} %add_add_fusion.own_ref), channel_id=1, source_target_pairs={{0,128},{64,192},{128,0},{192,64},{1,129},{65,193},{129,1},{193,65... | collective-permute-start | bytes 258056 | tf_op jit(solution)/shard_map/ppermute | solution.py:459
  82.2 5.7 %collective-permute-start.21 = (f32[7,24,128]{2,1,0:T(8,128)S(1)}, f32[7,24,128]{2,1,0:T(8,128)S(1)}, u32[]{:S(2)}, u32[]{:S(2)}) collective-permute-start(f32[7,24,128]{2,1,0:T(8,128)S(1)} %add_add_fusion.own_ref), channel_id=1, source_target_pairs={{0,192},{64,128},{128,64},{192,0},{1,193},{65,129},{129,65},{193,1... | collective-permute-start | bytes 258056 | tf_op jit(solution)/shard_map/ppermute | solution.py:459
  (4 other events, 4.4 us)

commit v10 on v7

--- a/solution.py
+++ b/solution.py
@@ -305,7 +305,7 @@
         in_specs=[space] * count,
         out_specs=(VMEM,) * len(out_shape),
         scratch_shapes=scratch,
-        compiler_params=params(24 if space is VMEM else 64),
+        compiler_params=params(24 if space is VMEM else 53),
         cost_estimate=pl.CostEstimate(flops=10**6, bytes_accessed=10**6, transcendentals=0),
         name=name,
     )

time: 88.6 us -> 89 us (level)
  starting transfers between devices: 35.9 us -> 38.6 us
  local copies, waits for them, and re-layouts: 4.53 us -> 2.09 us
  waiting for transfers between devices: 30.8 us -> 32.4 us
  Pallas kernels: 15.4 us -> 14 us
    unnamed x12 -> x10, local copies, waits for them, and re-layouts: 4.38 us -> 1.95 us
    ppermute x2, waiting for transfers between devices: 2.48 us -> 4.22 us  [local(): rows = [lax.ppermute(edges[k], HA, pairs(k)) for k in (1, 0)]]
    pallas_call x1, Pallas kernels: 1.59 us -> 0.16 us  [local(): small(row_edges_kernel, 'row_edges', edges, 2, [pltpu.VMEM((FR, 2, W, C),...]
    ppermute x9, starting transfers between devices: 13 us -> 14.1 us  [spread(): lax.ppermute(parts[k], ('x', 'y', 'core'), crossed(k, axes))]
where the time goes in v10:
time: 89 us; the launch traced here: 88.2 us
  starting transfers between devices  38.6 us (43%)
  waiting for transfers between devices  32.4 us (36%)
  Pallas kernels  14 us (16%)
  local copies, waits for them, and re-layouts  2.09 us (2%)
    ppermute x9, waiting for transfers between devices, spread(): lax.ppermute(parts[k], ('x', 'y', 'core'), crossed(k, axes))  18.6 us
    ppermute x9, starting transfers between devices, spread(): lax.ppermute(parts[k], ('x', 'y', 'core'), crossed(k, axes))  14.1 us
    ppermute x2, starting transfers between devices, local(): rows = [lax.ppermute(edges[k], HA, pairs(k)) for k in (1, 0)]  7.02 us
    ppermute x3, starting transfers between devices, spread(): return [lax.ppermute(parts[k], 'zl', swaps(k)) for k in (3, 2, 1)]  5.6 us
    pallas_call x2, Pallas kernels, adjoint(): pl.pallas_call(kernel, out_shape=jax.ShapeDtypeStruct(shape, f32), in_spe...  5.11 us
    ppermute x3, starting transfers between devices, local(): pieces = [chunk] + [lax.ppermute(chunk, 'x', swaps(k)) for k in (1, 2, 3)]  4.79 us
    ppermute x3, waiting for transfers between devices, spread(): return [lax.ppermute(parts[k], 'zl', swaps(k)) for k in (3, 2, 1)]  4.55 us
    ppermute x2, waiting for transfers between devices, local(): rows = [lax.ppermute(edges[k], HA, pairs(k)) for k in (1, 0)]  4.22 us
  transfers between devices with their start and end apart: 22, of which 15 were waited for; matrix products, arithmetic and copies ran while one was open for 0% of the time, Pallas kernels for 11%

profile of v10, /device:TPU:6, one launch (start us, length us, event | category | flops | bytes accessed | tf_op | source)
XLA Modules:
  0.0 88.2 jit_solution(12074462914298255746)
XLA Ops:
  2.7 6.9 %collective-permute-start = (f32[2,80,128]{2,1,0:T(8,128)S(1)}, f32[2,80,128]{2,1,0:T(8,128)S(1)}, u32[]{:S(2)}, u32[]{:S(2)}) collective-permute-start(f32[2,80,128]{2,1,0:T(8,128)S(1)} %get-tuple-element.62), channel_id=1, source_target_pairs={{16,32},{32,16},{48,64},{64,48},{80,96},{96,80},{112,128},{128,112... | collective-permute-start | bytes 245768 | tf_op jit(solution)/shard_map/ppermute | solution.py:415
  10.0 2.9 %collective-permute-done.row_second_ref = f32[2,80,128]{2,1,0:T(8,128)S(1)} collective-permute-done((f32[2,80,128]{2,1,0:T(8,128)S(1)}, f32[2,80,128]{2,1,0:T(8,128)S(1)}, u32[]{:S(2)}, u32[]{:S(2)}) %collective-permute-start) | collective-permute-done | bytes 81952 | tf_op jit(solution)/shard_map/ppermute | solution.py:415
  15.0 3.0 %collective-permute-start.3 = (f32[2,56,128]{2,1,0:T(8,128)S(1)}, f32[2,56,128]{2,1,0:T(8,128)S(1)}, u32[]{:S(2)}, u32[]{:S(2)}) collective-permute-start(f32[2,56,128]{2,1,0:T(8,128)S(1)} %get-tuple-element.75), channel_id=1, source_target_pairs={{0,1},{1,0},{2,3},{3,2},{4,5},{5,4},{6,7},{7,6},{8,9},{9,8},{10,11... | collective-permute-start | bytes 172040 | tf_op jit(solution)/shard_map/ppermute | solution.py:429
  18.9 1.5 %flow_terms.1 = (f32[4,4,2,7,16,128]{5,4,3,2,1,0:T(8,128)S(1)}, f32[4,4,2,7,16,128]{5,4,3,2,1,0:T(8,128)S(1)}, f32[2,10,18,128]{3,2,1,0:T(8,128)S(1)}) custom-call(bf16[512,128]{1,0:T(8,128)(2,1)S(1)} %get-tuple-element.81.flow_high, bf16[512,128]{1,0:T(8,128)(2,1)S(1)} %get-tuple-element.82.flow_low, ...), custom_call_target="tpu_custom_call" | custom-call | flops 2000000000 | bytes 5000000 | tf_op jit(solution)/shard_map/flow_terms/pallas_call | solution.py:315
  21.3 3.5 %block_gradient.1 = (bf16[3,18,32,256]{3,2,1,0:T(8,128)(2,1)S(1)}, bf16[3,18,32,256]{3,2,1,0:T(8,128)(2,1)S(1)}) custom-call(f32[2,16,32,128]{3,2,1,0:T(8,128)S(1)} %copy-done, f32[2,80,128]{2,1,0:T(8,128)S(1)} %collective-permute-done.row_second_ref, f32[2,80,128]{2,1,0:T(8,128)S(1)} %collective-permute-done.1.row_first_ref, ...), custom_call_target="tpu_custom_call" | custom-call | flops 5000000000 | bytes 6000000 | tf_op jit(solution)/shard_map/block_gradient/pallas_call | solution.py:328
  25.1 2.1 %block_terms.1 = (f32[4,4,2,7,8,128]{5,4,3,2,1,0:T(8,128)S(1)}, f32[4,4,2,7,8,128]{5,4,3,2,1,0:T(8,128)S(1)}) custom-call(bf16[256,512]{1,0:T(8,128)(2,1)S(1)} %get-tuple-element.67.feat_high, bf16[256,512]{1,0:T(8,128)(2,1)S(1)} %get-tuple-element.68.feat_low, bf16[3,18,32,256]{3,2,1,0:T(8,128)(2,1)S(1)} %get-tuple-element.112.grad_high_ref, ...), custom_call_target="tpu_custom_call" | custom-call | flops 1000000000 | bytes 1000000 | tf_op jit(solution)/shard_map/block_terms/pallas_call | solution.py:349
  28.9 2.9 %collective-permute-start.11 = (f32[4,2,7,16,128]{4,3,2,1,0:T(8,128)S(1)}, f32[4,2,7,16,128]{4,3,2,1,0:T(8,128)S(1)}, u32[]{:S(2)}, u32[]{:S(2)}) collective-permute-start(f32[4,2,7,16,128]{4,3,2,1,0:T(8,128)S(1)} %get-tuple-element.120), channel_id=1, source_target_pairs={{0,192},{1,7},{2,194},{3,5},{4,196},{5,3},{6,198},{7,1},{64,128},{... | collective-permute-start | bytes 1376264 | tf_op jit(solution)/shard_map/ppermute | solution.py:393
  33.2 4.6 %collective-permute-done.9.refs_5_ = f32[4,2,7,16,128]{4,3,2,1,0:T(8,128)S(1)} collective-permute-done((f32[4,2,7,16,128]{4,3,2,1,0:T(8,128)S(1)}, f32[4,2,7,16,128]{4,3,2,1,0:T(8,128)S(1)}, u32[]{:S(2)}, u32[]{:S(2)}) %collective-permute-start.9) | collective-permute-done | bytes 458784 | tf_op jit(solution)/shard_map/ppermute | solution.py:393
  37.8 2.3 %flow_adjoint.1 = f32[2,8,16,256]{3,2,1,0:T(8,128)} custom-call(f32[2,10,18,128]{3,2,1,0:T(8,128)S(1)} %get-tuple-element.98.cot_ref, f32[27,256,128]{2,1,0:T(8,128)S(1)} %bitcast.17), custom_call_target="tpu_custom_call" | custom-call | flops 2000000000 | bytes 5000000 | tf_op jit(solution)/shard_map/flow_adjoint/pallas_call | solution.py:361
  40.1 2.5 %collective-permute-done.11.refs_7_ = f32[4,2,7,16,128]{4,3,2,1,0:T(8,128)S(1)} collective-permute-done((f32[4,2,7,16,128]{4,3,2,1,0:T(8,128)S(1)}, f32[4,2,7,16,128]{4,3,2,1,0:T(8,128)S(1)}, u32[]{:S(2)}, u32[]{:S(2)}) %collective-permute-start.11) | collective-permute-done | bytes 458784 | tf_op jit(solution)/shard_map/ppermute | solution.py:393
  42.6 2.6 %collective-permute-done.6.refs_1_ = f32[4,2,7,8,128]{4,3,2,1,0:T(8,128)S(1)} collective-permute-done((f32[4,2,7,8,128]{4,3,2,1,0:T(8,128)S(1)}, f32[4,2,7,8,128]{4,3,2,1,0:T(8,128)S(1)}, u32[]{:S(2)}, u32[]{:S(2)}) %collective-permute-start.6) | collective-permute-done | bytes 229408 | tf_op jit(solution)/shard_map/ppermute | solution.py:393
  45.2 2.3 %collective-permute-done.8.refs_3_ = f32[4,2,7,8,128]{4,3,2,1,0:T(8,128)S(1)} collective-permute-done((f32[4,2,7,8,128]{4,3,2,1,0:T(8,128)S(1)}, f32[4,2,7,8,128]{4,3,2,1,0:T(8,128)S(1)}, u32[]{:S(2)}, u32[]{:S(2)}) %collective-permute-start.8) | collective-permute-done | bytes 229408 | tf_op jit(solution)/shard_map/ppermute | solution.py:393
  47.7 3.5 %collective-permute-start.12 = (f32[2,7,24,128]{3,2,1,0:T(8,128)S(1)}, f32[2,7,24,128]{3,2,1,0:T(8,128)S(1)}, u32[]{:S(2)}, u32[]{:S(2)}) collective-permute-start(f32[2,7,24,128]{3,2,1,0:T(8,128)S(1)} %get-tuple-element.107), channel_id=1, source_target_pairs={{0,4},{1,129},{2,6},{3,131},{4,0},{5,133},{6,2},{7,135},{64,68},{6... | collective-permute-start | bytes 516104 | tf_op jit(solution)/shard_map/ppermute | solution.py:393
  51.2 5.2 %collective-permute-start.13 = (f32[2,7,24,128]{3,2,1,0:T(8,128)S(1)}, f32[2,7,24,128]{3,2,1,0:T(8,128)S(1)}, u32[]{:S(2)}, u32[]{:S(2)}) collective-permute-start(f32[2,7,24,128]{3,2,1,0:T(8,128)S(1)} %get-tuple-element.108), channel_id=1, source_target_pairs={{0,2},{1,65},{2,0},{3,67},{4,6},{5,69},{6,4},{7,71},{64,66},{65,1}... | collective-permute-start | bytes 516104 | tf_op jit(solution)/shard_map/ppermute | solution.py:393
  56.4 5.2 %collective-permute-done.13.first = f32[2,7,24,128]{3,2,1,0:T(8,128)S(1)} collective-permute-done((f32[2,7,24,128]{3,2,1,0:T(8,128)S(1)}, f32[2,7,24,128]{3,2,1,0:T(8,128)S(1)}, u32[]{:S(2)}, u32[]{:S(2)}) %collective-permute-start.13) | collective-permute-done | bytes 172064 | tf_op jit(solution)/shard_map/ppermute | solution.py:393
  63.0 2.0 %collective-permute-start.15 = (f32[7,24,128]{2,1,0:T(8,128)S(1)}, f32[7,24,128]{2,1,0:T(8,128)S(1)}, u32[]{:S(2)}, u32[]{:S(2)}) collective-permute-start(f32[7,24,128]{2,1,0:T(8,128)S(1)} %get-tuple-element.110), channel_id=1, source_target_pairs={{0,56},{8,48},{16,40},{24,32},{32,24},{40,16},{48,8},{56,0},{1,57}... | collective-permute-start | bytes 258056 | tf_op jit(solution)/shard_map/ppermute | solution.py:451
  65.0 2.8 %feature_adjoint.1 = f32[2,16,32,128]{3,2,1,0:T(8,128)} custom-call(bf16[3,18,32,256]{3,2,1,0:T(8,128)(2,1)S(1)} %get-tuple-element.112.grad_high_ref, bf16[3,18,32,256]{3,2,1,0:T(8,128)(2,1)S(1)} %get-tuple-element.113.grad_low_ref, bf16[9,256,256]{2,1,0:T(8,128)(2,1)S(1)} %get-tuple-element.87.taps_high, bf16[9,256,256]{2,1,0:T(8,128)(2,1)S(1)} %get-tuple-element.88.taps_low), custom_call_target="tpu_custom_call" | custom-call | flops 2000000000 | bytes 5000000 | tf_op jit(solution)/shard_map/feature_adjoint/pallas_call | solution.py:361
  68.8 2.9 %collective-permute-start.17 = (f32[7,24,128]{2,1,0:T(8,128)S(1)}, f32[7,24,128]{2,1,0:T(8,128)S(1)}, u32[]{:S(2)}, u32[]{:S(2)}) collective-permute-start(f32[7,24,128]{2,1,0:T(8,128)S(1)} %add.20), channel_id=1, source_target_pairs={{0,32},{16,48},{32,0},{48,16},{1,33},{17,49},{33,1},{49,17},{2,34}... | collective-permute-start | bytes 258056 | tf_op jit(solution)/shard_map/ppermute | solution.py:392
  71.7 2.7 %collective-permute-start.18 = (f32[7,24,128]{2,1,0:T(8,128)S(1)}, f32[7,24,128]{2,1,0:T(8,128)S(1)}, u32[]{:S(2)}, u32[]{:S(2)}) collective-permute-start(f32[7,24,128]{2,1,0:T(8,128)S(1)} %add.20), channel_id=1, source_target_pairs={{0,48},{16,32},{32,16},{48,0},{1,49},{17,33},{33,17},{49,1},{2,50}... | collective-permute-start | bytes 258056 | tf_op jit(solution)/shard_map/ppermute | solution.py:392
  75.6 2.5 %collective-permute-done.18 = f32[7,24,128]{2,1,0:T(8,128)S(1)} collective-permute-done((f32[7,24,128]{2,1,0:T(8,128)S(1)}, f32[7,24,128]{2,1,0:T(8,128)S(1)}, u32[]{:S(2)}, u32[]{:S(2)}) %collective-permute-start.18) | collective-permute-done | bytes 86048 | tf_op jit(solution)/shard_map/ppermute | solution.py:392
  79.9 1.9 %collective-permute-start.20 = (f32[7,24,128]{2,1,0:T(8,128)S(1)}, f32[7,24,128]{2,1,0:T(8,128)S(1)}, u32[]{:S(2)}, u32[]{:S(2)}) collective-permute-start(f32[7,24,128]{2,1,0:T(8,128)S(1)} %add_add_fusion.own_ref), channel_id=1, source_target_pairs={{0,128},{64,192},{128,0},{192,64},{1,129},{65,193},{129,1},{193,65... | collective-permute-start | bytes 258056 | tf_op jit(solution)/shard_map/ppermute | solution.py:459
  81.8 2.0 %collective-permute-start.21 = (f32[7,24,128]{2,1,0:T(8,128)S(1)}, f32[7,24,128]{2,1,0:T(8,128)S(1)}, u32[]{:S(2)}, u32[]{:S(2)}) collective-permute-start(f32[7,24,128]{2,1,0:T(8,128)S(1)} %add_add_fusion.own_ref), channel_id=1, source_target_pairs={{0,192},{64,128},{128,64},{192,0},{1,193},{65,129},{129,65},{193,1... | collective-permute-start | bytes 258056 | tf_op jit(solution)/shard_map/ppermute | solution.py:459
  83.8 2.1 %collective-permute-done.20.two_ref = f32[7,24,128]{2,1,0:T(8,128)S(1)} collective-permute-done((f32[7,24,128]{2,1,0:T(8,128)S(1)}, f32[7,24,128]{2,1,0:T(8,128)S(1)}, u32[]{:S(2)}, u32[]{:S(2)}) %collective-permute-start.20) | collective-permute-done | bytes 86048 | tf_op jit(solution)/shard_map/ppermute | solution.py:459
  85.9 1.6 %collective-permute-done.21.three_ref = f32[7,24,128]{2,1,0:T(8,128)S(1)} collective-permute-done((f32[7,24,128]{2,1,0:T(8,128)S(1)}, f32[7,24,128]{2,1,0:T(8,128)S(1)}, u32[]{:S(2)}, u32[]{:S(2)}) %collective-permute-start.21) | collective-permute-done | bytes 86048 | tf_op jit(solution)/shard_map/ppermute | solution.py:459
  (48 shorter events, 15.9 us)
Async XLA Ops:
  2.6 15.4 %copy-start.1 = (f32[3,3,3,128,128]{4,3,2,1,0:T(8,128)S(1)}, f32[3,3,3,128,128]{4,3,2,1,0:T(8,128)}, u32[]{:S(2)}) copy-start(f32[3,3,3,128,128]{4,3,2,1,0:T(8,128)} %param.6) | copy-start | bytes 5308420
  2.6 15.4 %copy-start.3 = (f32[2,8,16,256]{3,2,1,0:T(8,128)S(1)}, f32[2,8,16,256]{3,2,1,0:T(8,128)}, u32[]{:S(2)}) copy-start(f32[2,8,16,256]{3,2,1,0:T(8,128)} %flow_ref) | copy-start | bytes 786436
  2.7 10.2 %collective-permute-start = (f32[2,80,128]{2,1,0:T(8,128)S(1)}, f32[2,80,128]{2,1,0:T(8,128)S(1)}, u32[]{:S(2)}, u32[]{:S(2)}) collective-permute-start(f32[2,80,128]{2,1,0:T(8,128)S(1)} %get-tuple-element.62), channel_id=1, source_target_pairs={{16,32},{32,16},{48,64},{64,48},{80,96},{96,80},{112,128},{128,112... | collective-permute-start | bytes 245768 | tf_op jit(solution)/shard_map/ppermute | solution.py:415
  9.7 4.5 %collective-permute-start.1 = (f32[2,80,128]{2,1,0:T(8,128)S(1)}, f32[2,80,128]{2,1,0:T(8,128)S(1)}, u32[]{:S(2)}, u32[]{:S(2)}) collective-permute-start(f32[2,80,128]{2,1,0:T(8,128)S(1)} %get-tuple-element.63), channel_id=1, source_target_pairs={{0,16},{16,0},{32,48},{48,32},{64,80},{80,64},{96,112},{112,96},{1... | collective-permute-start | bytes 245768 | tf_op jit(solution)/shard_map/ppermute | solution.py:415
  14.3 4.2 %collective-permute-start.2 = (f32[2,56,128]{2,1,0:T(8,128)S(1)}, f32[2,56,128]{2,1,0:T(8,128)S(1)}, u32[]{:S(2)}, u32[]{:S(2)}) collective-permute-start(f32[2,56,128]{2,1,0:T(8,128)S(1)} %get-tuple-element.74), channel_id=1, source_target_pairs={{1,2},{2,1},{3,4},{4,3},{5,6},{6,5},{7,8},{8,7},{9,10},{10,9},{11,... | collective-permute-start | bytes 172040 | tf_op jit(solution)/shard_map/ppermute | solution.py:429
  15.0 3.9 %collective-permute-start.3 = (f32[2,56,128]{2,1,0:T(8,128)S(1)}, f32[2,56,128]{2,1,0:T(8,128)S(1)}, u32[]{:S(2)}, u32[]{:S(2)}) collective-permute-start(f32[2,56,128]{2,1,0:T(8,128)S(1)} %get-tuple-element.75), channel_id=1, source_target_pairs={{0,1},{1,0},{2,3},{3,2},{4,5},{5,4},{6,7},{7,6},{8,9},{9,8},{10,11... | collective-permute-start | bytes 172040 | tf_op jit(solution)/shard_map/ppermute | solution.py:429
  20.3 4.4 %collective-permute-start.4 = (f32[4,4,2,7,16,128]{5,4,3,2,1,0:T(8,128)S(1)}, f32[4,4,2,7,16,128]{5,4,3,2,1,0:T(8,128)S(1)}, u32[]{:S(2)}, u32[]{:S(2)}) collective-permute-start(f32[4,4,2,7,16,128]{5,4,3,2,1,0:T(8,128)S(1)} %get-tuple-element.86), channel_id=1, source_target_pairs={{0,1},{1,0},{2,3},{3,2},{4,5},{5,4},{6,7},{7,6},{8,9},{9,8},{10,11... | collective-permute-start | bytes 5505032 | tf_op jit(solution)/shard_map/ppermute | solution.py:437
  27.1 4.7 %collective-permute-start.5 = (f32[4,4,2,7,8,128]{5,4,3,2,1,0:T(8,128)S(1)}, f32[4,4,2,7,8,128]{5,4,3,2,1,0:T(8,128)S(1)}, u32[]{:S(2)}, u32[]{:S(2)}) collective-permute-start(f32[4,4,2,7,8,128]{5,4,3,2,1,0:T(8,128)S(1)} %get-tuple-element.95), channel_id=1, source_target_pairs={{0,1},{1,0},{2,3},{3,2},{4,5},{5,4},{6,7},{7,6},{8,9},{9,8},{10,11... | collective-permute-start | bytes 2752520 | tf_op jit(solution)/shard_map/ppermute | solution.py:442
  27.6 10.2 %collective-permute-start.9 = (f32[4,2,7,16,128]{4,3,2,1,0:T(8,128)S(1)}, f32[4,2,7,16,128]{4,3,2,1,0:T(8,128)S(1)}, u32[]{:S(2)}, u32[]{:S(2)}) collective-permute-start(f32[4,2,7,16,128]{4,3,2,1,0:T(8,128)S(1)} %get-tuple-element.122), channel_id=1, source_target_pairs={{0,128},{1,5},{2,130},{3,7},{4,132},{5,1},{6,134},{7,3},{64,192},{... | collective-permute-start | bytes 1376264 | tf_op jit(solution)/shard_map/ppermute | solution.py:393
  28.9 11.2 %collective-permute-start.10 = (f32[4,2,7,16,128]{4,3,2,1,0:T(8,128)S(1)}, f32[4,2,7,16,128]{4,3,2,1,0:T(8,128)S(1)}, u32[]{:S(2)}, u32[]{:S(2)}) collective-permute-start(f32[4,2,7,16,128]{4,3,2,1,0:T(8,128)S(1)} %get-tuple-element.121), channel_id=1, source_target_pairs={{0,64},{1,3},{2,66},{3,1},{4,68},{5,7},{6,70},{7,5},{64,0},{65,67}... | collective-permute-start | bytes 1376264 | tf_op jit(solution)/shard_map/ppermute | solution.py:393
  28.9 13.7 %collective-permute-start.11 = (f32[4,2,7,16,128]{4,3,2,1,0:T(8,128)S(1)}, f32[4,2,7,16,128]{4,3,2,1,0:T(8,128)S(1)}, u32[]{:S(2)}, u32[]{:S(2)}) collective-permute-start(f32[4,2,7,16,128]{4,3,2,1,0:T(8,128)S(1)} %get-tuple-element.120), channel_id=1, source_target_pairs={{0,192},{1,7},{2,194},{3,5},{4,196},{5,3},{6,198},{7,1},{64,128},{... | collective-permute-start | bytes 1376264 | tf_op jit(solution)/shard_map/ppermute | solution.py:393
  32.0 13.2 %collective-permute-start.6 = (f32[4,2,7,8,128]{4,3,2,1,0:T(8,128)S(1)}, f32[4,2,7,8,128]{4,3,2,1,0:T(8,128)S(1)}, u32[]{:S(2)}, u32[]{:S(2)}) collective-permute-start(f32[4,2,7,8,128]{4,3,2,1,0:T(8,128)S(1)} %get-tuple-element.125), channel_id=1, source_target_pairs={{0,128},{1,5},{2,130},{3,7},{4,132},{5,1},{6,134},{7,3},{64,192},{... | collective-permute-start | bytes 688136 | tf_op jit(solution)/shard_map/ppermute | solution.py:393
  33.2 12.0 %collective-permute-start.7 = (f32[4,2,7,8,128]{4,3,2,1,0:T(8,128)S(1)}, f32[4,2,7,8,128]{4,3,2,1,0:T(8,128)S(1)}, u32[]{:S(2)}, u32[]{:S(2)}) collective-permute-start(f32[4,2,7,8,128]{4,3,2,1,0:T(8,128)S(1)} %get-tuple-element.124), channel_id=1, source_target_pairs={{0,64},{1,3},{2,66},{3,1},{4,68},{5,7},{6,70},{7,5},{64,0},{65,67}... | collective-permute-start | bytes 688136 | tf_op jit(solution)/shard_map/ppermute | solution.py:393
  37.8 9.7 %collective-permute-start.8 = (f32[4,2,7,8,128]{4,3,2,1,0:T(8,128)S(1)}, f32[4,2,7,8,128]{4,3,2,1,0:T(8,128)S(1)}, u32[]{:S(2)}, u32[]{:S(2)}) collective-permute-start(f32[4,2,7,8,128]{4,3,2,1,0:T(8,128)S(1)} %get-tuple-element.123), channel_id=1, source_target_pairs={{0,192},{1,7},{2,194},{3,5},{4,196},{5,3},{6,198},{7,1},{64,128},{... | collective-permute-start | bytes 688136 | tf_op jit(solution)/shard_map/ppermute | solution.py:393
  47.7 8.7 %collective-permute-start.12 = (f32[2,7,24,128]{3,2,1,0:T(8,128)S(1)}, f32[2,7,24,128]{3,2,1,0:T(8,128)S(1)}, u32[]{:S(2)}, u32[]{:S(2)}) collective-permute-start(f32[2,7,24,128]{3,2,1,0:T(8,128)S(1)} %get-tuple-element.107), channel_id=1, source_target_pairs={{0,4},{1,129},{2,6},{3,131},{4,0},{5,133},{6,2},{7,135},{64,68},{6... | collective-permute-start | bytes 516104 | tf_op jit(solution)/shard_map/ppermute | solution.py:393
  51.2 10.4 %collective-permute-start.13 = (f32[2,7,24,128]{3,2,1,0:T(8,128)S(1)}, f32[2,7,24,128]{3,2,1,0:T(8,128)S(1)}, u32[]{:S(2)}, u32[]{:S(2)}) collective-permute-start(f32[2,7,24,128]{3,2,1,0:T(8,128)S(1)} %get-tuple-element.108), channel_id=1, source_target_pairs={{0,2},{1,65},{2,0},{3,67},{4,6},{5,69},{6,4},{7,71},{64,66},{65,1}... | collective-permute-start | bytes 516104 | tf_op jit(solution)/shard_map/ppermute | solution.py:393
  56.4 6.6 %collective-permute-start.14 = (f32[2,7,24,128]{3,2,1,0:T(8,128)S(1)}, f32[2,7,24,128]{3,2,1,0:T(8,128)S(1)}, u32[]{:S(2)}, u32[]{:S(2)}) collective-permute-start(f32[2,7,24,128]{3,2,1,0:T(8,128)S(1)} %get-tuple-element.109), channel_id=1, source_target_pairs={{0,6},{1,193},{2,4},{3,195},{4,2},{5,197},{6,0},{7,199},{64,70},{6... | collective-permute-start | bytes 516104 | tf_op jit(solution)/shard_map/ppermute | solution.py:393
  63.0 5.8 %collective-permute-start.15 = (f32[7,24,128]{2,1,0:T(8,128)S(1)}, f32[7,24,128]{2,1,0:T(8,128)S(1)}, u32[]{:S(2)}, u32[]{:S(2)}) collective-permute-start(f32[7,24,128]{2,1,0:T(8,128)S(1)} %get-tuple-element.110), channel_id=1, source_target_pairs={{0,56},{8,48},{16,40},{24,32},{32,24},{40,16},{48,8},{56,0},{1,57}... | collective-permute-start | bytes 258056 | tf_op jit(solution)/shard_map/ppermute | solution.py:451
  68.8 6.8 %collective-permute-start.17 = (f32[7,24,128]{2,1,0:T(8,128)S(1)}, f32[7,24,128]{2,1,0:T(8,128)S(1)}, u32[]{:S(2)}, u32[]{:S(2)}) collective-permute-start(f32[7,24,128]{2,1,0:T(8,128)S(1)} %add.20), channel_id=1, source_target_pairs={{0,32},{16,48},{32,0},{48,16},{1,33},{17,49},{33,1},{49,17},{2,34}... | collective-permute-start | bytes 258056 | tf_op jit(solution)/shard_map/ppermute | solution.py:392
  71.7 6.3 %collective-permute-start.18 = (f32[7,24,128]{2,1,0:T(8,128)S(1)}, f32[7,24,128]{2,1,0:T(8,128)S(1)}, u32[]{:S(2)}, u32[]{:S(2)}) collective-permute-start(f32[7,24,128]{2,1,0:T(8,128)S(1)} %add.20), channel_id=1, source_target_pairs={{0,48},{16,32},{32,16},{48,0},{1,49},{17,33},{33,17},{49,1},{2,50}... | collective-permute-start | bytes 258056 | tf_op jit(solution)/shard_map/ppermute | solution.py:392
  74.4 4.6 %collective-permute-start.16 = (f32[7,24,128]{2,1,0:T(8,128)S(1)}, f32[7,24,128]{2,1,0:T(8,128)S(1)}, u32[]{:S(2)}, u32[]{:S(2)}) collective-permute-start(f32[7,24,128]{2,1,0:T(8,128)S(1)} %add.20), channel_id=1, source_target_pairs={{0,16},{16,0},{32,48},{48,32},{1,17},{17,1},{33,49},{49,33},{2,18}... | collective-permute-start | bytes 258056 | tf_op jit(solution)/shard_map/ppermute | solution.py:392
  79.0 4.8 %collective-permute-start.19 = (f32[7,24,128]{2,1,0:T(8,128)S(1)}, f32[7,24,128]{2,1,0:T(8,128)S(1)}, u32[]{:S(2)}, u32[]{:S(2)}) collective-permute-start(f32[7,24,128]{2,1,0:T(8,128)S(1)} %add_add_fusion.own_ref), channel_id=1, source_target_pairs={{0,64},{64,0},{128,192},{192,128},{1,65},{65,1},{129,193},{193,129... | collective-permute-start | bytes 258056 | tf_op jit(solution)/shard_map/ppermute | solution.py:459
  79.9 6.0 %collective-permute-start.20 = (f32[7,24,128]{2,1,0:T(8,128)S(1)}, f32[7,24,128]{2,1,0:T(8,128)S(1)}, u32[]{:S(2)}, u32[]{:S(2)}) collective-permute-start(f32[7,24,128]{2,1,0:T(8,128)S(1)} %add_add_fusion.own_ref), channel_id=1, source_target_pairs={{0,128},{64,192},{128,0},{192,64},{1,129},{65,193},{129,1},{193,65... | collective-permute-start | bytes 258056 | tf_op jit(solution)/shard_map/ppermute | solution.py:459
  81.8 5.7 %collective-permute-start.21 = (f32[7,24,128]{2,1,0:T(8,128)S(1)}, f32[7,24,128]{2,1,0:T(8,128)S(1)}, u32[]{:S(2)}, u32[]{:S(2)}) collective-permute-start(f32[7,24,128]{2,1,0:T(8,128)S(1)} %add_add_fusion.own_ref), channel_id=1, source_target_pairs={{0,192},{64,128},{128,64},{192,0},{1,193},{65,129},{129,65},{193,1... | collective-permute-start | bytes 258056 | tf_op jit(solution)/shard_map/ppermute | solution.py:459
  (3 other events, 7.9 us)

commit v11 on v7

--- a/solution.py
+++ b/solution.py
@@ -279,7 +279,7 @@
     send[...] = (own[1] + second[1]) + (first[1] + third[1])
 
 
-def gather_kernel(own_ref, one_ref, two_ref, three_ref, grad_one_ref, grad_two_ref):
+def gather_kernel(own_ref, two_ref, one_ref, three_ref, grad_one_ref, grad_two_ref):
     scale_one = 1.0 / (FR * R * W * 256) ** 0.5
     scale_two = 1.0 / (FR * R2 * W2 * 256) ** 0.5
     for k, ref in enumerate((own_ref, one_ref, two_ref, three_ref)):
@@ -456,7 +456,7 @@
     arrived, grad_features = lax.optimization_barrier((arrived, grad_features))
     chunk = keep + arrived
     chunk = summed(chunk, spread([chunk] * 4, "zl"))
-    pieces = [chunk] + [lax.ppermute(chunk, "x", swaps(k)) for k in (1, 2, 3)]
+    pieces = [chunk] + [lax.ppermute(chunk, "x", swaps(k)) for k in (2, 1, 3)]
     shares = tuple(jax.ShapeDtypeStruct((27, depth, C), f32) for depth in (8, 16))
     grad_one, grad_two = small(gather_kernel, "gather", shares, 4)(*pieces)
     grad_one = grad_one.reshape(3, 3, 3, 8, C)

time: 88.6 us -> 88.3 us (level)
  transfers between devices with their start and end apart: 22 -> 22, of which waited for: 15 -> 16; matrix products, arithmetic and copies ran while one was open for 0% -> 0% of each run, Pallas kernels for 11% -> 11%
where the time goes in v11:
time: 88.3 us; the launch traced here: 87.3 us
  starting transfers between devices  35.3 us (40%)
  waiting for transfers between devices  30.9 us (35%)
  Pallas kernels  15.4 us (17%)
  local copies, waits for them, and re-layouts  4.53 us (5%)
    ppermute x9, waiting for transfers between devices, spread(): lax.ppermute(parts[k], ('x', 'y', 'core'), crossed(k, axes))  18.6 us
    ppermute x9, starting transfers between devices, spread(): lax.ppermute(parts[k], ('x', 'y', 'core'), crossed(k, axes))  13 us
    ppermute x2, starting transfers between devices, local(): rows = [lax.ppermute(edges[k], HA, pairs(k)) for k in (1, 0)]  6.89 us
    ppermute x3, starting transfers between devices, spread(): return [lax.ppermute(parts[k], 'zl', swaps(k)) for k in (3, 2, 1)]  5.35 us
    pallas_call x2, Pallas kernels, adjoint(): pl.pallas_call(kernel, out_shape=jax.ShapeDtypeStruct(shape, f32), in_spe...  5.12 us
    ppermute x3, waiting for transfers between devices, spread(): return [lax.ppermute(parts[k], 'zl', swaps(k)) for k in (3, 2, 1)]  4.55 us
    unnamed x12, local copies, waits for them, and re-layouts  4.38 us
    ppermute x3, starting transfers between devices, local(): pieces = [chunk] + [lax.ppermute(chunk, 'x', swaps(k)) for k in (2, 1, 3)]  4.18 us
  transfers between devices with their start and end apart: 22, of which 16 were waited for; matrix products, arithmetic and copies ran while one was open for 0% of the time, Pallas kernels for 11%

profile of v11, /device:TPU:6, one launch (start us, length us, event | category | flops | bytes accessed | tf_op | source)
XLA Modules:
  0.0 87.3 jit_solution(8639317649075137612)
XLA Ops:
  0.6 1.6 %row_edges.1 = (f32[2,80,128]{2,1,0:T(8,128)}, f32[2,80,128]{2,1,0:T(8,128)}) custom-call(f32[2,16,32,128]{3,2,1,0:T(8,128)} %feat_ref.7, f32[2,8,16,128]{3,2,1,0:T(8,128)} %cot_ref.3), custom_call_target="tpu_custom_call" | custom-call | flops 1000000 | bytes 1000000 | tf_op jit(solution)/shard_map/row_edges/pallas_call | solution.py:405
  2.2 6.8 %collective-permute-start = (f32[2,80,128]{2,1,0:T(8,128)}, f32[2,80,128]{2,1,0:T(8,128)S(1)}, u32[]{:S(2)}, u32[]{:S(2)}) collective-permute-start(f32[2,80,128]{2,1,0:T(8,128)} %get-tuple-element.62), channel_id=1, source_target_pairs={{16,32},{32,16},{48,64},{64,48},{80,96},{96,80},{112,128},{128,112... | collective-permute-start | bytes 245768 | tf_op jit(solution)/shard_map/ppermute | solution.py:415
  14.5 3.0 %collective-permute-start.3 = (f32[2,56,128]{2,1,0:T(8,128)S(1)}, f32[2,56,128]{2,1,0:T(8,128)S(1)}, u32[]{:S(2)}, u32[]{:S(2)}) collective-permute-start(f32[2,56,128]{2,1,0:T(8,128)S(1)} %get-tuple-element.75), channel_id=1, source_target_pairs={{0,1},{1,0},{2,3},{3,2},{4,5},{5,4},{6,7},{7,6},{8,9},{9,8},{10,11... | collective-permute-start | bytes 172040 | tf_op jit(solution)/shard_map/ppermute | solution.py:429
  17.5 1.5 %copy-done.2 = f32[3,3,3,128,128]{4,3,2,1,0:T(8,128)S(1)} copy-done((f32[3,3,3,128,128]{4,3,2,1,0:T(8,128)S(1)}, f32[3,3,3,128,128]{4,3,2,1,0:T(8,128)}, u32[]{:S(2)}) %copy-start.2) | copy-done | bytes 1769496
  20.5 1.5 %flow_terms.1 = (f32[4,4,2,7,16,128]{5,4,3,2,1,0:T(8,128)S(1)}, f32[4,4,2,7,16,128]{5,4,3,2,1,0:T(8,128)S(1)}, f32[2,10,18,128]{3,2,1,0:T(8,128)S(1)}) custom-call(bf16[512,128]{1,0:T(8,128)(2,1)S(1)} %get-tuple-element.81.flow_high, bf16[512,128]{1,0:T(8,128)(2,1)S(1)} %get-tuple-element.82.flow_low, ...), custom_call_target="tpu_custom_call" | custom-call | flops 2000000000 | bytes 5000000 | tf_op jit(solution)/shard_map/flow_terms/pallas_call | solution.py:315
  22.1 3.5 %block_gradient.1 = (bf16[3,18,32,256]{3,2,1,0:T(8,128)(2,1)S(1)}, bf16[3,18,32,256]{3,2,1,0:T(8,128)(2,1)S(1)}) custom-call(f32[2,16,32,128]{3,2,1,0:T(8,128)S(1)} %copy-done.1, f32[2,80,128]{2,1,0:T(8,128)S(1)} %collective-permute-done.row_second_ref, f32[2,80,128]{2,1,0:T(8,128)S(1)} %collective-permute-done.1.row_first_ref, ...), custom_call_target="tpu_custom_call" | custom-call | flops 5000000000 | bytes 6000000 | tf_op jit(solution)/shard_map/block_gradient/pallas_call | solution.py:328
  26.1 2.1 %block_terms.1 = (f32[4,4,2,7,8,128]{5,4,3,2,1,0:T(8,128)S(1)}, f32[4,4,2,7,8,128]{5,4,3,2,1,0:T(8,128)S(1)}) custom-call(bf16[256,512]{1,0:T(8,128)(2,1)S(1)} %get-tuple-element.67.feat_high, bf16[256,512]{1,0:T(8,128)(2,1)S(1)} %get-tuple-element.68.feat_low, bf16[3,18,32,256]{3,2,1,0:T(8,128)(2,1)S(1)} %get-tuple-element.112.grad_high_ref, ...), custom_call_target="tpu_custom_call" | custom-call | flops 1000000000 | bytes 1000000 | tf_op jit(solution)/shard_map/block_terms/pallas_call | solution.py:349
  29.9 2.9 %collective-permute-start.11 = (f32[4,2,7,16,128]{4,3,2,1,0:T(8,128)S(1)}, f32[4,2,7,16,128]{4,3,2,1,0:T(8,128)S(1)}, u32[]{:S(2)}, u32[]{:S(2)}) collective-permute-start(f32[4,2,7,16,128]{4,3,2,1,0:T(8,128)S(1)} %get-tuple-element.120), channel_id=1, source_target_pairs={{0,192},{1,7},{2,194},{3,5},{4,196},{5,3},{6,198},{7,1},{64,128},{... | collective-permute-start | bytes 1376264 | tf_op jit(solution)/shard_map/ppermute | solution.py:393
  34.2 4.6 %collective-permute-done.9.refs_5_ = f32[4,2,7,16,128]{4,3,2,1,0:T(8,128)S(1)} collective-permute-done((f32[4,2,7,16,128]{4,3,2,1,0:T(8,128)S(1)}, f32[4,2,7,16,128]{4,3,2,1,0:T(8,128)S(1)}, u32[]{:S(2)}, u32[]{:S(2)}) %collective-permute-start.9) | collective-permute-done | bytes 458784 | tf_op jit(solution)/shard_map/ppermute | solution.py:393
  38.8 2.3 %flow_adjoint.1 = f32[2,8,16,256]{3,2,1,0:T(8,128)} custom-call(f32[2,10,18,128]{3,2,1,0:T(8,128)S(1)} %get-tuple-element.98.cot_ref, f32[27,256,128]{2,1,0:T(8,128)S(1)} %bitcast.17), custom_call_target="tpu_custom_call" | custom-call | flops 2000000000 | bytes 5000000 | tf_op jit(solution)/shard_map/flow_adjoint/pallas_call | solution.py:361
  41.1 2.5 %collective-permute-done.11.refs_7_ = f32[4,2,7,16,128]{4,3,2,1,0:T(8,128)S(1)} collective-permute-done((f32[4,2,7,16,128]{4,3,2,1,0:T(8,128)S(1)}, f32[4,2,7,16,128]{4,3,2,1,0:T(8,128)S(1)}, u32[]{:S(2)}, u32[]{:S(2)}) %collective-permute-start.11) | collective-permute-done | bytes 458784 | tf_op jit(solution)/shard_map/ppermute | solution.py:393
  43.6 2.6 %collective-permute-done.6.refs_1_ = f32[4,2,7,8,128]{4,3,2,1,0:T(8,128)S(1)} collective-permute-done((f32[4,2,7,8,128]{4,3,2,1,0:T(8,128)S(1)}, f32[4,2,7,8,128]{4,3,2,1,0:T(8,128)S(1)}, u32[]{:S(2)}, u32[]{:S(2)}) %collective-permute-start.6) | collective-permute-done | bytes 229408 | tf_op jit(solution)/shard_map/ppermute | solution.py:393
  46.2 2.3 %collective-permute-done.8.refs_3_ = f32[4,2,7,8,128]{4,3,2,1,0:T(8,128)S(1)} collective-permute-done((f32[4,2,7,8,128]{4,3,2,1,0:T(8,128)S(1)}, f32[4,2,7,8,128]{4,3,2,1,0:T(8,128)S(1)}, u32[]{:S(2)}, u32[]{:S(2)}) %collective-permute-start.8) | collective-permute-done | bytes 229408 | tf_op jit(solution)/shard_map/ppermute | solution.py:393
  48.6 3.0 %collective-permute-start.12 = (f32[2,7,24,128]{3,2,1,0:T(8,128)S(1)}, f32[2,7,24,128]{3,2,1,0:T(8,128)S(1)}, u32[]{:S(2)}, u32[]{:S(2)}) collective-permute-start(f32[2,7,24,128]{3,2,1,0:T(8,128)S(1)} %get-tuple-element.107), channel_id=1, source_target_pairs={{0,4},{1,129},{2,6},{3,131},{4,0},{5,133},{6,2},{7,135},{64,68},{6... | collective-permute-start | bytes 516104 | tf_op jit(solution)/shard_map/ppermute | solution.py:393
  51.6 4.6 %collective-permute-start.13 = (f32[2,7,24,128]{3,2,1,0:T(8,128)S(1)}, f32[2,7,24,128]{3,2,1,0:T(8,128)S(1)}, u32[]{:S(2)}, u32[]{:S(2)}) collective-permute-start(f32[2,7,24,128]{3,2,1,0:T(8,128)S(1)} %get-tuple-element.108), channel_id=1, source_target_pairs={{0,2},{1,65},{2,0},{3,67},{4,6},{5,69},{6,4},{7,71},{64,66},{65,1}... | collective-permute-start | bytes 516104 | tf_op jit(solution)/shard_map/ppermute | solution.py:393
  56.2 5.2 %collective-permute-done.13.first = f32[2,7,24,128]{3,2,1,0:T(8,128)S(1)} collective-permute-done((f32[2,7,24,128]{3,2,1,0:T(8,128)S(1)}, f32[2,7,24,128]{3,2,1,0:T(8,128)S(1)}, u32[]{:S(2)}, u32[]{:S(2)}) %collective-permute-start.13) | collective-permute-done | bytes 172064 | tf_op jit(solution)/shard_map/ppermute | solution.py:393
  62.9 1.7 %collective-permute-start.15 = (f32[7,24,128]{2,1,0:T(8,128)S(1)}, f32[7,24,128]{2,1,0:T(8,128)S(1)}, u32[]{:S(2)}, u32[]{:S(2)}) collective-permute-start(f32[7,24,128]{2,1,0:T(8,128)S(1)} %get-tuple-element.110), channel_id=1, source_target_pairs={{0,56},{8,48},{16,40},{24,32},{32,24},{40,16},{48,8},{56,0},{1,57}... | collective-permute-start | bytes 258056 | tf_op jit(solution)/shard_map/ppermute | solution.py:451
  64.6 2.8 %feature_adjoint.1 = f32[2,16,32,128]{3,2,1,0:T(8,128)} custom-call(bf16[3,18,32,256]{3,2,1,0:T(8,128)(2,1)S(1)} %get-tuple-element.112.grad_high_ref, bf16[3,18,32,256]{3,2,1,0:T(8,128)(2,1)S(1)} %get-tuple-element.113.grad_low_ref, bf16[9,256,256]{2,1,0:T(8,128)(2,1)S(1)} %get-tuple-element.87.taps_high, bf16[9,256,256]{2,1,0:T(8,128)(2,1)S(1)} %get-tuple-element.88.taps_low), custom_call_target="tpu_custom_call" | custom-call | flops 2000000000 | bytes 5000000 | tf_op jit(solution)/shard_map/feature_adjoint/pallas_call | solution.py:361
  68.7 2.6 %collective-permute-start.17 = (f32[7,24,128]{2,1,0:T(8,128)S(1)}, f32[7,24,128]{2,1,0:T(8,128)S(1)}, u32[]{:S(2)}, u32[]{:S(2)}) collective-permute-start(f32[7,24,128]{2,1,0:T(8,128)S(1)} %add.20), channel_id=1, source_target_pairs={{0,32},{16,48},{32,0},{48,16},{1,33},{17,49},{33,1},{49,17},{2,34}... | collective-permute-start | bytes 258056 | tf_op jit(solution)/shard_map/ppermute | solution.py:392
  71.3 2.7 %collective-permute-start.18 = (f32[7,24,128]{2,1,0:T(8,128)S(1)}, f32[7,24,128]{2,1,0:T(8,128)S(1)}, u32[]{:S(2)}, u32[]{:S(2)}) collective-permute-start(f32[7,24,128]{2,1,0:T(8,128)S(1)} %add.20), channel_id=1, source_target_pairs={{0,48},{16,32},{32,16},{48,0},{1,49},{17,33},{33,17},{49,1},{2,50}... | collective-permute-start | bytes 258056 | tf_op jit(solution)/shard_map/ppermute | solution.py:392
  75.2 2.4 %collective-permute-done.18 = f32[7,24,128]{2,1,0:T(8,128)S(1)} collective-permute-done((f32[7,24,128]{2,1,0:T(8,128)S(1)}, f32[7,24,128]{2,1,0:T(8,128)S(1)}, u32[]{:S(2)}, u32[]{:S(2)}) %collective-permute-start.18) | collective-permute-done | bytes 86048 | tf_op jit(solution)/shard_map/ppermute | solution.py:392
  78.6 2.3 %collective-permute-start.19 = (f32[7,24,128]{2,1,0:T(8,128)S(1)}, f32[7,24,128]{2,1,0:T(8,128)S(1)}, u32[]{:S(2)}, u32[]{:S(2)}) collective-permute-start(f32[7,24,128]{2,1,0:T(8,128)S(1)} %add_add_fusion.own_ref), channel_id=1, source_target_pairs={{0,128},{64,192},{128,0},{192,64},{1,129},{65,193},{129,1},{193,65... | collective-permute-start | bytes 258056 | tf_op jit(solution)/shard_map/ppermute | solution.py:459
  80.9 1.9 %collective-permute-start.21 = (f32[7,24,128]{2,1,0:T(8,128)S(1)}, f32[7,24,128]{2,1,0:T(8,128)S(1)}, u32[]{:S(2)}, u32[]{:S(2)}) collective-permute-start(f32[7,24,128]{2,1,0:T(8,128)S(1)} %add_add_fusion.own_ref), channel_id=1, source_target_pairs={{0,192},{64,128},{128,64},{192,0},{1,193},{65,129},{129,65},{193,1... | collective-permute-start | bytes 258056 | tf_op jit(solution)/shard_map/ppermute | solution.py:459
  82.8 1.9 %collective-permute-done.19.two_ref = f32[7,24,128]{2,1,0:T(8,128)S(1)} collective-permute-done((f32[7,24,128]{2,1,0:T(8,128)S(1)}, f32[7,24,128]{2,1,0:T(8,128)S(1)}, u32[]{:S(2)}, u32[]{:S(2)}) %collective-permute-start.19) | collective-permute-done | bytes 86048 | tf_op jit(solution)/shard_map/ppermute | solution.py:459
  (50 shorter events, 18.2 us)
Async XLA Ops:
  2.2 10.3 %collective-permute-start = (f32[2,80,128]{2,1,0:T(8,128)}, f32[2,80,128]{2,1,0:T(8,128)S(1)}, u32[]{:S(2)}, u32[]{:S(2)}) collective-permute-start(f32[2,80,128]{2,1,0:T(8,128)} %get-tuple-element.62), channel_id=1, source_target_pairs={{16,32},{32,16},{48,64},{64,48},{80,96},{96,80},{112,128},{128,112... | collective-permute-start | bytes 245768 | tf_op jit(solution)/shard_map/ppermute | solution.py:415
  9.0 4.7 %collective-permute-start.1 = (f32[2,80,128]{2,1,0:T(8,128)}, f32[2,80,128]{2,1,0:T(8,128)S(1)}, u32[]{:S(2)}, u32[]{:S(2)}) collective-permute-start(f32[2,80,128]{2,1,0:T(8,128)} %get-tuple-element.63), channel_id=1, source_target_pairs={{0,16},{16,0},{32,48},{48,32},{64,80},{80,64},{96,112},{112,96},{1... | collective-permute-start | bytes 245768 | tf_op jit(solution)/shard_map/ppermute | solution.py:415
  13.8 6.6 %collective-permute-start.2 = (f32[2,56,128]{2,1,0:T(8,128)S(1)}, f32[2,56,128]{2,1,0:T(8,128)S(1)}, u32[]{:S(2)}, u32[]{:S(2)}) collective-permute-start(f32[2,56,128]{2,1,0:T(8,128)S(1)} %get-tuple-element.74), channel_id=1, source_target_pairs={{1,2},{2,1},{3,4},{4,3},{5,6},{6,5},{7,8},{8,7},{9,10},{10,9},{11,... | collective-permute-start | bytes 172040 | tf_op jit(solution)/shard_map/ppermute | solution.py:429
  14.5 5.9 %collective-permute-start.3 = (f32[2,56,128]{2,1,0:T(8,128)S(1)}, f32[2,56,128]{2,1,0:T(8,128)S(1)}, u32[]{:S(2)}, u32[]{:S(2)}) collective-permute-start(f32[2,56,128]{2,1,0:T(8,128)S(1)} %get-tuple-element.75), channel_id=1, source_target_pairs={{0,1},{1,0},{2,3},{3,2},{4,5},{5,4},{6,7},{7,6},{8,9},{9,8},{10,11... | collective-permute-start | bytes 172040 | tf_op jit(solution)/shard_map/ppermute | solution.py:429
  20.5 1.6 %copy-start.1 = (f32[2,16,32,128]{3,2,1,0:T(8,128)S(1)}, f32[2,16,32,128]{3,2,1,0:T(8,128)}, u32[]{:S(2)}) copy-start(f32[2,16,32,128]{3,2,1,0:T(8,128)} %feat_ref.7) | copy-start | bytes 1572868
  22.0 3.9 %collective-permute-start.4 = (f32[4,4,2,7,16,128]{5,4,3,2,1,0:T(8,128)S(1)}, f32[4,4,2,7,16,128]{5,4,3,2,1,0:T(8,128)S(1)}, u32[]{:S(2)}, u32[]{:S(2)}) collective-permute-start(f32[4,4,2,7,16,128]{5,4,3,2,1,0:T(8,128)S(1)} %get-tuple-element.86), channel_id=1, source_target_pairs={{0,1},{1,0},{2,3},{3,2},{4,5},{5,4},{6,7},{7,6},{8,9},{9,8},{10,11... | collective-permute-start | bytes 5505032 | tf_op jit(solution)/shard_map/ppermute | solution.py:437
  28.2 4.6 %collective-permute-start.5 = (f32[4,4,2,7,8,128]{5,4,3,2,1,0:T(8,128)S(1)}, f32[4,4,2,7,8,128]{5,4,3,2,1,0:T(8,128)S(1)}, u32[]{:S(2)}, u32[]{:S(2)}) collective-permute-start(f32[4,4,2,7,8,128]{5,4,3,2,1,0:T(8,128)S(1)} %get-tuple-element.95), channel_id=1, source_target_pairs={{0,1},{1,0},{2,3},{3,2},{4,5},{5,4},{6,7},{7,6},{8,9},{9,8},{10,11... | collective-permute-start | bytes 2752520 | tf_op jit(solution)/shard_map/ppermute | solution.py:442
  28.6 10.2 %collective-permute-start.9 = (f32[4,2,7,16,128]{4,3,2,1,0:T(8,128)S(1)}, f32[4,2,7,16,128]{4,3,2,1,0:T(8,128)S(1)}, u32[]{:S(2)}, u32[]{:S(2)}) collective-permute-start(f32[4,2,7,16,128]{4,3,2,1,0:T(8,128)S(1)} %get-tuple-element.122), channel_id=1, source_target_pairs={{0,128},{1,5},{2,130},{3,7},{4,132},{5,1},{6,134},{7,3},{64,192},{... | collective-permute-start | bytes 1376264 | tf_op jit(solution)/shard_map/ppermute | solution.py:393
  29.8 11.2 %collective-permute-start.10 = (f32[4,2,7,16,128]{4,3,2,1,0:T(8,128)S(1)}, f32[4,2,7,16,128]{4,3,2,1,0:T(8,128)S(1)}, u32[]{:S(2)}, u32[]{:S(2)}) collective-permute-start(f32[4,2,7,16,128]{4,3,2,1,0:T(8,128)S(1)} %get-tuple-element.121), channel_id=1, source_target_pairs={{0,64},{1,3},{2,66},{3,1},{4,68},{5,7},{6,70},{7,5},{64,0},{65,67}... | collective-permute-start | bytes 1376264 | tf_op jit(solution)/shard_map/ppermute | solution.py:393
  29.9 13.7 %collective-permute-start.11 = (f32[4,2,7,16,128]{4,3,2,1,0:T(8,128)S(1)}, f32[4,2,7,16,128]{4,3,2,1,0:T(8,128)S(1)}, u32[]{:S(2)}, u32[]{:S(2)}) collective-permute-start(f32[4,2,7,16,128]{4,3,2,1,0:T(8,128)S(1)} %get-tuple-element.120), channel_id=1, source_target_pairs={{0,192},{1,7},{2,194},{3,5},{4,196},{5,3},{6,198},{7,1},{64,128},{... | collective-permute-start | bytes 1376264 | tf_op jit(solution)/shard_map/ppermute | solution.py:393
  32.8 6.0 %copy-start.5 = (f32[3,3,3,256,128]{4,3,2,1,0:T(8,128)S(1)}, f32[3,3,3,256,128]{4,3,2,1,0:T(8,128)}, u32[]{:S(2)}) copy-start(f32[3,3,3,256,128]{4,3,2,1,0:T(8,128)} %param.8) | copy-start | bytes 10616836
  32.9 13.2 %collective-permute-start.6 = (f32[4,2,7,8,128]{4,3,2,1,0:T(8,128)S(1)}, f32[4,2,7,8,128]{4,3,2,1,0:T(8,128)S(1)}, u32[]{:S(2)}, u32[]{:S(2)}) collective-permute-start(f32[4,2,7,8,128]{4,3,2,1,0:T(8,128)S(1)} %get-tuple-element.125), channel_id=1, source_target_pairs={{0,128},{1,5},{2,130},{3,7},{4,132},{5,1},{6,134},{7,3},{64,192},{... | collective-permute-start | bytes 688136 | tf_op jit(solution)/shard_map/ppermute | solution.py:393
  34.2 12.0 %collective-permute-start.7 = (f32[4,2,7,8,128]{4,3,2,1,0:T(8,128)S(1)}, f32[4,2,7,8,128]{4,3,2,1,0:T(8,128)S(1)}, u32[]{:S(2)}, u32[]{:S(2)}) collective-permute-start(f32[4,2,7,8,128]{4,3,2,1,0:T(8,128)S(1)} %get-tuple-element.124), channel_id=1, source_target_pairs={{0,64},{1,3},{2,66},{3,1},{4,68},{5,7},{6,70},{7,5},{64,0},{65,67}... | collective-permute-start | bytes 688136 | tf_op jit(solution)/shard_map/ppermute | solution.py:393
  38.8 9.7 %collective-permute-start.8 = (f32[4,2,7,8,128]{4,3,2,1,0:T(8,128)S(1)}, f32[4,2,7,8,128]{4,3,2,1,0:T(8,128)S(1)}, u32[]{:S(2)}, u32[]{:S(2)}) collective-permute-start(f32[4,2,7,8,128]{4,3,2,1,0:T(8,128)S(1)} %get-tuple-element.123), channel_id=1, source_target_pairs={{0,192},{1,7},{2,194},{3,5},{4,196},{5,3},{6,198},{7,1},{64,128},{... | collective-permute-start | bytes 688136 | tf_op jit(solution)/shard_map/ppermute | solution.py:393
  48.6 7.6 %collective-permute-start.12 = (f32[2,7,24,128]{3,2,1,0:T(8,128)S(1)}, f32[2,7,24,128]{3,2,1,0:T(8,128)S(1)}, u32[]{:S(2)}, u32[]{:S(2)}) collective-permute-start(f32[2,7,24,128]{3,2,1,0:T(8,128)S(1)} %get-tuple-element.107), channel_id=1, source_target_pairs={{0,4},{1,129},{2,6},{3,131},{4,0},{5,133},{6,2},{7,135},{64,68},{6... | collective-permute-start | bytes 516104 | tf_op jit(solution)/shard_map/ppermute | solution.py:393
  51.6 9.8 %collective-permute-start.13 = (f32[2,7,24,128]{3,2,1,0:T(8,128)S(1)}, f32[2,7,24,128]{3,2,1,0:T(8,128)S(1)}, u32[]{:S(2)}, u32[]{:S(2)}) collective-permute-start(f32[2,7,24,128]{3,2,1,0:T(8,128)S(1)} %get-tuple-element.108), channel_id=1, source_target_pairs={{0,2},{1,65},{2,0},{3,67},{4,6},{5,69},{6,4},{7,71},{64,66},{65,1}... | collective-permute-start | bytes 516104 | tf_op jit(solution)/shard_map/ppermute | solution.py:393
  56.2 6.6 %collective-permute-start.14 = (f32[2,7,24,128]{3,2,1,0:T(8,128)S(1)}, f32[2,7,24,128]{3,2,1,0:T(8,128)S(1)}, u32[]{:S(2)}, u32[]{:S(2)}) collective-permute-start(f32[2,7,24,128]{3,2,1,0:T(8,128)S(1)} %get-tuple-element.109), channel_id=1, source_target_pairs={{0,6},{1,193},{2,4},{3,195},{4,2},{5,197},{6,0},{7,199},{64,70},{6... | collective-permute-start | bytes 516104 | tf_op jit(solution)/shard_map/ppermute | solution.py:393
  62.9 5.8 %collective-permute-start.15 = (f32[7,24,128]{2,1,0:T(8,128)S(1)}, f32[7,24,128]{2,1,0:T(8,128)S(1)}, u32[]{:S(2)}, u32[]{:S(2)}) collective-permute-start(f32[7,24,128]{2,1,0:T(8,128)S(1)} %get-tuple-element.110), channel_id=1, source_target_pairs={{0,56},{8,48},{16,40},{24,32},{32,24},{40,16},{48,8},{56,0},{1,57}... | collective-permute-start | bytes 258056 | tf_op jit(solution)/shard_map/ppermute | solution.py:451
  68.7 6.6 %collective-permute-start.17 = (f32[7,24,128]{2,1,0:T(8,128)S(1)}, f32[7,24,128]{2,1,0:T(8,128)S(1)}, u32[]{:S(2)}, u32[]{:S(2)}) collective-permute-start(f32[7,24,128]{2,1,0:T(8,128)S(1)} %add.20), channel_id=1, source_target_pairs={{0,32},{16,48},{32,0},{48,16},{1,33},{17,49},{33,1},{49,17},{2,34}... | collective-permute-start | bytes 258056 | tf_op jit(solution)/shard_map/ppermute | solution.py:392
  71.3 6.3 %collective-permute-start.18 = (f32[7,24,128]{2,1,0:T(8,128)S(1)}, f32[7,24,128]{2,1,0:T(8,128)S(1)}, u32[]{:S(2)}, u32[]{:S(2)}) collective-permute-start(f32[7,24,128]{2,1,0:T(8,128)S(1)} %add.20), channel_id=1, source_target_pairs={{0,48},{16,32},{32,16},{48,0},{1,49},{17,33},{33,17},{49,1},{2,50}... | collective-permute-start | bytes 258056 | tf_op jit(solution)/shard_map/ppermute | solution.py:392
  74.0 4.6 %collective-permute-start.16 = (f32[7,24,128]{2,1,0:T(8,128)S(1)}, f32[7,24,128]{2,1,0:T(8,128)S(1)}, u32[]{:S(2)}, u32[]{:S(2)}) collective-permute-start(f32[7,24,128]{2,1,0:T(8,128)S(1)} %add.20), channel_id=1, source_target_pairs={{0,16},{16,0},{32,48},{48,32},{1,17},{17,1},{33,49},{49,33},{2,18}... | collective-permute-start | bytes 258056 | tf_op jit(solution)/shard_map/ppermute | solution.py:392
  78.6 6.1 %collective-permute-start.19 = (f32[7,24,128]{2,1,0:T(8,128)S(1)}, f32[7,24,128]{2,1,0:T(8,128)S(1)}, u32[]{:S(2)}, u32[]{:S(2)}) collective-permute-start(f32[7,24,128]{2,1,0:T(8,128)S(1)} %add_add_fusion.own_ref), channel_id=1, source_target_pairs={{0,128},{64,192},{128,0},{192,64},{1,129},{65,193},{129,1},{193,65... | collective-permute-start | bytes 258056 | tf_op jit(solution)/shard_map/ppermute | solution.py:459
  80.9 4.5 %collective-permute-start.20 = (f32[7,24,128]{2,1,0:T(8,128)S(1)}, f32[7,24,128]{2,1,0:T(8,128)S(1)}, u32[]{:S(2)}, u32[]{:S(2)}) collective-permute-start(f32[7,24,128]{2,1,0:T(8,128)S(1)} %add_add_fusion.own_ref), channel_id=1, source_target_pairs={{0,64},{64,0},{128,192},{192,128},{1,65},{65,1},{129,193},{193,129... | collective-permute-start | bytes 258056 | tf_op jit(solution)/shard_map/ppermute | solution.py:459
  80.9 5.7 %collective-permute-start.21 = (f32[7,24,128]{2,1,0:T(8,128)S(1)}, f32[7,24,128]{2,1,0:T(8,128)S(1)}, u32[]{:S(2)}, u32[]{:S(2)}) collective-permute-start(f32[7,24,128]{2,1,0:T(8,128)S(1)} %add_add_fusion.own_ref), channel_id=1, source_target_pairs={{0,192},{64,128},{128,64},{192,0},{1,193},{65,129},{129,65},{193,1... | collective-permute-start | bytes 258056 | tf_op jit(solution)/shard_map/ppermute | solution.py:459
  (4 other events, 4.4 us)

commit v12 on v11

--- a/solution.py
+++ b/solution.py
@@ -63,7 +63,7 @@
         for owner in range(8):
             slot_y = y ^ (owner % 4)
             slot_zh = zh ^ (owner // 4)
-            slots = [jnp.where(core == 0, slot_x, slot_y), jnp.where(core == 0, slot_y, slot_x)]
+            slots = [jnp.where(core == 1, slot_x, slot_y), jnp.where(core == 1, slot_y, slot_x)]
             first = part[2 * owner * depth : (2 * owner + 1) * depth]
             second = part[(2 * owner + 1) * depth : (2 * owner + 2) * depth]
             keep_ref[slots[0], slots[1], slot_zh, number % 7] = jnp.where(core == 0, first, second)
@@ -437,17 +437,17 @@
     terms_two = keep + lax.ppermute(send, "core", swap)
     grad_high, grad_low = block_gradient(features, *rows, *cols, *taps, cot)
     terms_two, grad_high, grad_low = lax.optimization_barrier((terms_two, grad_high, grad_low))
-    arrived_two = spread(terms_two, ("x", "y"))
+    arrived_two = spread(terms_two, ("y", "x"))
     keep, send = block_terms(*feats, grad_high, grad_low)
     terms_one = keep + lax.ppermute(send, "core", swap)
-    arrived_one = spread(terms_one, ("x", "y"))
+    arrived_one = spread(terms_one, ("y", "x"))
     terms_one, cot, kernel_two = lax.optimization_barrier((terms_one, cot, kernel_two))
     grad_flow = adjoint(flow_adjoint_kernel, "flow_adjoint", (FR, R2, W2, CF), cot, kernel_two)
     arrived_one, arrived_two, grad_flow = lax.optimization_barrier((arrived_one, arrived_two, grad_flow))
     parts = (jax.ShapeDtypeStruct((2, 7, 24, C), f32),) * 4
     parts = small(first_sum_kernel, "first_sum", parts, 8)(terms_one, *arrived_one, terms_two, *arrived_two)
     chunk = (jax.ShapeDtypeStruct((7, 24, C), f32),) * 2
-    keep, send = small(second_sum_kernel, "second_sum", chunk, 4)(parts[0], *spread(parts, ("y", "x")))
+    keep, send = small(second_sum_kernel, "second_sum", chunk, 4)(parts[0], *spread(parts, ("x", "y")))
     arrived = lax.ppermute(send, ("zl", "zh"), [(i, 7 - i) for i in range(8)])
     keep, grad_high, grad_low = lax.optimization_barrier((keep, grad_high, grad_low))
     grad_features = adjoint(

time: 88.3 us -> 88.2 us (level)
  starting transfers between devices: 35.3 us -> 44.2 us
  waiting for transfers between devices: 30.9 us -> 22.6 us
    ppermute x9, waiting for transfers between devices: 18.6 us -> 9.51 us  [spread(): lax.ppermute(parts[k], ('x', 'y', 'core'), crossed(k, axes))]
    ppermute x9, starting transfers between devices: 13 us -> 20.8 us  [spread(): lax.ppermute(parts[k], ('x', 'y', 'core'), crossed(k, axes))]
    ppermute x1, starting transfers between devices: 1.73 us -> 4.41 us  [local(): arrived = lax.ppermute(send, ('zl', 'zh'), [(i, 7 - i) for i in range(8)])]
    ppermute x3, starting transfers between devices: 5.35 us -> 3.76 us  [spread(): return [lax.ppermute(parts[k], 'zl', swaps(k)) for k in (3, 2, 1)]]
  transfers between devices with their start and end apart: 22 -> 22, of which waited for: 16 -> 14; matrix products, arithmetic and copies ran while one was open for 0% -> 0% of each run, Pallas kernels for 11% -> 11%
where the time goes in v12:
time: 88.2 us; the launch traced here: 87.9 us
  starting transfers between devices  44.2 us (50%)
  waiting for transfers between devices  22.6 us (26%)
  Pallas kernels  15.4 us (17%)
  local copies, waits for them, and re-layouts  4.53 us (5%)
    ppermute x9, starting transfers between devices, spread(): lax.ppermute(parts[k], ('x', 'y', 'core'), crossed(k, axes))  20.8 us
    ppermute x9, waiting for transfers between devices, spread(): lax.ppermute(parts[k], ('x', 'y', 'core'), crossed(k, axes))  9.51 us
    ppermute x2, starting transfers between devices, local(): rows = [lax.ppermute(edges[k], HA, pairs(k)) for k in (1, 0)]  6.89 us
    ppermute x3, waiting for transfers between devices, spread(): return [lax.ppermute(parts[k], 'zl', swaps(k)) for k in (3, 2, 1)]  5.38 us
    pallas_call x2, Pallas kernels, adjoint(): pl.pallas_call(kernel, out_shape=jax.ShapeDtypeStruct(shape, f32), in_spe...  5.12 us
    ppermute x1, starting transfers between devices, local(): arrived = lax.ppermute(send, ('zl', 'zh'), [(i, 7 - i) for i in range(8)])  4.41 us
    ppermute x3, waiting for transfers between devices, local(): pieces = [chunk] + [lax.ppermute(chunk, 'x', swaps(k)) for k in (2, 1, 3)]  4.41 us
    unnamed x12, local copies, waits for them, and re-layouts  4.38 us
  transfers between devices with their start and end apart: 22, of which 14 were waited for; matrix products, arithmetic and copies ran while one was open for 0% of the time, Pallas kernels for 11%

profile of v12, /device:TPU:6, one launch (start us, length us, event | category | flops | bytes accessed | tf_op | source)
XLA Modules:
  0.0 87.9 jit_solution(17899233649014060983)
XLA Ops:
  0.6 1.6 %row_edges.1 = (f32[2,80,128]{2,1,0:T(8,128)}, f32[2,80,128]{2,1,0:T(8,128)}) custom-call(f32[2,16,32,128]{3,2,1,0:T(8,128)} %feat_ref.7, f32[2,8,16,128]{3,2,1,0:T(8,128)} %cot_ref.3), custom_call_target="tpu_custom_call" | custom-call | flops 1000000 | bytes 1000000 | tf_op jit(solution)/shard_map/row_edges/pallas_call | solution.py:405
  2.2 6.8 %collective-permute-start = (f32[2,80,128]{2,1,0:T(8,128)}, f32[2,80,128]{2,1,0:T(8,128)S(1)}, u32[]{:S(2)}, u32[]{:S(2)}) collective-permute-start(f32[2,80,128]{2,1,0:T(8,128)} %get-tuple-element.62), channel_id=1, source_target_pairs={{16,32},{32,16},{48,64},{64,48},{80,96},{96,80},{112,128},{128,112... | collective-permute-start | bytes 245768 | tf_op jit(solution)/shard_map/ppermute | solution.py:415
  14.5 3.0 %collective-permute-start.3 = (f32[2,56,128]{2,1,0:T(8,128)S(1)}, f32[2,56,128]{2,1,0:T(8,128)S(1)}, u32[]{:S(2)}, u32[]{:S(2)}) collective-permute-start(f32[2,56,128]{2,1,0:T(8,128)S(1)} %get-tuple-element.75), channel_id=1, source_target_pairs={{0,1},{1,0},{2,3},{3,2},{4,5},{5,4},{6,7},{7,6},{8,9},{9,8},{10,11... | collective-permute-start | bytes 172040 | tf_op jit(solution)/shard_map/ppermute | solution.py:429
  17.5 1.5 %copy-done.2 = f32[3,3,3,128,128]{4,3,2,1,0:T(8,128)S(1)} copy-done((f32[3,3,3,128,128]{4,3,2,1,0:T(8,128)S(1)}, f32[3,3,3,128,128]{4,3,2,1,0:T(8,128)}, u32[]{:S(2)}) %copy-start.2) | copy-done | bytes 1769496
  22.1 3.5 %block_gradient.1 = (bf16[3,18,32,256]{3,2,1,0:T(8,128)(2,1)S(1)}, bf16[3,18,32,256]{3,2,1,0:T(8,128)(2,1)S(1)}) custom-call(f32[2,16,32,128]{3,2,1,0:T(8,128)S(1)} %copy-done.1, f32[2,80,128]{2,1,0:T(8,128)S(1)} %collective-permute-done.row_second_ref, f32[2,80,128]{2,1,0:T(8,128)S(1)} %collective-permute-done.1.row_first_ref, ...), custom_call_target="tpu_custom_call" | custom-call | flops 5000000000 | bytes 6000000 | tf_op jit(solution)/shard_map/block_gradient/pallas_call | solution.py:328
  26.1 2.1 %block_terms.1 = (f32[4,4,2,7,8,128]{5,4,3,2,1,0:T(8,128)S(1)}, f32[4,4,2,7,8,128]{5,4,3,2,1,0:T(8,128)S(1)}) custom-call(bf16[256,512]{1,0:T(8,128)(2,1)S(1)} %get-tuple-element.67.feat_high, bf16[256,512]{1,0:T(8,128)(2,1)S(1)} %get-tuple-element.68.feat_low, bf16[3,18,32,256]{3,2,1,0:T(8,128)(2,1)S(1)} %get-tuple-element.112.grad_high_ref, ...), custom_call_target="tpu_custom_call" | custom-call | flops 1000000000 | bytes 1000000 | tf_op jit(solution)/shard_map/block_terms/pallas_call | solution.py:349
  28.6 3.0 %collective-permute-start.9 = (f32[4,2,7,16,128]{4,3,2,1,0:T(8,128)S(1)}, f32[4,2,7,16,128]{4,3,2,1,0:T(8,128)S(1)}, u32[]{:S(2)}, u32[]{:S(2)}) collective-permute-start(f32[4,2,7,16,128]{4,3,2,1,0:T(8,128)S(1)} %get-tuple-element.122), channel_id=1, source_target_pairs={{0,4},{1,129},{2,6},{3,131},{4,0},{5,133},{6,2},{7,135},{64,68},{6... | collective-permute-start | bytes 1376264 | tf_op jit(solution)/shard_map/ppermute | solution.py:393
  31.6 4.6 %collective-permute-start.10 = (f32[4,2,7,16,128]{4,3,2,1,0:T(8,128)S(1)}, f32[4,2,7,16,128]{4,3,2,1,0:T(8,128)S(1)}, u32[]{:S(2)}, u32[]{:S(2)}) collective-permute-start(f32[4,2,7,16,128]{4,3,2,1,0:T(8,128)S(1)} %get-tuple-element.121), channel_id=1, source_target_pairs={{0,2},{1,65},{2,0},{3,67},{4,6},{5,69},{6,4},{7,71},{64,66},{65,1}... | collective-permute-start | bytes 1376264 | tf_op jit(solution)/shard_map/ppermute | solution.py:393
  36.3 2.1 %collective-permute-start.6 = (f32[4,2,7,8,128]{4,3,2,1,0:T(8,128)S(1)}, f32[4,2,7,8,128]{4,3,2,1,0:T(8,128)S(1)}, u32[]{:S(2)}, u32[]{:S(2)}) collective-permute-start(f32[4,2,7,8,128]{4,3,2,1,0:T(8,128)S(1)} %get-tuple-element.125), channel_id=1, source_target_pairs={{0,4},{1,129},{2,6},{3,131},{4,0},{5,133},{6,2},{7,135},{64,68},{6... | collective-permute-start | bytes 688136 | tf_op jit(solution)/shard_map/ppermute | solution.py:393
  38.5 2.0 %collective-permute-start.7 = (f32[4,2,7,8,128]{4,3,2,1,0:T(8,128)S(1)}, f32[4,2,7,8,128]{4,3,2,1,0:T(8,128)S(1)}, u32[]{:S(2)}, u32[]{:S(2)}) collective-permute-start(f32[4,2,7,8,128]{4,3,2,1,0:T(8,128)S(1)} %get-tuple-element.124), channel_id=1, source_target_pairs={{0,2},{1,65},{2,0},{3,67},{4,6},{5,69},{6,4},{7,71},{64,66},{65,1}... | collective-permute-start | bytes 688136 | tf_op jit(solution)/shard_map/ppermute | solution.py:393
  40.5 4.9 %collective-permute-start.8 = (f32[4,2,7,8,128]{4,3,2,1,0:T(8,128)S(1)}, f32[4,2,7,8,128]{4,3,2,1,0:T(8,128)S(1)}, u32[]{:S(2)}, u32[]{:S(2)}) collective-permute-start(f32[4,2,7,8,128]{4,3,2,1,0:T(8,128)S(1)} %get-tuple-element.123), channel_id=1, source_target_pairs={{0,6},{1,193},{2,4},{3,195},{4,2},{5,197},{6,0},{7,199},{64,70},{6... | collective-permute-start | bytes 688136 | tf_op jit(solution)/shard_map/ppermute | solution.py:393
  45.4 2.3 %flow_adjoint.1 = f32[2,8,16,256]{3,2,1,0:T(8,128)} custom-call(f32[2,10,18,128]{3,2,1,0:T(8,128)S(1)} %get-tuple-element.98.cot_ref, f32[27,256,128]{2,1,0:T(8,128)S(1)} %bitcast.17), custom_call_target="tpu_custom_call" | custom-call | flops 2000000000 | bytes 5000000 | tf_op jit(solution)/shard_map/flow_adjoint/pallas_call | solution.py:361
  48.3 4.2 %collective-permute-done.7.refs_2_ = f32[4,2,7,8,128]{4,3,2,1,0:T(8,128)S(1)} collective-permute-done((f32[4,2,7,8,128]{4,3,2,1,0:T(8,128)S(1)}, f32[4,2,7,8,128]{4,3,2,1,0:T(8,128)S(1)}, u32[]{:S(2)}, u32[]{:S(2)}) %collective-permute-start.7) | collective-permute-done | bytes 229408 | tf_op jit(solution)/shard_map/ppermute | solution.py:393
  54.2 2.7 %collective-permute-start.14 = (f32[2,7,24,128]{3,2,1,0:T(8,128)S(1)}, f32[2,7,24,128]{3,2,1,0:T(8,128)S(1)}, u32[]{:S(2)}, u32[]{:S(2)}) collective-permute-start(f32[2,7,24,128]{3,2,1,0:T(8,128)S(1)} %get-tuple-element.109), channel_id=1, source_target_pairs={{0,192},{1,7},{2,194},{3,5},{4,196},{5,3},{6,198},{7,1},{64,128},{... | collective-permute-start | bytes 516104 | tf_op jit(solution)/shard_map/ppermute | solution.py:393
  56.9 2.9 %collective-permute-done.12.second = f32[2,7,24,128]{3,2,1,0:T(8,128)S(1)} collective-permute-done((f32[2,7,24,128]{3,2,1,0:T(8,128)S(1)}, f32[2,7,24,128]{3,2,1,0:T(8,128)S(1)}, u32[]{:S(2)}, u32[]{:S(2)}) %collective-permute-start.12) | collective-permute-done | bytes 172064 | tf_op jit(solution)/shard_map/ppermute | solution.py:393
  59.8 1.8 %collective-permute-done.14.third = f32[2,7,24,128]{3,2,1,0:T(8,128)S(1)} collective-permute-done((f32[2,7,24,128]{3,2,1,0:T(8,128)S(1)}, f32[2,7,24,128]{3,2,1,0:T(8,128)S(1)}, u32[]{:S(2)}, u32[]{:S(2)}) %collective-permute-start.14) | collective-permute-done | bytes 172064 | tf_op jit(solution)/shard_map/ppermute | solution.py:393
  61.6 4.4 %collective-permute-start.15 = (f32[7,24,128]{2,1,0:T(8,128)S(1)}, f32[7,24,128]{2,1,0:T(8,128)S(1)}, u32[]{:S(2)}, u32[]{:S(2)}) collective-permute-start(f32[7,24,128]{2,1,0:T(8,128)S(1)} %get-tuple-element.110), channel_id=1, source_target_pairs={{0,56},{8,48},{16,40},{24,32},{32,24},{40,16},{48,8},{56,0},{1,57}... | collective-permute-start | bytes 258056 | tf_op jit(solution)/shard_map/ppermute | solution.py:451
  66.0 2.8 %feature_adjoint.1 = f32[2,16,32,128]{3,2,1,0:T(8,128)} custom-call(bf16[3,18,32,256]{3,2,1,0:T(8,128)(2,1)S(1)} %get-tuple-element.112.grad_high_ref, bf16[3,18,32,256]{3,2,1,0:T(8,128)(2,1)S(1)} %get-tuple-element.113.grad_low_ref, bf16[9,256,256]{2,1,0:T(8,128)(2,1)S(1)} %get-tuple-element.87.taps_high, bf16[9,256,256]{2,1,0:T(8,128)(2,1)S(1)} %get-tuple-element.88.taps_low), custom_call_target="tpu_custom_call" | custom-call | flops 2000000000 | bytes 5000000 | tf_op jit(solution)/shard_map/feature_adjoint/pallas_call | solution.py:361
  69.4 1.9 %collective-permute-start.17 = (f32[7,24,128]{2,1,0:T(8,128)S(1)}, f32[7,24,128]{2,1,0:T(8,128)S(1)}, u32[]{:S(2)}, u32[]{:S(2)}) collective-permute-start(f32[7,24,128]{2,1,0:T(8,128)S(1)} %add.20), channel_id=1, source_target_pairs={{0,32},{16,48},{32,0},{48,16},{1,33},{17,49},{33,1},{49,17},{2,34}... | collective-permute-start | bytes 258056 | tf_op jit(solution)/shard_map/ppermute | solution.py:392
  71.3 1.8 %collective-permute-start.18 = (f32[7,24,128]{2,1,0:T(8,128)S(1)}, f32[7,24,128]{2,1,0:T(8,128)S(1)}, u32[]{:S(2)}, u32[]{:S(2)}) collective-permute-start(f32[7,24,128]{2,1,0:T(8,128)S(1)} %add.20), channel_id=1, source_target_pairs={{0,48},{16,32},{32,16},{48,0},{1,49},{17,33},{33,17},{49,1},{2,50}... | collective-permute-start | bytes 258056 | tf_op jit(solution)/shard_map/ppermute | solution.py:392
  73.1 3.3 %collective-permute-done.17 = f32[7,24,128]{2,1,0:T(8,128)S(1)} collective-permute-done((f32[7,24,128]{2,1,0:T(8,128)S(1)}, f32[7,24,128]{2,1,0:T(8,128)S(1)}, u32[]{:S(2)}, u32[]{:S(2)}) %collective-permute-start.17) | collective-permute-done | bytes 86048 | tf_op jit(solution)/shard_map/ppermute | solution.py:392
  78.5 1.6 %collective-permute-start.19 = (f32[7,24,128]{2,1,0:T(8,128)S(1)}, f32[7,24,128]{2,1,0:T(8,128)S(1)}, u32[]{:S(2)}, u32[]{:S(2)}) collective-permute-start(f32[7,24,128]{2,1,0:T(8,128)S(1)} %add_add_fusion.own_ref), channel_id=1, source_target_pairs={{0,128},{64,192},{128,0},{192,64},{1,129},{65,193},{129,1},{193,65... | collective-permute-start | bytes 258056 | tf_op jit(solution)/shard_map/ppermute | solution.py:459
  82.7 1.9 %collective-permute-done.19.two_ref = f32[7,24,128]{2,1,0:T(8,128)S(1)} collective-permute-done((f32[7,24,128]{2,1,0:T(8,128)S(1)}, f32[7,24,128]{2,1,0:T(8,128)S(1)}, u32[]{:S(2)}, u32[]{:S(2)}) %collective-permute-start.19) | collective-permute-done | bytes 86048 | tf_op jit(solution)/shard_map/ppermute | solution.py:459
  84.8 2.3 %collective-permute-done.21.three_ref = f32[7,24,128]{2,1,0:T(8,128)S(1)} collective-permute-done((f32[7,24,128]{2,1,0:T(8,128)S(1)}, f32[7,24,128]{2,1,0:T(8,128)S(1)}, u32[]{:S(2)}, u32[]{:S(2)}) %collective-permute-start.21) | collective-permute-done | bytes 86048 | tf_op jit(solution)/shard_map/ppermute | solution.py:459
  (50 shorter events, 18.0 us)
Async XLA Ops:
  2.2 10.3 %collective-permute-start = (f32[2,80,128]{2,1,0:T(8,128)}, f32[2,80,128]{2,1,0:T(8,128)S(1)}, u32[]{:S(2)}, u32[]{:S(2)}) collective-permute-start(f32[2,80,128]{2,1,0:T(8,128)} %get-tuple-element.62), channel_id=1, source_target_pairs={{16,32},{32,16},{48,64},{64,48},{80,96},{96,80},{112,128},{128,112... | collective-permute-start | bytes 245768 | tf_op jit(solution)/shard_map/ppermute | solution.py:415
  9.0 4.7 %collective-permute-start.1 = (f32[2,80,128]{2,1,0:T(8,128)}, f32[2,80,128]{2,1,0:T(8,128)S(1)}, u32[]{:S(2)}, u32[]{:S(2)}) collective-permute-start(f32[2,80,128]{2,1,0:T(8,128)} %get-tuple-element.63), channel_id=1, source_target_pairs={{0,16},{16,0},{32,48},{48,32},{64,80},{80,64},{96,112},{112,96},{1... | collective-permute-start | bytes 245768 | tf_op jit(solution)/shard_map/ppermute | solution.py:415
  13.8 6.6 %collective-permute-start.2 = (f32[2,56,128]{2,1,0:T(8,128)S(1)}, f32[2,56,128]{2,1,0:T(8,128)S(1)}, u32[]{:S(2)}, u32[]{:S(2)}) collective-permute-start(f32[2,56,128]{2,1,0:T(8,128)S(1)} %get-tuple-element.74), channel_id=1, source_target_pairs={{1,2},{2,1},{3,4},{4,3},{5,6},{6,5},{7,8},{8,7},{9,10},{10,9},{11,... | collective-permute-start | bytes 172040 | tf_op jit(solution)/shard_map/ppermute | solution.py:429
  14.5 5.9 %collective-permute-start.3 = (f32[2,56,128]{2,1,0:T(8,128)S(1)}, f32[2,56,128]{2,1,0:T(8,128)S(1)}, u32[]{:S(2)}, u32[]{:S(2)}) collective-permute-start(f32[2,56,128]{2,1,0:T(8,128)S(1)} %get-tuple-element.75), channel_id=1, source_target_pairs={{0,1},{1,0},{2,3},{3,2},{4,5},{5,4},{6,7},{7,6},{8,9},{9,8},{10,11... | collective-permute-start | bytes 172040 | tf_op jit(solution)/shard_map/ppermute | solution.py:429
  20.5 1.6 %copy-start.1 = (f32[2,16,32,128]{3,2,1,0:T(8,128)S(1)}, f32[2,16,32,128]{3,2,1,0:T(8,128)}, u32[]{:S(2)}) copy-start(f32[2,16,32,128]{3,2,1,0:T(8,128)} %feat_ref.7) | copy-start | bytes 1572868
  22.0 3.9 %collective-permute-start.4 = (f32[4,4,2,7,16,128]{5,4,3,2,1,0:T(8,128)S(1)}, f32[4,4,2,7,16,128]{5,4,3,2,1,0:T(8,128)S(1)}, u32[]{:S(2)}, u32[]{:S(2)}) collective-permute-start(f32[4,4,2,7,16,128]{5,4,3,2,1,0:T(8,128)S(1)} %get-tuple-element.86), channel_id=1, source_target_pairs={{0,1},{1,0},{2,3},{3,2},{4,5},{5,4},{6,7},{7,6},{8,9},{9,8},{10,11... | collective-permute-start | bytes 5505032 | tf_op jit(solution)/shard_map/ppermute | solution.py:437
  28.2 8.0 %collective-permute-start.5 = (f32[4,4,2,7,8,128]{5,4,3,2,1,0:T(8,128)S(1)}, f32[4,4,2,7,8,128]{5,4,3,2,1,0:T(8,128)S(1)}, u32[]{:S(2)}, u32[]{:S(2)}) collective-permute-start(f32[4,4,2,7,8,128]{5,4,3,2,1,0:T(8,128)S(1)} %get-tuple-element.95), channel_id=1, source_target_pairs={{0,1},{1,0},{2,3},{3,2},{4,5},{5,4},{6,7},{7,6},{8,9},{9,8},{10,11... | collective-permute-start | bytes 2752520 | tf_op jit(solution)/shard_map/ppermute | solution.py:442
  28.6 11.9 %collective-permute-start.9 = (f32[4,2,7,16,128]{4,3,2,1,0:T(8,128)S(1)}, f32[4,2,7,16,128]{4,3,2,1,0:T(8,128)S(1)}, u32[]{:S(2)}, u32[]{:S(2)}) collective-permute-start(f32[4,2,7,16,128]{4,3,2,1,0:T(8,128)S(1)} %get-tuple-element.122), channel_id=1, source_target_pairs={{0,4},{1,129},{2,6},{3,131},{4,0},{5,133},{6,2},{7,135},{64,68},{6... | collective-permute-start | bytes 1376264 | tf_op jit(solution)/shard_map/ppermute | solution.py:393
  31.6 16.1 %collective-permute-start.10 = (f32[4,2,7,16,128]{4,3,2,1,0:T(8,128)S(1)}, f32[4,2,7,16,128]{4,3,2,1,0:T(8,128)S(1)}, u32[]{:S(2)}, u32[]{:S(2)}) collective-permute-start(f32[4,2,7,16,128]{4,3,2,1,0:T(8,128)S(1)} %get-tuple-element.121), channel_id=1, source_target_pairs={{0,2},{1,65},{2,0},{3,67},{4,6},{5,69},{6,4},{7,71},{64,66},{65,1}... | collective-permute-start | bytes 1376264 | tf_op jit(solution)/shard_map/ppermute | solution.py:393
  36.2 12.1 %collective-permute-start.11 = (f32[4,2,7,16,128]{4,3,2,1,0:T(8,128)S(1)}, f32[4,2,7,16,128]{4,3,2,1,0:T(8,128)S(1)}, u32[]{:S(2)}, u32[]{:S(2)}) collective-permute-start(f32[4,2,7,16,128]{4,3,2,1,0:T(8,128)S(1)} %get-tuple-element.120), channel_id=1, source_target_pairs={{0,6},{1,193},{2,4},{3,195},{4,2},{5,197},{6,0},{7,199},{64,70},{6... | collective-permute-start | bytes 1376264 | tf_op jit(solution)/shard_map/ppermute | solution.py:393
  36.2 9.2 %copy-start.5 = (f32[3,3,3,256,128]{4,3,2,1,0:T(8,128)S(1)}, f32[3,3,3,256,128]{4,3,2,1,0:T(8,128)}, u32[]{:S(2)}) copy-start(f32[3,3,3,256,128]{4,3,2,1,0:T(8,128)} %param.8) | copy-start | bytes 10616836
  36.3 12.0 %collective-permute-start.6 = (f32[4,2,7,8,128]{4,3,2,1,0:T(8,128)S(1)}, f32[4,2,7,8,128]{4,3,2,1,0:T(8,128)S(1)}, u32[]{:S(2)}, u32[]{:S(2)}) collective-permute-start(f32[4,2,7,8,128]{4,3,2,1,0:T(8,128)S(1)} %get-tuple-element.125), channel_id=1, source_target_pairs={{0,4},{1,129},{2,6},{3,131},{4,0},{5,133},{6,2},{7,135},{64,68},{6... | collective-permute-start | bytes 688136 | tf_op jit(solution)/shard_map/ppermute | solution.py:393
  38.5 14.1 %collective-permute-start.7 = (f32[4,2,7,8,128]{4,3,2,1,0:T(8,128)S(1)}, f32[4,2,7,8,128]{4,3,2,1,0:T(8,128)S(1)}, u32[]{:S(2)}, u32[]{:S(2)}) collective-permute-start(f32[4,2,7,8,128]{4,3,2,1,0:T(8,128)S(1)} %get-tuple-element.124), channel_id=1, source_target_pairs={{0,2},{1,65},{2,0},{3,67},{4,6},{5,69},{6,4},{7,71},{64,66},{65,1}... | collective-permute-start | bytes 688136 | tf_op jit(solution)/shard_map/ppermute | solution.py:393
  40.5 12.0 %collective-permute-start.8 = (f32[4,2,7,8,128]{4,3,2,1,0:T(8,128)S(1)}, f32[4,2,7,8,128]{4,3,2,1,0:T(8,128)S(1)}, u32[]{:S(2)}, u32[]{:S(2)}) collective-permute-start(f32[4,2,7,8,128]{4,3,2,1,0:T(8,128)S(1)} %get-tuple-element.123), channel_id=1, source_target_pairs={{0,6},{1,193},{2,4},{3,195},{4,2},{5,197},{6,0},{7,199},{64,70},{6... | collective-permute-start | bytes 688136 | tf_op jit(solution)/shard_map/ppermute | solution.py:393
  52.7 7.1 %collective-permute-start.12 = (f32[2,7,24,128]{3,2,1,0:T(8,128)S(1)}, f32[2,7,24,128]{3,2,1,0:T(8,128)S(1)}, u32[]{:S(2)}, u32[]{:S(2)}) collective-permute-start(f32[2,7,24,128]{3,2,1,0:T(8,128)S(1)} %get-tuple-element.107), channel_id=1, source_target_pairs={{0,128},{1,5},{2,130},{3,7},{4,132},{5,1},{6,134},{7,3},{64,192},{... | collective-permute-start | bytes 516104 | tf_op jit(solution)/shard_map/ppermute | solution.py:393
  54.1 5.6 %collective-permute-start.13 = (f32[2,7,24,128]{3,2,1,0:T(8,128)S(1)}, f32[2,7,24,128]{3,2,1,0:T(8,128)S(1)}, u32[]{:S(2)}, u32[]{:S(2)}) collective-permute-start(f32[2,7,24,128]{3,2,1,0:T(8,128)S(1)} %get-tuple-element.108), channel_id=1, source_target_pairs={{0,64},{1,3},{2,66},{3,1},{4,68},{5,7},{6,70},{7,5},{64,0},{65,67}... | collective-permute-start | bytes 516104 | tf_op jit(solution)/shard_map/ppermute | solution.py:393
  54.2 7.4 %collective-permute-start.14 = (f32[2,7,24,128]{3,2,1,0:T(8,128)S(1)}, f32[2,7,24,128]{3,2,1,0:T(8,128)S(1)}, u32[]{:S(2)}, u32[]{:S(2)}) collective-permute-start(f32[2,7,24,128]{3,2,1,0:T(8,128)S(1)} %get-tuple-element.109), channel_id=1, source_target_pairs={{0,192},{1,7},{2,194},{3,5},{4,196},{5,3},{6,198},{7,1},{64,128},{... | collective-permute-start | bytes 516104 | tf_op jit(solution)/shard_map/ppermute | solution.py:393
  61.6 7.8 %collective-permute-start.15 = (f32[7,24,128]{2,1,0:T(8,128)S(1)}, f32[7,24,128]{2,1,0:T(8,128)S(1)}, u32[]{:S(2)}, u32[]{:S(2)}) collective-permute-start(f32[7,24,128]{2,1,0:T(8,128)S(1)} %get-tuple-element.110), channel_id=1, source_target_pairs={{0,56},{8,48},{16,40},{24,32},{32,24},{40,16},{48,8},{56,0},{1,57}... | collective-permute-start | bytes 258056 | tf_op jit(solution)/shard_map/ppermute | solution.py:451
  69.4 7.1 %collective-permute-start.17 = (f32[7,24,128]{2,1,0:T(8,128)S(1)}, f32[7,24,128]{2,1,0:T(8,128)S(1)}, u32[]{:S(2)}, u32[]{:S(2)}) collective-permute-start(f32[7,24,128]{2,1,0:T(8,128)S(1)} %add.20), channel_id=1, source_target_pairs={{0,32},{16,48},{32,0},{48,16},{1,33},{17,49},{33,1},{49,17},{2,34}... | collective-permute-start | bytes 258056 | tf_op jit(solution)/shard_map/ppermute | solution.py:392
  71.3 6.4 %collective-permute-start.18 = (f32[7,24,128]{2,1,0:T(8,128)S(1)}, f32[7,24,128]{2,1,0:T(8,128)S(1)}, u32[]{:S(2)}, u32[]{:S(2)}) collective-permute-start(f32[7,24,128]{2,1,0:T(8,128)S(1)} %add.20), channel_id=1, source_target_pairs={{0,48},{16,32},{32,16},{48,0},{1,49},{17,33},{33,17},{49,1},{2,50}... | collective-permute-start | bytes 258056 | tf_op jit(solution)/shard_map/ppermute | solution.py:392
  73.1 5.4 %collective-permute-start.16 = (f32[7,24,128]{2,1,0:T(8,128)S(1)}, f32[7,24,128]{2,1,0:T(8,128)S(1)}, u32[]{:S(2)}, u32[]{:S(2)}) collective-permute-start(f32[7,24,128]{2,1,0:T(8,128)S(1)} %add.20), channel_id=1, source_target_pairs={{0,16},{16,0},{32,48},{48,32},{1,17},{17,1},{33,49},{49,33},{2,18}... | collective-permute-start | bytes 258056 | tf_op jit(solution)/shard_map/ppermute | solution.py:392
  78.5 6.1 %collective-permute-start.19 = (f32[7,24,128]{2,1,0:T(8,128)S(1)}, f32[7,24,128]{2,1,0:T(8,128)S(1)}, u32[]{:S(2)}, u32[]{:S(2)}) collective-permute-start(f32[7,24,128]{2,1,0:T(8,128)S(1)} %add_add_fusion.own_ref), channel_id=1, source_target_pairs={{0,128},{64,192},{128,0},{192,64},{1,129},{65,193},{129,1},{193,65... | collective-permute-start | bytes 258056 | tf_op jit(solution)/shard_map/ppermute | solution.py:459
  80.2 4.7 %collective-permute-start.20 = (f32[7,24,128]{2,1,0:T(8,128)S(1)}, f32[7,24,128]{2,1,0:T(8,128)S(1)}, u32[]{:S(2)}, u32[]{:S(2)}) collective-permute-start(f32[7,24,128]{2,1,0:T(8,128)S(1)} %add_add_fusion.own_ref), channel_id=1, source_target_pairs={{0,64},{64,0},{128,192},{192,128},{1,65},{65,1},{129,193},{193,129... | collective-permute-start | bytes 258056 | tf_op jit(solution)/shard_map/ppermute | solution.py:459
  81.4 5.7 %collective-permute-start.21 = (f32[7,24,128]{2,1,0:T(8,128)S(1)}, f32[7,24,128]{2,1,0:T(8,128)S(1)}, u32[]{:S(2)}, u32[]{:S(2)}) collective-permute-start(f32[7,24,128]{2,1,0:T(8,128)S(1)} %add_add_fusion.own_ref), channel_id=1, source_target_pairs={{0,192},{64,128},{128,64},{192,0},{1,193},{65,129},{129,65},{193,1... | collective-permute-start | bytes 258056 | tf_op jit(solution)/shard_map/ppermute | solution.py:459
  (4 other events, 4.4 us)

commit v13 on v11

--- a/solution.py
+++ b/solution.py
@@ -70,29 +70,20 @@
             send_ref[slots[1], slots[0], slot_zh, number % 7] = jnp.where(core == 0, second, first)
 
 
-def row_edges_kernel(
-    feat_ref, cot_ref, first_ref, second_ref, feat_top, feat_bottom, cot_top, cot_bottom, sems
-):
-    copies = [
-        pltpu.make_async_copy(feat_ref.at[:, 0:2], feat_top, sems.at[0]),
-        pltpu.make_async_copy(feat_ref.at[:, R - 2 : R], feat_bottom, sems.at[1]),
-        pltpu.make_async_copy(cot_ref.at[:, 0:1], cot_top, sems.at[2]),
-        pltpu.make_async_copy(cot_ref.at[:, R2 - 1 : R2], cot_bottom, sems.at[3]),
-    ]
+def row_edges_kernel(feat_ref, cot_ref, first_ref, second_ref, sems):
+    odd = lax.rem(lax.axis_index("zl"), 2)
+    copies = []
+    for ref, top in ((first_ref, odd), (second_ref, 1 - odd)):
+        row, cot_row = (1 - top) * (R - 2), (1 - top) * (R2 - 1)
+        pieces = [
+            (feat_ref.at[:, row + line // 2, (line % 2) * W2 : (line % 2 + 1) * W2], line) for line in range(4)
+        ]
+        for source, line in pieces + [(cot_ref.at[:, cot_row], 4)]:
+            copies.append(pltpu.make_async_copy(source, ref.at[:, line], sems.at[len(copies)]))
     for copy in copies:
         copy.start()
     for copy in copies:
         copy.wait()
-    odd = lax.rem(lax.axis_index("zl"), 2) == 1
-    for t in range(FR):
-        for row in range(2):
-            top, bottom = feat_top[t, row], feat_bottom[t, row]
-            lines = slice(row * W, (row + 1) * W)
-            first_ref[t, lines] = jnp.where(odd, top, bottom)
-            second_ref[t, lines] = jnp.where(odd, bottom, top)
-        top, bottom = cot_top[t, 0], cot_bottom[t, 0]
-        first_ref[t, 2 * W :] = jnp.where(odd, top, bottom)
-        second_ref[t, 2 * W :] = jnp.where(odd, bottom, top)
 
 
 def prepare_features_kernel(feat_ref, cot_ref, feat_high, feat_low, near_cot_ref):
@@ -401,17 +392,17 @@
 def local(features, weight_one, flow_feats, weight_two, cotangent):
     kernel_one = weight_one.reshape(27, C, C)
     kernel_two = weight_two.reshape(27, CF, C)
-    edges = (jax.ShapeDtypeStruct((FR, 2 * W + W2, C), f32),) * 2
-    edges = small(
+    edges = pl.pallas_call(
         row_edges_kernel,
-        "row_edges",
-        edges,
-        2,
-        [pltpu.VMEM((FR, 2, W, C), f32)] * 2
-        + [pltpu.VMEM((FR, 1, W2, C), f32)] * 2
-        + [pltpu.SemaphoreType.DMA((4,))],
-        HBM,
+        out_shape=(jax.ShapeDtypeStruct((FR, 5, W2, C), f32),) * 2,
+        in_specs=[HBM] * 2,
+        out_specs=(HBM,) * 2,
+        scratch_shapes=[pltpu.SemaphoreType.DMA((10,))],
+        compiler_params=params(64),
+        cost_estimate=pl.CostEstimate(flops=10**6, bytes_accessed=10**6, transcendentals=0),
+        name="row_edges",
     )(features, cotangent)
+    edges = [edge.reshape(FR, 2 * W + W2, C) for edge in edges]
     rows = [lax.ppermute(edges[k], HA, pairs(k)) for k in (1, 0)]
     feats = (jax.ShapeDtypeStruct((2 * C, R * W), bf16),) * 2
     near = (jax.ShapeDtypeStruct((FR, R2, W2, C), f32),)

time: 88.3 us -> 92.8 us (1.051)
  Pallas kernels: 15.4 us -> 20 us
    pallas_call x1, Pallas kernels: 1.59 us -> 6.17 us  [local(): pl.pallas_call(row_edges_kernel, out_shape=(jax.ShapeDtypeStruct((FR, 5,...]
  transfers between devices with their start and end apart: 22 -> 22, of which waited for: 16 -> 16; matrix products, arithmetic and copies ran while one was open for 0% -> 0% of each run, Pallas kernels for 11% -> 10%
where the time goes in v13:
time: 92.8 us; the launch traced here: 91.9 us
  starting transfers between devices  35.3 us (38%)
  waiting for transfers between devices  30.9 us (33%)
  Pallas kernels  20 us (22%)
  local copies, waits for them, and re-layouts  4.53 us (5%)
    ppermute x9, waiting for transfers between devices, spread(): lax.ppermute(parts[k], ('x', 'y', 'core'), crossed(k, axes))  18.6 us
    ppermute x9, starting transfers between devices, spread(): lax.ppermute(parts[k], ('x', 'y', 'core'), crossed(k, axes))  13 us
    ppermute x2, starting transfers between devices, local(): rows = [lax.ppermute(edges[k], HA, pairs(k)) for k in (1, 0)]  6.89 us
    pallas_call x1, Pallas kernels, local(): pl.pallas_call(row_edges_kernel, out_shape=(jax.ShapeDtypeStruct((FR, 5,...  6.17 us
    ppermute x3, starting transfers between devices, spread(): return [lax.ppermute(parts[k], 'zl', swaps(k)) for k in (3, 2, 1)]  5.36 us
    pallas_call x2, Pallas kernels, adjoint(): pl.pallas_call(kernel, out_shape=jax.ShapeDtypeStruct(shape, f32), in_spe...  5.12 us
    ppermute x3, waiting for transfers between devices, spread(): return [lax.ppermute(parts[k], 'zl', swaps(k)) for k in (3, 2, 1)]  4.54 us
    unnamed x12, local copies, waits for them, and re-layouts  4.38 us
  transfers between devices with their start and end apart: 22, of which 16 were waited for; matrix products, arithmetic and copies ran while one was open for 0% of the time, Pallas kernels for 10%

profile of v13, /device:TPU:6, one launch (start us, length us, event | category | flops | bytes accessed | tf_op | source)
XLA Modules:
  0.0 91.9 jit_solution(11976549975900494262)
XLA Ops:
  0.6 6.2 %row_edges.1 = (f32[2,5,16,128]{3,2,1,0:T(8,128)}, f32[2,5,16,128]{3,2,1,0:T(8,128)}) custom-call(f32[2,16,32,128]{3,2,1,0:T(8,128)} %feat_ref.7, f32[2,8,16,128]{3,2,1,0:T(8,128)} %cot_ref.3), custom_call_target="tpu_custom_call" | custom-call | flops 1000000 | bytes 1000000 | tf_op jit(solution)/shard_map/row_edges/pallas_call | solution.py:395
  6.8 6.8 %collective-permute-start = (f32[2,80,128]{2,1,0:T(8,128)}, f32[2,80,128]{2,1,0:T(8,128)S(1)}, u32[]{:S(2)}, u32[]{:S(2)}) collective-permute-start(f32[2,80,128]{2,1,0:T(8,128)} %bitcast.23), channel_id=1, source_target_pairs={{16,32},{32,16},{48,64},{64,48},{80,96},{96,80},{112,128},{128,112... | collective-permute-start | bytes 245768 | tf_op jit(solution)/shard_map/ppermute | solution.py:406
  19.1 3.0 %collective-permute-start.3 = (f32[2,56,128]{2,1,0:T(8,128)S(1)}, f32[2,56,128]{2,1,0:T(8,128)S(1)}, u32[]{:S(2)}, u32[]{:S(2)}) collective-permute-start(f32[2,56,128]{2,1,0:T(8,128)S(1)} %get-tuple-element.75), channel_id=1, source_target_pairs={{0,1},{1,0},{2,3},{3,2},{4,5},{5,4},{6,7},{7,6},{8,9},{9,8},{10,11... | collective-permute-start | bytes 172040 | tf_op jit(solution)/shard_map/ppermute | solution.py:420
  22.1 1.5 %copy-done.2 = f32[3,3,3,128,128]{4,3,2,1,0:T(8,128)S(1)} copy-done((f32[3,3,3,128,128]{4,3,2,1,0:T(8,128)S(1)}, f32[3,3,3,128,128]{4,3,2,1,0:T(8,128)}, u32[]{:S(2)}) %copy-start.2) | copy-done | bytes 1769496
  25.1 1.5 %flow_terms.1 = (f32[4,4,2,7,16,128]{5,4,3,2,1,0:T(8,128)S(1)}, f32[4,4,2,7,16,128]{5,4,3,2,1,0:T(8,128)S(1)}, f32[2,10,18,128]{3,2,1,0:T(8,128)S(1)}) custom-call(bf16[512,128]{1,0:T(8,128)(2,1)S(1)} %get-tuple-element.81.flow_high, bf16[512,128]{1,0:T(8,128)(2,1)S(1)} %get-tuple-element.82.flow_low, ...), custom_call_target="tpu_custom_call" | custom-call | flops 2000000000 | bytes 5000000 | tf_op jit(solution)/shard_map/flow_terms/pallas_call | solution.py:306
  26.6 3.5 %block_gradient.1 = (bf16[3,18,32,256]{3,2,1,0:T(8,128)(2,1)S(1)}, bf16[3,18,32,256]{3,2,1,0:T(8,128)(2,1)S(1)}) custom-call(f32[2,16,32,128]{3,2,1,0:T(8,128)S(1)} %copy-done.1, f32[2,80,128]{2,1,0:T(8,128)S(1)} %collective-permute-done.row_second_ref, f32[2,80,128]{2,1,0:T(8,128)S(1)} %collective-permute-done.1.row_first_ref, ...), custom_call_target="tpu_custom_call" | custom-call | flops 5000000000 | bytes 6000000 | tf_op jit(solution)/shard_map/block_gradient/pallas_call | solution.py:319
  30.7 2.1 %block_terms.1 = (f32[4,4,2,7,8,128]{5,4,3,2,1,0:T(8,128)S(1)}, f32[4,4,2,7,8,128]{5,4,3,2,1,0:T(8,128)S(1)}) custom-call(bf16[256,512]{1,0:T(8,128)(2,1)S(1)} %get-tuple-element.67.feat_high, bf16[256,512]{1,0:T(8,128)(2,1)S(1)} %get-tuple-element.68.feat_low, bf16[3,18,32,256]{3,2,1,0:T(8,128)(2,1)S(1)} %get-tuple-element.112.grad_high_ref, ...), custom_call_target="tpu_custom_call" | custom-call | flops 1000000000 | bytes 1000000 | tf_op jit(solution)/shard_map/block_terms/pallas_call | solution.py:340
  34.4 2.9 %collective-permute-start.11 = (f32[4,2,7,16,128]{4,3,2,1,0:T(8,128)S(1)}, f32[4,2,7,16,128]{4,3,2,1,0:T(8,128)S(1)}, u32[]{:S(2)}, u32[]{:S(2)}) collective-permute-start(f32[4,2,7,16,128]{4,3,2,1,0:T(8,128)S(1)} %get-tuple-element.120), channel_id=1, source_target_pairs={{0,192},{1,7},{2,194},{3,5},{4,196},{5,3},{6,198},{7,1},{64,128},{... | collective-permute-start | bytes 1376264 | tf_op jit(solution)/shard_map/ppermute | solution.py:384
  38.8 4.6 %collective-permute-done.9.refs_5_ = f32[4,2,7,16,128]{4,3,2,1,0:T(8,128)S(1)} collective-permute-done((f32[4,2,7,16,128]{4,3,2,1,0:T(8,128)S(1)}, f32[4,2,7,16,128]{4,3,2,1,0:T(8,128)S(1)}, u32[]{:S(2)}, u32[]{:S(2)}) %collective-permute-start.9) | collective-permute-done | bytes 458784 | tf_op jit(solution)/shard_map/ppermute | solution.py:384
  43.3 2.3 %flow_adjoint.1 = f32[2,8,16,256]{3,2,1,0:T(8,128)} custom-call(f32[2,10,18,128]{3,2,1,0:T(8,128)S(1)} %get-tuple-element.98.cot_ref, f32[27,256,128]{2,1,0:T(8,128)S(1)} %bitcast.19), custom_call_target="tpu_custom_call" | custom-call | flops 2000000000 | bytes 5000000 | tf_op jit(solution)/shard_map/flow_adjoint/pallas_call | solution.py:352
  45.6 2.5 %collective-permute-done.11.refs_7_ = f32[4,2,7,16,128]{4,3,2,1,0:T(8,128)S(1)} collective-permute-done((f32[4,2,7,16,128]{4,3,2,1,0:T(8,128)S(1)}, f32[4,2,7,16,128]{4,3,2,1,0:T(8,128)S(1)}, u32[]{:S(2)}, u32[]{:S(2)}) %collective-permute-start.11) | collective-permute-done | bytes 458784 | tf_op jit(solution)/shard_map/ppermute | solution.py:384
  48.2 2.6 %collective-permute-done.6.refs_1_ = f32[4,2,7,8,128]{4,3,2,1,0:T(8,128)S(1)} collective-permute-done((f32[4,2,7,8,128]{4,3,2,1,0:T(8,128)S(1)}, f32[4,2,7,8,128]{4,3,2,1,0:T(8,128)S(1)}, u32[]{:S(2)}, u32[]{:S(2)}) %collective-permute-start.6) | collective-permute-done | bytes 229408 | tf_op jit(solution)/shard_map/ppermute | solution.py:384
  50.8 2.3 %collective-permute-done.8.refs_3_ = f32[4,2,7,8,128]{4,3,2,1,0:T(8,128)S(1)} collective-permute-done((f32[4,2,7,8,128]{4,3,2,1,0:T(8,128)S(1)}, f32[4,2,7,8,128]{4,3,2,1,0:T(8,128)S(1)}, u32[]{:S(2)}, u32[]{:S(2)}) %collective-permute-start.8) | collective-permute-done | bytes 229408 | tf_op jit(solution)/shard_map/ppermute | solution.py:384
  53.2 3.0 %collective-permute-start.12 = (f32[2,7,24,128]{3,2,1,0:T(8,128)S(1)}, f32[2,7,24,128]{3,2,1,0:T(8,128)S(1)}, u32[]{:S(2)}, u32[]{:S(2)}) collective-permute-start(f32[2,7,24,128]{3,2,1,0:T(8,128)S(1)} %get-tuple-element.107), channel_id=1, source_target_pairs={{0,4},{1,129},{2,6},{3,131},{4,0},{5,133},{6,2},{7,135},{64,68},{6... | collective-permute-start | bytes 516104 | tf_op jit(solution)/shard_map/ppermute | solution.py:384
  56.2 4.6 %collective-permute-start.13 = (f32[2,7,24,128]{3,2,1,0:T(8,128)S(1)}, f32[2,7,24,128]{3,2,1,0:T(8,128)S(1)}, u32[]{:S(2)}, u32[]{:S(2)}) collective-permute-start(f32[2,7,24,128]{3,2,1,0:T(8,128)S(1)} %get-tuple-element.108), channel_id=1, source_target_pairs={{0,2},{1,65},{2,0},{3,67},{4,6},{5,69},{6,4},{7,71},{64,66},{65,1}... | collective-permute-start | bytes 516104 | tf_op jit(solution)/shard_map/ppermute | solution.py:384
  60.8 5.2 %collective-permute-done.13.first = f32[2,7,24,128]{3,2,1,0:T(8,128)S(1)} collective-permute-done((f32[2,7,24,128]{3,2,1,0:T(8,128)S(1)}, f32[2,7,24,128]{3,2,1,0:T(8,128)S(1)}, u32[]{:S(2)}, u32[]{:S(2)}) %collective-permute-start.13) | collective-permute-done | bytes 172064 | tf_op jit(solution)/shard_map/ppermute | solution.py:384
  67.4 1.7 %collective-permute-start.15 = (f32[7,24,128]{2,1,0:T(8,128)S(1)}, f32[7,24,128]{2,1,0:T(8,128)S(1)}, u32[]{:S(2)}, u32[]{:S(2)}) collective-permute-start(f32[7,24,128]{2,1,0:T(8,128)S(1)} %get-tuple-element.110), channel_id=1, source_target_pairs={{0,56},{8,48},{16,40},{24,32},{32,24},{40,16},{48,8},{56,0},{1,57}... | collective-permute-start | bytes 258056 | tf_op jit(solution)/shard_map/ppermute | solution.py:442
  69.2 2.8 %feature_adjoint.1 = f32[2,16,32,128]{3,2,1,0:T(8,128)} custom-call(bf16[3,18,32,256]{3,2,1,0:T(8,128)(2,1)S(1)} %get-tuple-element.112.grad_high_ref, bf16[3,18,32,256]{3,2,1,0:T(8,128)(2,1)S(1)} %get-tuple-element.113.grad_low_ref, bf16[9,256,256]{2,1,0:T(8,128)(2,1)S(1)} %get-tuple-element.87.taps_high, bf16[9,256,256]{2,1,0:T(8,128)(2,1)S(1)} %get-tuple-element.88.taps_low), custom_call_target="tpu_custom_call" | custom-call | flops 2000000000 | bytes 5000000 | tf_op jit(solution)/shard_map/feature_adjoint/pallas_call | solution.py:352
  73.2 2.6 %collective-permute-start.17 = (f32[7,24,128]{2,1,0:T(8,128)S(1)}, f32[7,24,128]{2,1,0:T(8,128)S(1)}, u32[]{:S(2)}, u32[]{:S(2)}) collective-permute-start(f32[7,24,128]{2,1,0:T(8,128)S(1)} %add.20), channel_id=1, source_target_pairs={{0,32},{16,48},{32,0},{48,16},{1,33},{17,49},{33,1},{49,17},{2,34}... | collective-permute-start | bytes 258056 | tf_op jit(solution)/shard_map/ppermute | solution.py:383
  75.9 2.7 %collective-permute-start.18 = (f32[7,24,128]{2,1,0:T(8,128)S(1)}, f32[7,24,128]{2,1,0:T(8,128)S(1)}, u32[]{:S(2)}, u32[]{:S(2)}) collective-permute-start(f32[7,24,128]{2,1,0:T(8,128)S(1)} %add.20), channel_id=1, source_target_pairs={{0,48},{16,32},{32,16},{48,0},{1,49},{17,33},{33,17},{49,1},{2,50}... | collective-permute-start | bytes 258056 | tf_op jit(solution)/shard_map/ppermute | solution.py:383
  79.8 2.4 %collective-permute-done.18 = f32[7,24,128]{2,1,0:T(8,128)S(1)} collective-permute-done((f32[7,24,128]{2,1,0:T(8,128)S(1)}, f32[7,24,128]{2,1,0:T(8,128)S(1)}, u32[]{:S(2)}, u32[]{:S(2)}) %collective-permute-start.18) | collective-permute-done | bytes 86048 | tf_op jit(solution)/shard_map/ppermute | solution.py:383
  83.2 2.3 %collective-permute-start.19 = (f32[7,24,128]{2,1,0:T(8,128)S(1)}, f32[7,24,128]{2,1,0:T(8,128)S(1)}, u32[]{:S(2)}, u32[]{:S(2)}) collective-permute-start(f32[7,24,128]{2,1,0:T(8,128)S(1)} %add_add_fusion.own_ref), channel_id=1, source_target_pairs={{0,128},{64,192},{128,0},{192,64},{1,129},{65,193},{129,1},{193,65... | collective-permute-start | bytes 258056 | tf_op jit(solution)/shard_map/ppermute | solution.py:450
  85.4 1.9 %collective-permute-start.21 = (f32[7,24,128]{2,1,0:T(8,128)S(1)}, f32[7,24,128]{2,1,0:T(8,128)S(1)}, u32[]{:S(2)}, u32[]{:S(2)}) collective-permute-start(f32[7,24,128]{2,1,0:T(8,128)S(1)} %add_add_fusion.own_ref), channel_id=1, source_target_pairs={{0,192},{64,128},{128,64},{192,0},{1,193},{65,129},{129,65},{193,1... | collective-permute-start | bytes 258056 | tf_op jit(solution)/shard_map/ppermute | solution.py:450
  87.3 1.9 %collective-permute-done.19.two_ref = f32[7,24,128]{2,1,0:T(8,128)S(1)} collective-permute-done((f32[7,24,128]{2,1,0:T(8,128)S(1)}, f32[7,24,128]{2,1,0:T(8,128)S(1)}, u32[]{:S(2)}, u32[]{:S(2)}) %collective-permute-start.19) | collective-permute-done | bytes 86048 | tf_op jit(solution)/shard_map/ppermute | solution.py:450
  (50 shorter events, 18.2 us)
Async XLA Ops:
  6.8 10.3 %collective-permute-start = (f32[2,80,128]{2,1,0:T(8,128)}, f32[2,80,128]{2,1,0:T(8,128)S(1)}, u32[]{:S(2)}, u32[]{:S(2)}) collective-permute-start(f32[2,80,128]{2,1,0:T(8,128)} %bitcast.23), channel_id=1, source_target_pairs={{16,32},{32,16},{48,64},{64,48},{80,96},{96,80},{112,128},{128,112... | collective-permute-start | bytes 245768 | tf_op jit(solution)/shard_map/ppermute | solution.py:406
  13.6 4.7 %collective-permute-start.1 = (f32[2,80,128]{2,1,0:T(8,128)}, f32[2,80,128]{2,1,0:T(8,128)S(1)}, u32[]{:S(2)}, u32[]{:S(2)}) collective-permute-start(f32[2,80,128]{2,1,0:T(8,128)} %bitcast.22), channel_id=1, source_target_pairs={{0,16},{16,0},{32,48},{48,32},{64,80},{80,64},{96,112},{112,96},{1... | collective-permute-start | bytes 245768 | tf_op jit(solution)/shard_map/ppermute | solution.py:406
  18.4 6.6 %collective-permute-start.2 = (f32[2,56,128]{2,1,0:T(8,128)S(1)}, f32[2,56,128]{2,1,0:T(8,128)S(1)}, u32[]{:S(2)}, u32[]{:S(2)}) collective-permute-start(f32[2,56,128]{2,1,0:T(8,128)S(1)} %get-tuple-element.74), channel_id=1, source_target_pairs={{1,2},{2,1},{3,4},{4,3},{5,6},{6,5},{7,8},{8,7},{9,10},{10,9},{11,... | collective-permute-start | bytes 172040 | tf_op jit(solution)/shard_map/ppermute | solution.py:420
  19.1 5.9 %collective-permute-start.3 = (f32[2,56,128]{2,1,0:T(8,128)S(1)}, f32[2,56,128]{2,1,0:T(8,128)S(1)}, u32[]{:S(2)}, u32[]{:S(2)}) collective-permute-start(f32[2,56,128]{2,1,0:T(8,128)S(1)} %get-tuple-element.75), channel_id=1, source_target_pairs={{0,1},{1,0},{2,3},{3,2},{4,5},{5,4},{6,7},{7,6},{8,9},{9,8},{10,11... | collective-permute-start | bytes 172040 | tf_op jit(solution)/shard_map/ppermute | solution.py:420
  25.0 1.6 %copy-start.1 = (f32[2,16,32,128]{3,2,1,0:T(8,128)S(1)}, f32[2,16,32,128]{3,2,1,0:T(8,128)}, u32[]{:S(2)}) copy-start(f32[2,16,32,128]{3,2,1,0:T(8,128)} %feat_ref.7) | copy-start | bytes 1572868
  26.5 3.9 %collective-permute-start.4 = (f32[4,4,2,7,16,128]{5,4,3,2,1,0:T(8,128)S(1)}, f32[4,4,2,7,16,128]{5,4,3,2,1,0:T(8,128)S(1)}, u32[]{:S(2)}, u32[]{:S(2)}) collective-permute-start(f32[4,4,2,7,16,128]{5,4,3,2,1,0:T(8,128)S(1)} %get-tuple-element.86), channel_id=1, source_target_pairs={{0,1},{1,0},{2,3},{3,2},{4,5},{5,4},{6,7},{7,6},{8,9},{9,8},{10,11... | collective-permute-start | bytes 5505032 | tf_op jit(solution)/shard_map/ppermute | solution.py:428
  32.7 4.6 %collective-permute-start.5 = (f32[4,4,2,7,8,128]{5,4,3,2,1,0:T(8,128)S(1)}, f32[4,4,2,7,8,128]{5,4,3,2,1,0:T(8,128)S(1)}, u32[]{:S(2)}, u32[]{:S(2)}) collective-permute-start(f32[4,4,2,7,8,128]{5,4,3,2,1,0:T(8,128)S(1)} %get-tuple-element.95), channel_id=1, source_target_pairs={{0,1},{1,0},{2,3},{3,2},{4,5},{5,4},{6,7},{7,6},{8,9},{9,8},{10,11... | collective-permute-start | bytes 2752520 | tf_op jit(solution)/shard_map/ppermute | solution.py:433
  33.2 10.2 %collective-permute-start.9 = (f32[4,2,7,16,128]{4,3,2,1,0:T(8,128)S(1)}, f32[4,2,7,16,128]{4,3,2,1,0:T(8,128)S(1)}, u32[]{:S(2)}, u32[]{:S(2)}) collective-permute-start(f32[4,2,7,16,128]{4,3,2,1,0:T(8,128)S(1)} %get-tuple-element.122), channel_id=1, source_target_pairs={{0,128},{1,5},{2,130},{3,7},{4,132},{5,1},{6,134},{7,3},{64,192},{... | collective-permute-start | bytes 1376264 | tf_op jit(solution)/shard_map/ppermute | solution.py:384
  34.4 11.2 %collective-permute-start.10 = (f32[4,2,7,16,128]{4,3,2,1,0:T(8,128)S(1)}, f32[4,2,7,16,128]{4,3,2,1,0:T(8,128)S(1)}, u32[]{:S(2)}, u32[]{:S(2)}) collective-permute-start(f32[4,2,7,16,128]{4,3,2,1,0:T(8,128)S(1)} %get-tuple-element.121), channel_id=1, source_target_pairs={{0,64},{1,3},{2,66},{3,1},{4,68},{5,7},{6,70},{7,5},{64,0},{65,67}... | collective-permute-start | bytes 1376264 | tf_op jit(solution)/shard_map/ppermute | solution.py:384
  34.4 13.7 %collective-permute-start.11 = (f32[4,2,7,16,128]{4,3,2,1,0:T(8,128)S(1)}, f32[4,2,7,16,128]{4,3,2,1,0:T(8,128)S(1)}, u32[]{:S(2)}, u32[]{:S(2)}) collective-permute-start(f32[4,2,7,16,128]{4,3,2,1,0:T(8,128)S(1)} %get-tuple-element.120), channel_id=1, source_target_pairs={{0,192},{1,7},{2,194},{3,5},{4,196},{5,3},{6,198},{7,1},{64,128},{... | collective-permute-start | bytes 1376264 | tf_op jit(solution)/shard_map/ppermute | solution.py:384
  37.4 6.0 %copy-start.5 = (f32[3,3,3,256,128]{4,3,2,1,0:T(8,128)S(1)}, f32[3,3,3,256,128]{4,3,2,1,0:T(8,128)}, u32[]{:S(2)}) copy-start(f32[3,3,3,256,128]{4,3,2,1,0:T(8,128)} %param.8) | copy-start | bytes 10616836
  37.5 13.2 %collective-permute-start.6 = (f32[4,2,7,8,128]{4,3,2,1,0:T(8,128)S(1)}, f32[4,2,7,8,128]{4,3,2,1,0:T(8,128)S(1)}, u32[]{:S(2)}, u32[]{:S(2)}) collective-permute-start(f32[4,2,7,8,128]{4,3,2,1,0:T(8,128)S(1)} %get-tuple-element.125), channel_id=1, source_target_pairs={{0,128},{1,5},{2,130},{3,7},{4,132},{5,1},{6,134},{7,3},{64,192},{... | collective-permute-start | bytes 688136 | tf_op jit(solution)/shard_map/ppermute | solution.py:384
  38.8 12.0 %collective-permute-start.7 = (f32[4,2,7,8,128]{4,3,2,1,0:T(8,128)S(1)}, f32[4,2,7,8,128]{4,3,2,1,0:T(8,128)S(1)}, u32[]{:S(2)}, u32[]{:S(2)}) collective-permute-start(f32[4,2,7,8,128]{4,3,2,1,0:T(8,128)S(1)} %get-tuple-element.124), channel_id=1, source_target_pairs={{0,64},{1,3},{2,66},{3,1},{4,68},{5,7},{6,70},{7,5},{64,0},{65,67}... | collective-permute-start | bytes 688136 | tf_op jit(solution)/shard_map/ppermute | solution.py:384
  43.3 9.7 %collective-permute-start.8 = (f32[4,2,7,8,128]{4,3,2,1,0:T(8,128)S(1)}, f32[4,2,7,8,128]{4,3,2,1,0:T(8,128)S(1)}, u32[]{:S(2)}, u32[]{:S(2)}) collective-permute-start(f32[4,2,7,8,128]{4,3,2,1,0:T(8,128)S(1)} %get-tuple-element.123), channel_id=1, source_target_pairs={{0,192},{1,7},{2,194},{3,5},{4,196},{5,3},{6,198},{7,1},{64,128},{... | collective-permute-start | bytes 688136 | tf_op jit(solution)/shard_map/ppermute | solution.py:384
  53.2 7.6 %collective-permute-start.12 = (f32[2,7,24,128]{3,2,1,0:T(8,128)S(1)}, f32[2,7,24,128]{3,2,1,0:T(8,128)S(1)}, u32[]{:S(2)}, u32[]{:S(2)}) collective-permute-start(f32[2,7,24,128]{3,2,1,0:T(8,128)S(1)} %get-tuple-element.107), channel_id=1, source_target_pairs={{0,4},{1,129},{2,6},{3,131},{4,0},{5,133},{6,2},{7,135},{64,68},{6... | collective-permute-start | bytes 516104 | tf_op jit(solution)/shard_map/ppermute | solution.py:384
  56.2 9.8 %collective-permute-start.13 = (f32[2,7,24,128]{3,2,1,0:T(8,128)S(1)}, f32[2,7,24,128]{3,2,1,0:T(8,128)S(1)}, u32[]{:S(2)}, u32[]{:S(2)}) collective-permute-start(f32[2,7,24,128]{3,2,1,0:T(8,128)S(1)} %get-tuple-element.108), channel_id=1, source_target_pairs={{0,2},{1,65},{2,0},{3,67},{4,6},{5,69},{6,4},{7,71},{64,66},{65,1}... | collective-permute-start | bytes 516104 | tf_op jit(solution)/shard_map/ppermute | solution.py:384
  60.8 6.6 %collective-permute-start.14 = (f32[2,7,24,128]{3,2,1,0:T(8,128)S(1)}, f32[2,7,24,128]{3,2,1,0:T(8,128)S(1)}, u32[]{:S(2)}, u32[]{:S(2)}) collective-permute-start(f32[2,7,24,128]{3,2,1,0:T(8,128)S(1)} %get-tuple-element.109), channel_id=1, source_target_pairs={{0,6},{1,193},{2,4},{3,195},{4,2},{5,197},{6,0},{7,199},{64,70},{6... | collective-permute-start | bytes 516104 | tf_op jit(solution)/shard_map/ppermute | solution.py:384
  67.4 5.8 %collective-permute-start.15 = (f32[7,24,128]{2,1,0:T(8,128)S(1)}, f32[7,24,128]{2,1,0:T(8,128)S(1)}, u32[]{:S(2)}, u32[]{:S(2)}) collective-permute-start(f32[7,24,128]{2,1,0:T(8,128)S(1)} %get-tuple-element.110), channel_id=1, source_target_pairs={{0,56},{8,48},{16,40},{24,32},{32,24},{40,16},{48,8},{56,0},{1,57}... | collective-permute-start | bytes 258056 | tf_op jit(solution)/shard_map/ppermute | solution.py:442
  73.2 6.6 %collective-permute-start.17 = (f32[7,24,128]{2,1,0:T(8,128)S(1)}, f32[7,24,128]{2,1,0:T(8,128)S(1)}, u32[]{:S(2)}, u32[]{:S(2)}) collective-permute-start(f32[7,24,128]{2,1,0:T(8,128)S(1)} %add.20), channel_id=1, source_target_pairs={{0,32},{16,48},{32,0},{48,16},{1,33},{17,49},{33,1},{49,17},{2,34}... | collective-permute-start | bytes 258056 | tf_op jit(solution)/shard_map/ppermute | solution.py:383
  75.9 6.3 %collective-permute-start.18 = (f32[7,24,128]{2,1,0:T(8,128)S(1)}, f32[7,24,128]{2,1,0:T(8,128)S(1)}, u32[]{:S(2)}, u32[]{:S(2)}) collective-permute-start(f32[7,24,128]{2,1,0:T(8,128)S(1)} %add.20), channel_id=1, source_target_pairs={{0,48},{16,32},{32,16},{48,0},{1,49},{17,33},{33,17},{49,1},{2,50}... | collective-permute-start | bytes 258056 | tf_op jit(solution)/shard_map/ppermute | solution.py:383
  78.6 4.5 %collective-permute-start.16 = (f32[7,24,128]{2,1,0:T(8,128)S(1)}, f32[7,24,128]{2,1,0:T(8,128)S(1)}, u32[]{:S(2)}, u32[]{:S(2)}) collective-permute-start(f32[7,24,128]{2,1,0:T(8,128)S(1)} %add.20), channel_id=1, source_target_pairs={{0,16},{16,0},{32,48},{48,32},{1,17},{17,1},{33,49},{49,33},{2,18}... | collective-permute-start | bytes 258056 | tf_op jit(solution)/shard_map/ppermute | solution.py:383
  83.2 6.1 %collective-permute-start.19 = (f32[7,24,128]{2,1,0:T(8,128)S(1)}, f32[7,24,128]{2,1,0:T(8,128)S(1)}, u32[]{:S(2)}, u32[]{:S(2)}) collective-permute-start(f32[7,24,128]{2,1,0:T(8,128)S(1)} %add_add_fusion.own_ref), channel_id=1, source_target_pairs={{0,128},{64,192},{128,0},{192,64},{1,129},{65,193},{129,1},{193,65... | collective-permute-start | bytes 258056 | tf_op jit(solution)/shard_map/ppermute | solution.py:450
  85.4 4.5 %collective-permute-start.20 = (f32[7,24,128]{2,1,0:T(8,128)S(1)}, f32[7,24,128]{2,1,0:T(8,128)S(1)}, u32[]{:S(2)}, u32[]{:S(2)}) collective-permute-start(f32[7,24,128]{2,1,0:T(8,128)S(1)} %add_add_fusion.own_ref), channel_id=1, source_target_pairs={{0,64},{64,0},{128,192},{192,128},{1,65},{65,1},{129,193},{193,129... | collective-permute-start | bytes 258056 | tf_op jit(solution)/shard_map/ppermute | solution.py:450
  85.4 5.7 %collective-permute-start.21 = (f32[7,24,128]{2,1,0:T(8,128)S(1)}, f32[7,24,128]{2,1,0:T(8,128)S(1)}, u32[]{:S(2)}, u32[]{:S(2)}) collective-permute-start(f32[7,24,128]{2,1,0:T(8,128)S(1)} %add_add_fusion.own_ref), channel_id=1, source_target_pairs={{0,192},{64,128},{128,64},{192,0},{1,193},{65,129},{129,65},{193,1... | collective-permute-start | bytes 258056 | tf_op jit(solution)/shard_map/ppermute | solution.py:450
  (4 other events, 4.4 us)
